TPU v7x, 32 devices: a whole 2x2x4 slice. The times are simulated.
32 devices in a mesh: dp: 16 (over z, y, core), tensor: 2 (over x).
Axes of the slice: x: 2, y: 2, z: 4, core: 2. Of those that a mesh axis runs over, the one named last changes fastest.
Arguments:
- tokens: bfloat16 [8192, 2048], P('dp'), may hold values from -6 to 6
- w_query: float32 [2048, 1536], P('dp', 'tensor'), may hold values from -0.125 to 0.125
- w_keyval: float32 [2048, 768], P('dp'), may hold values from -0.125 to 0.125
- w_out: float32 [1536, 2048], P('tensor', 'dp'), may hold values from -2.5 to 2.5
- w_gateup: float32 [2048, 2, 5120], P('dp', None, 'tensor'), may hold values from -0.125 to 0.125
- w_down: float32 [5120, 2048], P('tensor', 'dp'), may hold values from -0.15625 to 0.15625
- attn_gain: float32 [2048], P('dp'), may hold values from 0.1 to 1.9
- ffn_gain: float32 [2048], P('dp'), may hold values from 0.1 to 1.9
- qk_gain: float32 [2, 64], P(None, 'dp'), may hold values from 1 to 2
- segments: int32 [8192], P('dp'), may hold values from 0 to 3, as said below
- positions: int32 [8192], P('dp'), may hold values from 0 to 8191, as said below
- cotangent: bfloat16 [8192, 2048], P('dp'), may hold values from -6 to 6
Outputs:
- output: bfloat16 [8192, 2048], P('dp')
- input_grad: bfloat16 [8192, 2048], P('dp')
- grad_query: float32 [2048, 1536], P('dp', 'tensor')
- grad_keyval: float32 [2048, 768], P('dp')
- grad_out: float32 [1536, 2048], P('tensor', 'dp')
- grad_gateup: float32 [2048, 2, 5120], P('dp', None, 'tensor')
- grad_down: float32 [5120, 2048], P('tensor', 'dp')
- grad_attn_gain: float32 [2048], P('dp')
- grad_ffn_gain: float32 [2048], P('dp')
- grad_qk_gain: float32 [2, 64], P(None, 'dp')
Inputs may be any that keep to these rules, and one draw needn't show every extreme that they name: `segments`: each sequence of 8192 tokens holds 4 documents, contiguous runs of tokens numbered 0, 1, 2 ... in order; the numbering starts again in each sequence. Within a document each token has the position of the one before plus one. A document's first position is below 1024 and at most 8192 minus its length, except the last document of each sequence, whose positions are the tokens' places in their sequence.
All inputs are finite; a program needn't handle non-finite values.
Results may differ from a plain program's by a relative error of at most 0.02.
The roundings to bfloat16 on the way count: a program that leaves them out, or rounds other values in their place, can miss the bound.
Values may be sent and summed in bfloat16 or wider, within the bound.
No kernel may reach another device: no remote copies, remote signals or barrier semaphores. Data moves between devices by JAX's collectives and lax.ppermute only.
A program may use at most 320 MiB of HBM per device.

v0:
```python
import math

import jax
import jax.numpy as jnp
from jax import lax
from jax.sharding import PartitionSpec as P

QH = 24
KVH = 6
HD = 64
WINDOW = 1024
SEQ_LEN = 8192


EPSILON = 1e-06
SCORE_SCALE = 0.125
MASKED = -1e30
ROPE_BASE = 10000.0


def from_behind(shard, axis, by):
    length = lax.axis_size(axis)
    pairs = [(i, i + by) for i in range(length) if 0 <= i + by < length]
    return lax.ppermute(shard, axis, pairs)


def rms_norm(values, weight):
    return values * lax.rsqrt(jnp.mean(values * values, axis=-1, keepdims=True) + EPSILON) * weight


def rotate(values, cos_table, sin_table):
    half_width = values.shape[-1] // 2
    first_half = values[..., :half_width]
    second_half = values[..., half_width:]
    return jnp.concatenate(
        [
            first_half * cos_table - second_half * sin_table,
            second_half * cos_table + first_half * sin_table,
        ],
        axis=-1,
    )


def angles_of(positions):
    half_width = HD // 2
    frequency = jnp.exp(
        jnp.arange(half_width, dtype=jnp.float32) * (-math.log(ROPE_BASE) / half_width)
    )
    phases = positions.astype(jnp.float32)[:, None] * frequency[None, :]
    return (jnp.cos(phases)[:, None, :], jnp.sin(phases)[:, None, :])


def swiglu(gate_up):
    return jax.nn.silu(gate_up[:, 0]) * gate_up[:, 1]


def shards(
    tokens,
    w_query,
    w_keyval,
    w_out,
    w_gateup,
    w_down,
    attn_gain,
    ffn_gain,
    qk_gain,
    segments,
    positions,
    cotangent,
):
    row_count = tokens.shape[0]
    bf16 = jnp.bfloat16
    f32 = jnp.float32
    residual = tokens.astype(f32)
    query_full, keyval_full, out_full, attn_weight, head_gains = (
        lax.all_gather(w_query.astype(bf16), "dp", axis=0, tiled=True),
        lax.all_gather(w_keyval.astype(bf16), "dp", axis=0, tiled=True),
        lax.all_gather(w_out.astype(bf16), "dp", axis=1, tiled=True),
        lax.all_gather(attn_gain.astype(bf16), "dp", axis=0, tiled=True),
        lax.all_gather(qk_gain.astype(bf16), "dp", axis=1, tiled=True),
    )
    attn_weight = attn_weight.astype(f32)
    gain_query = head_gains[0].astype(f32)
    gain_key = head_gains[1].astype(f32)
    local_heads = query_full.shape[1] // HD
    kv_width = keyval_full.shape[1] // 2
    cos_table, sin_table = angles_of(positions)

    def prepare(raw_heads, head_weight):
        return rotate(rms_norm(raw_heads, head_weight), cos_table, sin_table)

    normed, norm_pull = jax.vjp(rms_norm, residual, attn_weight)
    normed_low = normed.astype(bf16)
    query_raw = jnp.dot(normed_low, query_full, preferred_element_type=f32).reshape(
        row_count, local_heads, HD
    )
    keyval_raw = jnp.dot(normed_low, keyval_full, preferred_element_type=f32)
    key_raw = keyval_raw[:, :kv_width].reshape(row_count, KVH, HD)
    query_rot, query_pull = jax.vjp(prepare, query_raw, gain_query)
    key_rot, key_pull = jax.vjp(prepare, key_raw, gain_key)
    query_low = query_rot.astype(bf16)
    keyval_low = jnp.concatenate(
        [key_rot.reshape(row_count, kv_width), keyval_raw[:, kv_width:]], axis=1
    ).astype(bf16)
    marks = (segments + 1).astype(bf16)
    dp_index = lax.axis_index("dp")
    seq_devices = min(SEQ_LEN // row_count, lax.axis_size("dp"))
    own_sequence = dp_index // seq_devices
    reach_count = -(-WINDOW // row_count)
    halo_keyval = []
    halo_marks = []
    for step_back in range(reach_count, 0, -1):
        got_keyval, got_marks = from_behind((keyval_low, marks), "dp", step_back)
        same_sequence = ((dp_index - step_back) // seq_devices == own_sequence).astype(bf16)
        halo_keyval.append(got_keyval)
        halo_marks.append(got_marks * same_sequence)
    key_keyval = jnp.concatenate(halo_keyval + [keyval_low], axis=0)
    key_marks = jnp.concatenate(halo_marks + [marks], axis=0)
    key_count = key_keyval.shape[0]
    owner_head = (
        lax.axis_index("tensor") * local_heads + jnp.arange(local_heads, dtype=jnp.int32)
    ) // (QH // KVH)
    selector = (owner_head[:, None] == jnp.arange(KVH, dtype=jnp.int32)[None, :]).astype(bf16)
    key_heads = jnp.einsum(
        "kmd,lm->kld",
        key_keyval[:, :kv_width].reshape(key_count, KVH, HD),
        selector,
        preferred_element_type=f32,
    ).astype(bf16)
    value_heads = jnp.einsum(
        "kmd,lm->kld",
        key_keyval[:, kv_width:].reshape(key_count, KVH, HD),
        selector,
        preferred_element_type=f32,
    ).astype(bf16)
    block_rows = min(row_count, 512)
    key_offset = reach_count * row_count - WINDOW
    key_span = WINDOW + block_rows

    def block_scores(first_row):
        key_start = first_row + key_offset
        scores = (
            jnp.einsum("qld,kld->lqk", query_low, key_heads, preferred_element_type=f32)
            * SCORE_SCALE
        )
        distance = (first_row + jnp.arange(block_rows, dtype=jnp.int32))[:, None] - (
            key_start - reach_count * row_count + jnp.arange(key_span, dtype=jnp.int32)
        )[None, :]
        allowed = (distance >= 0) & (distance < WINDOW) & (marks[:, None] == key_marks[None, :])
        return jnp.where(allowed[None], scores, MASKED)

    first_row = 0
    key_start = first_row + key_offset
    scores = block_scores(first_row)
    row_max = jnp.max(scores, axis=-1, keepdims=True)
    scaled = jnp.exp(scores - row_max)
    row_total = jnp.sum(scaled, axis=-1, keepdims=True)
    probability = (scaled / row_total).astype(bf16)
    out_blocks = jnp.einsum("lqk,kld->qld", probability, value_heads, preferred_element_type=f32)
    lse_blocks = [row_max + jnp.log(row_total)]
    attended_low = out_blocks.reshape(row_count, local_heads * HD).astype(bf16)
    mid = residual + lax.psum(
        jnp.dot(attended_low, out_full, preferred_element_type=f32).astype(jnp.bfloat16), "tensor"
    ).astype(jnp.float32)
    gateup_full, down_full, ffn_weight = (
        lax.all_gather(w_gateup.astype(bf16), "dp", axis=0, tiled=True),
        lax.all_gather(w_down.astype(bf16), "dp", axis=1, tiled=True),
        lax.all_gather(ffn_gain.astype(bf16), "dp", axis=0, tiled=True),
    )
    ffn_weight = ffn_weight.astype(f32)
    normed2, norm2_pull = jax.vjp(rms_norm, mid, ffn_weight)
    normed2_low = normed2.astype(bf16)
    gate_up = jnp.einsum("td,dcf->tcf", normed2_low, gateup_full, preferred_element_type=f32)
    act, act_pull = jax.vjp(swiglu, gate_up)
    act_low = act.astype(bf16)
    result = mid + lax.psum(
        jnp.dot(act_low, down_full, preferred_element_type=f32).astype(jnp.bfloat16), "tensor"
    ).astype(jnp.float32)
    output = result.astype(bf16)
    grad_out_f = cotangent.astype(f32)
    gateup_full, down_full = (
        lax.all_gather(w_gateup.astype(bf16), "dp", axis=0, tiled=True),
        lax.all_gather(w_down.astype(bf16), "dp", axis=1, tiled=True),
    )
    d_act = jnp.dot(cotangent, down_full.T, preferred_element_type=f32)
    d_down = jnp.dot(act_low.T, cotangent, preferred_element_type=f32)
    (d_gate_up,) = act_pull(d_act)
    d_gate_up_low = d_gate_up.astype(bf16)
    d_gateup_w = jnp.einsum("td,tcf->dcf", normed2_low, d_gate_up_low, preferred_element_type=f32)
    d_normed2 = lax.psum(
        jnp.einsum("tcf,dcf->td", d_gate_up_low, gateup_full, preferred_element_type=f32).astype(
            jnp.bfloat16
        ),
        "tensor",
    ).astype(jnp.float32)
    d_mid_norm, d_ffn_weight = norm2_pull(d_normed2)
    d_mid = grad_out_f + d_mid_norm
    grad_gateup, grad_down, grad_ffn_gain = (
        lax.psum_scatter(d_gateup_w, "dp", scatter_dimension=0, tiled=True),
        lax.psum_scatter(d_down, "dp", scatter_dimension=1, tiled=True),
        lax.psum_scatter(d_ffn_weight, "dp", scatter_dimension=0, tiled=True),
    )
    query_full, keyval_full, out_full = (
        lax.all_gather(w_query.astype(bf16), "dp", axis=0, tiled=True),
        lax.all_gather(w_keyval.astype(bf16), "dp", axis=0, tiled=True),
        lax.all_gather(w_out.astype(bf16), "dp", axis=1, tiled=True),
    )
    d_mid_low = d_mid.astype(bf16)
    d_attended_low = jnp.dot(d_mid_low, out_full.T, preferred_element_type=f32).astype(bf16)
    d_attended_low = d_attended_low.reshape(row_count, local_heads, HD)
    d_out_w = jnp.dot(attended_low.T, d_mid_low, preferred_element_type=f32)
    d_key_heads = jnp.zeros((key_count, local_heads, HD), f32)
    d_value_heads = jnp.zeros((key_count, local_heads, HD), f32)
    d_query_blocks = []
    for block_number, first_row in enumerate(range(0, row_count, block_rows)):
        key_start = first_row + key_offset
        probability = jnp.exp(block_scores(first_row) - lse_blocks[block_number])
        d_prob = jnp.einsum("qld,kld->lqk", d_attended_low, value_heads, preferred_element_type=f32)
        row_delta = jnp.sum(d_prob * probability, axis=-1, keepdims=True)
        d_scores = (probability * (d_prob - row_delta)).astype(bf16)
        d_query_blocks.append(
            jnp.einsum("lqk,kld->qld", d_scores, key_heads, preferred_element_type=f32)
            * SCORE_SCALE
        )
        d_key_heads = d_key_heads.at[key_start : key_start + key_span].add(
            jnp.einsum("lqk,qld->kld", d_scores, query_low, preferred_element_type=f32)
            * SCORE_SCALE
        )
        d_value_heads = d_value_heads.at[key_start : key_start + key_span].add(
            jnp.einsum(
                "lqk,qld->kld", probability.astype(bf16), d_attended_low, preferred_element_type=f32
            )
        )
    selector_f = selector.astype(f32)
    d_keyval_all = jnp.concatenate(
        [
            jnp.einsum("kld,lm->kmd", d_key_heads, selector_f).reshape(key_count, kv_width),
            jnp.einsum("kld,lm->kmd", d_value_heads, selector_f).reshape(key_count, kv_width),
        ],
        axis=1,
    )
    own_grad = d_keyval_all[reach_count * row_count :]
    for step_back in range(1, reach_count + 1):
        piece_start = (reach_count - step_back) * row_count
        own_grad = own_grad + from_behind(
            d_keyval_all[piece_start : piece_start + row_count].astype(jnp.bfloat16),
            "dp",
            -step_back,
        ).astype(jnp.float32)
    d_query_raw, d_gain_query = query_pull(d_query_blocks[0])
    d_key_raw, d_gain_key = key_pull(own_grad[:, :kv_width].reshape(row_count, KVH, HD))
    d_query_low = d_query_raw.reshape(row_count, local_heads * HD).astype(bf16)
    d_keyval_low = jnp.concatenate(
        [d_key_raw.reshape(row_count, kv_width), own_grad[:, kv_width:]], axis=1
    ).astype(bf16)
    d_query_w = jnp.dot(normed_low.T, d_query_low, preferred_element_type=f32)
    d_keyval_w = jnp.dot(normed_low.T, d_keyval_low, preferred_element_type=f32)
    d_normed = lax.psum(
        (
            jnp.dot(d_query_low, query_full.T, preferred_element_type=f32)
            + jnp.dot(d_keyval_low, keyval_full.T, preferred_element_type=f32)
        ).astype(jnp.bfloat16),
        "tensor",
    ).astype(jnp.float32)
    d_input_norm, d_attn_weight = norm_pull(d_normed)
    input_grad = (d_mid + d_input_norm).astype(bf16)
    d_head_gains = jnp.stack([d_gain_query, d_gain_key], axis=0)
    grad_query, grad_keyval, grad_out, grad_attn_gain, grad_heads = (
        lax.psum_scatter(d_query_w, "dp", scatter_dimension=0, tiled=True),
        lax.psum_scatter(d_keyval_w, "dp", scatter_dimension=0, tiled=True),
        lax.psum_scatter(d_out_w, "dp", scatter_dimension=1, tiled=True),
        lax.psum_scatter(d_attn_weight, "dp", scatter_dimension=0, tiled=True),
        lax.psum_scatter(d_head_gains, "dp", scatter_dimension=1, tiled=True),
    )
    grad_keyval, grad_heads = (
        lax.psum(grad_keyval.astype(jnp.bfloat16), "tensor").astype(jnp.float32),
        lax.psum(grad_heads.astype(jnp.bfloat16), "tensor").astype(jnp.float32),
    )
    return (
        output,
        input_grad,
        grad_query,
        grad_keyval,
        grad_out,
        grad_gateup,
        grad_down,
        grad_attn_gain,
        grad_ffn_gain,
        grad_heads,
    )


def solution(mesh):
    in_specs = (
        P("dp", None),
        P("dp", "tensor"),
        P("dp", None),
        P("tensor", "dp"),
        P("dp", None, "tensor"),
        P("tensor", "dp"),
        P("dp"),
        P("dp"),
        P(None, "dp"),
        P("dp"),
        P("dp"),
        P("dp", None),
    )
    out_specs = (
        P("dp", None),
        P("dp", None),
        P("dp", "tensor"),
        P("dp", None),
        P("tensor", "dp"),
        P("dp", None, "tensor"),
        P("tensor", "dp"),
        P("dp"),
        P("dp"),
        P(None, "dp"),
    )
    return jax.shard_map(shards, mesh=mesh, in_specs=in_specs, out_specs=out_specs, check_vma=False)
```

profile of v0, /device:TPU:0, one launch (start us, length us, event | category | flops | bytes accessed | tf_op | source)
XLA Modules:
  0.0 1708.4 jit_solution(9634610463161028483)
XLA Ops:
  7.2 1.8 convert_element_type.186
  9.1 1.7 convert_element_type.196
  11.6 2.3 collective-permute-start.3
  14.0 4.4 collective-permute-start.2
  18.4 1.7 convert_element_type.205
  22.7 19.4 %all-gather.1 = bf16[16,4,2]{1,2,0:T(2,128)(2,1)S(1)} all-gather(bf16[1,4,2]{1,2,0:T(2,128)(2,1)S(1)} %convert_bitcast_fusion.1), channel_id=1, replica_groups=mesh['dp'=16,'tensor'=2] {'dp'}, dimensions={0}, use_global_device_ids=true | all-gather | bytes 272 | tf_op jit(solution)/shard_map/all_gather | solution.py:80
  42.2 17.3 %all-gather = bf16[16,1,128]{2,1,0:T(2,128)(2,1)S(1)} all-gather(bf16[1,1,128]{2,1,0:T(2,128)(2,1)S(1)} %convert_bitcast_fusion.2), channel_id=1, replica_groups=mesh['dp'=16,'tensor'=2] {'dp'}, dimensions={0}, use_global_device_ids=true | all-gather | bytes 4352 | tf_op jit(solution)/shard_map/all_gather | solution.py:79
  60.1 1.9 fusion.42
  61.9 3.7 fusion.94
  70.1 1.9 copy.58
  72.0 1.9 pad_maximum_fusion.1
  73.9 3.1 collective-permute-start.1
  77.0 2.8 collective-permute-start
  79.8 35.2 %all-gather.11.cloned.1.call-done = bf16[2048,768]{1,0:T(8,128)(2,1)} async-done(((bf16[128,768]{1,0:T(8,128)(2,1)}), bf16[2048,768]{1,0:T(8,128)(2,1)}) %all-gather.11.cloned.1.call-update) | async-done | bytes 3145744 | tf_op jit(solution)/shard_map/all_gather | solution.py:76
  115.0 3.8 fusion.92
  122.0 1.6 fusion.99
  123.7 1.7 copy.59
  125.4 2.4 copy.62
  127.8 4.3 fusion.38
  132.1 2.7 fusion.37
  134.8 20.8 %fusion.100 = (f32[12,512]{1,0:T(8,128)S(1)}, f32[12,512,1536]{2,1,0:T(8,128)}) fusion(bf16[1536,12,64]{0,1,2:T(8,128)(2,1)} %fusion.38, bf16[512,12,32]{0,2,1:T(8,128)(2,1)S(1)} %copy-done.14, bf16[512,12,32]{0,2,1:T(8,128)(2,1)S(1)} %copy-done.12, pred[512,1536]{1,0:T(8,128)(4,1)S(1)} %copy-done.11), kind=kOutput, calls=%fused_computation.174 | convolution fusion | flops 1237837824 | bytes 41705472 | tf_op jit(solution)/shard_map/qld,kld->lqk/dot_general | solution.py:143
  155.6 16.6 fusion
  172.2 15.3 fusion.58
  187.6 5.3 convolution_convert_fusion.2
  193.0 3.3 copy.105
  197.3 19.6 %all-gather.2 = bf16[16,1,128]{2,1,0:T(2,128)(2,1)S(1)} all-gather(bf16[1,1,128]{2,1,0:T(2,128)(2,1)S(1)} %convert_bitcast_fusion), channel_id=1, replica_groups=mesh['dp'=16,'tensor'=2] {'dp'}, dimensions={0}, use_global_device_ids=true | all-gather | bytes 4352 | tf_op jit(solution)/shard_map/all_gather | solution.py:168
  217.0 38.6 %all-reduce.15.cloned.1.call-done = bf16[512,2048]{1,0:T(8,128)(2,1)} async-done(((bf16[512,2048]{1,0:T(8,128)(2,1)}), bf16[512,2048]{1,0:T(8,128)(2,1)}) %all-reduce.15.cloned.1.call-update) | async-done | bytes 2097168 | tf_op jit(solution)/shard_map/psum | solution.py:162
  255.5 2.3 multiply_reduce_fusion.1
  257.9 108.5 %all-gather.15.cloned.1.call-done = bf16[2048,2,2560]{2,0,1:T(8,128)(2,1)} async-done(((bf16[128,2,2560]{2,0,1:T(8,128)(2,1)}), bf16[2048,2,2560]{2,0,1:T(8,128)(2,1)}) %all-gather.15.cloned.1.call-update) | async-done | bytes 20971536 | tf_op jit(solution)/shard_map/all_gather | solution.py:166
  366.4 18.6 %fusion.87 = f32[512,2,2560]{2,0,1:T(8,128)} fusion(bf16[2048,2,2560]{2,0,1:T(8,128)(2,1)} %all-gather.15.cloned.1.call-done, bf16[512,2048]{1,0:T(8,128)(2,1)} %all-reduce.15.cloned.1.call-done, bf16[512,2048]{1,0:T(8,128)(2,1)S(1)} %copy-done, f32[2048]{0:T(1024)S(1)} %bitcast.137, f32[512]{0:T(512)S(1)} %fusion.79), kind=kOutput, calls=%fused_computation.168 | convolution fusion | flops 10743709696 | bytes 35661824 | tf_op jit(solution)/shard_map/td,dcf->tcf/dot_general | solution.py:173
  385.0 75.1 %all-gather.17.cloned.1.call-done = bf16[2560,2048]{1,0:T(8,128)(2,1)} async-done(((bf16[2560,128]{1,0:T(8,128)(2,1)}), bf16[2560,2048]{1,0:T(8,128)(2,1)}) %all-gather.17.cloned.1.call-update) | async-done | bytes 10485776 | tf_op jit(solution)/shard_map/all_gather | solution.py:167
  460.0 15.6 multiply_bitcast_fusion
  475.7 19.2 %bitcast_convert_fusion = bf16[512,2048]{1,0:T(8,128)(2,1)} fusion(bf16[2048,2,2560]{2,0,1:T(8,128)(2,1)} %all-gather.15.cloned.1.call-done, f32[512,1,2560]{2,0,1:T(8,128)} %get-tuple-element.95, f32[512,1,2560]{2,0,1:T(8,128)} %get-tuple-element.94), kind=kOutput, calls=%fused_computation.55 | convolution fusion | flops 10743709696 | bytes 33554432 | tf_op jit(solution)/shard_map/tcf,dcf->td/dot_general | solution.py:191
  494.9 11.0 reduce-scatter.9.cloned.1.call-start
  505.9 50.2 %all-reduce.17.cloned.1.call-done = bf16[512,2048]{1,0:T(8,128)(2,1)} async-done(((bf16[512,2048]{1,0:T(8,128)(2,1)}), bf16[512,2048]{1,0:T(8,128)(2,1)}) %all-reduce.17.cloned.1.call-update) | async-done | bytes 2097168 | tf_op jit(solution)/shard_map/psum | solution.py:190
  556.1 4.7 fusion.21
  560.9 5.7 convolution_convert_fusion.4
  568.0 16.6 fusion.28
  584.6 31.9 %multiply_reduce_fusion = (f32[12,512]{1,0:T(8,128)S(1)}, f32[12,512,1536]{2,1,0:T(8,128)}) fusion(f32[12,512,1536]{2,1,0:T(8,128)} %get-tuple-element.116, f32[12,512]{1,0:T(8,128)S(1)} %log_add_fusion, bf16[512,12,64]{0,2,1:T(8,128)(2,1)S(1)} %bitcast.120, bf16[1536,12,64]{0,1,2:T(8,128)(2,1)} %fusion.37), kind=kOutput, calls=%fused_computation.1 | convolution fusion | flops 1236264960 | bytes 78692352 | tf_op jit(solution)/shard_map/qld,kld->lqk/dot_general | solution.py:218
  618.0 2.8 copy.73
  620.8 31.5 %multiply_convert_fusion = bf16[12,512,1536]{2,1,0:T(8,128)(2,1)} fusion(f32[12,512,1536]{2,1,0:T(8,128)} %get-tuple-element.118, f32[12,512,1536]{2,1,0:T(8,128)} %get-tuple-element.116, f32[12,512]{1,0:T(8,128)S(1)} %get-tuple-element.117, f32[12,512]{1,0:T(8,128)S(1)} %log_add_fusion), kind=kLoop, calls=%fused_computation | loop fusion | flops 37748736 | bytes 94420992 | tf_op jit(solution)/shard_map/convert_element_type | solution.py:220
  652.3 9.7 multiply_bitcast_fusion.1
  669.7 26.0 %collective-permute-done.5 = bf16[512,768]{0,1:T(8,128)(2,1)S(1)} collective-permute-done((bf16[512,768]{0,1:T(8,128)(2,1)S(1)}, bf16[512,768]{0,1:T(8,128)(2,1)S(1)}, u32[]{:S(2)}, u32[]{:S(2)}) %collective-permute-start.5) | collective-permute-done | bytes 786464 | tf_op jit(solution)/shard_map/ppermute | solution.py:24
  697.6 4.8 fusion.66
  702.5 10.7 convolution_convert_fusion.3
  713.2 10.4 multiply_bitcast_fusion.2
  726.9 1.8 fusion.101
  729.0 3.2 add_convert_fusion.1
  732.1 55.6 %reduce-scatter.9.cloned.1.call-done = f32[128,768]{1,0:T(8,128)} async-done(((f32[2048,768]{1,0:T(8,128)}), f32[128,768]{1,0:T(8,128)}) %reduce-scatter.9.cloned.1.call-update) | async-done | bytes 393232 | tf_op jit(solution)/shard_map/reduce_scatter | solution.py:270
  787.8 1.7 convert_element_type.232
  789.5 23.1 %fusion.65 = f32[2048,2,2560]{2,0,1:T(8,128)} fusion(f32[512,1,2560]{2,0,1:T(8,128)} %get-tuple-element.95, f32[512,1,2560]{2,0,1:T(8,128)} %get-tuple-element.94, bf16[512,2048]{1,0:T(8,128)(2,1)} %all-reduce.15.cloned.1.call-done, bf16[512,2048]{1,0:T(8,128)(2,1)S(1)} %copy-done, f32[2048]{0:T(1024)S(1)} %bitcast.140, f32[512]{0:T(512)S(1)} %fusion.79), kind=kOutput, calls=%fused_computation.116 | convolution fusion | flops 10748952576 | bytes 56633344 | tf_op jit(solution)/shard_map/td,tcf->dcf/dot_general | solution.py:189
  813.4 7.9 fusion.61
  821.3 4.7 fusion.90
  826.1 12.2 fusion.102
  840.3 63.1 %all-reduce.19.cloned.1.call-done = (bf16[512,2048]{1,0:T(8,128)(2,1)}, bf16[512,2048]{1,0:T(8,128)(2,1)}, bf16[128,768]{1,0:T(8,128)(2,1)}) async-done(((bf16[512,2048]{1,0:T(8,128)(2,1)}, bf16[512,2048]{1,0:T(8,128)(2,1)}, bf16[128,768]{1,0:T(8,128)(2,1)}), (bf16[512,2048]{1,0:T(8,128)(2,1)}, bf16[512,2048]{1,0:T(8,128)(2,1)}, bf16[128,768]{1,0:T(8,128)(2,1)})) %all-reduce.19.cloned.1.call-update) | async-done | bytes 4390928 | tf_op jit(solution)/shard_map/psum | solution.py:176
  903.4 3.4 fusion.22
  906.8 61.2 %all-reduce.9 = (f32[2048]{0:T(1024)S(1)}, f32[2048]{0:T(1024)S(1)}, bf16[2,64]{1,0:T(2,128)(2,1)S(1)}) all-reduce(f32[2048]{0:T(1024)S(1)} %get-tuple-element.82, f32[2048]{0:T(1024)S(1)} %copy-done.39, f32[2,64]{1,0:T(2,128)S(1)} %pad_maximum_fusion.10), channel_id=7, replica_groups=mesh['dp'=16,'tensor'=2] {'dp'}, use_global_device_ids=true, to_apply=%region_22.23.clone | all-reduce | flops 4224 | bytes 33536
  968.7 4.9 psum.47
  976.1 8.0 fusion.25
  984.2 323.8 %reduce-scatter.13.cloned.1.call-done = f32[128,2,2560]{2,0,1:T(8,128)} async-done(((f32[2048,2,2560]{2,0,1:T(8,128)}), f32[128,2,2560]{2,0,1:T(8,128)}) %reduce-scatter.13.cloned.1.call-update) | async-done | bytes 2621456 | tf_op jit(solution)/shard_map/reduce_scatter | solution.py:199
  1308.0 5.3 copy.75
  1313.2 84.2 %reduce-scatter.11.cloned.1.call-done = f32[768,128]{1,0:T(8,128)} async-done(((f32[768,2048]{1,0:T(8,128)}), f32[768,128]{1,0:T(8,128)}) %reduce-scatter.11.cloned.1.call-update) | async-done | bytes 393232 | tf_op jit(solution)/shard_map/reduce_scatter | solution.py:271
  1397.4 88.9 %reduce-scatter.7.cloned.1.call-done = f32[128,768]{1,0:T(8,128)} async-done(((f32[2048,768]{1,0:T(8,128)}), f32[128,768]{1,0:T(8,128)}) %reduce-scatter.7.cloned.1.call-update) | async-done | bytes 393232 | tf_op jit(solution)/shard_map/reduce_scatter | solution.py:269
  1486.4 215.3 %reduce-scatter.15.cloned.1.call-done = f32[2560,128]{1,0:T(8,128)} async-done(((f32[2560,2048]{1,0:T(8,128)}), f32[2560,128]{1,0:T(8,128)}) %reduce-scatter.15.cloned.1.call-update) | async-done | bytes 1310736 | tf_op jit(solution)/shard_map/reduce_scatter | solution.py:200
  (205 shorter events, 33.0 us)
Async XLA Ops:
  7.2 14.4 copy-start
  7.2 15.5 copy-start.50
  7.2 54.7 %all-gather.9.cloned.1.call-start = ((), (), s32[]{:S(2)}) async-start(), calls=%async_computation.5 | async-start | bytes 3342336 | tf_op jit(solution)/shard_map/all_gather | solution.py:77
  9.1 105.9 %all-gather.11.cloned.1.call-start = ((), (), s32[]{:S(2)}) async-start(), calls=%async_computation.6 | async-start | bytes 3342336 | tf_op jit(solution)/shard_map/all_gather | solution.py:76
  10.9 176.7 %all-gather.13.cloned.1.call-start = ((), (), s32[]{:S(2)}) async-start(), calls=%async_computation.7 | async-start | bytes 3342336 | tf_op jit(solution)/shard_map/all_gather | solution.py:78
  11.6 48.4 %collective-permute-start.3 = (bf16[512]{0:T(512)(128)(2,1)S(1)}, bf16[512]{0:T(512)(128)(2,1)S(1)}, u32[]{:S(2)}, u32[]{:S(2)}) collective-permute-start(bf16[512]{0:T(512)(128)(2,1)S(1)} %add_convert_fusion.7), channel_id=1, source_target_pairs={{0,2},{2,4},{4,6},{6,8},{8,10},{10,12},{12,14},{14,16},{16,18},{18... | collective-permute-start | bytes 3080 | tf_op jit(solution)/shard_map/ppermute | solution.py:24
  14.0 46.1 %collective-permute-start.2 = (bf16[512]{0:T(512)(128)(2,1)S(1)}, bf16[512]{0:T(512)(128)(2,1)S(1)}, u32[]{:S(2)}, u32[]{:S(2)}) collective-permute-start(bf16[512]{0:T(512)(128)(2,1)S(1)} %add_convert_fusion.7), channel_id=1, source_target_pairs={{0,4},{2,6},{4,8},{6,10},{8,12},{10,14},{12,16},{14,18},{16,20},{1... | collective-permute-start | bytes 3080 | tf_op jit(solution)/shard_map/ppermute | solution.py:24
  20.1 235.4 %all-reduce.15.cloned.1.call-start = ((), (), s32[]{:S(2)}) async-start(), calls=%async_computation.8 | async-start | bytes 4194304 | tf_op jit(solution)/shard_map/psum | solution.py:162
  20.3 111.8 %copy-start.42 = (s32[12]{0:T(128)}, s32[12]{0:T(128)S(1)}, u32[]{:S(2)}) copy-start(s32[12]{0:T(128)S(1)} %and_select_fusion) | copy-start | bytes 148
  22.7 92.3 %copy-start.37 = (f32[512]{0:T(512)}, f32[512]{0:T(512)S(1)}, u32[]{:S(2)}) copy-start(f32[512]{0:T(512)S(1)} %fusion.78) | copy-start | bytes 6148
  42.2 26.8 %copy-start.44 = (f32[64]{0:T(128)}, f32[64]{0:T(128)S(1)}, u32[]{:S(2)}) copy-start(f32[64]{0:T(128)S(1)} %get-tuple-element.114) | copy-start | bytes 772
  42.2 76.9 %copy-start.48 = (f32[64]{0:T(128)}, f32[64]{0:T(128)S(1)}, u32[]{:S(2)}) copy-start(f32[64]{0:T(128)S(1)} %get-tuple-element.113) | copy-start | bytes 772
  59.9 59.7 %copy-start.18 = (f32[512,32]{0,1:T(8,128)}, f32[512,32]{0,1:T(8,128)S(1)}, u32[]{:S(2)}) copy-start(f32[512,32]{0,1:T(8,128)S(1)} %get-tuple-element.111) | copy-start | bytes 196612
  59.9 59.7 %copy-start.20 = (f32[512,32]{0,1:T(8,128)}, f32[512,32]{0,1:T(8,128)S(1)}, u32[]{:S(2)}) copy-start(f32[512,32]{0,1:T(8,128)S(1)} %get-tuple-element.112) | copy-start | bytes 196612
  60.0 55.0 %copy-start.26 = (f32[16,1,128]{2,1,0:T(1,128)}, f32[16,1,128]{2,1,0:T(1,128)S(1)}, u32[]{:S(2)}) copy-start(f32[16,1,128]{2,1,0:T(1,128)S(1)} %convert_element_type.238) | copy-start | bytes 24580
  68.1 5.8 copy-start.6
  73.9 46.8 %collective-permute-start.1 = (bf16[512,768]{1,0:T(8,128)(2,1)}, bf16[512,768]{1,0:T(8,128)(2,1)}, u32[]{:S(2)}, u32[]{:S(2)}) collective-permute-start(bf16[512,768]{1,0:T(8,128)(2,1)} %pad_maximum_fusion.1), channel_id=1, source_target_pairs={{0,2},{2,4},{4,6},{6,8},{8,10},{10,12},{12,14},{14,16},{16,18},{18... | collective-permute-start | bytes 2359304 | tf_op jit(solution)/shard_map/ppermute | solution.py:24
  77.0 43.7 %collective-permute-start = (bf16[512,768]{1,0:T(8,128)(2,1)}, bf16[512,768]{1,0:T(8,128)(2,1)S(1)}, u32[]{:S(2)}, u32[]{:S(2)}) collective-permute-start(bf16[512,768]{1,0:T(8,128)(2,1)} %pad_maximum_fusion.1), channel_id=1, source_target_pairs={{0,4},{2,6},{4,8},{6,10},{8,12},{10,14},{12,16},{14,18},{16,20},{1... | collective-permute-start | bytes 2359304 | tf_op jit(solution)/shard_map/ppermute | solution.py:24
  118.8 1.9 copy-start.2
  119.1 1.6 copy-start.30
  119.1 1.6 copy-start.16
  119.1 1.6 copy-start.28
  132.1 2.7 copy-start.11
  132.1 2.7 copy-start.12
  132.1 2.7 copy-start.14
  155.6 16.6 copy-start.9
  187.5 5.3 copy-start.25
  192.9 3.4 copy-start.24
  192.9 4.4 copy-start.53
  192.9 173.5 %all-gather.15.cloned.1.call-start = ((), (), s32[]{:S(2)}) async-start(), calls=%async_computation.9 | async-start | bytes 22282240 | tf_op jit(solution)/shard_map/all_gather | solution.py:166
  196.3 263.8 %all-gather.17.cloned.1.call-start = ((), (), s32[]{:S(2)}) async-start(), calls=%async_computation.10 | async-start | bytes 11141120 | tf_op jit(solution)/shard_map/all_gather | solution.py:167
  197.3 358.9 %all-reduce.17.cloned.1.call-start = ((), (), s32[]{:S(2)}) async-start(), calls=%async_computation.11 | async-start | bytes 4194304 | tf_op jit(solution)/shard_map/psum | solution.py:190
  494.9 292.9 %reduce-scatter.9.cloned.1.call-start = ((), (), s32[]{:S(2)}) async-start(), calls=%async_computation.13 | async-start | bytes 6684672 | tf_op jit(solution)/shard_map/reduce_scatter | solution.py:270
  556.1 4.7 copy-start.8
  556.1 4.7 copy-start.10
  556.1 4.7 copy-start.17
  560.9 5.7 copy-start.46
  584.6 32.0 %copy-start.4 = (bf16[1536,12,64]{0,2,1:T(8,128)(2,1)S(1)}, bf16[1536,12,64]{0,2,1:T(8,128)(2,1)}, u32[]{:S(2)}) copy-start(bf16[1536,12,64]{0,2,1:T(8,128)(2,1)} %fusion.28) | copy-start | bytes 7077892
  584.6 32.0 %copy-start.43 = (s32[12]{0:T(128)S(1)}, s32[12]{0:T(128)}, u32[]{:S(2)}) copy-start(s32[12]{0:T(128)} %copy-done.42) | copy-start | bytes 148
  620.8 31.5 %copy-start.13 = (bf16[512,12,32]{0,2,1:T(8,128)(2,1)S(1)}, bf16[512,12,32]{0,2,1:T(8,128)(2,1)}, u32[]{:S(2)}) copy-start(bf16[512,12,32]{0,2,1:T(8,128)(2,1)} %get-tuple-element.105) | copy-start | bytes 1179652
  620.8 31.5 %copy-start.15 = (bf16[512,12,32]{0,2,1:T(8,128)(2,1)S(1)}, bf16[512,12,32]{0,2,1:T(8,128)(2,1)}, u32[]{:S(2)}) copy-start(bf16[512,12,32]{0,2,1:T(8,128)(2,1)} %get-tuple-element.106) | copy-start | bytes 1179652
  663.4 1.7 copy-start.5
  665.5 4.2 collective-permute-start.4
  666.8 29.4 %copy-start.19 = (f32[512,32]{0,1:T(8,128)S(1)}, f32[512,32]{0,1:T(8,128)}, u32[]{:S(2)}) copy-start(f32[512,32]{0,1:T(8,128)} %copy-done.18) | copy-start | bytes 196612
  666.8 29.4 %copy-start.21 = (f32[512,32]{0,1:T(8,128)S(1)}, f32[512,32]{0,1:T(8,128)}, u32[]{:S(2)}) copy-start(f32[512,32]{0,1:T(8,128)} %copy-done.20) | copy-start | bytes 196612
  666.8 28.9 %collective-permute-start.5 = (bf16[512,768]{0,1:T(8,128)(2,1)S(1)}, bf16[512,768]{0,1:T(8,128)(2,1)S(1)}, u32[]{:S(2)}, u32[]{:S(2)}) collective-permute-start(bf16[512,768]{0,1:T(8,128)(2,1)S(1)} %get-tuple-element.100), channel_id=1, source_target_pairs={{4,0},{6,2},{8,4},{10,6},{12,8},{14,10},{16,12},{18,14},{20,16},{2... | collective-permute-start | bytes 2359304 | tf_op jit(solution)/shard_map/ppermute | solution.py:24
  696.1 1.5 copy-start.27
  696.1 1.5 copy-start.38
  697.6 4.8 copy-start.22
  702.4 201.0 %all-reduce.19.cloned.1.call-start = ((), (), s32[]{:S(2)}) async-start(), calls=%async_computation.17 | async-start | bytes 8781824 | tf_op jit(solution)/shard_map/psum | solution.py:176
  702.5 10.7 copy-start.1
  723.6 1.5 copy-start.3
  723.6 1.4 copy-start.29
  723.6 2.1 copy-start.31
  725.0 1.9 copy-start.52
  726.9 1.9 copy-start.23
  726.9 2.0 copy-start.51
  789.5 518.5 %reduce-scatter.13.cloned.1.call-start = ((), (), s32[]{:S(2)}) async-start(), calls=%async_computation.15 | async-start | bytes 44564480 | tf_op jit(solution)/shard_map/reduce_scatter | solution.py:199
  812.7 584.7 %reduce-scatter.11.cloned.1.call-start = ((), (), s32[]{:S(2)}) async-start(), calls=%async_computation.14 | async-start | bytes 6684672 | tf_op jit(solution)/shard_map/reduce_scatter | solution.py:271
  821.3 665.1 %reduce-scatter.7.cloned.1.call-start = ((), (), s32[]{:S(2)}) async-start(), calls=%async_computation.12 | async-start | bytes 6684672 | tf_op jit(solution)/shard_map/reduce_scatter | solution.py:269
  826.1 875.5 %reduce-scatter.15.cloned.1.call-start = ((), (), s32[]{:S(2)}) async-start(), calls=%async_computation.16 | async-start | bytes 22282240 | tf_op jit(solution)/shard_map/reduce_scatter | solution.py:200
  838.4 68.4 %copy-start.39 = (f32[2048]{0:T(1024)S(1)}, f32[2048]{0:T(1024)}, u32[]{:S(2)}) copy-start(f32[2048]{0:T(1024)} %get-tuple-element.80) | copy-start | bytes 24580
  838.4 137.7 %copy-start.41 = (f32[512]{0:T(512)S(1)}, f32[512]{0:T(512)}, u32[]{:S(2)}) copy-start(f32[512]{0:T(512)} %copy-done.40) | copy-start | bytes 6148
  903.4 72.0 %copy-start.34 = (bf16[128,768]{1,0:T(8,128)(2,1)S(1)}, bf16[128,768]{1,0:T(8,128)(2,1)}, u32[]{:S(2)}) copy-start(bf16[128,768]{1,0:T(8,128)(2,1)} %get-tuple-element.93) | copy-start | bytes 589828
  (10 other events, 10.0 us)
Sparse Core Ops, SparseCore 0:
  10.9 47.9 all-gather.8
  61.7 53.2 all-gather.10
  117.2 46.8 all-gather.12
  193.0 62.4 all-reduce.14
  257.6 108.7 all-gather.14
  369.2 90.7 all-gather.16
  495.0 61.0 all-reduce.16
  702.6 85.1 reduce-scatter.8
  791.3 112.0 all-reduce.18
  908.1 399.8 reduce-scatter.12
  1313.0 84.3 reduce-scatter.10
  1401.8 84.5 reduce-scatter.6
  1491.6 209.9 reduce-scatter.14
where the time goes:
time: 1720 us; the launch traced here: 1710 us
  waiting for transfers between devices  1170 us (68%)
  matrix products  255 us (15%)
  blocking collectives  122 us (7%)
  other arithmetic  89.3 us (5%)
  local copies, waits for them, and re-layouts  32.1 us (2%)
  starting transfers between devices  26.9 us (2%)
    reduce_scatter x1, waiting for transfers between devices, shards(): lax.psum_scatter(d_gateup_w, 'dp', scatter_dimension=0, tiled=True)  324 us
    reduce_scatter x1, waiting for transfers between devices, shards(): lax.psum_scatter(d_down, 'dp', scatter_dimension=1, tiled=True)  215 us
    all_gather x1, waiting for transfers between devices, shards(): lax.all_gather(w_gateup.astype(bf16), 'dp', axis=0, tiled=True)  109 us
    reduce_scatter x1, waiting for transfers between devices, shards(): lax.psum_scatter(d_query_w, 'dp', scatter_dimension=0, tiled=True)  88.9 us
    reduce_scatter x1, waiting for transfers between devices, shards(): lax.psum_scatter(d_out_w, 'dp', scatter_dimension=1, tiled=True)  84.2 us
    all_gather x1, waiting for transfers between devices, shards(): lax.all_gather(w_down.astype(bf16), 'dp', axis=1, tiled=True)  75.1 us
    psum x1, waiting for transfers between devices, shards(): lax.psum(jnp.dot(act_low, down_full, preferred_element_type=f32).astype(j...  63.1 us
    unnamed x1, blocking collectives  61.2 us
  transfers between devices with their start and end apart: 19, of which 13 were waited for; matrix products, arithmetic and copies ran while one was open for 12% of the time, Pallas kernels for 0%

commit v1 on v0

v1 whole, which is shorter than its diff:
```python
import math

import jax
import jax.numpy as jnp
from jax import lax
from jax.sharding import PartitionSpec as P

QH = 24
KVH = 6
HD = 64
GROUP = QH // KVH
WINDOW = 1024
SEQ_LEN = 8192
LANES = 128

EPSILON = 1e-06
SCORE_SCALE = 0.125
MASKED = -1e30
ROPE_BASE = 10000.0

bf16 = jnp.bfloat16
f32 = jnp.float32


def angles_of(positions):
    half_width = HD // 2
    frequency = jnp.exp(
        jnp.arange(half_width, dtype=f32) * (-math.log(ROPE_BASE) / half_width)
    )
    phases = positions.astype(f32)[:, None] * frequency[None, :]
    return jnp.cos(phases)[:, None, :], jnp.sin(phases)[:, None, :]


def rotate(values, cos_table, sin_table):
    half_width = values.shape[-1] // 2
    first_half = values[..., :half_width]
    second_half = values[..., half_width:]
    return jnp.concatenate(
        [
            first_half * cos_table - second_half * sin_table,
            second_half * cos_table + first_half * sin_table,
        ],
        axis=-1,
    )


def inverse_rms(values):
    return lax.rsqrt(jnp.mean(values * values, axis=-1, keepdims=True) + EPSILON)


def rms_back(values, scale, weight, d_out):
    weighted = d_out * weight
    pull = jnp.mean(weighted * values, axis=-1, keepdims=True)
    return scale * weighted - values * (scale * scale * scale * pull)


class Ring:
    def __init__(self):
        self.count = lax.axis_size("dp")
        self.outer = self.count // 4
        index = lax.axis_index("dp")
        self.index = index
        self.core = index % 2
        self.mid = (index // 2) % 2
        self.place = index // 4
        self.core_pairs = [(i, i ^ 1) for i in range(self.count)]
        self.mid_pairs = [(i, i ^ 2) for i in range(self.count)]

    def pick(self, array, bit, axis):
        return lax.dynamic_index_in_dim(array, bit, axis, keepdims=False)

    def columns(self, array):
        tokens, width = array.shape
        blocks = array.reshape(tokens, self.outer, 2, 2, width // self.count)
        halves = []
        for bit in (1 - self.core, self.core):
            half = self.pick(blocks, bit, 3)
            both = [self.pick(half, self.mid, 2), self.pick(half, 1 - self.mid, 2)]
            halves.append([part.reshape(tokens, width // 4) for part in both])
        return halves

    def rows(self, array):
        width, count = array.shape
        blocks = array.reshape(self.outer, 2, 2, width // self.count, count)
        halves = []
        for bit in (1 - self.core, self.core):
            half = self.pick(blocks, bit, 2)
            both = [self.pick(half, self.mid, 1), self.pick(half, 1 - self.mid, 1)]
            halves.append([part.reshape(width // 4, count) for part in both])
        return halves

    def chain(self, blocks):
        outer = self.outer
        from_above = None
        from_below = None
        for step in range(outer - 1):
            down_block = jnp.clip(step - outer + 1 + self.place, 0, outer - 1)
            up_block = jnp.clip(self.place + outer - 1 - step, 0, outer - 1)
            down = self.pick(blocks, down_block, 0)
            up = self.pick(blocks, up_block, 0)
            if step > 0:
                down = (down.astype(f32) + from_above.astype(f32)).astype(bf16)
                up = (up.astype(f32) + from_below.astype(f32)).astype(bf16)
            down_pairs = []
            up_pairs = []
            for i in range(self.count):
                place = i // 4
                if place >= max(1, outer - 1 - step):
                    down_pairs.append((i, i - 4))
                if place <= min(outer - 2, step):
                    up_pairs.append((i, i + 4))
            from_above = lax.ppermute(down, "dp", down_pairs)
            from_below = lax.ppermute(up, "dp", up_pairs)
        total = self.pick(blocks, self.place, 0).astype(f32)
        if outer > 1:
            total = total + (from_above.astype(f32) + from_below.astype(f32))
        return total

    def scatter(self, make):
        to_core = [make(0, part).astype(bf16) for part in (1, 0)]
        got = [lax.ppermute(part, "dp", self.core_pairs) for part in to_core]
        to_mid = (make(1, 1) + got[0].astype(f32)).astype(bf16)
        got_mid = lax.ppermute(to_mid, "dp", self.mid_pairs)
        kept = (make(1, 0) + got[1].astype(f32) + got_mid.astype(f32)).astype(bf16)
        return self.chain(kept.reshape((self.outer, -1) + kept.shape[1:]))


def other_tensor(array):
    count = lax.axis_size("tensor")
    return lax.ppermute(array, "tensor", [(i, (i + 1) % count) for i in range(count)])


def tensor_sum(partial):
    low = partial.astype(bf16)
    return low.astype(f32) + other_tensor(low).astype(f32)


def from_behind(shard, by):
    length = lax.axis_size("dp")
    pairs = [(i, i + by) for i in range(length) if 0 <= i + by < length]
    return lax.ppermute(shard, "dp", pairs)


def tn_dot(left, right):
    return lax.dot_general(left, right, (((0,), (0,)), ((), ())), preferred_element_type=f32)


def nt_dot(left, right):
    return lax.dot_general(left, right, (((1,), (1,)), ((), ())), preferred_element_type=f32)


def nn_dot(left, right):
    return jnp.dot(left, right, preferred_element_type=f32)


def shards(
    tokens,
    w_query,
    w_keyval,
    w_out,
    w_gateup,
    w_down,
    attn_gain,
    ffn_gain,
    qk_gain,
    segments,
    positions,
    cotangent,
):
    ring = Ring()
    row_count = tokens.shape[0]
    depth = w_query.shape[0]
    model = tokens.shape[1]
    hidden = w_gateup.shape[2]
    tensor = lax.axis_index("tensor")
    query_width = w_query.shape[1]
    local_heads = query_width // HD
    local_kv = local_heads // GROUP
    kv_width = local_kv * HD
    all_kv = w_keyval.shape[1] // 2
    gain_count = 2 * qk_gain.shape[1]

    own_keyval = lax.dynamic_index_in_dim(
        w_keyval.reshape(depth, 2, all_kv // kv_width, kv_width), tensor, 2, keepdims=False
    ).reshape(depth, 2 * kv_width)
    head_gain_column = jnp.pad(qk_gain.reshape(gain_count), (0, depth - gain_count))
    gains = jnp.stack([attn_gain, ffn_gain, head_gain_column], axis=1)
    gains = jnp.pad(gains, ((0, 0), (0, LANES - gains.shape[1])))
    attn_pack = jnp.concatenate([w_query, own_keyval, w_out.T, gains], axis=1).astype(bf16)
    attn_full = lax.all_gather(attn_pack, "dp", axis=0, tiled=True)
    gateup_full = lax.all_gather(
        w_gateup.reshape(depth, 2 * hidden).astype(bf16), "dp", axis=0, tiled=True
    )
    down_full = lax.all_gather(w_down.T.astype(bf16), "dp", axis=0, tiled=True)

    marks = (segments + 1).astype(bf16)
    seq_devices = min(SEQ_LEN // row_count, ring.count)
    own_sequence = ring.index // seq_devices
    reach_count = -(-WINDOW // row_count)
    halo_marks = []
    for step_back in range(reach_count, 0, -1):
        same_sequence = ((ring.index - step_back) // seq_devices == own_sequence).astype(bf16)
        halo_marks.append(from_behind(marks, step_back) * same_sequence)
    key_marks = jnp.concatenate(halo_marks + [marks], axis=0)
    key_count = key_marks.shape[0]
    cos_table, sin_table = angles_of(positions)

    residual = tokens.astype(f32)
    attn_scale = inverse_rms(residual)

    qkv_full = attn_full[:, : query_width + 2 * kv_width]
    query_full = qkv_full[:, :query_width]
    keyval_full = qkv_full[:, query_width:]
    out_start = query_width + 2 * kv_width
    out_full = attn_full[:, out_start : out_start + query_width]
    gain_start = out_start + query_width
    gain_columns = attn_full[:, gain_start : gain_start + 3].astype(f32)
    attn_weight = gain_columns[:, 0]
    ffn_weight = gain_columns[:, 1]
    head_gains = gain_columns[:, 2].reshape(ring.count, depth)[:, :gain_count]
    head_gains = head_gains.reshape(ring.count, 2, qk_gain.shape[1]).transpose(1, 0, 2).reshape(2, HD)
    gain_query = head_gains[0]
    gain_key = head_gains[1]

    normed_low = (residual * attn_scale * attn_weight).astype(bf16)
    query_raw = nn_dot(normed_low, query_full).reshape(row_count, local_heads, HD)
    keyval_raw = nn_dot(normed_low, keyval_full)
    key_raw = keyval_raw[:, :kv_width].reshape(row_count, local_kv, HD)
    query_scale = inverse_rms(query_raw)
    key_scale = inverse_rms(key_raw)
    query_low = rotate(query_raw * query_scale * gain_query, cos_table, sin_table).astype(bf16)
    key_low = rotate(key_raw * key_scale * gain_key, cos_table, sin_table).astype(bf16)
    keyval_low = jnp.concatenate(
        [key_low.reshape(row_count, kv_width), keyval_raw[:, kv_width:].astype(bf16)], axis=1
    )
    halo = [from_behind(keyval_low, step_back) for step_back in range(reach_count, 0, -1)]
    key_keyval = jnp.concatenate(halo + [keyval_low], axis=0)
    keys = key_keyval[:, :kv_width].reshape(key_count, local_kv, HD)
    values = key_keyval[:, kv_width:].reshape(key_count, local_kv, HD)
    query_groups = query_low.reshape(row_count, local_kv, GROUP, HD)
    distance = (jnp.arange(row_count, dtype=jnp.int32) + reach_count * row_count)[
        :, None
    ] - jnp.arange(key_count, dtype=jnp.int32)[None, :]
    allowed = (distance >= 0) & (distance < WINDOW) & (marks[:, None] == key_marks[None, :])

    def masked_scores():
        scores = jnp.einsum("qhgd,khd->hgqk", query_groups, keys, preferred_element_type=f32)
        return jnp.where(allowed[None, None], scores * SCORE_SCALE, MASKED)

    scores = masked_scores()
    row_max = jnp.max(scores, axis=-1, keepdims=True)
    scaled = jnp.exp(scores - row_max)
    row_total = jnp.sum(scaled, axis=-1, keepdims=True)
    probability = (scaled / row_total).astype(bf16)
    attended = jnp.einsum("hgqk,khd->qhgd", probability, values, preferred_element_type=f32)
    row_lse = row_max + jnp.log(row_total)
    attended_low = attended.reshape(row_count, query_width).astype(bf16)
    mid = residual + tensor_sum(nt_dot(attended_low, out_full))

    ffn_scale = inverse_rms(mid)
    normed2_low = (mid * ffn_scale * ffn_weight).astype(bf16)
    gate = nn_dot(normed2_low, gateup_full[:, :hidden])
    up = nn_dot(normed2_low, gateup_full[:, hidden:])
    gate_sigmoid = jax.nn.sigmoid(gate)
    gate_silu = gate * gate_sigmoid
    act_low = (gate_silu * up).astype(bf16)
    cotangent_parts = ring.columns(cotangent)
    grad_down = ring.scatter(lambda core, mid_at: tn_dot(cotangent_parts[core][mid_at], act_low)).T

    d_act = nn_dot(cotangent, down_full)
    d_gate = (d_act * up * gate_sigmoid * (1.0 + gate * (1.0 - gate_sigmoid))).astype(bf16)
    d_up = (d_act * gate_silu).astype(bf16)
    d_normed2 = tensor_sum(
        nt_dot(d_gate, gateup_full[:, :hidden]) + nt_dot(d_up, gateup_full[:, hidden:])
    )
    normed2_parts = ring.columns(normed2_low)
    grad_gate = ring.scatter(lambda core, mid_at: tn_dot(normed2_parts[core][mid_at], d_gate))
    grad_up = ring.scatter(lambda core, mid_at: tn_dot(normed2_parts[core][mid_at], d_up))
    grad_gateup = jnp.stack([grad_gate, grad_up], axis=1)
    result = mid + tensor_sum(nt_dot(act_low, down_full))
    output = result.astype(bf16)
    d_ffn_weight = jnp.sum(d_normed2 * mid * ffn_scale, axis=0)
    d_mid = cotangent.astype(f32) + rms_back(mid, ffn_scale, ffn_weight, d_normed2)

    d_mid_low = d_mid.astype(bf16)
    d_mid_parts = ring.columns(d_mid_low)
    grad_out = ring.scatter(lambda core, mid_at: tn_dot(d_mid_parts[core][mid_at], attended_low)).T
    d_attended = nn_dot(d_mid_low, out_full).astype(bf16)
    d_groups = d_attended.reshape(row_count, local_kv, GROUP, HD)
    probability = jnp.exp(masked_scores() - row_lse)
    d_prob = jnp.einsum("qhgd,khd->hgqk", d_groups, values, preferred_element_type=f32)
    row_delta = jnp.sum(d_prob * probability, axis=-1, keepdims=True)
    d_scores = (probability * (d_prob - row_delta)).astype(bf16)
    d_query = jnp.einsum("hgqk,khd->qhgd", d_scores, keys, preferred_element_type=f32) * SCORE_SCALE
    d_keys = (
        jnp.einsum("hgqk,qhgd->khd", d_scores, query_groups, preferred_element_type=f32)
        * SCORE_SCALE
    )
    d_values = jnp.einsum(
        "hgqk,qhgd->khd", probability.astype(bf16), d_groups, preferred_element_type=f32
    )
    d_keyval_all = jnp.concatenate(
        [d_keys.reshape(key_count, kv_width), d_values.reshape(key_count, kv_width)], axis=1
    )
    own_grad = d_keyval_all[reach_count * row_count :]
    for step_back in range(1, reach_count + 1):
        piece_start = (reach_count - step_back) * row_count
        piece = d_keyval_all[piece_start : piece_start + row_count].astype(bf16)
        own_grad = own_grad + from_behind(piece, -step_back).astype(f32)

    def head_back(raw, scale, gain, d_rotated):
        d_normed_head = rotate(d_rotated, cos_table, -sin_table)
        d_gain = jnp.sum(d_normed_head * raw * scale, axis=(0, 1))
        return rms_back(raw, scale, gain, d_normed_head), d_gain

    d_query_raw, d_gain_query = head_back(
        query_raw, query_scale, gain_query, d_query.reshape(row_count, local_heads, HD)
    )
    d_key_raw, d_gain_key = head_back(
        key_raw, key_scale, gain_key, own_grad[:, :kv_width].reshape(row_count, local_kv, HD)
    )
    d_qkv_low = jnp.concatenate(
        [
            d_query_raw.reshape(row_count, query_width),
            d_key_raw.reshape(row_count, kv_width),
            own_grad[:, kv_width:],
        ],
        axis=1,
    ).astype(bf16)
    d_normed_part = nt_dot(d_qkv_low, qkv_full)
    d_normed = tensor_sum(d_normed_part)
    d_attn_part = jnp.sum(d_normed_part * residual * attn_scale, axis=0)

    head_rows = jnp.stack([d_gain_query, d_gain_key], axis=0).reshape(2, ring.count, gain_count // 2)
    head_rows = head_rows.transpose(1, 0, 2).reshape(ring.count, gain_count)
    head_column = jnp.pad(head_rows, ((0, 0), (0, depth - gain_count))).reshape(model)
    gain_grads = jnp.stack([d_attn_part, d_ffn_weight, head_column], axis=1)
    gain_grads = jnp.pad(gain_grads, ((0, 0), (0, LANES - gain_grads.shape[1])))
    gain_parts = ring.rows(gain_grads)
    normed_parts = ring.columns(normed_low)
    grad_qkv = ring.scatter(
        lambda core, mid_at: jnp.concatenate(
            [tn_dot(normed_parts[core][mid_at], d_qkv_low), gain_parts[core][mid_at]], axis=1
        )
    )
    grad_query = grad_qkv[:, :query_width]
    shared = grad_qkv[:, query_width:].astype(bf16)
    shared_other = other_tensor(shared).astype(f32)
    shared = shared.astype(f32)
    first = tensor == 0
    keyval_mine = shared[:, : 2 * kv_width].reshape(depth, 2, 1, kv_width)
    keyval_theirs = shared_other[:, : 2 * kv_width].reshape(depth, 2, 1, kv_width)
    grad_keyval = jnp.concatenate(
        [
            jnp.where(first, keyval_mine, keyval_theirs),
            jnp.where(first, keyval_theirs, keyval_mine),
        ],
        axis=2,
    ).reshape(depth, 2 * all_kv)
    gains_mine = shared[:, 2 * kv_width :]
    gains_sum = gains_mine + shared_other[:, 2 * kv_width :]
    grad_attn_gain = gains_sum[:, 0]
    grad_ffn_gain = gains_mine[:, 1]
    grad_heads = gains_sum[:gain_count, 2].reshape(2, gain_count // 2)
    input_grad = (d_mid + rms_back(residual, attn_scale, attn_weight, d_normed)).astype(bf16)
    return (
        output,
        input_grad,
        grad_query,
        grad_keyval,
        grad_out,
        grad_gateup,
        grad_down,
        grad_attn_gain,
        grad_ffn_gain,
        grad_heads,
    )


def solution(mesh):
    in_specs = (
        P("dp", None),
        P("dp", "tensor"),
        P("dp", None),
        P("tensor", "dp"),
        P("dp", None, "tensor"),
        P("tensor", "dp"),
        P("dp"),
        P("dp"),
        P(None, "dp"),
        P("dp"),
        P("dp"),
        P("dp", None),
    )
    out_specs = (
        P("dp", None),
        P("dp", None),
        P("dp", "tensor"),
        P("dp", None),
        P("tensor", "dp"),
        P("dp", None, "tensor"),
        P("tensor", "dp"),
        P("dp"),
        P("dp"),
        P(None, "dp"),
    )
    return jax.shard_map(shards, mesh=mesh, in_specs=in_specs, out_specs=out_specs, check_vma=False)
```

time: 1720 us -> 1070 us (0.62)
  waiting for transfers between devices: 1170 us -> 388 us
  blocking collectives: 122 us -> 0 us
  starting transfers between devices: 26.9 us -> 141 us
  local copies, waits for them, and re-layouts: 32.1 us -> 132 us
  other arithmetic: 89.3 us -> 141 us
    reduce_scatter x5 -> x0, waiting for transfers between devices: 768 us -> none  [the longest x1 324 us: shards(): lax.psum_scatter(d_gateup_w, 'dp', scatter_dimension=0, tiled=True)]
    ppermute x6 -> x56, waiting for transfers between devices: 27.4 us -> 271 us  [the longest x5 136 us: scatter(): got_mid = lax.ppermute(to_mid, 'dp', self.mid_pairs)]
    psum x3 -> x0, waiting for transfers between devices: 152 us -> none  [the longest x1 63.1 us: shards(): lax.psum(jnp.dot(act_low, down_full, preferred_element_type=f32).astype(j...]
    ppermute x6 -> x56, starting transfers between devices: 15.4 us -> 141 us  [the longest x15 93.7 us: chain(): from_below = lax.ppermute(up, 'dp', up_pairs)]
    all_gather x5 -> x3, waiting for transfers between devices: 219 us -> 117 us  [the longest x1 65.1 us: shards(): attn_full = lax.all_gather(attn_pack, 'dp', axis=0, tiled=True)]
    unnamed x1 -> x0, blocking collectives: 61.2 us -> none
    all_gather x3 -> x0, blocking collectives: 56.3 us -> none  [the longest x1 19.6 us: shards(): lax.all_gather(ffn_gain.astype(bf16), 'dp', axis=0, tiled=True)]
    unnamed x116 -> x204, local copies, waits for them, and re-layouts: 16.2 us -> 60 us
  transfers between devices with their start and end apart: 19 -> 59, of which waited for: 13 -> 20; matrix products, arithmetic and copies ran while one was open for 12% -> 43% of each run, Pallas kernels for 0% -> 0%
where the time goes in v1:
time: 1070 us; the launch traced here: 1060 us
  waiting for transfers between devices  388 us (36%)
  matrix products  247 us (23%)
  starting transfers between devices  141 us (13%)
  other arithmetic  141 us (13%)
  local copies, waits for them, and re-layouts  132 us (12%)
  between operations  16 us (1%)
    ppermute x5, waiting for transfers between devices, scatter(): got_mid = lax.ppermute(to_mid, 'dp', self.mid_pairs)  136 us
    ppermute x15, starting transfers between devices, chain(): from_below = lax.ppermute(up, 'dp', up_pairs)  93.7 us
    ppermute x5, waiting for transfers between devices, other_tensor(): lax.ppermute(array, 'tensor', [(i, (i + 1) % count) for i in range(count)])  68.4 us
    all_gather x1, waiting for transfers between devices, shards(): attn_full = lax.all_gather(attn_pack, 'dp', axis=0, tiled=True)  65.1 us
    dot_general x20, matrix products, tn_dot(): lax.dot_general(left, right, (((0,), (0,)), ((), ())), preferred_element_...  63.9 us
    ppermute x15, waiting for transfers between devices, chain(): from_below = lax.ppermute(up, 'dp', up_pairs)  61.5 us
    unnamed x204, local copies, waits for them, and re-layouts  60 us
    all_gather x1, waiting for transfers between devices, shards(): lax.all_gather(w_gateup.reshape(depth, 2 * hidden).astype(bf16), 'dp', ax...  51.8 us
  transfers between devices with their start and end apart: 59, of which 20 were waited for; matrix products, arithmetic and copies ran while one was open for 43% of the time, Pallas kernels for 0%

profile of v1, /device:TPU:0, one launch (start us, length us, event | category | flops | bytes accessed | tf_op | source)
XLA Modules:
  0.0 1064.4 jit_solution(17610749793697152887)
XLA Ops:
  20.4 4.4 collective-permute-start.2
  28.9 65.1 %all-gather.4.cloned.1.call-done = bf16[2048,2048]{0,1:T(8,128)(2,1)} async-done(((bf16[128,2048]{0,1:T(8,128)(2,1)}), bf16[2048,2048]{0,1:T(8,128)(2,1)}) %all-gather.4.cloned.1.call-update) | async-done | bytes 8388624 | tf_op jit(solution)/shard_map/all_gather | solution.py:190
  103.4 4.1 collective-permute-start
  107.7 5.5 fusion.32
  120.6 15.4 %fusion.100 = (f32[3,4,512]{2,1,0:T(4,128)S(1)}, f32[3,4,512,1536]{2,3,1,0:T(8,128)}) fusion(bf16[1536,3,64,1]{0,2,3,1:T(8,128)(2,1)S(1)} %bitcast.330, bf16[512,3,4,32]{0,3,2,1:T(8,128)(2,1)S(1)} %bitcast.343, bf16[512,3,4,32]{0,3,2,1:T(8,128)(2,1)S(1)} %bitcast.341, pred[512,1536]{0,1:T(8,128)(4,1)S(1)} %copy-done.48), kind=kOutput, calls=%fused_computation.285 | convolution fusion | flops 1237837824 | bytes 39936000 | tf_op jit(solution)/shard_map/qhgd,khd->hgqk/dot_general | solution.py:247
  136.0 15.4 %fusion.3 = f32[3,4,512]{2,1,0:T(4,128)S(1)} fusion(f32[3,4,512,1536]{2,3,1,0:T(8,128)} %get-tuple-element.143, f32[3,4,512]{2,1,0:T(4,128)S(1)} %get-tuple-element.142), kind=kLoop, calls=%fused_computation.9 | loop fusion | flops 18868224 | bytes 37797888 | tf_op jit(solution)/shard_map/reduce_sum | solution.py:253
  151.4 14.6 %fusion.51 = bf16[3,64,4,512]{3,1,2,0:T(8,128)(2,1)S(1)} fusion(bf16[1536,3,64,1]{0,2,3,1:T(8,128)(2,1)S(1)} %bitcast.332, f32[3,4,512,1536]{2,3,1,0:T(8,128)} %get-tuple-element.143, f32[3,4,512]{2,1,0:T(4,128)S(1)} %fusion.3, f32[3,4,512]{2,1,0:T(4,128)S(1)} %get-tuple-element.142), kind=kOutput, calls=%fused_computation.106 | convolution fusion | flops 1236664320 | bytes 39174144 | tf_op jit(solution)/shard_map/hgqk,khd->qhgd/dot_general | solution.py:255
  166.0 5.3 convolution_convert_fusion.8
  173.1 3.9 copy.295
  180.0 4.4 reshape.592
  190.1 6.8 constant_dynamic-slice_fusion.36
  210.1 7.4 collective-permute-done.4
  227.7 5.4 constant_dynamic-slice_fusion.13
  243.7 10.0 fusion.102
  253.7 51.8 %all-gather.6.cloned.1.call-done = bf16[2048,5120]{1,0:T(8,128)(2,1)} async-done(((bf16[128,5120]{1,0:T(8,128)(2,1)}), bf16[2048,5120]{1,0:T(8,128)(2,1)}) %all-gather.6.cloned.1.call-update) | async-done | bytes 20971536 | tf_op jit(solution)/shard_map/all_gather | solution.py:191
  305.5 11.8 %fusion.11 = f32[512,2560]{1,0:T(8,128)} fusion(bf16[512,2048]{1,0:T(8,128)(2,1)} %multiply_convert_fusion.3, bf16[2048,5120]{1,0:T(8,128)(2,1)} %all-gather.6.cloned.1.call-done), kind=kOutput, calls=%fused_computation.22 | convolution fusion | flops 5368709120 | bytes 17825792 | tf_op jit(solution)/shard_map/dot_general | solution.py:153
  317.3 11.9 %multiply_convert_fusion.1 = (bf16[512,2560]{1,0:T(8,128)(2,1)S(1)}, bf16[512,2560]{1,0:T(8,128)(2,1)S(1)}, bf16[512,2560]{1,0:T(8,128)(2,1)S(1)}) fusion(f32[512,2560]{1,0:T(8,128)} %fusion.102, f32[512,2560]{1,0:T(8,128)} %fusion.11, bf16[512,2048]{1,0:T(8,128)(2,1)S(1)} %copy-done.18, bf16[2048,5120]{1,0:T(8,128)(2,1)} %all-gather.6.cloned.1.call-done), kind=kOutput, calls=%fused_computation.35 | convolution fusion | flops 5388369920 | bytes 30932992 | tf_op jit(solution)/shard_map/dot_general | solution.py:153
  329.2 3.6 convolution_convert_fusion.4
  341.8 3.9 fusion.106
  345.8 3.9 fusion.107
  353.4 8.3 fusion.9
  361.7 8.8 add_convert_fusion.6
  375.1 3.8 fusion.108
  378.9 11.3 %convolution_convert_fusion.9 = bf16[512,2048]{1,0:T(8,128)(2,1)} fusion(bf16[512,2560]{1,0:T(8,128)(2,1)S(1)} %get-tuple-element.60, bf16[2048,2560]{0,1:T(8,128)(2,1)} %all-gather.8.cloned.1.call-done), kind=kOutput, calls=%fused_computation.76 | convolution fusion | flops 5369757696 | bytes 15204352 | tf_op jit(solution)/shard_map/dot_general | solution.py:149
  390.2 28.2 %collective-permute-done.6 = bf16[512,2048]{1,0:T(8,128)(2,1)S(1)} collective-permute-done((bf16[512,2048]{1,0:T(8,128)(2,1)S(1)}, bf16[512,2048]{1,0:T(8,128)(2,1)S(1)}, u32[]{:S(2)}, u32[]{:S(2)}) %collective-permute-start.6) | collective-permute-done | bytes 2097184 | tf_op jit(solution)/shard_map/ppermute | solution.py:130
  425.7 5.2 fusion.48
  432.4 16.0 %fusion.5 = f32[3,64,1536,1]{2,1,3,0:T(8,128)} fusion(bf16[512,3,4,64]{0,3,2,1:T(8,128)(2,1)S(1)} %bitcast.305, f32[3,4,512,1536]{2,3,1,0:T(8,128)} %get-tuple-element.143, f32[3,4,512]{2,1,0:T(4,128)S(1)} %log_add_fusion), kind=kOutput, calls=%fused_computation.11 | convolution fusion | flops 1226833920 | bytes 39739392 | tf_op jit(solution)/shard_map/hgqk,qhgd->khd/dot_general | solution.py:299
  448.4 27.5 %fusion = (f32[3,4,512]{2,1,0:T(4,128)S(1)}, f32[3,1536,512,4]{2,1,3,0:T(8,128)}) fusion(f32[3,4,512,1536]{2,3,1,0:T(8,128)} %get-tuple-element.143, f32[3,4,512]{2,1,0:T(4,128)S(1)} %log_add_fusion, bf16[1536,3,64,1]{0,2,3,1:T(8,128)(2,1)S(1)} %bitcast.333, bf16[512,3,4,64]{0,3,2,1:T(8,128)(2,1)S(1)} %bitcast.306), kind=kOutput, calls=%fused_computation.2 | convolution fusion | flops 1236264960 | bytes 76922880 | tf_op jit(solution)/shard_map/qhgd,khd->hgqk/dot_general | solution.py:291
  475.9 31.3 %fusion.2 = bf16[3,4,512,1536]{2,3,1,0:T(8,128)(2,1)} fusion(f32[3,1536,512,4]{2,1,3,0:T(8,128)} %get-tuple-element.145, f32[3,4,512,1536]{2,3,1,0:T(8,128)} %get-tuple-element.143, f32[3,4,512]{2,1,0:T(4,128)S(1)} %get-tuple-element.144, f32[3,4,512]{2,1,0:T(4,128)S(1)} %log_add_fusion), kind=kLoop, calls=%fused_computation.4 | loop fusion | flops 37748736 | bytes 94420992 | tf_op jit(solution)/shard_map/convert_element_type | solution.py:293
  507.2 9.9 fusion.44
  517.1 11.1 %convolution_multiply_fusion = f32[3,64,4,512]{3,1,2,0:T(8,128)} fusion(bf16[1536,3,64,1]{0,2,3,1:T(8,128)(2,1)} %bitcast.331, bf16[3,4,512,1536]{2,3,1,0:T(8,128)(2,1)} %fusion.2), kind=kOutput, calls=%fused_computation.102 | convolution fusion | flops 1208352768 | bytes 21037056 | tf_op jit(solution)/shard_map/hgqk,khd->qhgd/dot_general | solution.py:294
  531.0 5.5 constant_dynamic-slice_fusion.24
  561.9 4.2 multiply_reduce_fusion.3
  567.7 3.9 copy.325
  591.2 7.2 fusion.101
  606.1 4.9 add_convert_fusion.3
  611.0 9.9 collective-permute-done.22
  624.1 4.3 collective-permute-start.26
  628.4 5.5 add_convert_fusion.5
  641.1 16.8 %collective-permute-start.28 = (bf16[128,768]{0,1:T(8,128)(2,1)S(1)}, bf16[128,768]{0,1:T(8,128)(2,1)S(1)}, u32[]{:S(2)}, u32[]{:S(2)}) collective-permute-start(bf16[128,768]{0,1:T(8,128)(2,1)S(1)} %fusion.75), channel_id=1, source_target_pairs={{0,8},{2,10},{4,12},{6,14},{8,16},{10,18},{12,20},{14,22},{16,24},... | collective-permute-start | bytes 589832 | tf_op jit(solution)/shard_map/ppermute | solution.py:113
  659.6 5.7 add_convert_fusion.1
  667.8 29.8 %collective-permute-done.9 = bf16[512,2048]{1,0:T(8,128)(2,1)} collective-permute-done((bf16[512,2048]{1,0:T(8,128)(2,1)}, bf16[512,2048]{1,0:T(8,128)(2,1)}, u32[]{:S(2)}, u32[]{:S(2)}) %collective-permute-start.9) | collective-permute-done | bytes 2097184 | tf_op jit(solution)/shard_map/ppermute | solution.py:130
  697.9 5.1 fusion.28
  711.6 8.9 fusion.26
  720.9 36.8 %collective-permute-done.49 = bf16[512,2560]{1,0:T(8,128)(2,1)} collective-permute-done((bf16[512,2560]{1,0:T(8,128)(2,1)}, bf16[512,2560]{1,0:T(8,128)(2,1)}, u32[]{:S(2)}, u32[]{:S(2)}) %collective-permute-start.49) | collective-permute-done | bytes 2621472 | tf_op jit(solution)/shard_map/ppermute | solution.py:123
  757.7 3.9 add_convert_fusion
  766.0 47.8 %collective-permute-done.31 = bf16[512,2560]{1,0:T(8,128)(2,1)} collective-permute-done((bf16[512,2560]{1,0:T(8,128)(2,1)}, bf16[512,2560]{1,0:T(8,128)(2,1)}, u32[]{:S(2)}, u32[]{:S(2)}) %collective-permute-start.31) | collective-permute-done | bytes 2621472 | tf_op jit(solution)/shard_map/ppermute | solution.py:123
  813.9 4.6 collective-permute-start.53
  818.5 5.1 add_convert_fusion.4
  826.5 41.8 %collective-permute-done.40 = bf16[512,2560]{1,0:T(8,128)(2,1)} collective-permute-done((bf16[512,2560]{1,0:T(8,128)(2,1)}, bf16[512,2560]{1,0:T(8,128)(2,1)}, u32[]{:S(2)}, u32[]{:S(2)}) %collective-permute-start.40) | collective-permute-done | bytes 2621472 | tf_op jit(solution)/shard_map/ppermute | solution.py:123
  893.1 5.4 collective-permute-done.35
  901.1 22.3 %collective-permute-done.54 = bf16[128,2560]{0,1:T(8,128)(2,1)S(1)} collective-permute-done((bf16[128,2560]{0,1:T(8,128)(2,1)S(1)}, bf16[128,2560]{0,1:T(8,128)(2,1)S(1)}, u32[]{:S(2)}, u32[]{:S(2)}) %collective-permute-start.54) | collective-permute-done | bytes 655392 | tf_op jit(solution)/shard_map/ppermute | solution.py:113
  925.9 21.1 %collective-permute-start.55 = (bf16[128,2560]{0,1:T(8,128)(2,1)}, bf16[128,2560]{0,1:T(8,128)(2,1)}, u32[]{:S(2)}, u32[]{:S(2)}) collective-permute-start(bf16[128,2560]{0,1:T(8,128)(2,1)} %fusion.53), channel_id=1, source_target_pairs={{0,8},{2,10},{4,12},{6,14},{8,16},{10,18},{12,20},{14,22},{16,24},... | collective-permute-start | bytes 1966088 | tf_op jit(solution)/shard_map/ppermute | solution.py:113
  949.3 10.9 %collective-permute-start.36 = (bf16[128,2560]{1,0:T(8,128)(2,1)S(1)}, bf16[128,2560]{1,0:T(8,128)(2,1)S(1)}, u32[]{:S(2)}, u32[]{:S(2)}) collective-permute-start(bf16[128,2560]{1,0:T(8,128)(2,1)S(1)} %get-tuple-element.73), channel_id=1, source_target_pairs={{0,8},{2,10},{4,12},{6,14},{8,16},{10,18},{12,20},{14,22},{1,9},{3... | collective-permute-start | bytes 1966088 | tf_op jit(solution)/shard_map/ppermute | solution.py:113
  961.5 9.2 collective-permute-done.36
  970.6 4.4 collective-permute-start.45
  976.1 7.0 collective-permute-done.45
  986.7 6.5 collective-permute-start.37
  997.3 4.0 collective-permute-start.46
  1001.3 4.8 collective-permute-start.16
  1010.7 11.5 %collective-permute-done.16 = bf16[128,1280]{0,1:T(8,128)(2,1)} collective-permute-done((bf16[128,1280]{0,1:T(8,128)(2,1)S(1)}, bf16[128,1280]{0,1:T(8,128)(2,1)}, u32[]{:S(2)}, u32[]{:S(2)}) %collective-permute-start.16) | collective-permute-done | bytes 327712 | tf_op jit(solution)/shard_map/ppermute | solution.py:113
  1024.0 4.5 collective-permute-start.17
  1035.8 4.4 collective-permute-start.18
  1045.6 3.7 collective-permute-done.15
  (462 shorter events, 261.0 us)
Async XLA Ops:
  7.2 86.8 %all-gather.4.cloned.1.call-start = ((), (), s32[]{:S(2)}) async-start(), calls=%async_computation | async-start | bytes 8912896 | tf_op jit(solution)/shard_map/all_gather | solution.py:190
  13.0 230.7 %all-gather.8.cloned.1.call-start = ((), (), s32[]{:S(2)}) async-start(), calls=%async_computation.2 | async-start | bytes 11141120 | tf_op jit(solution)/shard_map/all_gather | solution.py:194
  14.0 291.5 %all-gather.6.cloned.1.call-start = ((), (), s32[]{:S(2)}) async-start(), calls=%async_computation.1 | async-start | bytes 22282240 | tf_op jit(solution)/shard_map/all_gather | solution.py:191
  18.0 8.9 collective-permute-start.3
  20.4 6.6 collective-permute-start.2
  26.0 69.3 %copy-start.68 = (f32[512]{0:T(512)}, f32[512]{0:T(512)S(1)}, u32[]{:S(2)}) copy-start(f32[512]{0:T(512)S(1)} %add_rsqrt_fusion.3) | copy-start | bytes 6148
  27.0 91.6 %copy-start.38 = (f32[512,32]{0,1:T(8,128)}, f32[512,32]{0,1:T(8,128)S(1)}, u32[]{:S(2)}) copy-start(f32[512,32]{0,1:T(8,128)S(1)} %get-tuple-element.141) | copy-start | bytes 196612
  99.7 85.4 %copy-start.73 = (f32[64]{0:T(128)}, f32[64]{0:T(128)S(1)}, u32[]{:S(2)}) copy-start(f32[64]{0:T(128)S(1)} %mul.556) | copy-start | bytes 772
  101.2 17.7 %collective-permute-start.1 = (bf16[512,384]{0,1:T(8,128)(2,1)}, bf16[512,384]{0,1:T(8,128)(2,1)S(1)}, u32[]{:S(2)}, u32[]{:S(2)}) collective-permute-start(bf16[512,384]{0,1:T(8,128)(2,1)} %pad_maximum_fusion.9), channel_id=1, source_target_pairs={{0,2},{2,4},{4,6},{6,8},{8,10},{10,12},{12,14},{14,16},{16,18},{18... | collective-permute-start | bytes 1179656 | tf_op jit(solution)/shard_map/ppermute | solution.py:141
  103.4 16.1 %collective-permute-start = (bf16[512,384]{0,1:T(8,128)(2,1)}, bf16[512,384]{0,1:T(8,128)(2,1)}, u32[]{:S(2)}, u32[]{:S(2)}) collective-permute-start(bf16[512,384]{0,1:T(8,128)(2,1)} %pad_maximum_fusion.9), channel_id=1, source_target_pairs={{0,4},{2,6},{4,8},{6,10},{8,12},{10,14},{12,16},{14,18},{16,20},{1... | collective-permute-start | bytes 1179656 | tf_op jit(solution)/shard_map/ppermute | solution.py:141
  107.6 76.8 %copy-start.75 = (f32[64]{0:T(128)}, f32[64]{0:T(128)S(1)}, u32[]{:S(2)}) copy-start(f32[64]{0:T(128)S(1)} %mul.577) | copy-start | bytes 772
  171.3 46.2 %collective-permute-start.4 = (bf16[512,2048]{1,0:T(8,128)(2,1)}, bf16[512,2048]{1,0:T(8,128)(2,1)}, u32[]{:S(2)}, u32[]{:S(2)}) collective-permute-start(bf16[512,2048]{1,0:T(8,128)(2,1)} %convolution_convert_fusion.8), channel_id=1, source_target_pairs={{0,1},{1,0},{2,3},{3,2},{4,5},{5,4},{6,7},{7,6},{8,9},{9,8},{10,11... | collective-permute-start | bytes 6291464 | tf_op jit(solution)/shard_map/ppermute | solution.py:130
  349.6 255.0 %collective-permute-start.39 = (bf16[512,2560]{1,0:T(8,128)(2,1)}, bf16[512,2560]{1,0:T(8,128)(2,1)}, u32[]{:S(2)}, u32[]{:S(2)}) collective-permute-start(bf16[512,2560]{1,0:T(8,128)(2,1)} %convolution_convert_fusion.2), channel_id=1, source_target_pairs={{0,2},{2,0},{4,6},{6,4},{8,10},{10,8},{12,14},{14,12},{16,18},{18,... | collective-permute-start | bytes 7864328 | tf_op jit(solution)/shard_map/ppermute | solution.py:121
  349.9 274.2 %collective-permute-start.30 = (bf16[512,2560]{1,0:T(8,128)(2,1)}, bf16[512,2560]{1,0:T(8,128)(2,1)}, u32[]{:S(2)}, u32[]{:S(2)}) collective-permute-start(bf16[512,2560]{1,0:T(8,128)(2,1)} %convolution_convert_fusion.4), channel_id=1, source_target_pairs={{0,2},{2,0},{4,6},{6,4},{8,10},{10,8},{12,14},{14,12},{16,18},{18,... | collective-permute-start | bytes 7864328 | tf_op jit(solution)/shard_map/ppermute | solution.py:121
  353.1 304.9 %collective-permute-start.48 = (bf16[512,2560]{1,0:T(8,128)(2,1)}, bf16[512,2560]{1,0:T(8,128)(2,1)}, u32[]{:S(2)}, u32[]{:S(2)}) collective-permute-start(bf16[512,2560]{1,0:T(8,128)(2,1)} %convolution_convert_fusion), channel_id=1, source_target_pairs={{0,2},{2,0},{4,6},{6,4},{8,10},{10,8},{12,14},{14,12},{16,18},{18,... | collective-permute-start | bytes 7864328 | tf_op jit(solution)/shard_map/ppermute | solution.py:121
  370.5 47.9 %collective-permute-start.6 = (bf16[512,2048]{1,0:T(8,128)(2,1)S(1)}, bf16[512,2048]{1,0:T(8,128)(2,1)S(1)}, u32[]{:S(2)}, u32[]{:S(2)}) collective-permute-start(bf16[512,2048]{1,0:T(8,128)(2,1)S(1)} %add_convert_fusion.6), channel_id=1, source_target_pairs={{0,1},{1,0},{2,3},{3,2},{4,5},{5,4},{6,7},{7,6},{8,9},{9,8},{10,11... | collective-permute-start | bytes 6291464 | tf_op jit(solution)/shard_map/ppermute | solution.py:130
  554.8 21.2 %collective-permute-start.7 = (bf16[512,384]{1,0:T(8,128)(2,1)}, bf16[512,384]{1,0:T(8,128)(2,1)}, u32[]{:S(2)}, u32[]{:S(2)}) collective-permute-start(bf16[512,384]{1,0:T(8,128)(2,1)} %get-tuple-element.111), channel_id=1, source_target_pairs={{2,0},{4,2},{6,4},{8,6},{10,8},{12,10},{14,12},{16,14},{18,16},{20... | collective-permute-start | bytes 1179656 | tf_op jit(solution)/shard_map/ppermute | solution.py:141
  556.2 20.9 %collective-permute-start.8 = (bf16[512,384]{1,0:T(8,128)(2,1)}, bf16[512,384]{1,0:T(8,128)(2,1)}, u32[]{:S(2)}, u32[]{:S(2)}) collective-permute-start(bf16[512,384]{1,0:T(8,128)(2,1)} %get-tuple-element.112), channel_id=1, source_target_pairs={{4,0},{6,2},{8,4},{10,6},{12,8},{14,10},{16,12},{18,14},{20,16},{2... | collective-permute-start | bytes 1179656 | tf_op jit(solution)/shard_map/ppermute | solution.py:141
  576.0 22.4 %collective-permute-start.21 = (bf16[512,768]{1,0:T(8,128)(2,1)}, bf16[512,768]{1,0:T(8,128)(2,1)}, u32[]{:S(2)}, u32[]{:S(2)}) collective-permute-start(bf16[512,768]{1,0:T(8,128)(2,1)} %convolution_convert_fusion.10), channel_id=1, source_target_pairs={{0,2},{2,0},{4,6},{6,4},{8,10},{10,8},{12,14},{14,12},{16,18},{18,... | collective-permute-start | bytes 2359304 | tf_op jit(solution)/shard_map/ppermute | solution.py:121
  577.1 33.9 %collective-permute-start.20 = (bf16[512,768]{1,0:T(8,128)(2,1)}, bf16[512,768]{1,0:T(8,128)(2,1)}, u32[]{:S(2)}, u32[]{:S(2)}) collective-permute-start(bf16[512,768]{1,0:T(8,128)(2,1)} %convolution_convert_fusion.11), channel_id=1, source_target_pairs={{0,2},{2,0},{4,6},{6,4},{8,10},{10,8},{12,14},{14,12},{16,18},{18,... | collective-permute-start | bytes 2359304 | tf_op jit(solution)/shard_map/ppermute | solution.py:121
  600.3 20.6 %collective-permute-start.22 = (bf16[512,768]{1,0:T(8,128)(2,1)S(1)}, bf16[512,768]{1,0:T(8,128)(2,1)S(1)}, u32[]{:S(2)}, u32[]{:S(2)}) collective-permute-start(bf16[512,768]{1,0:T(8,128)(2,1)S(1)} %add_convert_fusion.9), channel_id=1, source_target_pairs={{0,4},{2,6},{4,0},{6,2},{8,12},{10,14},{12,8},{14,10},{16,20},{18,... | collective-permute-start | bytes 2359304 | tf_op jit(solution)/shard_map/ppermute | solution.py:123
  604.6 105.3 %collective-permute-start.5 = (bf16[512,2048]{1,0:T(8,128)(2,1)}, bf16[512,2048]{1,0:T(8,128)(2,1)}, u32[]{:S(2)}, u32[]{:S(2)}) collective-permute-start(bf16[512,2048]{1,0:T(8,128)(2,1)} %convolution_convert_fusion.9), channel_id=1, source_target_pairs={{0,1},{1,0},{2,3},{3,2},{4,5},{5,4},{6,7},{7,6},{8,9},{9,8},{10,11... | collective-permute-start | bytes 6291464 | tf_op jit(solution)/shard_map/ppermute | solution.py:130
  611.0 213.8 %collective-permute-start.38 = (bf16[512,2560]{1,0:T(8,128)(2,1)}, bf16[512,2560]{1,0:T(8,128)(2,1)}, u32[]{:S(2)}, u32[]{:S(2)}) collective-permute-start(bf16[512,2560]{1,0:T(8,128)(2,1)} %convolution_convert_fusion.3), channel_id=1, source_target_pairs={{0,2},{2,0},{4,6},{6,4},{8,10},{10,8},{12,14},{14,12},{16,18},{18,... | collective-permute-start | bytes 7864328 | tf_op jit(solution)/shard_map/ppermute | solution.py:121
  620.9 76.7 %collective-permute-start.9 = (bf16[512,2048]{1,0:T(8,128)(2,1)}, bf16[512,2048]{1,0:T(8,128)(2,1)}, u32[]{:S(2)}, u32[]{:S(2)}) collective-permute-start(bf16[512,2048]{1,0:T(8,128)(2,1)} %get-tuple-element.146), channel_id=1, source_target_pairs={{0,1},{1,0},{2,3},{3,2},{4,5},{5,4},{6,7},{7,6},{8,9},{9,8},{10,11... | collective-permute-start | bytes 6291464 | tf_op jit(solution)/shard_map/ppermute | solution.py:130
  624.1 10.7 %collective-permute-start.26 = (bf16[128,768]{0,1:T(8,128)(2,1)S(1)}, bf16[128,768]{0,1:T(8,128)(2,1)S(1)}, u32[]{:S(2)}, u32[]{:S(2)}) collective-permute-start(bf16[128,768]{0,1:T(8,128)(2,1)S(1)} %bitcast.375), channel_id=1, source_target_pairs={{0,8},{2,10},{4,12},{6,14},{1,9},{3,11},{5,13},{7,15}} | collective-permute-start | bytes 589832 | tf_op jit(solution)/shard_map/ppermute | solution.py:113
  634.8 0.7 collective-permute-start.23
  635.6 4.8 collective-permute-start.27
  640.4 0.7 collective-permute-start.24
  641.1 24.3 %collective-permute-start.28 = (bf16[128,768]{0,1:T(8,128)(2,1)S(1)}, bf16[128,768]{0,1:T(8,128)(2,1)S(1)}, u32[]{:S(2)}, u32[]{:S(2)}) collective-permute-start(bf16[128,768]{0,1:T(8,128)(2,1)S(1)} %fusion.75), channel_id=1, source_target_pairs={{0,8},{2,10},{4,12},{6,14},{8,16},{10,18},{12,20},{14,22},{16,24},... | collective-permute-start | bytes 589832 | tf_op jit(solution)/shard_map/ppermute | solution.py:113
  658.1 7.7 collective-permute-start.25
  665.5 100.1 %collective-permute-start.29 = (bf16[512,2560]{1,0:T(8,128)(2,1)}, bf16[512,2560]{1,0:T(8,128)(2,1)}, u32[]{:S(2)}, u32[]{:S(2)}) collective-permute-start(bf16[512,2560]{1,0:T(8,128)(2,1)} %convolution_convert_fusion.5), channel_id=1, source_target_pairs={{0,2},{2,0},{4,6},{6,4},{8,10},{10,8},{12,14},{14,12},{16,18},{18,... | collective-permute-start | bytes 7864328 | tf_op jit(solution)/shard_map/ppermute | solution.py:121
  665.7 54.8 %collective-permute-start.47 = (bf16[512,2560]{1,0:T(8,128)(2,1)}, bf16[512,2560]{1,0:T(8,128)(2,1)}, u32[]{:S(2)}, u32[]{:S(2)}) collective-permute-start(bf16[512,2560]{1,0:T(8,128)(2,1)} %convolution_convert_fusion.1), channel_id=1, source_target_pairs={{0,2},{2,0},{4,6},{6,4},{8,10},{10,8},{12,14},{14,12},{16,18},{18,... | collective-permute-start | bytes 7864328 | tf_op jit(solution)/shard_map/ppermute | solution.py:121
  697.6 60.1 %collective-permute-start.49 = (bf16[512,2560]{1,0:T(8,128)(2,1)}, bf16[512,2560]{1,0:T(8,128)(2,1)}, u32[]{:S(2)}, u32[]{:S(2)}) collective-permute-start(bf16[512,2560]{1,0:T(8,128)(2,1)} %add_convert_fusion.1), channel_id=1, source_target_pairs={{0,4},{2,6},{4,0},{6,2},{8,12},{10,14},{12,8},{14,10},{16,20},{18,... | collective-permute-start | bytes 7864328 | tf_op jit(solution)/shard_map/ppermute | solution.py:123
  709.9 104.0 %collective-permute-start.31 = (bf16[512,2560]{1,0:T(8,128)(2,1)}, bf16[512,2560]{1,0:T(8,128)(2,1)}, u32[]{:S(2)}, u32[]{:S(2)}) collective-permute-start(bf16[512,2560]{1,0:T(8,128)(2,1)} %add_convert_fusion.5), channel_id=1, source_target_pairs={{0,4},{2,6},{4,0},{6,2},{8,12},{10,14},{12,8},{14,10},{16,20},{18,... | collective-permute-start | bytes 7864328 | tf_op jit(solution)/shard_map/ppermute | solution.py:123
  720.6 147.8 %collective-permute-start.40 = (bf16[512,2560]{1,0:T(8,128)(2,1)}, bf16[512,2560]{1,0:T(8,128)(2,1)}, u32[]{:S(2)}, u32[]{:S(2)}) collective-permute-start(bf16[512,2560]{1,0:T(8,128)(2,1)} %add_convert_fusion.3), channel_id=1, source_target_pairs={{0,4},{2,6},{4,0},{6,2},{8,12},{10,14},{12,8},{14,10},{16,20},{18,... | collective-permute-start | bytes 7864328 | tf_op jit(solution)/shard_map/ppermute | solution.py:123
  757.7 122.3 %collective-permute-start.11 = (bf16[512,1280]{1,0:T(8,128)(2,1)}, bf16[512,1280]{1,0:T(8,128)(2,1)}, u32[]{:S(2)}, u32[]{:S(2)}) collective-permute-start(bf16[512,1280]{1,0:T(8,128)(2,1)} %pad_maximum_fusion.4), channel_id=1, source_target_pairs={{0,2},{2,0},{4,6},{6,4},{8,10},{10,8},{12,14},{14,12},{16,18},{18,... | collective-permute-start | bytes 3932168 | tf_op jit(solution)/shard_map/ppermute | solution.py:121
  765.5 219.9 %collective-permute-start.10 = (bf16[512,1280]{1,0:T(8,128)(2,1)}, bf16[512,1280]{1,0:T(8,128)(2,1)}, u32[]{:S(2)}, u32[]{:S(2)}) collective-permute-start(bf16[512,1280]{1,0:T(8,128)(2,1)} %pad_maximum_fusion.3), channel_id=1, source_target_pairs={{0,2},{2,0},{4,6},{6,4},{8,10},{10,8},{12,14},{14,12},{16,18},{18,... | collective-permute-start | bytes 3932168 | tf_op jit(solution)/shard_map/ppermute | solution.py:121
  813.9 54.5 %slice-start.1 = ((s8[5242880]{0:T(1024)(128)(4,1)}), s8[1048576]{0:T(1024)(128)(4,1)S(1)}, s32[]{:S(2)}) async-start(s8[5242880]{0:T(1024)(128)(4,1)} %bitcast.288), calls=%async_computation.4 | async-start | bytes 2097152
  813.9 71.6 %collective-permute-start.53 = (bf16[128,2560]{0,1:T(8,128)(2,1)}, bf16[128,2560]{0,1:T(8,128)(2,1)}, u32[]{:S(2)}, u32[]{:S(2)}) collective-permute-start(bf16[128,2560]{0,1:T(8,128)(2,1)} %bitcast.349), channel_id=1, source_target_pairs={{0,8},{2,10},{4,12},{6,14},{1,9},{3,11},{5,13},{7,15}} | collective-permute-start | bytes 1966088 | tf_op jit(solution)/shard_map/ppermute | solution.py:113
  824.8 64.8 %collective-permute-start.32 = (bf16[128,2560]{1,0:T(8,128)(2,1)}, bf16[128,2560]{1,0:T(8,128)(2,1)}, u32[]{:S(2)}, u32[]{:S(2)}) collective-permute-start(bf16[128,2560]{1,0:T(8,128)(2,1)} %get-tuple-element.74), channel_id=1, source_target_pairs={{24,16},{26,18},{28,20},{30,22},{25,17},{27,19},{29,21},{31,23}} | collective-permute-start | bytes 1966088 | tf_op jit(solution)/shard_map/ppermute | solution.py:112
  879.2 8.8 collective-permute-start.50
  880.0 18.5 %collective-permute-start.35 = (bf16[128,2560]{1,0:T(8,128)(2,1)}, bf16[128,2560]{1,0:T(8,128)(2,1)S(1)}, u32[]{:S(2)}, u32[]{:S(2)}) collective-permute-start(bf16[128,2560]{1,0:T(8,128)(2,1)} %get-tuple-element.75), channel_id=1, source_target_pairs={{0,8},{2,10},{4,12},{6,14},{1,9},{3,11},{5,13},{7,15}} | collective-permute-start | bytes 1966088 | tf_op jit(solution)/shard_map/ppermute | solution.py:113
  885.5 6.7 collective-permute-start.41
  888.1 60.0 %collective-permute-start.44 = (bf16[128,2560]{1,0:T(8,128)(2,1)S(1)}, bf16[128,2560]{1,0:T(8,128)(2,1)S(1)}, u32[]{:S(2)}, u32[]{:S(2)}) collective-permute-start(bf16[128,2560]{1,0:T(8,128)(2,1)S(1)} %copy-done.49), channel_id=1, source_target_pairs={{0,8},{2,10},{4,12},{6,14},{1,9},{3,11},{5,13},{7,15}} | collective-permute-start | bytes 1966088 | tf_op jit(solution)/shard_map/ppermute | solution.py:113
  889.6 33.8 %collective-permute-start.54 = (bf16[128,2560]{0,1:T(8,128)(2,1)S(1)}, bf16[128,2560]{0,1:T(8,128)(2,1)S(1)}, u32[]{:S(2)}, u32[]{:S(2)}) collective-permute-start(bf16[128,2560]{0,1:T(8,128)(2,1)S(1)} %fusion.52), channel_id=1, source_target_pairs={{0,8},{2,10},{4,12},{6,14},{8,16},{10,18},{12,20},{14,22},{1,9},{3... | collective-permute-start | bytes 1966088 | tf_op jit(solution)/shard_map/ppermute | solution.py:113
  892.2 7.0 collective-permute-start.33
  898.5 27.4 %collective-permute-start.51 = (bf16[128,2560]{0,1:T(8,128)(2,1)S(1)}, bf16[128,2560]{0,1:T(8,128)(2,1)S(1)}, u32[]{:S(2)}, u32[]{:S(2)}) collective-permute-start(bf16[128,2560]{0,1:T(8,128)(2,1)S(1)} %fusion.54), channel_id=1, source_target_pairs={{16,8},{18,10},{20,12},{22,14},{24,16},{26,18},{28,20},{30,22},{17... | collective-permute-start | bytes 1966088 | tf_op jit(solution)/shard_map/ppermute | solution.py:112
  899.2 50.1 %collective-permute-start.42 = (bf16[128,2560]{1,0:T(8,128)(2,1)S(1)}, bf16[128,2560]{1,0:T(8,128)(2,1)S(1)}, u32[]{:S(2)}, u32[]{:S(2)}) collective-permute-start(bf16[128,2560]{1,0:T(8,128)(2,1)S(1)} %fusion.59), channel_id=1, source_target_pairs={{16,8},{18,10},{20,12},{22,14},{24,16},{26,18},{28,20},{30,22},{17... | collective-permute-start | bytes 1966088 | tf_op jit(solution)/shard_map/ppermute | solution.py:112
  923.4 63.3 %collective-permute-start.12 = (bf16[512,1280]{1,0:T(8,128)(2,1)S(1)}, bf16[512,1280]{1,0:T(8,128)(2,1)S(1)}, u32[]{:S(2)}, u32[]{:S(2)}) collective-permute-start(bf16[512,1280]{1,0:T(8,128)(2,1)S(1)} %fusion.43), channel_id=1, source_target_pairs={{0,4},{2,6},{4,0},{6,2},{8,12},{10,14},{12,8},{14,10},{16,20},{18,... | collective-permute-start | bytes 3932168 | tf_op jit(solution)/shard_map/ppermute | solution.py:123
  925.9 71.4 %collective-permute-start.55 = (bf16[128,2560]{0,1:T(8,128)(2,1)}, bf16[128,2560]{0,1:T(8,128)(2,1)}, u32[]{:S(2)}, u32[]{:S(2)}) collective-permute-start(bf16[128,2560]{0,1:T(8,128)(2,1)} %fusion.53), channel_id=1, source_target_pairs={{0,8},{2,10},{4,12},{6,14},{8,16},{10,18},{12,20},{14,22},{16,24},... | collective-permute-start | bytes 1966088 | tf_op jit(solution)/shard_map/ppermute | solution.py:113
  948.0 53.3 %collective-permute-start.52 = (bf16[128,2560]{0,1:T(8,128)(2,1)}, bf16[128,2560]{0,1:T(8,128)(2,1)}, u32[]{:S(2)}, u32[]{:S(2)}) collective-permute-start(bf16[128,2560]{0,1:T(8,128)(2,1)} %fusion.55), channel_id=1, source_target_pairs={{8,0},{10,2},{12,4},{14,6},{16,8},{18,10},{20,12},{22,14},{24,16},... | collective-permute-start | bytes 1966088 | tf_op jit(solution)/shard_map/ppermute | solution.py:112
  949.3 21.3 %collective-permute-start.36 = (bf16[128,2560]{1,0:T(8,128)(2,1)S(1)}, bf16[128,2560]{1,0:T(8,128)(2,1)S(1)}, u32[]{:S(2)}, u32[]{:S(2)}) collective-permute-start(bf16[128,2560]{1,0:T(8,128)(2,1)S(1)} %get-tuple-element.73), channel_id=1, source_target_pairs={{0,8},{2,10},{4,12},{6,14},{8,16},{10,18},{12,20},{14,22},{1,9},{3... | collective-permute-start | bytes 1966088 | tf_op jit(solution)/shard_map/ppermute | solution.py:113
  970.6 12.5 %collective-permute-start.45 = (bf16[128,2560]{1,0:T(8,128)(2,1)S(1)}, bf16[128,2560]{1,0:T(8,128)(2,1)S(1)}, u32[]{:S(2)}, u32[]{:S(2)}) collective-permute-start(bf16[128,2560]{1,0:T(8,128)(2,1)S(1)} %get-tuple-element.77), channel_id=1, source_target_pairs={{0,8},{2,10},{4,12},{6,14},{8,16},{10,18},{12,20},{14,22},{1,9},{3... | collective-permute-start | bytes 1966088 | tf_op jit(solution)/shard_map/ppermute | solution.py:113
  983.1 45.5 %collective-permute-start.34 = (bf16[128,2560]{1,0:T(8,128)(2,1)}, bf16[128,2560]{1,0:T(8,128)(2,1)}, u32[]{:S(2)}, u32[]{:S(2)}) collective-permute-start(bf16[128,2560]{1,0:T(8,128)(2,1)} %get-tuple-element.72), channel_id=1, source_target_pairs={{8,0},{10,2},{12,4},{14,6},{16,8},{18,10},{20,12},{22,14},{24,16},... | collective-permute-start | bytes 1966088 | tf_op jit(solution)/shard_map/ppermute | solution.py:112
  985.4 45.7 %collective-permute-start.43 = (bf16[128,2560]{1,0:T(8,128)(2,1)}, bf16[128,2560]{1,0:T(8,128)(2,1)}, u32[]{:S(2)}, u32[]{:S(2)}) collective-permute-start(bf16[128,2560]{1,0:T(8,128)(2,1)} %get-tuple-element.76), channel_id=1, source_target_pairs={{8,0},{10,2},{12,4},{14,6},{16,8},{18,10},{20,12},{22,14},{24,16},... | collective-permute-start | bytes 1966088 | tf_op jit(solution)/shard_map/ppermute | solution.py:112
  986.7 42.7 %collective-permute-start.37 = (bf16[128,2560]{1,0:T(8,128)(2,1)}, bf16[128,2560]{1,0:T(8,128)(2,1)}, u32[]{:S(2)}, u32[]{:S(2)}) collective-permute-start(bf16[128,2560]{1,0:T(8,128)(2,1)} %fusion.63), channel_id=1, source_target_pairs={{0,8},{2,10},{4,12},{6,14},{8,16},{10,18},{12,20},{14,22},{16,24},... | collective-permute-start | bytes 1966088 | tf_op jit(solution)/shard_map/ppermute | solution.py:113
  997.3 33.8 %collective-permute-start.46 = (bf16[128,2560]{1,0:T(8,128)(2,1)}, bf16[128,2560]{1,0:T(8,128)(2,1)}, u32[]{:S(2)}, u32[]{:S(2)}) collective-permute-start(bf16[128,2560]{1,0:T(8,128)(2,1)} %fusion.58), channel_id=1, source_target_pairs={{0,8},{2,10},{4,12},{6,14},{8,16},{10,18},{12,20},{14,22},{16,24},... | collective-permute-start | bytes 1966088 | tf_op jit(solution)/shard_map/ppermute | solution.py:113
  1001.3 20.9 %collective-permute-start.16 = (bf16[128,1280]{0,1:T(8,128)(2,1)S(1)}, bf16[128,1280]{0,1:T(8,128)(2,1)}, u32[]{:S(2)}, u32[]{:S(2)}) collective-permute-start(bf16[128,1280]{0,1:T(8,128)(2,1)S(1)} %bitcast.369), channel_id=1, source_target_pairs={{0,8},{2,10},{4,12},{6,14},{1,9},{3,11},{5,13},{7,15}} | collective-permute-start | bytes 983048 | tf_op jit(solution)/shard_map/ppermute | solution.py:113
  1022.2 1.7 collective-permute-start.13
  1024.0 11.8 %collective-permute-start.17 = (bf16[128,1280]{0,1:T(8,128)(2,1)S(1)}, bf16[128,1280]{0,1:T(8,128)(2,1)S(1)}, u32[]{:S(2)}, u32[]{:S(2)}) collective-permute-start(bf16[128,1280]{0,1:T(8,128)(2,1)S(1)} %fusion.70), channel_id=1, source_target_pairs={{0,8},{2,10},{4,12},{6,14},{8,16},{10,18},{12,20},{14,22},{1,9},{3... | collective-permute-start | bytes 983048 | tf_op jit(solution)/shard_map/ppermute | solution.py:113
  1028.6 11.6 %collective-permute-start.14 = (bf16[128,1280]{0,1:T(8,128)(2,1)S(1)}, bf16[128,1280]{0,1:T(8,128)(2,1)S(1)}, u32[]{:S(2)}, u32[]{:S(2)}) collective-permute-start(bf16[128,1280]{0,1:T(8,128)(2,1)S(1)} %fusion.72), channel_id=1, source_target_pairs={{16,8},{18,10},{20,12},{22,14},{24,16},{26,18},{28,20},{30,22},{17... | collective-permute-start | bytes 983048 | tf_op jit(solution)/shard_map/ppermute | solution.py:112
  1035.8 9.8 collective-permute-start.18
  1040.3 9.0 collective-permute-start.15
  1050.4 5.0 collective-permute-start.19
  (79 other events, 991.6 us)
Sparse Core Ops, SparseCore 0:
  13.1 80.8 all-gather.3
  96.1 100.1 all-gather.7
  198.5 106.9 all-gather.5

commit v2 on v1

v2 whole, which is shorter than its diff:
```python
import functools
import math

import jax
import jax.numpy as jnp
from jax import lax
from jax.experimental import pallas as pl
from jax.experimental.pallas import tpu as pltpu
from jax.sharding import PartitionSpec as P

QH = 24
KVH = 6
HD = 64
GROUP = QH // KVH
WINDOW = 1024
SEQ_LEN = 8192
LANES = 128

EPSILON = 1e-06
SCORE_SCALE = 0.125
MASKED = -1e30
ROPE_BASE = 10000.0
EXP2_SCALE = SCORE_SCALE * math.log2(math.e)
TILE = 256
SUM_ROWS = 16

bf16 = jnp.bfloat16
f32 = jnp.float32


def angles_of(positions):
    half_width = HD // 2
    frequency = jnp.exp(
        jnp.arange(half_width, dtype=f32) * (-math.log(ROPE_BASE) / half_width)
    )
    phases = frequency[:, None] * positions.astype(f32)[None, :]
    return jnp.cos(phases)[None], jnp.sin(phases)[None]


def rotate(values, cos_table, sin_table):
    half_width = values.shape[1] // 2
    first_half = values[:, :half_width]
    second_half = values[:, half_width:]
    return jnp.concatenate(
        [
            first_half * cos_table - second_half * sin_table,
            second_half * cos_table + first_half * sin_table,
        ],
        axis=1,
    )


def inverse_rms(values, axis):
    return lax.rsqrt(jnp.mean(values * values, axis=axis, keepdims=True) + EPSILON)


def rms_back(values, scale, weight, d_out, axis):
    weighted = d_out * weight
    pull = jnp.mean(weighted * values, axis=axis, keepdims=True)
    return scale * weighted - values * (scale * scale * scale * pull)


class Ring:
    def __init__(self):
        self.count = lax.axis_size("dp")
        self.outer = self.count // 4
        index = lax.axis_index("dp")
        self.index = index
        self.core = index % 2
        self.mid = (index // 2) % 2
        self.place = index // 4
        self.core_pairs = [(i, i ^ 1) for i in range(self.count)]
        self.mid_pairs = [(i, i ^ 2) for i in range(self.count)]

    def pick(self, array, bit, axis):
        return lax.dynamic_index_in_dim(array, bit, axis, keepdims=False)

    def rows(self, array):
        width, count = array.shape
        blocks = array.reshape(self.outer, 2, 2, width // self.count, count)
        halves = []
        for bit in (1 - self.core, self.core):
            half = self.pick(blocks, bit, 2)
            both = [self.pick(half, self.mid, 1), self.pick(half, 1 - self.mid, 1)]
            halves.append(jnp.concatenate([part.reshape(width // 4, count) for part in both]))
        return halves

    def chain(self, blocks):
        total = self.pick(blocks, self.place, 0).astype(f32)
        for shift in range(1, self.outer):
            pairs = [(i, (i + 4 * shift) % self.count) for i in range(self.count)]
            sent = self.pick(blocks, (self.place + shift) % self.outer, 0)
            total = total + lax.ppermute(sent, "dp", pairs).astype(f32)
        return total

    def scatter(self, make):
        got = lax.ppermute(make(0).astype(bf16), "dp", self.core_pairs)
        both = make(1) + got.astype(f32)
        half = both.shape[0] // 2
        got_mid = lax.ppermute(both[half:].astype(bf16), "dp", self.mid_pairs)
        kept = (both[:half] + got_mid.astype(f32)).astype(bf16)
        return self.chain(kept.reshape((self.outer, -1) + kept.shape[1:]))


def other_tensor(array):
    count = lax.axis_size("tensor")
    return lax.ppermute(array, "tensor", [(i, (i + 1) % count) for i in range(count)])


def tensor_sum(partial):
    low = partial.astype(bf16)
    return low.astype(f32) + other_tensor(low).astype(f32)


def from_behind(shard, by):
    length = lax.axis_size("dp")
    pairs = [(i, i + by) for i in range(length) if 0 <= i + by < length]
    return lax.ppermute(shard, "dp", pairs)


def tn_dot(left, right):
    return lax.dot_general(left, right, (((0,), (0,)), ((), ())), preferred_element_type=f32)


def nt_dot(left, right):
    return lax.dot_general(left, right, (((1,), (1,)), ((), ())), preferred_element_type=f32)


def nn_dot(left, right):
    return jnp.dot(left, right, preferred_element_type=f32)


def attend_kernel(shift, q_ref, k_ref, v_ref, bias_ref, out_ref, inverse_ref):
    rows = q_ref.shape[1]
    for first in range(0, rows, TILE):
        at = slice(first, first + TILE)
        for head in range(GROUP):
            of = slice(head * HD, (head + 1) * HD)
            query = q_ref[of, at]
            total = jnp.zeros((HD + SUM_ROWS, TILE), f32)
            for start in range(first + shift, first + shift + WINDOW + TILE, TILE):
                near = slice(start, start + TILE)
                scores = nn_dot(k_ref[0, near, :], query)
                weight = jnp.exp2(scores * EXP2_SCALE + bias_ref[near, at]).astype(bf16)
                total = total + nn_dot(v_ref[0, :, near], weight)
            inverse = 1.0 / total[HD : HD + 1]
            out_ref[of, at] = (total[:HD] * inverse).astype(bf16)
            inverse_ref[0, head : head + 1, at] = inverse


def attend_back_kernel(shift, q_ref, k_ref, kt_ref, v_ref, d_ref, o_ref, inverse_ref, bias_ref, dq_ref, dk_ref, dv_ref):
    rows = q_ref.shape[1]
    dk_ref[...] = jnp.zeros_like(dk_ref)
    dv_ref[...] = jnp.zeros_like(dv_ref)
    for first in range(0, rows, TILE):
        at = slice(first, first + TILE)
        deltas = []
        for head in range(GROUP):
            of = slice(head * HD, (head + 1) * HD)
            deltas.append(jnp.sum(d_ref[of, at].astype(f32) * o_ref[of, at].astype(f32), axis=0, keepdims=True))
        d_query = [jnp.zeros((HD, TILE), f32) for _ in range(GROUP)]
        for start in range(first + shift, first + shift + WINDOW + TILE, TILE):
            near = slice(start, start + TILE)
            d_key = jnp.zeros((HD, TILE), f32)
            d_value = jnp.zeros((HD, TILE), f32)
            for head in range(GROUP):
                of = slice(head * HD, (head + 1) * HD)
                query = q_ref[of, at]
                d_out = d_ref[of, at]
                scores = nn_dot(k_ref[0, near, :], query)
                prob = jnp.exp2(scores * EXP2_SCALE + bias_ref[near, at]) * inverse_ref[0, head : head + 1, at]
                d_prob = nn_dot(v_ref[0, near, :], d_out)
                d_scores = (prob * (d_prob - deltas[head])).astype(bf16)
                d_query[head] = d_query[head] + nn_dot(kt_ref[:, near], d_scores)
                d_key = d_key + nt_dot(query, d_scores)
                d_value = d_value + nt_dot(d_out, prob.astype(bf16))
            dk_ref[:, near] += d_key
            dv_ref[:, near] += d_value
        for head in range(GROUP):
            dq_ref[head * HD : (head + 1) * HD, at] = d_query[head]


def attend(q_t, k, v_t, bias):
    kv, keys, _ = k.shape
    rows = q_t.shape[1]
    ones = jnp.ones((kv, SUM_ROWS, keys), bf16)
    v_ones = jnp.concatenate([v_t.reshape(kv, HD, keys), ones], axis=1)
    return pl.pallas_call(
        functools.partial(attend_kernel, keys - rows - WINDOW),
        grid=(kv,),
        in_specs=[
            pl.BlockSpec((GROUP * HD, rows), lambda h: (h, 0)),
            pl.BlockSpec((1, keys, HD), lambda h: (h, 0, 0)),
            pl.BlockSpec((1, HD + SUM_ROWS, keys), lambda h: (h, 0, 0)),
            pl.BlockSpec((keys, rows), lambda h: (0, 0)),
        ],
        out_specs=[
            pl.BlockSpec((GROUP * HD, rows), lambda h: (h, 0)),
            pl.BlockSpec((1, 8, rows), lambda h: (h, 0, 0)),
        ],
        out_shape=[jax.ShapeDtypeStruct((kv * GROUP * HD, rows), bf16), jax.ShapeDtypeStruct((kv, 8, rows), f32)],
        compiler_params=pltpu.CompilerParams(vmem_limit_bytes=40 * 2**20),
        cost_estimate=pl.CostEstimate(flops=4 * kv * GROUP * HD * rows * (WINDOW + TILE), bytes_accessed=8 * 2**20, transcendentals=kv * GROUP * rows * (WINDOW + TILE)),
    )(q_t, k, v_ones, bias)


def attend_back(q_t, k, k_t, v, d_t, o_t, inverse, bias):
    kv, keys, _ = k.shape
    rows = q_t.shape[1]
    head_block = pl.BlockSpec((GROUP * HD, rows), lambda h: (h, 0))
    key_block = pl.BlockSpec((1, keys, HD), lambda h: (h, 0, 0))
    key_t_block = pl.BlockSpec((HD, keys), lambda h: (h, 0))
    return pl.pallas_call(
        functools.partial(attend_back_kernel, keys - rows - WINDOW),
        grid=(kv,),
        in_specs=[head_block, key_block, key_t_block, key_block, head_block, head_block,
            pl.BlockSpec((1, 8, rows), lambda h: (h, 0, 0)),
            pl.BlockSpec((keys, rows), lambda h: (0, 0)),
        ],
        out_specs=[head_block, key_t_block, key_t_block],
        out_shape=[jax.ShapeDtypeStruct((kv * GROUP * HD, rows), f32), jax.ShapeDtypeStruct((kv * HD, keys), f32), jax.ShapeDtypeStruct((kv * HD, keys), f32)],
        compiler_params=pltpu.CompilerParams(vmem_limit_bytes=40 * 2**20),
        cost_estimate=pl.CostEstimate(flops=10 * kv * GROUP * HD * rows * (WINDOW + TILE), bytes_accessed=12 * 2**20, transcendentals=kv * GROUP * rows * (WINDOW + TILE)),
    )(q_t, k, k_t, v, d_t, o_t, inverse, bias)


def shards(
    tokens,
    w_query,
    w_keyval,
    w_out,
    w_gateup,
    w_down,
    attn_gain,
    ffn_gain,
    qk_gain,
    segments,
    positions,
    cotangent,
):
    ring = Ring()
    row_count = tokens.shape[0]
    depth = w_query.shape[0]
    model = tokens.shape[1]
    hidden = w_gateup.shape[2]
    tensor = lax.axis_index("tensor")
    query_width = w_query.shape[1]
    local_heads = query_width // HD
    local_kv = local_heads // GROUP
    kv_width = local_kv * HD
    all_kv = w_keyval.shape[1] // 2
    qkv_width = query_width + 2 * kv_width
    gain_count = 2 * qk_gain.shape[1]

    own_keyval = lax.dynamic_index_in_dim(
        w_keyval.reshape(depth, 2, all_kv // kv_width, kv_width), tensor, 2, keepdims=False
    ).reshape(depth, 2 * kv_width)
    head_gain_column = jnp.pad(qk_gain.reshape(gain_count), (0, depth - gain_count))
    gains = jnp.stack([attn_gain, ffn_gain, head_gain_column], axis=1)
    gains = jnp.pad(gains, ((0, 0), (0, LANES - gains.shape[1])))
    first_pack = jnp.concatenate([w_query, own_keyval, w_out.T, gains, w_down.T], axis=1)
    first_full = lax.all_gather(first_pack.astype(bf16), "dp", axis=0, tiled=True)
    gateup_full = lax.all_gather(
        w_gateup.reshape(depth, 2 * hidden).astype(bf16), "dp", axis=0, tiled=True
    )
    qkv_full = first_full[:, :qkv_width]
    gain_start = qkv_width + query_width
    out_full = first_full[:, qkv_width:gain_start]
    down_full = first_full[:, gain_start + LANES :]
    gain_columns = first_full[:, gain_start : gain_start + 3].astype(f32)
    attn_weight = gain_columns[:, 0]
    ffn_weight = gain_columns[:, 1]
    head_gains = gain_columns[:, 2].reshape(ring.count, depth)[:, :gain_count]
    head_gains = head_gains.reshape(ring.count, 2, qk_gain.shape[1]).transpose(1, 0, 2).reshape(2, HD)
    gain_query = head_gains[0][:, None]
    gain_key = head_gains[1][:, None]

    marks = (segments + 1).astype(bf16)
    seq_devices = min(SEQ_LEN // row_count, ring.count)
    own_sequence = ring.index // seq_devices
    reach_count = -(-WINDOW // row_count)
    halo_marks = []
    for step_back in range(reach_count, 0, -1):
        same_sequence = ((ring.index - step_back) // seq_devices == own_sequence).astype(bf16)
        halo_marks.append(from_behind(marks, step_back) * same_sequence)
    key_marks = jnp.concatenate(halo_marks + [marks], axis=0)
    key_count = key_marks.shape[0]
    distance = (jnp.arange(row_count, dtype=jnp.int32) + reach_count * row_count)[
        None, :
    ] - jnp.arange(key_count, dtype=jnp.int32)[:, None]
    allowed = (distance >= 0) & (distance < WINDOW) & (key_marks[:, None] == marks[None, :])
    bias = jnp.where(allowed, 0.0, MASKED).astype(f32)
    cos_table, sin_table = angles_of(positions)

    residual = tokens.astype(f32)
    attn_scale = inverse_rms(residual, 1)

    normed_low = (residual * attn_scale * attn_weight).astype(bf16)
    qkv_raw = lax.dot_general(
        qkv_full, normed_low, (((0,), (1,)), ((), ())), preferred_element_type=f32
    )
    query_raw = qkv_raw[:query_width].reshape(local_heads, HD, row_count)
    key_raw = qkv_raw[query_width : query_width + kv_width].reshape(local_kv, HD, row_count)
    query_scale = inverse_rms(query_raw, 1)
    key_scale = inverse_rms(key_raw, 1)
    query_low = rotate(query_raw * query_scale * gain_query, cos_table, sin_table).astype(bf16)
    key_low = rotate(key_raw * key_scale * gain_key, cos_table, sin_table).astype(bf16)
    query_low = query_low.reshape(query_width, row_count)
    keyval_low = jnp.concatenate(
        [key_low.reshape(kv_width, row_count), qkv_raw[query_width + kv_width :].astype(bf16)], axis=0
    )
    halo = [from_behind(keyval_low, step_back) for step_back in range(reach_count, 0, -1)]
    key_keyval = jnp.concatenate(halo + [keyval_low], axis=1)
    keys_t = key_keyval[:kv_width]
    values_t = key_keyval[kv_width:]
    keys = keys_t.reshape(local_kv, HD, key_count).transpose(0, 2, 1)
    values = values_t.reshape(local_kv, HD, key_count).transpose(0, 2, 1)
    attended, inverse_total = attend(query_low, keys, values_t, bias)
    mid_part = lax.dot_general(
        attended, out_full, (((0,), (1,)), ((), ())), preferred_element_type=f32
    )
    mid = residual + tensor_sum(mid_part)

    d_act = nn_dot(cotangent, down_full)
    ffn_scale = inverse_rms(mid, 1)
    normed2_low = (mid * ffn_scale * ffn_weight).astype(bf16)
    gate = nn_dot(normed2_low, gateup_full[:, :hidden])
    up = nn_dot(normed2_low, gateup_full[:, hidden:])
    gate_sigmoid = jax.nn.sigmoid(gate)
    gate_silu = gate * gate_sigmoid
    act_low = (gate_silu * up).astype(bf16)
    d_gate = (d_act * up * gate_sigmoid * (1.0 + gate * (1.0 - gate_sigmoid))).astype(bf16)
    d_up = (d_act * gate_silu).astype(bf16)
    d_normed2 = tensor_sum(
        nt_dot(d_gate, gateup_full[:, :hidden]) + nt_dot(d_up, gateup_full[:, hidden:])
    )
    grad_down = lax.psum_scatter(
        tn_dot(cotangent, act_low).astype(bf16), "dp", scatter_dimension=0, tiled=True
    )
    grad_down = grad_down.astype(f32).T
    normed2_rows = ring.rows(normed2_low.T)
    pieces = []
    piece_width = hidden // 2
    for source in (d_gate, d_up):
        for start in range(0, hidden, piece_width):
            piece = source[:, start : start + piece_width]
            pieces.append(ring.scatter(lambda part, piece=piece: nn_dot(normed2_rows[part], piece)))
    grad_gateup = jnp.concatenate(pieces, axis=1).reshape(depth, 2, hidden)
    result = mid + tensor_sum(nt_dot(act_low, down_full))
    output = result.astype(bf16)
    d_ffn_weight = jnp.sum(d_normed2 * mid * ffn_scale, axis=0)
    d_mid = cotangent.astype(f32) + rms_back(mid, ffn_scale, ffn_weight, d_normed2, 1)

    d_mid_low = d_mid.astype(bf16)
    d_mid_rows = ring.rows(d_mid_low.T)
    grad_out = ring.scatter(lambda part: nt_dot(d_mid_rows[part], attended)).T
    d_attended = lax.dot_general(
        out_full, d_mid_low, (((0,), (1,)), ((), ())), preferred_element_type=f32
    ).astype(bf16)
    d_query, d_keys, d_values = attend_back(
        query_low, keys, keys_t, values, d_attended, attended, inverse_total, bias
    )
    d_keyval_all = jnp.concatenate([d_keys * SCORE_SCALE, d_values], axis=0)
    own_grad = d_keyval_all[:, reach_count * row_count :]
    for step_back in range(1, reach_count + 1):
        piece_start = (reach_count - step_back) * row_count
        piece = d_keyval_all[:, piece_start : piece_start + row_count].astype(bf16)
        own_grad = own_grad + from_behind(piece, -step_back).astype(f32)

    def head_back(raw, scale, gain, d_rotated):
        d_normed_head = rotate(d_rotated, cos_table, -sin_table)
        d_gain = jnp.sum(d_normed_head * raw * scale, axis=(0, 2))
        return rms_back(raw, scale, gain, d_normed_head, 1), d_gain

    d_query_raw, d_gain_query = head_back(
        query_raw,
        query_scale,
        gain_query,
        d_query.reshape(local_heads, HD, row_count) * SCORE_SCALE,
    )
    d_key_raw, d_gain_key = head_back(
        key_raw, key_scale, gain_key, own_grad[:kv_width].reshape(local_kv, HD, row_count)
    )
    d_qkv_low = jnp.concatenate(
        [
            d_query_raw.reshape(query_width, row_count),
            d_key_raw.reshape(kv_width, row_count),
            own_grad[kv_width:],
        ],
        axis=0,
    ).astype(bf16)
    d_normed_part = lax.dot_general(
        d_qkv_low, qkv_full, (((0,), (1,)), ((), ())), preferred_element_type=f32
    )
    d_normed = tensor_sum(d_normed_part)
    d_attn_part = jnp.sum(d_normed_part * residual * attn_scale, axis=0)

    head_rows = jnp.stack([d_gain_query, d_gain_key], axis=0).reshape(2, ring.count, gain_count // 2)
    head_rows = head_rows.transpose(1, 0, 2).reshape(ring.count, gain_count)
    head_column = jnp.pad(head_rows, ((0, 0), (0, depth - gain_count))).reshape(model)
    gain_grads = jnp.stack([d_attn_part, d_ffn_weight, head_column], axis=1)
    gain_grads = jnp.pad(gain_grads, ((0, 0), (0, LANES - gain_grads.shape[1])))
    grad_qkv = lax.dot_general(
        normed_low, d_qkv_low, (((0,), (1,)), ((), ())), preferred_element_type=f32
    )
    grad_qkv = lax.psum_scatter(
        jnp.concatenate([grad_qkv, gain_grads], axis=1).astype(bf16),
        "dp",
        scatter_dimension=0,
        tiled=True,
    )
    grad_query = grad_qkv[:, :query_width].astype(f32)
    shared = grad_qkv[:, query_width:]
    shared_other = other_tensor(shared).astype(f32)
    shared = shared.astype(f32)
    first = tensor == 0
    keyval_mine = shared[:, : 2 * kv_width].reshape(depth, 2, 1, kv_width)
    keyval_theirs = shared_other[:, : 2 * kv_width].reshape(depth, 2, 1, kv_width)
    grad_keyval = jnp.concatenate(
        [
            jnp.where(first, keyval_mine, keyval_theirs),
            jnp.where(first, keyval_theirs, keyval_mine),
        ],
        axis=2,
    ).reshape(depth, 2 * all_kv)
    gains_mine = shared[:, 2 * kv_width :]
    gains_sum = gains_mine + shared_other[:, 2 * kv_width :]
    grad_attn_gain = gains_sum[:, 0]
    grad_ffn_gain = gains_mine[:, 1]
    grad_heads = gains_sum[:gain_count, 2].reshape(2, gain_count // 2)
    input_grad = (d_mid + rms_back(residual, attn_scale, attn_weight, d_normed, 1)).astype(bf16)
    return (
        output,
        input_grad,
        grad_query,
        grad_keyval,
        grad_out,
        grad_gateup,
        grad_down,
        grad_attn_gain,
        grad_ffn_gain,
        grad_heads,
    )


def solution(mesh):
    in_specs = (
        P("dp", None),
        P("dp", "tensor"),
        P("dp", None),
        P("tensor", "dp"),
        P("dp", None, "tensor"),
        P("tensor", "dp"),
        P("dp"),
        P("dp"),
        P(None, "dp"),
        P("dp"),
        P("dp"),
        P("dp", None),
    )
    out_specs = (
        P("dp", None),
        P("dp", None),
        P("dp", "tensor"),
        P("dp", None),
        P("tensor", "dp"),
        P("dp", None, "tensor"),
        P("tensor", "dp"),
        P("dp"),
        P("dp"),
        P(None, "dp"),
    )
    return jax.shard_map(shards, mesh=mesh, in_specs=in_specs, out_specs=out_specs, check_vma=False)
```

time: 1070 us -> 910 us (0.85)
  matrix products: 247 us -> 138 us
  other arithmetic: 141 us -> 60.5 us
  Pallas kernels: 0 us -> 45.3 us
  waiting for transfers between devices: 388 us -> 430 us
  starting transfers between devices: 141 us -> 100 us
  local copies, waits for them, and re-layouts: 132 us -> 112 us
    ppermute x5, waiting for transfers between devices: 68.4 us -> 141 us  [other_tensor(): lax.ppermute(array, 'tensor', [(i, (i + 1) % count) for i in range(count)])]
    dot_general x6 -> x5, matrix products: 94.4 us -> 26.3 us  [the longest x1 7.29 us: shards(): lax.dot_general(d_qkv_low, qkv_full, (((0,), (1,)), ((), ())), preferred_...]
    convert_element_type x32 -> x8, other arithmetic: 76.3 us -> 9.83 us  [the longest x1 6.08 us: shards(): (d_mid + rms_back(residual, attn_scale, attn_weight, d_normed, 1)).astype...]
    dot_general x20 -> x1, matrix products: 63.9 us -> 10.6 us  [tn_dot(): lax.dot_general(left, right, (((0,), (0,)), ((), ())), preferred_element_...]
    ppermute x45 -> x25, waiting for transfers between devices: 202 us -> 153 us  [the longest x5 118 us: scatter(): got_mid = lax.ppermute(both[half:].astype(bf16), 'dp', self.mid_pairs)]
    pallas_call x0 -> x2, Pallas kernels: none -> 45.3 us  [the longest x1 32.1 us: attend_back(): pl.pallas_call(functools.partial(attend_back_kernel, keys - rows - WINDOW...]
    ppermute x45 -> x25, starting transfers between devices: 118 us -> 76.8 us  [the longest x15 70.3 us: chain(): total = total + lax.ppermute(sent, 'dp', pairs).astype(f32)]
    all_gather x1, waiting for transfers between devices: 51.8 us -> 14.1 us  [shards(): lax.all_gather(w_gateup.reshape(depth, 2 * hidden).astype(bf16), 'dp', ax...]
  transfers between devices with their start and end apart: 59 -> 40, of which waited for: 20 -> 19; matrix products, arithmetic and copies ran while one was open for 43% -> 23% of each run, Pallas kernels for 0% -> 1%
where the time goes in v2:
time: 910 us; the launch traced here: 901 us
  waiting for transfers between devices  430 us (47%)
  matrix products  138 us (15%)
  local copies, waits for them, and re-layouts  112 us (12%)
  starting transfers between devices  100 us (11%)
  other arithmetic  60.5 us (7%)
  Pallas kernels  45.3 us (5%)
  between operations  15.4 us (2%)
    ppermute x5, waiting for transfers between devices, other_tensor(): lax.ppermute(array, 'tensor', [(i, (i + 1) % count) for i in range(count)])  141 us
    ppermute x5, waiting for transfers between devices, scatter(): got_mid = lax.ppermute(both[half:].astype(bf16), 'dp', self.mid_pairs)  118 us
    all_gather x1, waiting for transfers between devices, shards(): lax.all_gather(first_pack.astype(bf16), 'dp', axis=0, tiled=True)  98.1 us
    ppermute x15, starting transfers between devices, chain(): total = total + lax.ppermute(sent, 'dp', pairs).astype(f32)  70.3 us
    unnamed x142, local copies, waits for them, and re-layouts  65.3 us
    dot_general x11, matrix products, nn_dot(): return jnp.dot(left, right, preferred_element_type=f32)  64.9 us
    dot_general x5, matrix products, nt_dot(): lax.dot_general(left, right, (((1,), (1,)), ((), ())), preferred_element_...  36.2 us
    ppermute x15, waiting for transfers between devices, chain(): total = total + lax.ppermute(sent, 'dp', pairs).astype(f32)  35.5 us
  transfers between devices with their start and end apart: 40, of which 19 were waited for; matrix products, arithmetic and copies ran while one was open for 23% of the time, Pallas kernels for 1%

profile of v2, /device:TPU:0, one launch (start us, length us, event | category | flops | bytes accessed | tf_op | source)
XLA Modules:
  0.0 901.5 jit_solution(9591201280503262921)
XLA Ops:
  21.8 4.4 collective-permute-start.2
  28.7 98.1 %all-gather.3.cloned.1.call-done = bf16[2048,4608]{0,1:T(8,128)(2,1)} async-done(((bf16[128,4608]{0,1:T(8,128)(2,1)}), bf16[2048,4608]{0,1:T(8,128)(2,1)}) %all-gather.3.cloned.1.call-update) | async-done | bytes 18874384 | tf_op jit(solution)/shard_map/all_gather | solution.py:262
  128.2 5.3 fusion.29
  143.9 4.1 collective-permute-start
  157.4 8.1 collective-permute-done
  173.7 13.2 %shard_map.195 = (bf16[768,512]{1,0:T(8,128)(2,1)S(1)}, f32[3,8,512]{2,1,0:T(8,128)S(1)}) custom-call(bf16[768,512]{1,0:T(8,128)(2,1)S(1)} %bitcast.180, bf16[3,1536,64]{2,1,0:T(8,128)(2,1)S(1)} %bitcast.177, bf16[3,80,1536]{2,1,0:T(8,128)(2,1)S(1)} %concatenate.70.v_ref, f32[1536,512]{1,0:T(8,128)S(1)} %fusion.38.bias_ref), custom_call_target="tpu_custom_call" | custom-call | flops 2013265920 | bytes 8388608 | tf_op jit(solution)/shard_map/pallas_call | solution.py:188
  186.9 4.1 convolution_convert_fusion.6
  192.6 10.0 %fusion.1 = f32[2560,512]{0,1:T(8,128)} fusion(bf16[512,2048]{1,0:T(8,128)(2,1)S(1)} %copy-done.25, bf16[2048,4608]{0,1:T(8,128)(2,1)} %all-gather.3.cloned.1.call-done), kind=kOutput, calls=%fused_computation.8 | convolution fusion | flops 5368709120 | bytes 17825792 | tf_op jit(solution)/shard_map/dot_general | solution.py:130
  202.6 25.9 %collective-permute-done.4 = bf16[512,2048]{1,0:T(8,128)(2,1)S(1)} collective-permute-done((bf16[512,2048]{1,0:T(8,128)(2,1)S(1)}, bf16[512,2048]{1,0:T(8,128)(2,1)S(1)}, u32[]{:S(2)}, u32[]{:S(2)}) %collective-permute-start.4) | collective-permute-done | bytes 2097184 | tf_op jit(solution)/shard_map/ppermute | solution.py:107
  231.4 14.1 %all-gather.5.cloned.1.call-done = bf16[2048,5120]{1,0:T(8,128)(2,1)} async-done(((bf16[128,5120]{1,0:T(8,128)(2,1)}), bf16[2048,5120]{1,0:T(8,128)(2,1)}) %all-gather.5.cloned.1.call-update) | async-done | bytes 20971536 | tf_op jit(solution)/shard_map/all_gather | solution.py:263
  245.5 12.6 %fusion.11 = f32[512,2560]{1,0:T(8,128)} fusion(bf16[2048,5120]{1,0:T(8,128)(2,1)} %all-gather.5.cloned.1.call-done, f32[512,2048]{1,0:T(8,128)} %get-tuple-element.67, f32[2048]{0:T(1024)S(1)} %bitcast.236, f32[512]{0:T(512)S(1)} %add_rsqrt_fusion.2), kind=kOutput, calls=%fused_computation.18 | convolution fusion | flops 5371854848 | bytes 19933184 | tf_op jit(solution)/shard_map/dot_general | solution.py:130
  258.0 13.4 %fusion.15 = (bf16[512,2560]{1,0:T(8,128)(2,1)}, bf16[512,2560]{1,0:T(8,128)(2,1)S(1)}, bf16[512,2560]{1,0:T(8,128)(2,1)}) fusion(f32[2560,512]{0,1:T(8,128)} %fusion.1, f32[512,2560]{1,0:T(8,128)} %fusion.11, bf16[2048,5120]{1,0:T(8,128)(2,1)} %all-gather.5.cloned.1.call-done, f32[512,2048]{1,0:T(8,128)S(1)} %copy-done.9, f32[2048]{0:T(1024)S(1)} %bitcast.237, ...), kind=kOutput, calls=%fused_computation.26 | convolution fusion | flops 5391515648 | bytes 33040384 | tf_op jit(solution)/shard_map/dot_general | solution.py:130
  271.4 10.7 %fusion.5 = f32[512,2048]{1,0:T(8,128)} fusion(bf16[512,2560]{1,0:T(8,128)(2,1)S(1)} %get-tuple-element.69, bf16[2048,5120]{1,0:T(8,128)(2,1)} %all-gather.5.cloned.1.call-done), kind=kOutput, calls=%fused_computation.12 | convolution fusion | flops 5368709120 | bytes 17301504 | tf_op jit(solution)/shard_map/dot_general | solution.py:126
  282.1 10.9 %add_convert_fusion = bf16[512,2048]{1,0:T(8,128)(2,1)} fusion(f32[512,2048]{1,0:T(8,128)} %fusion.5, bf16[512,2560]{1,0:T(8,128)(2,1)} %get-tuple-element.68, bf16[2048,5120]{1,0:T(8,128)(2,1)} %all-gather.5.cloned.1.call-done), kind=kOutput, calls=%fused_computation.49 | convolution fusion | flops 5370806272 | bytes 19398656 | tf_op jit(solution)/shard_map/dot_general | solution.py:126
  294.7 8.7 fusion.39
  306.2 35.6 %collective-permute-done.6 = bf16[512,2048]{1,0:T(8,128)(2,1)} collective-permute-done((bf16[512,2048]{1,0:T(8,128)(2,1)}, bf16[512,2048]{1,0:T(8,128)(2,1)}, u32[]{:S(2)}, u32[]{:S(2)}) %collective-permute-start.6) | collective-permute-done | bytes 2097184 | tf_op jit(solution)/shard_map/ppermute | solution.py:107
  341.8 4.8 multiply_reduce_fusion
  346.6 39.1 %collective-permute-done.5 = bf16[512,2048]{1,0:T(8,128)(2,1)} collective-permute-done((bf16[512,2048]{1,0:T(8,128)(2,1)}, bf16[512,2048]{1,0:T(8,128)(2,1)}, u32[]{:S(2)}, u32[]{:S(2)}) %collective-permute-start.5) | collective-permute-done | bytes 2097184 | tf_op jit(solution)/shard_map/ppermute | solution.py:107
  385.8 6.8 convert_bitcast_fusion.1
  392.6 5.3 fusion.54.d_ref
  398.0 32.1 %shard_map.196 = (f32[768,512]{1,0:T(8,128)S(1)}, f32[192,1536]{1,0:T(8,128)S(1)}, f32[192,1536]{1,0:T(8,128)S(1)}) custom-call(bf16[768,512]{1,0:T(8,128)(2,1)S(1)} %bitcast.181, bf16[3,1536,64]{2,1,0:T(8,128)(2,1)S(1)} %bitcast.178, bf16[192,1536]{1,0:T(8,128)(2,1)S(1)} %copy-done.3, bf16[3,1536,64]{2,1,0:T(8,128)(2,1)S(1)} %bitcast.179, ...), custom_call_target="tpu_custom_call" | custom-call | flops 5033164800 | bytes 12582912 | tf_op jit(solution)/shard_map/pallas_call | solution.py:213
  435.8 16.0 %collective-permute-done.8 = bf16[384,512]{1,0:T(8,128)(2,1)S(1)} collective-permute-done((bf16[384,512]{1,0:T(8,128)(2,1)S(1)}, bf16[384,512]{1,0:T(8,128)(2,1)S(1)}, u32[]{:S(2)}, u32[]{:S(2)}) %collective-permute-start.8) | collective-permute-done | bytes 393248 | tf_op jit(solution)/shard_map/ppermute | solution.py:118
  452.9 7.3 fusion.130
  462.6 4.3 convolution_convert_fusion.1
  467.0 38.8 %collective-permute-done.9 = bf16[512,2048]{1,0:T(8,128)(2,1)} collective-permute-done((bf16[512,2048]{1,0:T(8,128)(2,1)}, bf16[512,2048]{1,0:T(8,128)(2,1)}, u32[]{:S(2)}, u32[]{:S(2)}) %collective-permute-start.9) | collective-permute-done | bytes 2097184 | tf_op jit(solution)/shard_map/ppermute | solution.py:107
  505.8 4.0 fusion.26
  512.8 7.8 copy.114
  520.7 10.6 %fusion = bf16[2048,2560]{0,1:T(8,128)(2,1)} fusion(bf16[512,2560]{1,0:T(8,128)(2,1)} %get-tuple-element.70, bf16[512,2048]{1,0:T(8,128)(2,1)} %param.23), kind=kOutput, calls=%fused_computation.1 | convolution fusion | flops 5373952000 | bytes 15204352 | tf_op jit(solution)/shard_map/dot_general | solution.py:122
  531.3 14.2 %copy.116 = bf16[2048,2560]{1,0:T(8,128)(2,1)} copy(bf16[2048,2560]{0,1:T(8,128)(2,1)} %fusion) | data formatting | bytes 20971520
  545.6 3.9 fusion.142
  549.6 4.5 reshape.419
  554.1 6.8 constant_dynamic-slice_fusion.3
  560.9 3.5 copy.127
  564.4 3.5 copy.128
  567.9 4.7 convolution_convert_fusion.5
  572.6 3.0 convolution_convert_fusion.4
  582.6 3.5 copy.125
  588.4 4.6 reshape.413
  593.0 7.1 constant_dynamic-slice_fusion.11
  602.5 3.5 copy.123
  606.0 3.2 convolution_convert_fusion.7
  611.6 3.5 copy.121
  615.2 4.7 convert_add_fusion.4
  622.2 3.6 convert_add_fusion.3
  626.2 3.6 convert_add_fusion.2
  631.9 3.3 convert_add_fusion.1
  641.7 23.5 %collective-permute-done.17 = bf16[512,1280]{1,0:T(8,128)(2,1)S(1)} collective-permute-done((bf16[512,1280]{1,0:T(8,128)(2,1)S(1)}, bf16[512,1280]{1,0:T(8,128)(2,1)S(1)}, u32[]{:S(2)}, u32[]{:S(2)}) %collective-permute-start.17) | collective-permute-done | bytes 1310752 | tf_op jit(solution)/shard_map/ppermute | solution.py:100
  667.5 34.2 %collective-permute-done.22 = bf16[512,1280]{1,0:T(8,128)(2,1)S(1)} collective-permute-done((bf16[512,1280]{1,0:T(8,128)(2,1)S(1)}, bf16[512,1280]{1,0:T(8,128)(2,1)S(1)}, u32[]{:S(2)}, u32[]{:S(2)}) %collective-permute-start.22) | collective-permute-done | bytes 1310752 | tf_op jit(solution)/shard_map/ppermute | solution.py:100
  701.7 4.8 collective-permute-start.19
  707.0 36.1 %collective-permute-done.27 = bf16[512,1280]{1,0:T(8,128)(2,1)S(1)} collective-permute-done((bf16[512,1280]{1,0:T(8,128)(2,1)S(1)}, bf16[512,1280]{1,0:T(8,128)(2,1)S(1)}, u32[]{:S(2)}, u32[]{:S(2)}) %collective-permute-start.27) | collective-permute-done | bytes 1310752 | tf_op jit(solution)/shard_map/ppermute | solution.py:100
  743.1 4.1 collective-permute-start.20
  747.5 23.7 %collective-permute-done.32 = bf16[512,1280]{1,0:T(8,128)(2,1)S(1)} collective-permute-done((bf16[512,1280]{1,0:T(8,128)(2,1)S(1)}, bf16[512,1280]{1,0:T(8,128)(2,1)S(1)}, u32[]{:S(2)}, u32[]{:S(2)}) %collective-permute-start.32) | collective-permute-done | bytes 1310752 | tf_op jit(solution)/shard_map/ppermute | solution.py:100
  773.6 3.0 collective-permute-start.24
  778.8 5.4 collective-permute-done.23
  784.2 14.5 %collective-permute-start.29 = (bf16[128,1280]{1,0:T(8,128)(2,1)S(1)}, bf16[128,1280]{1,0:T(8,128)(2,1)S(1)}, u32[]{:S(2)}, u32[]{:S(2)}) collective-permute-start(bf16[128,1280]{1,0:T(8,128)(2,1)S(1)} %get-tuple-element.98), channel_id=1, source_target_pairs={{0,16},{2,18},{4,20},{6,22},{8,24},{10,26},{12,28},{14,30},{16,0},... | collective-permute-start | bytes 983048 | tf_op jit(solution)/shard_map/ppermute | solution.py:93
  798.7 18.5 %collective-permute-start.30 = (bf16[128,1280]{1,0:T(8,128)(2,1)S(1)}, bf16[128,1280]{1,0:T(8,128)(2,1)S(1)}, u32[]{:S(2)}, u32[]{:S(2)}) collective-permute-start(bf16[128,1280]{1,0:T(8,128)(2,1)S(1)} %get-tuple-element.97), channel_id=1, source_target_pairs={{0,24},{2,26},{4,28},{6,30},{8,0},{10,2},{12,4},{14,6},{16,8},{18,... | collective-permute-start | bytes 983048 | tf_op jit(solution)/shard_map/ppermute | solution.py:93
  817.2 5.0 collective-permute-start.33
  822.4 4.5 collective-permute-start.34
  826.9 12.4 %collective-permute-done.29 = bf16[128,1280]{1,0:T(8,128)(2,1)S(1)} collective-permute-done((bf16[128,1280]{1,0:T(8,128)(2,1)S(1)}, bf16[128,1280]{1,0:T(8,128)(2,1)S(1)}, u32[]{:S(2)}, u32[]{:S(2)}) %collective-permute-start.29) | collective-permute-done | bytes 327712 | tf_op jit(solution)/shard_map/ppermute | solution.py:93
  842.0 11.4 %collective-permute-done.34 = bf16[128,1280]{1,0:T(8,128)(2,1)S(1)} collective-permute-done((bf16[128,1280]{1,0:T(8,128)(2,1)S(1)}, bf16[128,1280]{1,0:T(8,128)(2,1)S(1)}, u32[]{:S(2)}, u32[]{:S(2)}) %collective-permute-start.34) | collective-permute-done | bytes 327712 | tf_op jit(solution)/shard_map/ppermute | solution.py:93
  857.7 4.5 reshape.428
  864.2 5.1 collective-permute-start.13
  872.9 6.1 fusion.24
  879.0 3.7 collective-permute-done.14
  (318 shorter events, 124.8 us)
Async XLA Ops:
  7.2 119.6 %all-gather.3.cloned.1.call-start = ((), (), s32[]{:S(2)}) async-start(), calls=%async_computation.2 | async-start | bytes 20054016 | tf_op jit(solution)/shard_map/all_gather | solution.py:262
  8.4 8.7 copy-start.24
  17.1 228.4 %all-gather.5.cloned.1.call-start = ((), (), s32[]{:S(2)}) async-start(), calls=%async_computation.3 | async-start | bytes 22282240 | tf_op jit(solution)/shard_map/all_gather | solution.py:263
  19.3 864.3 %reduce-scatter.7.cloned.1.call-start = ((), (), s32[]{:S(2)}) async-start(), calls=%async_computation.4 | async-start | bytes 5570560
  19.4 8.4 collective-permute-start.3
  21.8 6.1 collective-permute-start.2
  26.8 100.8 %copy-start.42 = (f32[512]{0:T(512)}, f32[512]{0:T(512)S(1)}, u32[]{:S(2)}) copy-start(f32[512]{0:T(512)S(1)} %add_rsqrt_fusion.3) | copy-start | bytes 6148
  135.0 17.1 %copy-start.21 = (f32[192,512]{1,0:T(8,128)}, f32[192,512]{1,0:T(8,128)S(1)}, u32[]{:S(2)}) copy-start(f32[192,512]{1,0:T(8,128)S(1)} %slice.235) | copy-start | bytes 1179652
  139.1 11.7 %copy-start.19 = (f32[1152,512]{1,0:T(8,128)S(1)}, f32[1152,512]{1,0:T(8,128)}, u32[]{:S(2)}) copy-start(f32[1152,512]{1,0:T(8,128)} %copy-done.18) | copy-start | bytes 7077892
  143.9 21.6 %collective-permute-start = (bf16[384,512]{1,0:T(8,128)(2,1)}, bf16[384,512]{1,0:T(8,128)(2,1)}, u32[]{:S(2)}, u32[]{:S(2)}) collective-permute-start(bf16[384,512]{1,0:T(8,128)(2,1)} %pad_maximum_fusion.10), channel_id=1, source_target_pairs={{0,4},{2,6},{4,8},{6,10},{8,12},{10,14},{12,16},{14,18},{16,20},{1... | collective-permute-start | bytes 1179656 | tf_op jit(solution)/shard_map/ppermute | solution.py:118
  148.0 17.4 %collective-permute-start.1 = (bf16[384,512]{1,0:T(8,128)(2,1)}, bf16[384,512]{1,0:T(8,128)(2,1)}, u32[]{:S(2)}, u32[]{:S(2)}) collective-permute-start(bf16[384,512]{1,0:T(8,128)(2,1)} %pad_maximum_fusion.10), channel_id=1, source_target_pairs={{0,2},{2,4},{4,6},{6,8},{8,10},{10,12},{12,14},{14,16},{16,18},{18... | collective-permute-start | bytes 1179656 | tf_op jit(solution)/shard_map/ppermute | solution.py:118
  155.2 10.2 %copy-start.28 = (bf16[192,512]{1,0:T(8,128)(2,1)S(1)}, bf16[192,512]{1,0:T(8,128)(2,1)}, u32[]{:S(2)}) copy-start(bf16[192,512]{1,0:T(8,128)(2,1)} %slice.398) | copy-start | bytes 589828
  155.2 10.2 %copy-start.30 = (bf16[3,64,512]{2,1,0:T(8,128)(2,1)S(1)}, bf16[3,64,512]{2,1,0:T(8,128)(2,1)}, u32[]{:S(2)}) copy-start(bf16[3,64,512]{2,1,0:T(8,128)(2,1)} %copy-done.29) | copy-start | bytes 589828
  191.0 37.4 %copy-start.12 = (bf16[512,2048]{1,0:T(8,128)(2,1)S(1)}, bf16[512,2048]{1,0:T(8,128)(2,1)}, u32[]{:S(2)}) copy-start(bf16[512,2048]{1,0:T(8,128)(2,1)} %param.12) | copy-start | bytes 6291460
  191.1 37.4 %collective-permute-start.4 = (bf16[512,2048]{1,0:T(8,128)(2,1)S(1)}, bf16[512,2048]{1,0:T(8,128)(2,1)S(1)}, u32[]{:S(2)}, u32[]{:S(2)}) collective-permute-start(bf16[512,2048]{1,0:T(8,128)(2,1)S(1)} %convolution_convert_fusion.6), channel_id=1, source_target_pairs={{0,1},{1,0},{2,3},{3,2},{4,5},{5,4},{6,7},{7,6},{8,9},{9,8},{10,11... | collective-permute-start | bytes 6291464 | tf_op jit(solution)/shard_map/ppermute | solution.py:107
  245.5 12.6 %copy-start.9 = (f32[512,2048]{1,0:T(8,128)S(1)}, f32[512,2048]{1,0:T(8,128)}, u32[]{:S(2)}) copy-start(f32[512,2048]{1,0:T(8,128)} %get-tuple-element.67) | copy-start | bytes 12582916
  271.4 10.7 %copy-start.49 = (bf16[512,2560]{1,0:T(8,128)(2,1)}, bf16[512,2560]{1,0:T(8,128)(2,1)S(1)}, u32[]{:S(2)}) copy-start(bf16[512,2560]{1,0:T(8,128)(2,1)S(1)} %get-tuple-element.69) | copy-start | bytes 7864324
  271.4 23.3 %slice-start = ((s8[18874368]{0:T(1024)(128)(4,1)}), s8[4194304]{0:T(1024)(128)(4,1)S(1)}, s32[]{:S(2)}) async-start(s8[18874368]{0:T(1024)(128)(4,1)} %bitcast.211), calls=%async_computation.6 | async-start | bytes 8388608
  271.4 23.3 %slice-start.1 = ((s8[18874368]{0:T(1024)(128)(4,1)}), s8[4194304]{0:T(1024)(128)(4,1)S(1)}, s32[]{:S(2)}) async-start(s8[18874368]{0:T(1024)(128)(4,1)} %bitcast.211), calls=%async_computation.7 | async-start | bytes 8388608
  271.4 23.3 %slice-start.2 = ((s8[18874368]{0:T(1024)(128)(4,1)}), s8[4194304]{0:T(1024)(128)(4,1)S(1)}, s32[]{:S(2)}) async-start(s8[18874368]{0:T(1024)(128)(4,1)} %bitcast.211), calls=%async_computation.8 | async-start | bytes 8388608
  282.1 12.6 %slice-start.3 = ((s8[18874368]{0:T(1024)(128)(4,1)}), s8[4194304]{0:T(1024)(128)(4,1)S(1)}, s32[]{:S(2)}) async-start(s8[18874368]{0:T(1024)(128)(4,1)} %bitcast.211), calls=%async_computation.9 | async-start | bytes 8388608
  282.1 12.6 %slice-start.4 = ((s8[18874368]{0:T(1024)(128)(4,1)}), s8[2097152]{0:T(1024)(128)(4,1)S(1)}, s32[]{:S(2)}) async-start(s8[18874368]{0:T(1024)(128)(4,1)} %bitcast.211), calls=%async_computation.10 | async-start | bytes 4194304
  293.0 48.8 %collective-permute-start.6 = (bf16[512,2048]{1,0:T(8,128)(2,1)}, bf16[512,2048]{1,0:T(8,128)(2,1)}, u32[]{:S(2)}, u32[]{:S(2)}) collective-permute-start(bf16[512,2048]{1,0:T(8,128)(2,1)} %add_convert_fusion), channel_id=1, source_target_pairs={{0,1},{1,0},{2,3},{3,2},{4,5},{5,4},{6,7},{7,6},{8,9},{9,8},{10,11... | collective-permute-start | bytes 6291464 | tf_op jit(solution)/shard_map/ppermute | solution.py:107
  294.7 9.1 %copy-start.46 = (f32[64]{0:T(128)S(1)}, f32[64]{0:T(128)}, u32[]{:S(2)}) copy-start(f32[64]{0:T(128)} %mul.557) | copy-start | bytes 772
  303.4 82.4 %collective-permute-start.5 = (bf16[512,2048]{1,0:T(8,128)(2,1)}, bf16[512,2048]{1,0:T(8,128)(2,1)}, u32[]{:S(2)}, u32[]{:S(2)}) collective-permute-start(bf16[512,2048]{1,0:T(8,128)(2,1)} %fusion.39), channel_id=1, source_target_pairs={{0,1},{1,0},{2,3},{3,2},{4,5},{5,4},{6,7},{7,6},{8,9},{9,8},{10,11... | collective-permute-start | bytes 6291464 | tf_op jit(solution)/shard_map/ppermute | solution.py:107
  306.2 79.6 %copy-start.10 = (f32[512,2048]{1,0:T(8,128)S(1)}, f32[512,2048]{1,0:T(8,128)}, u32[]{:S(2)}) copy-start(f32[512,2048]{1,0:T(8,128)} %get-tuple-element.67) | copy-start | bytes 12582916
  306.2 79.6 %copy-start.26 = (bf16[512,2048]{1,0:T(8,128)(2,1)S(1)}, bf16[512,2048]{1,0:T(8,128)(2,1)}, u32[]{:S(2)}) copy-start(bf16[512,2048]{1,0:T(8,128)(2,1)} %param.23) | copy-start | bytes 6291460
  430.6 5.2 collective-permute-start.7
  432.0 19.8 %collective-permute-start.8 = (bf16[384,512]{1,0:T(8,128)(2,1)S(1)}, bf16[384,512]{1,0:T(8,128)(2,1)S(1)}, u32[]{:S(2)}, u32[]{:S(2)}) collective-permute-start(bf16[384,512]{1,0:T(8,128)(2,1)S(1)} %get-tuple-element.103), channel_id=1, source_target_pairs={{4,0},{6,2},{8,4},{10,6},{12,8},{14,10},{16,12},{18,14},{20,16},{2... | collective-permute-start | bytes 1179656 | tf_op jit(solution)/shard_map/ppermute | solution.py:118
  435.8 17.1 %copy-start.32 = (bf16[768,512]{1,0:T(8,128)(2,1)}, bf16[768,512]{1,0:T(8,128)(2,1)S(1)}, u32[]{:S(2)}) copy-start(bf16[768,512]{1,0:T(8,128)(2,1)S(1)} %get-tuple-element.73) | copy-start | bytes 2359300
  435.8 16.4 %copy-start.22 = (f32[192,512]{1,0:T(8,128)S(1)}, f32[192,512]{1,0:T(8,128)}, u32[]{:S(2)}) copy-start(f32[192,512]{1,0:T(8,128)} %copy-done.21) | copy-start | bytes 1179652
  452.9 9.7 %copy-start.13 = (bf16[512,2048]{1,0:T(8,128)(2,1)S(1)}, bf16[512,2048]{1,0:T(8,128)(2,1)}, u32[]{:S(2)}) copy-start(bf16[512,2048]{1,0:T(8,128)(2,1)} %param.12) | copy-start | bytes 6291460
  452.9 9.7 %copy-start.39 = (f32[2048,1]{0,1:T(1,128)S(1)}, f32[2048,1]{0,1:T(1,128)}, u32[]{:S(2)}) copy-start(f32[2048,1]{0,1:T(1,128)} %copy-done.38) | copy-start | bytes 24580
  452.9 9.7 %copy-start.43 = (f32[512]{0:T(512)S(1)}, f32[512]{0:T(512)}, u32[]{:S(2)}) copy-start(f32[512]{0:T(512)} %copy-done.42) | copy-start | bytes 6148
  460.2 45.6 %collective-permute-start.9 = (bf16[512,2048]{1,0:T(8,128)(2,1)}, bf16[512,2048]{1,0:T(8,128)(2,1)}, u32[]{:S(2)}, u32[]{:S(2)}) collective-permute-start(bf16[512,2048]{1,0:T(8,128)(2,1)} %get-tuple-element.126), channel_id=1, source_target_pairs={{0,1},{1,0},{2,3},{3,2},{4,5},{5,4},{6,7},{7,6},{8,9},{9,8},{10,11... | collective-permute-start | bytes 6291464 | tf_op jit(solution)/shard_map/ppermute | solution.py:107
  462.6 43.2 %copy-start.23 = (f32[512,2048]{1,0:T(8,128)S(1)}, f32[512,2048]{1,0:T(8,128)}, u32[]{:S(2)}) copy-start(f32[512,2048]{1,0:T(8,128)} %get-tuple-element.127) | copy-start | bytes 12582916
  520.7 371.5 %reduce-scatter.9.cloned.1.call-start = ((), (), s32[]{:S(2)}) async-start(), calls=%async_computation.5 | async-start | bytes 11141120
  572.6 42.6 %collective-permute-start.16 = (bf16[1024,1280]{1,0:T(8,128)(2,1)}, bf16[1024,1280]{1,0:T(8,128)(2,1)}, u32[]{:S(2)}, u32[]{:S(2)}) collective-permute-start(bf16[1024,1280]{1,0:T(8,128)(2,1)} %convolution_convert_fusion.5), channel_id=1, source_target_pairs={{0,2},{2,0},{4,6},{6,4},{8,10},{10,8},{12,14},{14,12},{16,18},{18,... | collective-permute-start | bytes 7864328 | tf_op jit(solution)/shard_map/ppermute | solution.py:97
  575.7 46.5 %collective-permute-start.21 = (bf16[1024,1280]{1,0:T(8,128)(2,1)}, bf16[1024,1280]{1,0:T(8,128)(2,1)}, u32[]{:S(2)}, u32[]{:S(2)}) collective-permute-start(bf16[1024,1280]{1,0:T(8,128)(2,1)} %convolution_convert_fusion.4), channel_id=1, source_target_pairs={{0,2},{2,0},{4,6},{6,4},{8,10},{10,8},{12,14},{14,12},{16,18},{18,... | collective-permute-start | bytes 7864328 | tf_op jit(solution)/shard_map/ppermute | solution.py:97
  579.2 47.1 %collective-permute-start.26 = (bf16[1024,1280]{1,0:T(8,128)(2,1)}, bf16[1024,1280]{1,0:T(8,128)(2,1)}, u32[]{:S(2)}, u32[]{:S(2)}) collective-permute-start(bf16[1024,1280]{1,0:T(8,128)(2,1)} %convolution_convert_fusion.3), channel_id=1, source_target_pairs={{0,2},{2,0},{4,6},{6,4},{8,10},{10,8},{12,14},{14,12},{16,18},{18,... | collective-permute-start | bytes 7864328 | tf_op jit(solution)/shard_map/ppermute | solution.py:97
  582.2 49.7 %collective-permute-start.31 = (bf16[1024,1280]{1,0:T(8,128)(2,1)}, bf16[1024,1280]{1,0:T(8,128)(2,1)}, u32[]{:S(2)}, u32[]{:S(2)}) collective-permute-start(bf16[1024,1280]{1,0:T(8,128)(2,1)} %convolution_convert_fusion.2), channel_id=1, source_target_pairs={{0,2},{2,0},{4,6},{6,4},{8,10},{10,8},{12,14},{14,12},{16,18},{18,... | collective-permute-start | bytes 7864328 | tf_op jit(solution)/shard_map/ppermute | solution.py:97
  609.2 26.4 %collective-permute-start.11 = (bf16[1024,768]{1,0:T(8,128)(2,1)}, bf16[1024,768]{1,0:T(8,128)(2,1)}, u32[]{:S(2)}, u32[]{:S(2)}) collective-permute-start(bf16[1024,768]{1,0:T(8,128)(2,1)} %convolution_convert_fusion.7), channel_id=1, source_target_pairs={{0,2},{2,0},{4,6},{6,4},{8,10},{10,8},{12,14},{14,12},{16,18},{18,... | collective-permute-start | bytes 4718600 | tf_op jit(solution)/shard_map/ppermute | solution.py:97
  620.0 45.2 %collective-permute-start.17 = (bf16[512,1280]{1,0:T(8,128)(2,1)S(1)}, bf16[512,1280]{1,0:T(8,128)(2,1)S(1)}, u32[]{:S(2)}, u32[]{:S(2)}) collective-permute-start(bf16[512,1280]{1,0:T(8,128)(2,1)S(1)} %slice.395), channel_id=1, source_target_pairs={{0,4},{2,6},{4,0},{6,2},{8,12},{10,14},{12,8},{14,10},{16,20},{18,... | collective-permute-start | bytes 3932168 | tf_op jit(solution)/shard_map/ppermute | solution.py:100
  626.0 75.8 %collective-permute-start.22 = (bf16[512,1280]{1,0:T(8,128)(2,1)S(1)}, bf16[512,1280]{1,0:T(8,128)(2,1)S(1)}, u32[]{:S(2)}, u32[]{:S(2)}) collective-permute-start(bf16[512,1280]{1,0:T(8,128)(2,1)S(1)} %slice.394), channel_id=1, source_target_pairs={{0,4},{2,6},{4,0},{6,2},{8,12},{10,14},{12,8},{14,10},{16,20},{18,... | collective-permute-start | bytes 3932168 | tf_op jit(solution)/shard_map/ppermute | solution.py:100
  629.9 113.2 %collective-permute-start.27 = (bf16[512,1280]{1,0:T(8,128)(2,1)S(1)}, bf16[512,1280]{1,0:T(8,128)(2,1)S(1)}, u32[]{:S(2)}, u32[]{:S(2)}) collective-permute-start(bf16[512,1280]{1,0:T(8,128)(2,1)S(1)} %slice.393), channel_id=1, source_target_pairs={{0,4},{2,6},{4,0},{6,2},{8,12},{10,14},{12,8},{14,10},{16,20},{18,... | collective-permute-start | bytes 3932168 | tf_op jit(solution)/shard_map/ppermute | solution.py:100
  635.3 135.9 %collective-permute-start.32 = (bf16[512,1280]{1,0:T(8,128)(2,1)S(1)}, bf16[512,1280]{1,0:T(8,128)(2,1)S(1)}, u32[]{:S(2)}, u32[]{:S(2)}) collective-permute-start(bf16[512,1280]{1,0:T(8,128)(2,1)S(1)} %slice.392), channel_id=1, source_target_pairs={{0,4},{2,6},{4,0},{6,2},{8,12},{10,14},{12,8},{14,10},{16,20},{18,... | collective-permute-start | bytes 3932168 | tf_op jit(solution)/shard_map/ppermute | solution.py:100
  640.8 221.4 %collective-permute-start.12 = (bf16[512,768]{1,0:T(8,128)(2,1)S(1)}, bf16[512,768]{1,0:T(8,128)(2,1)}, u32[]{:S(2)}, u32[]{:S(2)}) collective-permute-start(bf16[512,768]{1,0:T(8,128)(2,1)S(1)} %slice.396), channel_id=1, source_target_pairs={{0,4},{2,6},{4,0},{6,2},{8,12},{10,14},{12,8},{14,10},{16,20},{18,... | collective-permute-start | bytes 2359304 | tf_op jit(solution)/shard_map/ppermute | solution.py:100
  665.7 107.9 %collective-permute-start.18 = (bf16[128,1280]{1,0:T(8,128)(2,1)S(1)}, bf16[128,1280]{1,0:T(8,128)(2,1)S(1)}, u32[]{:S(2)}, u32[]{:S(2)}) collective-permute-start(bf16[128,1280]{1,0:T(8,128)(2,1)S(1)} %get-tuple-element.90), channel_id=1, source_target_pairs={{0,8},{2,10},{4,12},{6,14},{8,16},{10,18},{12,20},{14,22},{16,24},... | collective-permute-start | bytes 983048 | tf_op jit(solution)/shard_map/ppermute | solution.py:93
  701.7 74.9 %collective-permute-start.19 = (bf16[128,1280]{1,0:T(8,128)(2,1)S(1)}, bf16[128,1280]{1,0:T(8,128)(2,1)S(1)}, u32[]{:S(2)}, u32[]{:S(2)}) collective-permute-start(bf16[128,1280]{1,0:T(8,128)(2,1)S(1)} %get-tuple-element.92), channel_id=1, source_target_pairs={{0,16},{2,18},{4,20},{6,22},{8,24},{10,26},{12,28},{14,30},{16,0},... | collective-permute-start | bytes 983048 | tf_op jit(solution)/shard_map/ppermute | solution.py:93
  743.1 34.4 %collective-permute-start.20 = (bf16[128,1280]{1,0:T(8,128)(2,1)S(1)}, bf16[128,1280]{1,0:T(8,128)(2,1)S(1)}, u32[]{:S(2)}, u32[]{:S(2)}) collective-permute-start(bf16[128,1280]{1,0:T(8,128)(2,1)S(1)} %get-tuple-element.91), channel_id=1, source_target_pairs={{0,24},{2,26},{4,28},{6,30},{8,0},{10,2},{12,4},{14,6},{16,8},{18,... | collective-permute-start | bytes 983048 | tf_op jit(solution)/shard_map/ppermute | solution.py:93
  771.2 13.0 %collective-permute-start.23 = (bf16[128,1280]{1,0:T(8,128)(2,1)S(1)}, bf16[128,1280]{1,0:T(8,128)(2,1)S(1)}, u32[]{:S(2)}, u32[]{:S(2)}) collective-permute-start(bf16[128,1280]{1,0:T(8,128)(2,1)S(1)} %get-tuple-element.93), channel_id=1, source_target_pairs={{0,8},{2,10},{4,12},{6,14},{8,16},{10,18},{12,20},{14,22},{16,24},... | collective-permute-start | bytes 983048 | tf_op jit(solution)/shard_map/ppermute | solution.py:93
  773.6 25.1 %collective-permute-start.24 = (bf16[128,1280]{1,0:T(8,128)(2,1)S(1)}, bf16[128,1280]{1,0:T(8,128)(2,1)S(1)}, u32[]{:S(2)}, u32[]{:S(2)}) collective-permute-start(bf16[128,1280]{1,0:T(8,128)(2,1)S(1)} %get-tuple-element.95), channel_id=1, source_target_pairs={{0,16},{2,18},{4,20},{6,22},{8,24},{10,26},{12,28},{14,30},{16,0},... | collective-permute-start | bytes 983048 | tf_op jit(solution)/shard_map/ppermute | solution.py:93
  776.6 40.6 %collective-permute-start.25 = (bf16[128,1280]{1,0:T(8,128)(2,1)S(1)}, bf16[128,1280]{1,0:T(8,128)(2,1)S(1)}, u32[]{:S(2)}, u32[]{:S(2)}) collective-permute-start(bf16[128,1280]{1,0:T(8,128)(2,1)S(1)} %get-tuple-element.94), channel_id=1, source_target_pairs={{0,24},{2,26},{4,28},{6,30},{8,0},{10,2},{12,4},{14,6},{16,8},{18,... | collective-permute-start | bytes 983048 | tf_op jit(solution)/shard_map/ppermute | solution.py:93
  777.5 44.9 %collective-permute-start.28 = (bf16[128,1280]{1,0:T(8,128)(2,1)S(1)}, bf16[128,1280]{1,0:T(8,128)(2,1)S(1)}, u32[]{:S(2)}, u32[]{:S(2)}) collective-permute-start(bf16[128,1280]{1,0:T(8,128)(2,1)S(1)} %get-tuple-element.96), channel_id=1, source_target_pairs={{0,8},{2,10},{4,12},{6,14},{8,16},{10,18},{12,20},{14,22},{16,24},... | collective-permute-start | bytes 983048 | tf_op jit(solution)/shard_map/ppermute | solution.py:93
  784.2 55.0 %collective-permute-start.29 = (bf16[128,1280]{1,0:T(8,128)(2,1)S(1)}, bf16[128,1280]{1,0:T(8,128)(2,1)S(1)}, u32[]{:S(2)}, u32[]{:S(2)}) collective-permute-start(bf16[128,1280]{1,0:T(8,128)(2,1)S(1)} %get-tuple-element.98), channel_id=1, source_target_pairs={{0,16},{2,18},{4,20},{6,22},{8,24},{10,26},{12,28},{14,30},{16,0},... | collective-permute-start | bytes 983048 | tf_op jit(solution)/shard_map/ppermute | solution.py:93
  798.7 43.1 %collective-permute-start.30 = (bf16[128,1280]{1,0:T(8,128)(2,1)S(1)}, bf16[128,1280]{1,0:T(8,128)(2,1)S(1)}, u32[]{:S(2)}, u32[]{:S(2)}) collective-permute-start(bf16[128,1280]{1,0:T(8,128)(2,1)S(1)} %get-tuple-element.97), channel_id=1, source_target_pairs={{0,24},{2,26},{4,28},{6,30},{8,0},{10,2},{12,4},{14,6},{16,8},{18,... | collective-permute-start | bytes 983048 | tf_op jit(solution)/shard_map/ppermute | solution.py:93
  817.2 24.8 %collective-permute-start.33 = (bf16[128,1280]{1,0:T(8,128)(2,1)S(1)}, bf16[128,1280]{1,0:T(8,128)(2,1)S(1)}, u32[]{:S(2)}, u32[]{:S(2)}) collective-permute-start(bf16[128,1280]{1,0:T(8,128)(2,1)S(1)} %get-tuple-element.99), channel_id=1, source_target_pairs={{0,8},{2,10},{4,12},{6,14},{8,16},{10,18},{12,20},{14,22},{16,24},... | collective-permute-start | bytes 983048 | tf_op jit(solution)/shard_map/ppermute | solution.py:93
  822.4 31.0 %collective-permute-start.34 = (bf16[128,1280]{1,0:T(8,128)(2,1)S(1)}, bf16[128,1280]{1,0:T(8,128)(2,1)S(1)}, u32[]{:S(2)}, u32[]{:S(2)}) collective-permute-start(bf16[128,1280]{1,0:T(8,128)(2,1)S(1)} %get-tuple-element.101), channel_id=1, source_target_pairs={{0,16},{2,18},{4,20},{6,22},{8,24},{10,26},{12,28},{14,30},{16,0},... | collective-permute-start | bytes 983048 | tf_op jit(solution)/shard_map/ppermute | solution.py:93
  839.2 16.6 %collective-permute-start.35 = (bf16[128,1280]{1,0:T(8,128)(2,1)S(1)}, bf16[128,1280]{1,0:T(8,128)(2,1)S(1)}, u32[]{:S(2)}, u32[]{:S(2)}) collective-permute-start(bf16[128,1280]{1,0:T(8,128)(2,1)S(1)} %get-tuple-element.100), channel_id=1, source_target_pairs={{0,24},{2,26},{4,28},{6,30},{8,0},{10,2},{12,4},{14,6},{16,8},{18,... | collective-permute-start | bytes 983048 | tf_op jit(solution)/shard_map/ppermute | solution.py:93
  862.2 10.7 %copy-start.45 = (f32[512]{0:T(512)S(1)}, f32[512]{0:T(512)}, u32[]{:S(2)}) copy-start(f32[512]{0:T(512)} %copy-done.44) | copy-start | bytes 6148
  864.2 14.8 %collective-permute-start.13 = (bf16[128,768]{0,1:T(8,128)(2,1)S(1)}, bf16[128,768]{0,1:T(8,128)(2,1)S(1)}, u32[]{:S(2)}, u32[]{:S(2)}) collective-permute-start(bf16[128,768]{0,1:T(8,128)(2,1)S(1)} %bitcast.233), channel_id=1, source_target_pairs={{0,8},{2,10},{4,12},{6,14},{8,16},{10,18},{12,20},{14,22},{16,24},... | collective-permute-start | bytes 589832 | tf_op jit(solution)/shard_map/ppermute | solution.py:93
  869.4 13.2 %collective-permute-start.14 = (bf16[128,768]{0,1:T(8,128)(2,1)S(1)}, bf16[128,768]{0,1:T(8,128)(2,1)S(1)}, u32[]{:S(2)}, u32[]{:S(2)}) collective-permute-start(bf16[128,768]{0,1:T(8,128)(2,1)S(1)} %bitcast.234), channel_id=1, source_target_pairs={{0,16},{2,18},{4,20},{6,22},{8,24},{10,26},{12,28},{14,30},{16,0},... | collective-permute-start | bytes 589832 | tf_op jit(solution)/shard_map/ppermute | solution.py:93
  871.7 11.0 %collective-permute-start.15 = (bf16[128,768]{0,1:T(8,128)(2,1)}, bf16[128,768]{0,1:T(8,128)(2,1)S(1)}, u32[]{:S(2)}, u32[]{:S(2)}) collective-permute-start(bf16[128,768]{0,1:T(8,128)(2,1)} %bitcast.235), channel_id=1, source_target_pairs={{0,24},{2,26},{4,28},{6,30},{8,0},{10,2},{12,4},{14,6},{16,8},{18,... | collective-permute-start | bytes 589832 | tf_op jit(solution)/shard_map/ppermute | solution.py:93
  884.6 5.3 collective-permute-start.10
  (35 other events, 133.8 us)
Sparse Core Ops, SparseCore 0:
  17.2 109.5 all-gather.2
  129.0 116.4 all-gather.4
  520.8 79.3 reduce-scatter.6
  604.1 151.5 reduce-scatter.8

commit v3 on v2

--- a/solution.py
+++ b/solution.py
@@ -85,21 +85,42 @@
             halves.append(jnp.concatenate([part.reshape(width // 4, count) for part in both]))
         return halves
 
-    def chain(self, blocks):
-        total = self.pick(blocks, self.place, 0).astype(f32)
+    def chosen(self, array):
+        depth = array.shape[1] // self.count
+        if depth % LANES:
+            return self.rows(array.T)
+        order = []
+        for core in (1 - self.core, self.core):
+            for mid in (self.mid, 1 - self.mid):
+                order += [4 * place + 2 * mid + core for place in range(self.outer)]
+        return transposed_blocks(jnp.stack(order).astype(jnp.int32), array, depth)
+
+    def to_core(self, lefts, right):
+        got = lax.ppermute(nn_dot(lefts[0], right).astype(bf16), "dp", self.core_pairs)
+        return got
+
+    def to_mid(self, lefts, right, got):
+        both = nn_dot(lefts[1], right) + got.astype(f32)
+        half = both.shape[0] // 2
+        kept = both[:half]
+        return kept, lax.ppermute(both[half:].astype(bf16), "dp", self.mid_pairs)
+
+    def to_outer(self, kept, got):
+        blocks = (kept + got.astype(f32)).astype(bf16)
+        blocks = blocks.reshape((self.outer, -1) + blocks.shape[1:])
+        own = self.pick(blocks, self.place, 0)
+        others = []
         for shift in range(1, self.outer):
             pairs = [(i, (i + 4 * shift) % self.count) for i in range(self.count)]
             sent = self.pick(blocks, (self.place + shift) % self.outer, 0)
-            total = total + lax.ppermute(sent, "dp", pairs).astype(f32)
+            others.append(lax.ppermute(sent, "dp", pairs))
+        return own, others
+
+    def total(self, own, others):
+        total = own.astype(f32)
+        for other in others:
+            total = total + other.astype(f32)
         return total
-
-    def scatter(self, make):
-        got = lax.ppermute(make(0).astype(bf16), "dp", self.core_pairs)
-        both = make(1) + got.astype(f32)
-        half = both.shape[0] // 2
-        got_mid = lax.ppermute(both[half:].astype(bf16), "dp", self.mid_pairs)
-        kept = (both[:half] + got_mid.astype(f32)).astype(bf16)
-        return self.chain(kept.reshape((self.outer, -1) + kept.shape[1:]))
 
 
 def other_tensor(array):
@@ -107,9 +128,12 @@
     return lax.ppermute(array, "tensor", [(i, (i + 1) % count) for i in range(count)])
 
 
-def tensor_sum(partial):
+def tensor_sum(partial, *before):
     low = partial.astype(bf16)
-    return low.astype(f32) + other_tensor(low).astype(f32)
+    other = other_tensor(low)
+    if before:
+        other = tie(other, *before)
+    return low.astype(f32) + other.astype(f32)
 
 
 def from_behind(shard, by):
@@ -128,6 +152,52 @@
 
 def nn_dot(left, right):
     return jnp.dot(left, right, preferred_element_type=f32)
+
+
+def tie(array, *others):
+    def kernel(*refs):
+        del refs
+
+    return pl.pallas_call(
+        kernel,
+        in_specs=[pl.BlockSpec(memory_space=pl.ANY)] * (1 + len(others)),
+        out_specs=pl.BlockSpec(memory_space=pl.ANY),
+        out_shape=jax.ShapeDtypeStruct(array.shape, array.dtype),
+        input_output_aliases={0: 0},
+    )(array, *others)
+
+
+def transposed_blocks(order, array, depth):
+    tokens, width = array.shape
+    half = width // depth // 2
+
+    def kernel(order_ref, in_ref, first_ref, second_ref):
+        del order_ref
+        block = in_ref[...].astype(f32).T.astype(in_ref.dtype)
+
+        @pl.when(pl.program_id(0) < half)
+        def _():
+            first_ref[...] = block
+
+        @pl.when(pl.program_id(0) >= half)
+        def _():
+            second_ref[...] = block
+
+    out = jax.ShapeDtypeStruct((width // 2, tokens), array.dtype)
+    return pl.pallas_call(
+        kernel,
+        grid_spec=pltpu.PrefetchScalarGridSpec(
+            num_scalar_prefetch=1,
+            grid=(2 * half,),
+            in_specs=[pl.BlockSpec((tokens, depth), lambda i, order: (0, order[i]))],
+            out_specs=[
+                pl.BlockSpec((depth, tokens), lambda i, order: (jnp.minimum(i, half - 1), 0)),
+                pl.BlockSpec((depth, tokens), lambda i, order: (jnp.maximum(i - half, 0), 0)),
+            ],
+        ),
+        out_shape=[out, out],
+        cost_estimate=pl.CostEstimate(flops=0, bytes_accessed=4 * tokens * width, transcendentals=0),
+    )(order, array)
 
 
 def attend_kernel(shift, q_ref, k_ref, v_ref, bias_ref, out_ref, inverse_ref):
@@ -331,35 +401,44 @@
     act_low = (gate_silu * up).astype(bf16)
     d_gate = (d_act * up * gate_sigmoid * (1.0 + gate * (1.0 - gate_sigmoid))).astype(bf16)
     d_up = (d_act * gate_silu).astype(bf16)
-    d_normed2 = tensor_sum(
-        nt_dot(d_gate, gateup_full[:, :hidden]) + nt_dot(d_up, gateup_full[:, hidden:])
-    )
-    grad_down = lax.psum_scatter(
-        tn_dot(cotangent, act_low).astype(bf16), "dp", scatter_dimension=0, tiled=True
-    )
-    grad_down = grad_down.astype(f32).T
-    normed2_rows = ring.rows(normed2_low.T)
-    pieces = []
+    d_normed2_part = nt_dot(d_gate, gateup_full[:, :hidden]) + nt_dot(
+        d_up, gateup_full[:, hidden:]
+    )
+    down_part = tn_dot(cotangent, act_low).astype(bf16)
+    grad_down = lax.psum_scatter(down_part, "dp", scatter_dimension=0, tiled=True)
+    normed2_rows = ring.chosen(normed2_low)
     piece_width = hidden // 2
-    for source in (d_gate, d_up):
-        for start in range(0, hidden, piece_width):
-            piece = source[:, start : start + piece_width]
-            pieces.append(ring.scatter(lambda part, piece=piece: nn_dot(normed2_rows[part], piece)))
-    grad_gateup = jnp.concatenate(pieces, axis=1).reshape(depth, 2, hidden)
+    rights = [
+        source[:, start : start + piece_width]
+        for source in (d_gate, d_up)
+        for start in range(0, hidden, piece_width)
+    ]
+    core_got = [ring.to_core(normed2_rows, right) for right in rights]
+    d_normed2 = tensor_sum(d_normed2_part, *[got[: 2 * 8, :LANES] for got in core_got])
+    mid_got = [
+        ring.to_mid(normed2_rows, right, got) for right, got in zip(rights, core_got, strict=True)
+    ]
+    outer_got = [ring.to_outer(kept, got) for kept, got in mid_got]
     result = mid + tensor_sum(nt_dot(act_low, down_full))
     output = result.astype(bf16)
     d_ffn_weight = jnp.sum(d_normed2 * mid * ffn_scale, axis=0)
     d_mid = cotangent.astype(f32) + rms_back(mid, ffn_scale, ffn_weight, d_normed2, 1)
 
     d_mid_low = d_mid.astype(bf16)
-    d_mid_rows = ring.rows(d_mid_low.T)
-    grad_out = ring.scatter(lambda part: nt_dot(d_mid_rows[part], attended)).T
+    d_mid_rows = ring.chosen(d_mid_low)
+    attended_back = attended.T
+    out_core = ring.to_core(d_mid_rows, attended_back)
+    out_kept, out_mid = ring.to_mid(d_mid_rows, attended_back, out_core)
+    out_own, out_others = ring.to_outer(out_kept, out_mid)
+    grad_out = ring.total(out_own, out_others).T
     d_attended = lax.dot_general(
         out_full, d_mid_low, (((0,), (1,)), ((), ())), preferred_element_type=f32
     ).astype(bf16)
+    d_attended = tie(d_attended, mid_got[0][1])
     d_query, d_keys, d_values = attend_back(
         query_low, keys, keys_t, values, d_attended, attended, inverse_total, bias
     )
+    d_keys = tie(d_keys, mid_got[1][1], *outer_got[0][1])
     d_keyval_all = jnp.concatenate([d_keys * SCORE_SCALE, d_values], axis=0)
     own_grad = d_keyval_all[:, reach_count * row_count :]
     for step_back in range(1, reach_count + 1):
@@ -389,6 +468,7 @@
         ],
         axis=0,
     ).astype(bf16)
+    d_qkv_low = tie(d_qkv_low, mid_got[2][1], *outer_got[1][1])
     d_normed_part = lax.dot_general(
         d_qkv_low, qkv_full, (((0,), (1,)), ((), ())), preferred_element_type=f32
     )
@@ -428,6 +508,9 @@
     grad_attn_gain = gains_sum[:, 0]
     grad_ffn_gain = gains_mine[:, 1]
     grad_heads = gains_sum[:gain_count, 2].reshape(2, gain_count // 2)
+    pieces = [ring.total(own, others) for own, others in outer_got]
+    grad_gateup = jnp.concatenate(pieces, axis=1).reshape(depth, 2, hidden)
+    grad_down = grad_down.astype(f32).T
     input_grad = (d_mid + rms_back(residual, attn_scale, attn_weight, d_normed, 1)).astype(bf16)
     return (
         output,

time: 910 us -> 833 us (0.915)
  waiting for transfers between devices: 430 us -> 370 us
  starting transfers between devices: 100 us -> 77.2 us
  local copies, waits for them, and re-layouts: 112 us -> 89.6 us
  Pallas kernels: 45.3 us -> 67.1 us
  other arithmetic: 60.5 us -> 75.3 us
    ppermute x5, waiting for transfers between devices: 141 us -> 97.1 us  [other_tensor(): lax.ppermute(array, 'tensor', [(i, (i + 1) % count) for i in range(count)])]
    unnamed x6, waiting for transfers between devices: 0.07 us -> 37.2 us
    ppermute x25, waiting for transfers between devices: 153 us -> 126 us  [the longest x15 101 us: to_outer(): others.append(lax.ppermute(sent, 'dp', pairs))]
    ppermute x25, starting transfers between devices: 76.8 us -> 54 us  [the longest x15 34.3 us: to_outer(): others.append(lax.ppermute(sent, 'dp', pairs))]
    pallas_call x0 -> x6, Pallas kernels: none -> 21.6 us  [the longest x2 21.6 us: transposed_blocks(): pl.pallas_call(kernel, grid_spec=pltpu.PrefetchScalarGridSpec(num_scalar_...]
    all_gather x1, waiting for transfers between devices: 14.1 us -> 0.01 us  [shards(): lax.all_gather(w_gateup.reshape(depth, 2 * hidden).astype(bf16), 'dp', ax...]
    ppermute x6, waiting for transfers between devices: 24.1 us -> 13 us  [from_behind(): return lax.ppermute(shard, 'dp', pairs)]
    dynamic_slice x6 -> x4, local copies, waits for them, and re-layouts: 15.1 us -> 4.11 us  [pick(): return lax.dynamic_index_in_dim(array, bit, axis, keepdims=False)]
  transfers between devices with their start and end apart: 40 -> 40, of which waited for: 19 -> 16; matrix products, arithmetic and copies ran while one was open for 23% -> 23% of each run, Pallas kernels for 1% -> 8%
where the time goes in v3:
time: 833 us; the launch traced here: 825 us
  waiting for transfers between devices  370 us (44%)
  matrix products  129 us (15%)
  local copies, waits for them, and re-layouts  89.6 us (11%)
  starting transfers between devices  77.2 us (9%)
  other arithmetic  75.3 us (9%)
  Pallas kernels  67.1 us (8%)
  between operations  15.6 us (2%)
    ppermute x15, waiting for transfers between devices, to_outer(): others.append(lax.ppermute(sent, 'dp', pairs))  101 us
    all_gather x1, waiting for transfers between devices, shards(): lax.all_gather(first_pack.astype(bf16), 'dp', axis=0, tiled=True)  97.6 us
    ppermute x5, waiting for transfers between devices, other_tensor(): lax.ppermute(array, 'tensor', [(i, (i + 1) % count) for i in range(count)])  97.1 us
    dot_general x13, matrix products, nn_dot(): return jnp.dot(left, right, preferred_element_type=f32)  60.8 us
    unnamed x188, local copies, waits for them, and re-layouts  55.3 us
    unnamed x6, waiting for transfers between devices  37.2 us
    ppermute x15, starting transfers between devices, to_outer(): others.append(lax.ppermute(sent, 'dp', pairs))  34.3 us
    pallas_call x1, Pallas kernels, attend_back(): pl.pallas_call(functools.partial(attend_back_kernel, keys - rows - WINDOW...  32.2 us
  transfers between devices with their start and end apart: 40, of which 16 were waited for; matrix products, arithmetic and copies ran while one was open for 23% of the time, Pallas kernels for 8%

profile of v3, /device:TPU:0, one launch (start us, length us, event | category | flops | bytes accessed | tf_op | source)
XLA Modules:
  0.0 824.6 jit_solution(13702024387746566770)
XLA Ops:
  19.4 2.4 collective-permute-start.3
  21.8 4.4 collective-permute-start.2
  29.2 97.6 %all-gather.3.cloned.1.call-done = bf16[2048,4608]{0,1:T(8,128)(2,1)} async-done(((bf16[128,4608]{0,1:T(8,128)(2,1)}), bf16[2048,4608]{0,1:T(8,128)(2,1)}) %all-gather.3.cloned.1.call-update) | async-done | bytes 18874384 | tf_op jit(solution)/shard_map/all_gather | solution.py:332
  128.2 5.3 fusion.29
  141.9 2.9 collective-permute-start.1
  144.8 3.1 collective-permute-start
  153.1 12.3 %collective-permute-done = bf16[384,512]{1,0:T(8,128)(2,1)} collective-permute-done((bf16[384,512]{1,0:T(8,128)(2,1)}, bf16[384,512]{1,0:T(8,128)(2,1)}, u32[]{:S(2)}, u32[]{:S(2)}) %collective-permute-start) | collective-permute-done | bytes 393248 | tf_op jit(solution)/shard_map/ppermute | solution.py:142
  167.7 2.4 copy.81
  173.7 13.2 %shard_map.195 = (bf16[768,512]{1,0:T(8,128)(2,1)S(1)}, f32[3,8,512]{2,1,0:T(8,128)S(1)}) custom-call(bf16[768,512]{1,0:T(8,128)(2,1)S(1)} %bitcast.193, bf16[3,1536,64]{2,1,0:T(8,128)(2,1)S(1)} %bitcast.190, bf16[3,80,1536]{2,1,0:T(8,128)(2,1)S(1)} %concatenate.58.v_ref, f32[1536,512]{1,0:T(8,128)S(1)} %fusion.38.bias_ref), custom_call_target="tpu_custom_call" | custom-call | flops 2013265920 | bytes 8388608 | tf_op jit(solution)/shard_map/pallas_call | solution.py:258
  187.0 5.4 convolution_convert_fusion.6
  194.5 10.0 %fusion.1 = f32[2560,512]{0,1:T(8,128)} fusion(bf16[512,2048]{1,0:T(8,128)(2,1)S(1)} %copy-done.21, bf16[2048,4608]{0,1:T(8,128)(2,1)} %all-gather.3.cloned.1.call-done), kind=kOutput, calls=%fused_computation.8 | convolution fusion | flops 5368709120 | bytes 17825792 | tf_op jit(solution)/shard_map/dot_general | solution.py:154
  204.4 27.7 %collective-permute-done.4 = bf16[512,2048]{1,0:T(8,128)(2,1)} collective-permute-done((bf16[512,2048]{1,0:T(8,128)(2,1)}, bf16[512,2048]{1,0:T(8,128)(2,1)}, u32[]{:S(2)}, u32[]{:S(2)}) %collective-permute-start.4) | collective-permute-done | bytes 2097184 | tf_op jit(solution)/shard_map/ppermute | solution.py:128
  232.2 3.2 multiply_reduce_fusion.2
  239.1 10.8 %shard_map.196 = (bf16[1024,512]{1,0:T(8,128)(2,1)}, bf16[1024,512]{1,0:T(8,128)(2,1)}) custom-call(s32[16]{0:T(128)} %stack.125.order_ref, bf16[512,2048]{1,0:T(8,128)(2,1)} %multiply_convert_fusion.1.in_ref), custom_call_target="tpu_custom_call" | custom-call | bytes 4194304 | tf_op jit(solution)/shard_map/pallas_call | solution.py:187
  249.9 9.1 %fusion.11 = f32[512,2560]{1,0:T(8,128)S(1)} fusion(bf16[512,2048]{1,0:T(8,128)(2,1)} %multiply_convert_fusion.1.in_ref, bf16[2048,5120]{1,0:T(8,128)(2,1)} %all-gather.5.cloned.1.call-done), kind=kOutput, calls=%fused_computation.18 | convolution fusion | flops 5368709120 | bytes 17825792 | tf_op jit(solution)/shard_map/dot_general | solution.py:154
  259.0 12.0 %fusion.15 = (bf16[512,2560]{1,0:T(8,128)(2,1)S(1)}, bf16[512,2560]{1,0:T(8,128)(2,1)S(1)}, bf16[512,2560]{1,0:T(8,128)(2,1)}) fusion(f32[2560,512]{0,1:T(8,128)} %fusion.1, f32[512,2560]{1,0:T(8,128)S(1)} %fusion.11, bf16[512,2048]{1,0:T(8,128)(2,1)S(1)} %copy-done.24, bf16[2048,5120]{1,0:T(8,128)(2,1)} %all-gather.5.cloned.1.call-done), kind=kOutput, calls=%fused_computation.26 | convolution fusion | flops 5388369920 | bytes 30932992 | tf_op jit(solution)/shard_map/dot_general | solution.py:154
  271.0 3.1 convolution_convert_fusion.5
  274.1 3.0 convolution_convert_fusion.4
  277.1 3.1 convolution_convert_fusion.3
  280.2 3.0 convolution_convert_fusion.2
  283.2 8.9 %collective-permute-start.7 = (bf16[1024,1280]{1,0:T(8,128)(2,1)}, bf16[1024,1280]{1,0:T(8,128)(2,1)}, u32[]{:S(2)}, u32[]{:S(2)}) collective-permute-start(bf16[1024,1280]{1,0:T(8,128)(2,1)} %convolution_convert_fusion.5), channel_id=1, source_target_pairs={{0,2},{2,0},{4,6},{6,4},{8,10},{10,8},{12,14},{14,12},{16,18},{18,... | collective-permute-start | bytes 7864328 | tf_op jit(solution)/shard_map/ppermute | solution.py:99
  292.7 7.2 fusion.5
  299.9 11.1 %add_convert_fusion = bf16[512,2048]{1,0:T(8,128)(2,1)} fusion(f32[512,2048]{1,0:T(8,128)} %fusion.5, bf16[512,2560]{1,0:T(8,128)(2,1)} %copy-done.78, bf16[2048,5120]{1,0:T(8,128)(2,1)} %all-gather.5.cloned.1.call-done), kind=kOutput, calls=%fused_computation.49 | convolution fusion | flops 5370806272 | bytes 19398656 | tf_op jit(solution)/shard_map/dot_general | solution.py:150
  320.2 39.1 %collective-permute-done.6.refs_0_ = bf16[512,2048]{1,0:T(8,128)(2,1)S(1)} collective-permute-done((bf16[512,2048]{1,0:T(8,128)(2,1)}, bf16[512,2048]{1,0:T(8,128)(2,1)S(1)}, u32[]{:S(2)}, u32[]{:S(2)}) %collective-permute-start.6) | collective-permute-done | bytes 2097184 | tf_op jit(solution)/shard_map/ppermute | solution.py:128
  360.6 5.5 multiply_reduce_fusion
  366.2 3.3 convert_add_fusion.4
  369.6 3.0 collective-permute-start.11
  372.7 3.3 convert_add_fusion.3
  379.6 3.4 convert_add_fusion.2
  386.2 2.9 fusion.112.in_ref
  389.2 5.4 fusion.54.refs_0_
  394.6 7.7 collective-permute-done.11.refs_1_
  416.0 32.2 %shard_map.199 = (f32[768,512]{1,0:T(8,128)S(1)}, f32[192,1536]{1,0:T(8,128)S(1)}, f32[192,1536]{1,0:T(8,128)S(1)}) custom-call(bf16[768,512]{1,0:T(8,128)(2,1)S(1)} %bitcast.194, bf16[3,1536,64]{2,1,0:T(8,128)(2,1)S(1)} %bitcast.191, bf16[192,1536]{1,0:T(8,128)(2,1)S(1)} %copy-done.5, bf16[3,1536,64]{2,1,0:T(8,128)(2,1)S(1)} %bitcast.192, ...), custom_call_target="tpu_custom_call" | custom-call | flops 5033164800 | bytes 12582912 | tf_op jit(solution)/shard_map/pallas_call | solution.py:283
  448.4 2.6 fusion.47
  459.1 3.6 collective-permute-start.19
  466.0 3.7 collective-permute-start.21
  471.8 13.6 %collective-permute-done.19.refs_2_ = bf16[128,1280]{1,0:T(8,128)(2,1)S(1)} collective-permute-done((bf16[128,1280]{1,0:T(8,128)(2,1)S(1)}, bf16[128,1280]{1,0:T(8,128)(2,1)S(1)}, u32[]{:S(2)}, u32[]{:S(2)}) %collective-permute-start.19) | collective-permute-done | bytes 327712 | tf_op jit(solution)/shard_map/ppermute | solution.py:116
  485.4 9.9 %collective-permute-done.20.refs_3_ = bf16[128,1280]{1,0:T(8,128)(2,1)S(1)} collective-permute-done((bf16[128,1280]{1,0:T(8,128)(2,1)S(1)}, bf16[128,1280]{1,0:T(8,128)(2,1)S(1)}, u32[]{:S(2)}, u32[]{:S(2)}) %collective-permute-start.20) | collective-permute-done | bytes 327712 | tf_op jit(solution)/shard_map/ppermute | solution.py:116
  496.0 8.4 %fusion.117 = (bf16[512,2048]{1,0:T(8,128)(2,1)}, f32[512,2048]{1,0:T(8,128)}) fusion(bf16[1152,512]{1,0:T(8,128)(2,1)} %shard_map.201, bf16[2048,4608]{0,1:T(8,128)(2,1)} %all-gather.3.cloned.1.call-done), kind=kOutput, calls=%fused_computation.242 | convolution fusion | flops 2416967680 | bytes 12189696 | tf_op jit(solution)/shard_map/dot_general | solution.py:472
  506.6 4.5 convolution_convert_fusion.1
  511.1 29.3 %collective-permute-done.22 = bf16[512,2048]{1,0:T(8,128)(2,1)} collective-permute-done((bf16[512,2048]{1,0:T(8,128)(2,1)}, bf16[512,2048]{1,0:T(8,128)(2,1)}, u32[]{:S(2)}, u32[]{:S(2)}) %collective-permute-start.22) | collective-permute-done | bytes 2097184 | tf_op jit(solution)/shard_map/ppermute | solution.py:128
  540.4 4.0 fusion.26
  544.4 2.9 pad_maximum_fusion
  547.3 7.9 copy.94
  555.5 10.2 %fusion = bf16[2048,2560]{0,1:T(8,128)(2,1)} fusion(bf16[512,2560]{1,0:T(8,128)(2,1)} %get-tuple-element.76, bf16[512,2048]{1,0:T(8,128)(2,1)} %param.23), kind=kOutput, calls=%fused_computation.1 | convolution fusion | flops 5373952000 | bytes 15204352 | tf_op jit(solution)/shard_map/dot_general | solution.py:146
  565.7 14.2 %copy.96 = bf16[2048,2560]{1,0:T(8,128)(2,1)} copy(bf16[2048,2560]{0,1:T(8,128)(2,1)} %fusion) | data formatting | bytes 20971520
  579.9 4.4 convert_add_fusion.1
  587.9 4.3 collective-permute-start.32
  592.2 11.1 %fusion.39 = bf16[512,2048]{1,0:T(8,128)(2,1)} fusion(bf16[512,2560]{1,0:T(8,128)(2,1)S(1)} %copy-done.80, bf16[2048,4608]{0,1:T(8,128)(2,1)} %all-gather.3.cloned.1.call-done), kind=kOutput, calls=%fused_computation.69 | convolution fusion | flops 5369757696 | bytes 15204352 | tf_op jit(solution)/shard_map/dot_general | solution.py:150
  604.8 10.8 %shard_map.202 = (bf16[1024,512]{1,0:T(8,128)(2,1)}, bf16[1024,512]{1,0:T(8,128)(2,1)}) custom-call(s32[16]{0:T(128)} %stack.125.order_ref, bf16[512,2048]{1,0:T(8,128)(2,1)} %copy-done.23), custom_call_target="tpu_custom_call" | custom-call | bytes 4194304 | tf_op jit(solution)/shard_map/pallas_call | solution.py:187
  617.9 16.6 %collective-permute-done.32 = bf16[512,1280]{1,0:T(8,128)(2,1)} collective-permute-done((bf16[512,1280]{1,0:T(8,128)(2,1)}, bf16[512,1280]{1,0:T(8,128)(2,1)}, u32[]{:S(2)}, u32[]{:S(2)}) %collective-permute-start.32) | collective-permute-done | bytes 1310752 | tf_op jit(solution)/shard_map/ppermute | solution.py:106
  634.5 2.4 fusion.45
  637.0 5.8 collective-permute-start.35
  643.9 2.4 fusion.46
  646.4 2.8 collective-permute-start.31
  653.8 3.9 collective-permute-done.35
  659.2 22.1 %collective-permute-done.34 = bf16[128,1280]{1,0:T(8,128)(2,1)S(1)} collective-permute-done((bf16[128,1280]{1,0:T(8,128)(2,1)S(1)}, bf16[128,1280]{1,0:T(8,128)(2,1)S(1)}, u32[]{:S(2)}, u32[]{:S(2)}) %collective-permute-start.34) | collective-permute-done | bytes 327712 | tf_op jit(solution)/shard_map/ppermute | solution.py:116
  683.7 24.9 %collective-permute-done.30 = bf16[128,1280]{1,0:T(8,128)(2,1)S(1)} collective-permute-done((bf16[128,1280]{1,0:T(8,128)(2,1)S(1)}, bf16[128,1280]{1,0:T(8,128)(2,1)S(1)}, u32[]{:S(2)}, u32[]{:S(2)}) %collective-permute-start.30) | collective-permute-done | bytes 327712 | tf_op jit(solution)/shard_map/ppermute | solution.py:116
  713.0 6.6 collective-permute-start.27
  722.7 3.3 pad_maximum_fusion.2
  726.0 4.5 reshape.364
  730.7 26.7 %collective-permute-done.27 = bf16[128,768]{0,1:T(8,128)(2,1)S(1)} collective-permute-done((bf16[128,768]{0,1:T(8,128)(2,1)}, bf16[128,768]{0,1:T(8,128)(2,1)S(1)}, u32[]{:S(2)}, u32[]{:S(2)}) %collective-permute-start.27) | collective-permute-done | bytes 196640 | tf_op jit(solution)/shard_map/ppermute | solution.py:116
  759.2 10.4 %fusion.24 = (bf16[512,2048]{1,0:T(8,128)(2,1)}, bf16[512,2048]{1,0:T(8,128)(2,1)}) fusion(bf16[512,2048]{1,0:T(8,128)(2,1)S(1)} %copy-done.16, bf16[512,2048]{1,0:T(8,128)(2,1)} %collective-permute-done.22, bf16[512,2048]{1,0:T(8,128)(2,1)} %get-tuple-element.125, f32[512]{0:T(512)S(1)} %fusion.111, f32[2048]{0:T(1024)S(1)} %bitcast.234, ...), kind=kLoop, calls=%fused_computation.41 | loop fusion | flops 25165824 | bytes 25190400 | tf_op jit(solution)/shard_map/convert_element_type | solution.py:514
  777.9 37.1 %reduce-scatter.9.cloned.1.call-done = bf16[128,2560]{1,0:T(8,128)(2,1)} async-done(((bf16[2048,2560]{1,0:T(8,128)(2,1)}), bf16[128,2560]{1,0:T(8,128)(2,1)}) %reduce-scatter.9.cloned.1.call-update) | async-done | bytes 655376
  (372 shorter events, 127.1 us)
Async XLA Ops:
  7.2 119.6 %all-gather.3.cloned.1.call-start = ((), (), s32[]{:S(2)}) async-start(), calls=%async_computation.2 | async-start | bytes 20054016 | tf_op jit(solution)/shard_map/all_gather | solution.py:332
  17.1 232.8 %all-gather.5.cloned.1.call-start = ((), (), s32[]{:S(2)}) async-start(), calls=%async_computation.3 | async-start | bytes 22282240 | tf_op jit(solution)/shard_map/all_gather | solution.py:333
  19.4 750.3 %reduce-scatter.7.cloned.1.call-start = ((), (), s32[]{:S(2)}) async-start(), calls=%async_computation.4 | async-start | bytes 5570560
  19.4 8.9 %collective-permute-start.3 = (bf16[512]{0:T(512)(128)(2,1)S(1)}, bf16[512]{0:T(512)(128)(2,1)S(1)}, u32[]{:S(2)}, u32[]{:S(2)}) collective-permute-start(bf16[512]{0:T(512)(128)(2,1)S(1)} %add_convert_fusion.4), channel_id=1, source_target_pairs={{0,2},{2,4},{4,6},{6,8},{8,10},{10,12},{12,14},{14,16},{16,18},{18... | collective-permute-start | bytes 3080 | tf_op jit(solution)/shard_map/ppermute | solution.py:142
  21.8 6.6 collective-permute-start.2
  27.4 106.1 %copy-start.59 = (f32[512]{0:T(512)}, f32[512]{0:T(512)S(1)}, u32[]{:S(2)}) copy-start(f32[512]{0:T(512)S(1)} %add_rsqrt_fusion.3) | copy-start | bytes 6148
  29.2 142.1 %copy-start.1 = (f32[1536,512]{1,0:T(8,128)}, f32[1536,512]{1,0:T(8,128)S(1)}, u32[]{:S(2)}) copy-start(f32[1536,512]{1,0:T(8,128)S(1)} %fusion.38.bias_ref) | copy-start | bytes 9437188
  136.7 14.3 %copy-start.65 = (f32[64]{0:T(128)}, f32[64]{0:T(128)S(1)}, u32[]{:S(2)}) copy-start(f32[64]{0:T(128)S(1)} %mul.593) | copy-start | bytes 772
  141.9 11.2 %collective-permute-start.1 = (bf16[384,512]{1,0:T(8,128)(2,1)}, bf16[384,512]{1,0:T(8,128)(2,1)}, u32[]{:S(2)}, u32[]{:S(2)}) collective-permute-start(bf16[384,512]{1,0:T(8,128)(2,1)} %pad_maximum_fusion.6), channel_id=1, source_target_pairs={{0,2},{2,4},{4,6},{6,8},{8,10},{10,12},{12,14},{14,16},{16,18},{18... | collective-permute-start | bytes 1179656 | tf_op jit(solution)/shard_map/ppermute | solution.py:142
  144.8 20.6 %collective-permute-start = (bf16[384,512]{1,0:T(8,128)(2,1)}, bf16[384,512]{1,0:T(8,128)(2,1)}, u32[]{:S(2)}, u32[]{:S(2)}) collective-permute-start(bf16[384,512]{1,0:T(8,128)(2,1)} %pad_maximum_fusion.6), channel_id=1, source_target_pairs={{0,4},{2,6},{4,8},{6,10},{8,12},{10,14},{12,16},{14,18},{16,20},{1... | collective-permute-start | bytes 1179656 | tf_op jit(solution)/shard_map/ppermute | solution.py:142
  151.0 14.4 %copy-start.39 = (bf16[3,64,512]{2,1,0:T(8,128)(2,1)S(1)}, bf16[3,64,512]{2,1,0:T(8,128)(2,1)}, u32[]{:S(2)}) copy-start(bf16[3,64,512]{2,1,0:T(8,128)(2,1)} %copy-done.38) | copy-start | bytes 589828
  192.4 39.7 %collective-permute-start.4 = (bf16[512,2048]{1,0:T(8,128)(2,1)}, bf16[512,2048]{1,0:T(8,128)(2,1)}, u32[]{:S(2)}, u32[]{:S(2)}) collective-permute-start(bf16[512,2048]{1,0:T(8,128)(2,1)} %convolution_convert_fusion.6), channel_id=1, source_target_pairs={{0,1},{1,0},{2,3},{3,2},{4,5},{5,4},{6,7},{7,6},{8,9},{9,8},{10,11... | collective-permute-start | bytes 6291464 | tf_op jit(solution)/shard_map/ppermute | solution.py:128
  194.4 37.7 %copy-start.15 = (bf16[512,2048]{1,0:T(8,128)(2,1)S(1)}, bf16[512,2048]{1,0:T(8,128)(2,1)}, u32[]{:S(2)}) copy-start(bf16[512,2048]{1,0:T(8,128)(2,1)} %param.12) | copy-start | bytes 6291460
  204.4 32.9 %copy-start.47 = (f32[2048,1]{0,1:T(1,128)S(1)}, f32[2048,1]{0,1:T(1,128)}, u32[]{:S(2)}) copy-start(f32[2048,1]{0,1:T(1,128)} %get-tuple-element.117) | copy-start | bytes 24580
  235.4 150.3 %copy-start.55 = (f32[512]{0:T(512)}, f32[512]{0:T(512)S(1)}, u32[]{:S(2)}) copy-start(f32[512]{0:T(512)S(1)} %add_rsqrt_fusion.2) | copy-start | bytes 6148
  259.0 12.0 %copy-start.75 = (bf16[1024,512]{1,0:T(8,128)(2,1)S(1)}, bf16[1024,512]{1,0:T(8,128)(2,1)}, u32[]{:S(2)}) copy-start(bf16[1024,512]{1,0:T(8,128)(2,1)} %get-tuple-element.20) | copy-start | bytes 3145732
  271.0 21.6 %copy-start.76 = (bf16[512,2560]{1,0:T(8,128)(2,1)}, bf16[512,2560]{1,0:T(8,128)(2,1)S(1)}, u32[]{:S(2)}) copy-start(bf16[512,2560]{1,0:T(8,128)(2,1)S(1)} %get-tuple-element.75) | copy-start | bytes 7864324
  271.0 21.6 %slice-start = ((s8[20971520]{0:T(1024)(128)(4,1)}), s8[4194304]{0:T(1024)(128)(4,1)S(1)}, s32[]{:S(2)}) async-start(s8[20971520]{0:T(1024)(128)(4,1)} %bitcast.239), calls=%async_computation.6 | async-start | bytes 8388608
  271.0 21.6 %slice-start.1 = ((s8[20971520]{0:T(1024)(128)(4,1)}), s8[4194304]{0:T(1024)(128)(4,1)S(1)}, s32[]{:S(2)}) async-start(s8[20971520]{0:T(1024)(128)(4,1)} %bitcast.239), calls=%async_computation.7 | async-start | bytes 8388608
  274.1 18.5 %slice-start.2 = ((s8[20971520]{0:T(1024)(128)(4,1)}), s8[4194304]{0:T(1024)(128)(4,1)S(1)}, s32[]{:S(2)}) async-start(s8[20971520]{0:T(1024)(128)(4,1)} %bitcast.239), calls=%async_computation.8 | async-start | bytes 8388608
  277.1 15.5 %slice-start.3 = ((s8[20971520]{0:T(1024)(128)(4,1)}), s8[4194304]{0:T(1024)(128)(4,1)S(1)}, s32[]{:S(2)}) async-start(s8[20971520]{0:T(1024)(128)(4,1)} %bitcast.239), calls=%async_computation.9 | async-start | bytes 8388608
  280.2 12.5 %slice-start.4 = ((s8[20971520]{0:T(1024)(128)(4,1)}), s8[4194304]{0:T(1024)(128)(4,1)S(1)}, s32[]{:S(2)}) async-start(s8[20971520]{0:T(1024)(128)(4,1)} %bitcast.239), calls=%async_computation.10 | async-start | bytes 8388608
  283.2 32.0 %collective-permute-start.7 = (bf16[1024,1280]{1,0:T(8,128)(2,1)}, bf16[1024,1280]{1,0:T(8,128)(2,1)}, u32[]{:S(2)}, u32[]{:S(2)}) collective-permute-start(bf16[1024,1280]{1,0:T(8,128)(2,1)} %convolution_convert_fusion.5), channel_id=1, source_target_pairs={{0,2},{2,0},{4,6},{6,4},{8,10},{10,8},{12,14},{14,12},{16,18},{18,... | collective-permute-start | bytes 7864328 | tf_op jit(solution)/shard_map/ppermute | solution.py:99
  292.1 24.3 %collective-permute-start.8 = (bf16[1024,1280]{1,0:T(8,128)(2,1)}, bf16[1024,1280]{1,0:T(8,128)(2,1)}, u32[]{:S(2)}, u32[]{:S(2)}) collective-permute-start(bf16[1024,1280]{1,0:T(8,128)(2,1)} %convolution_convert_fusion.4), channel_id=1, source_target_pairs={{0,2},{2,0},{4,6},{6,4},{8,10},{10,8},{12,14},{14,12},{16,18},{18,... | collective-permute-start | bytes 7864328 | tf_op jit(solution)/shard_map/ppermute | solution.py:99
  292.1 25.6 %collective-permute-start.9 = (bf16[1024,1280]{1,0:T(8,128)(2,1)}, bf16[1024,1280]{1,0:T(8,128)(2,1)}, u32[]{:S(2)}, u32[]{:S(2)}) collective-permute-start(bf16[1024,1280]{1,0:T(8,128)(2,1)} %convolution_convert_fusion.3), channel_id=1, source_target_pairs={{0,2},{2,0},{4,6},{6,4},{8,10},{10,8},{12,14},{14,12},{16,18},{18,... | collective-permute-start | bytes 7864328 | tf_op jit(solution)/shard_map/ppermute | solution.py:99
  292.6 26.4 %collective-permute-start.10 = (bf16[1024,1280]{1,0:T(8,128)(2,1)}, bf16[1024,1280]{1,0:T(8,128)(2,1)}, u32[]{:S(2)}, u32[]{:S(2)}) collective-permute-start(bf16[1024,1280]{1,0:T(8,128)(2,1)} %convolution_convert_fusion.2), channel_id=1, source_target_pairs={{0,2},{2,0},{4,6},{6,4},{8,10},{10,8},{12,14},{14,12},{16,18},{18,... | collective-permute-start | bytes 7864328 | tf_op jit(solution)/shard_map/ppermute | solution.py:99
  299.9 12.6 %copy-start.66 = (f32[64]{0:T(128)S(1)}, f32[64]{0:T(128)}, u32[]{:S(2)}) copy-start(f32[64]{0:T(128)} %copy-done.65) | copy-start | bytes 772
  299.9 13.3 %copy-start.69 = (f32[64]{0:T(128)S(1)}, f32[64]{0:T(128)}, u32[]{:S(2)}) copy-start(f32[64]{0:T(128)} %copy-done.68) | copy-start | bytes 772
  299.9 13.9 %copy-start.29 = (bf16[192,1536]{1,0:T(8,128)(2,1)S(1)}, bf16[192,1536]{1,0:T(8,128)(2,1)}, u32[]{:S(2)}) copy-start(bf16[192,1536]{1,0:T(8,128)(2,1)} %get-tuple-element.103) | copy-start | bytes 1769476
  311.0 48.3 %collective-permute-start.6 = (bf16[512,2048]{1,0:T(8,128)(2,1)}, bf16[512,2048]{1,0:T(8,128)(2,1)S(1)}, u32[]{:S(2)}, u32[]{:S(2)}) collective-permute-start(bf16[512,2048]{1,0:T(8,128)(2,1)} %add_convert_fusion), channel_id=1, source_target_pairs={{0,1},{1,0},{2,3},{3,2},{4,5},{5,4},{6,7},{7,6},{8,9},{9,8},{10,11... | collective-permute-start | bytes 6291464 | tf_op jit(solution)/shard_map/ppermute | solution.py:128
  366.2 19.5 %copy-start.57 = (f32[512]{0:T(512)}, f32[512]{0:T(512)S(1)}, u32[]{:S(2)}) copy-start(f32[512]{0:T(512)S(1)} %fusion.110) | copy-start | bytes 6148
  369.6 32.7 %collective-permute-start.11 = (bf16[512,1280]{1,0:T(8,128)(2,1)S(1)}, bf16[512,1280]{1,0:T(8,128)(2,1)S(1)}, u32[]{:S(2)}, u32[]{:S(2)}) collective-permute-start(bf16[512,1280]{1,0:T(8,128)(2,1)S(1)} %slice.415), channel_id=1, source_target_pairs={{0,4},{2,6},{4,0},{6,2},{8,12},{10,14},{12,8},{14,10},{16,20},{18,... | collective-permute-start | bytes 3932168 | tf_op jit(solution)/shard_map/ppermute | solution.py:106
  379.0 69.4 %collective-permute-start.12 = (bf16[512,1280]{1,0:T(8,128)(2,1)}, bf16[512,1280]{1,0:T(8,128)(2,1)}, u32[]{:S(2)}, u32[]{:S(2)}) collective-permute-start(bf16[512,1280]{1,0:T(8,128)(2,1)} %slice.414), channel_id=1, source_target_pairs={{0,4},{2,6},{4,0},{6,2},{8,12},{10,14},{12,8},{14,10},{16,20},{18,... | collective-permute-start | bytes 3932168 | tf_op jit(solution)/shard_map/ppermute | solution.py:106
  384.3 87.5 %collective-permute-start.18 = (bf16[512,1280]{1,0:T(8,128)(2,1)}, bf16[512,1280]{1,0:T(8,128)(2,1)}, u32[]{:S(2)}, u32[]{:S(2)}) collective-permute-start(bf16[512,1280]{1,0:T(8,128)(2,1)} %slice.413), channel_id=1, source_target_pairs={{0,4},{2,6},{4,0},{6,2},{8,12},{10,14},{12,8},{14,10},{16,20},{18,... | collective-permute-start | bytes 3932168 | tf_op jit(solution)/shard_map/ppermute | solution.py:106
  405.4 49.0 %collective-permute-start.13 = (bf16[128,1280]{1,0:T(8,128)(2,1)}, bf16[128,1280]{1,0:T(8,128)(2,1)}, u32[]{:S(2)}, u32[]{:S(2)}) collective-permute-start(bf16[128,1280]{1,0:T(8,128)(2,1)} %get-tuple-element.100), channel_id=1, source_target_pairs={{0,8},{2,10},{4,12},{6,14},{8,16},{10,18},{12,20},{14,22},{16,24},... | collective-permute-start | bytes 983048 | tf_op jit(solution)/shard_map/ppermute | solution.py:116
  407.0 47.4 %collective-permute-start.14 = (bf16[128,1280]{1,0:T(8,128)(2,1)}, bf16[128,1280]{1,0:T(8,128)(2,1)}, u32[]{:S(2)}, u32[]{:S(2)}) collective-permute-start(bf16[128,1280]{1,0:T(8,128)(2,1)} %get-tuple-element.99), channel_id=1, source_target_pairs={{0,16},{2,18},{4,20},{6,22},{8,24},{10,26},{12,28},{14,30},{16,0},... | collective-permute-start | bytes 983048 | tf_op jit(solution)/shard_map/ppermute | solution.py:116
  408.6 45.8 %collective-permute-start.15 = (bf16[128,1280]{1,0:T(8,128)(2,1)}, bf16[128,1280]{1,0:T(8,128)(2,1)}, u32[]{:S(2)}, u32[]{:S(2)}) collective-permute-start(bf16[128,1280]{1,0:T(8,128)(2,1)} %get-tuple-element.98), channel_id=1, source_target_pairs={{0,24},{2,26},{4,28},{6,30},{8,0},{10,2},{12,4},{14,6},{16,8},{18,... | collective-permute-start | bytes 983048 | tf_op jit(solution)/shard_map/ppermute | solution.py:116
  456.1 9.9 %collective-permute-start.17 = (bf16[384,512]{1,0:T(8,128)(2,1)S(1)}, bf16[384,512]{1,0:T(8,128)(2,1)S(1)}, u32[]{:S(2)}, u32[]{:S(2)}) collective-permute-start(bf16[384,512]{1,0:T(8,128)(2,1)S(1)} %get-tuple-element.102), channel_id=1, source_target_pairs={{4,0},{6,2},{8,4},{10,6},{12,8},{14,10},{16,12},{18,14},{20,16},{2... | collective-permute-start | bytes 1179656 | tf_op jit(solution)/shard_map/ppermute | solution.py:142
  457.6 12.0 %collective-permute-start.16 = (bf16[384,512]{1,0:T(8,128)(2,1)S(1)}, bf16[384,512]{1,0:T(8,128)(2,1)S(1)}, u32[]{:S(2)}, u32[]{:S(2)}) collective-permute-start(bf16[384,512]{1,0:T(8,128)(2,1)S(1)} %get-tuple-element.101), channel_id=1, source_target_pairs={{2,0},{4,2},{6,4},{8,6},{10,8},{12,10},{14,12},{16,14},{18,16},{20... | collective-permute-start | bytes 1179656 | tf_op jit(solution)/shard_map/ppermute | solution.py:142
  459.1 26.4 %collective-permute-start.19 = (bf16[128,1280]{1,0:T(8,128)(2,1)S(1)}, bf16[128,1280]{1,0:T(8,128)(2,1)S(1)}, u32[]{:S(2)}, u32[]{:S(2)}) collective-permute-start(bf16[128,1280]{1,0:T(8,128)(2,1)S(1)} %get-tuple-element.97), channel_id=1, source_target_pairs={{0,8},{2,10},{4,12},{6,14},{8,16},{10,18},{12,20},{14,22},{16,24},... | collective-permute-start | bytes 983048 | tf_op jit(solution)/shard_map/ppermute | solution.py:116
  462.6 32.6 %collective-permute-start.20 = (bf16[128,1280]{1,0:T(8,128)(2,1)S(1)}, bf16[128,1280]{1,0:T(8,128)(2,1)S(1)}, u32[]{:S(2)}, u32[]{:S(2)}) collective-permute-start(bf16[128,1280]{1,0:T(8,128)(2,1)S(1)} %get-tuple-element.96), channel_id=1, source_target_pairs={{0,16},{2,18},{4,20},{6,22},{8,24},{10,26},{12,28},{14,30},{16,0},... | collective-permute-start | bytes 983048 | tf_op jit(solution)/shard_map/ppermute | solution.py:116
  466.0 29.3 %collective-permute-start.21 = (bf16[128,1280]{1,0:T(8,128)(2,1)S(1)}, bf16[128,1280]{1,0:T(8,128)(2,1)}, u32[]{:S(2)}, u32[]{:S(2)}) collective-permute-start(bf16[128,1280]{1,0:T(8,128)(2,1)S(1)} %get-tuple-element.95), channel_id=1, source_target_pairs={{0,24},{2,26},{4,28},{6,30},{8,0},{10,2},{12,4},{14,6},{16,8},{18,... | collective-permute-start | bytes 983048 | tf_op jit(solution)/shard_map/ppermute | solution.py:116
  504.4 36.0 %collective-permute-start.22 = (bf16[512,2048]{1,0:T(8,128)(2,1)}, bf16[512,2048]{1,0:T(8,128)(2,1)}, u32[]{:S(2)}, u32[]{:S(2)}) collective-permute-start(bf16[512,2048]{1,0:T(8,128)(2,1)} %get-tuple-element.125), channel_id=1, source_target_pairs={{0,1},{1,0},{2,3},{3,2},{4,5},{5,4},{6,7},{7,6},{8,9},{9,8},{10,11... | collective-permute-start | bytes 6291464 | tf_op jit(solution)/shard_map/ppermute | solution.py:128
  506.6 33.8 %copy-start.33 = (f32[512,2048]{1,0:T(8,128)S(1)}, f32[512,2048]{1,0:T(8,128)}, u32[]{:S(2)}) copy-start(f32[512,2048]{1,0:T(8,128)} %get-tuple-element.126) | copy-start | bytes 12582916
  555.2 259.8 %reduce-scatter.9.cloned.1.call-start = ((), (), s32[]{:S(2)}) async-start(), calls=%async_computation.5 | async-start | bytes 11141120
  579.9 12.3 %copy-start.80 = (bf16[512,2560]{1,0:T(8,128)(2,1)S(1)}, bf16[512,2560]{1,0:T(8,128)(2,1)}, u32[]{:S(2)}) copy-start(bf16[512,2560]{1,0:T(8,128)(2,1)} %get-tuple-element.76) | copy-start | bytes 7864324
  587.9 46.6 %collective-permute-start.32 = (bf16[512,1280]{1,0:T(8,128)(2,1)}, bf16[512,1280]{1,0:T(8,128)(2,1)}, u32[]{:S(2)}, u32[]{:S(2)}) collective-permute-start(bf16[512,1280]{1,0:T(8,128)(2,1)} %slice.412), channel_id=1, source_target_pairs={{0,4},{2,6},{4,0},{6,2},{8,12},{10,14},{12,8},{14,10},{16,20},{18,... | collective-permute-start | bytes 3932168 | tf_op jit(solution)/shard_map/ppermute | solution.py:106
  603.3 155.9 %collective-permute-start.5 = (bf16[512,2048]{1,0:T(8,128)(2,1)}, bf16[512,2048]{1,0:T(8,128)(2,1)}, u32[]{:S(2)}, u32[]{:S(2)}) collective-permute-start(bf16[512,2048]{1,0:T(8,128)(2,1)} %fusion.39), channel_id=1, source_target_pairs={{0,1},{1,0},{2,3},{3,2},{4,5},{5,4},{6,7},{7,6},{8,9},{9,8},{10,11... | collective-permute-start | bytes 6291464 | tf_op jit(solution)/shard_map/ppermute | solution.py:128
  617.9 28.5 %collective-permute-start.24 = (bf16[1024,768]{1,0:T(8,128)(2,1)S(1)}, bf16[1024,768]{1,0:T(8,128)(2,1)S(1)}, u32[]{:S(2)}, u32[]{:S(2)}) collective-permute-start(bf16[1024,768]{1,0:T(8,128)(2,1)S(1)} %convolution_convert_fusion.7), channel_id=1, source_target_pairs={{0,2},{2,0},{4,6},{6,4},{8,10},{10,8},{12,14},{14,12},{16,18},{18,... | collective-permute-start | bytes 4718600 | tf_op jit(solution)/shard_map/ppermute | solution.py:99
  637.0 20.7 %collective-permute-start.35 = (bf16[128,1280]{1,0:T(8,128)(2,1)S(1)}, bf16[128,1280]{1,0:T(8,128)(2,1)S(1)}, u32[]{:S(2)}, u32[]{:S(2)}) collective-permute-start(bf16[128,1280]{1,0:T(8,128)(2,1)S(1)} %get-tuple-element.93), channel_id=1, source_target_pairs={{0,24},{2,26},{4,28},{6,30},{8,0},{10,2},{12,4},{14,6},{16,8},{18,... | collective-permute-start | bytes 983048 | tf_op jit(solution)/shard_map/ppermute | solution.py:116
  642.8 38.5 %collective-permute-start.34 = (bf16[128,1280]{1,0:T(8,128)(2,1)S(1)}, bf16[128,1280]{1,0:T(8,128)(2,1)S(1)}, u32[]{:S(2)}, u32[]{:S(2)}) collective-permute-start(bf16[128,1280]{1,0:T(8,128)(2,1)S(1)} %get-tuple-element.94), channel_id=1, source_target_pairs={{0,16},{2,18},{4,20},{6,22},{8,24},{10,26},{12,28},{14,30},{16,0},... | collective-permute-start | bytes 983048 | tf_op jit(solution)/shard_map/ppermute | solution.py:116
  642.8 38.5 %collective-permute-start.33 = (bf16[128,1280]{1,0:T(8,128)(2,1)S(1)}, bf16[128,1280]{1,0:T(8,128)(2,1)S(1)}, u32[]{:S(2)}, u32[]{:S(2)}) collective-permute-start(bf16[128,1280]{1,0:T(8,128)(2,1)S(1)} %get-tuple-element.92), channel_id=1, source_target_pairs={{0,8},{2,10},{4,12},{6,14},{8,16},{10,18},{12,20},{14,22},{16,24},... | collective-permute-start | bytes 983048 | tf_op jit(solution)/shard_map/ppermute | solution.py:116
  646.4 37.3 %collective-permute-start.31 = (bf16[128,1280]{1,0:T(8,128)(2,1)S(1)}, bf16[128,1280]{1,0:T(8,128)(2,1)S(1)}, u32[]{:S(2)}, u32[]{:S(2)}) collective-permute-start(bf16[128,1280]{1,0:T(8,128)(2,1)S(1)} %get-tuple-element.90), channel_id=1, source_target_pairs={{0,24},{2,26},{4,28},{6,30},{8,0},{10,2},{12,4},{14,6},{16,8},{18,... | collective-permute-start | bytes 983048 | tf_op jit(solution)/shard_map/ppermute | solution.py:116
  657.7 50.9 %collective-permute-start.30 = (bf16[128,1280]{1,0:T(8,128)(2,1)S(1)}, bf16[128,1280]{1,0:T(8,128)(2,1)S(1)}, u32[]{:S(2)}, u32[]{:S(2)}) collective-permute-start(bf16[128,1280]{1,0:T(8,128)(2,1)S(1)} %get-tuple-element.91), channel_id=1, source_target_pairs={{0,16},{2,18},{4,20},{6,22},{8,24},{10,26},{12,28},{14,30},{16,0},... | collective-permute-start | bytes 983048 | tf_op jit(solution)/shard_map/ppermute | solution.py:116
  681.3 27.3 %collective-permute-start.29 = (bf16[128,1280]{1,0:T(8,128)(2,1)S(1)}, bf16[128,1280]{1,0:T(8,128)(2,1)S(1)}, u32[]{:S(2)}, u32[]{:S(2)}) collective-permute-start(bf16[128,1280]{1,0:T(8,128)(2,1)S(1)} %get-tuple-element.89), channel_id=1, source_target_pairs={{0,8},{2,10},{4,12},{6,14},{8,16},{10,18},{12,20},{14,22},{16,24},... | collective-permute-start | bytes 983048 | tf_op jit(solution)/shard_map/ppermute | solution.py:116
  681.3 28.3 %collective-permute-start.25 = (bf16[512,768]{1,0:T(8,128)(2,1)S(1)}, bf16[512,768]{1,0:T(8,128)(2,1)S(1)}, u32[]{:S(2)}, u32[]{:S(2)}) collective-permute-start(bf16[512,768]{1,0:T(8,128)(2,1)S(1)} %slice.416), channel_id=1, source_target_pairs={{0,4},{2,6},{4,0},{6,2},{8,12},{10,14},{12,8},{14,10},{16,20},{18,... | collective-permute-start | bytes 2359304 | tf_op jit(solution)/shard_map/ppermute | solution.py:106
  712.2 18.4 %collective-permute-start.28 = (bf16[128,768]{0,1:T(8,128)(2,1)}, bf16[128,768]{0,1:T(8,128)(2,1)}, u32[]{:S(2)}, u32[]{:S(2)}) collective-permute-start(bf16[128,768]{0,1:T(8,128)(2,1)} %bitcast.228), channel_id=1, source_target_pairs={{0,24},{2,26},{4,28},{6,30},{8,0},{10,2},{12,4},{14,6},{16,8},{18,... | collective-permute-start | bytes 589832 | tf_op jit(solution)/shard_map/ppermute | solution.py:116
  713.0 44.4 %collective-permute-start.27 = (bf16[128,768]{0,1:T(8,128)(2,1)}, bf16[128,768]{0,1:T(8,128)(2,1)S(1)}, u32[]{:S(2)}, u32[]{:S(2)}) collective-permute-start(bf16[128,768]{0,1:T(8,128)(2,1)} %bitcast.229), channel_id=1, source_target_pairs={{0,16},{2,18},{4,20},{6,22},{8,24},{10,26},{12,28},{14,30},{16,0},... | collective-permute-start | bytes 589832 | tf_op jit(solution)/shard_map/ppermute | solution.py:116
  720.4 37.0 %collective-permute-start.26 = (bf16[128,768]{0,1:T(8,128)(2,1)}, bf16[128,768]{0,1:T(8,128)(2,1)S(1)}, u32[]{:S(2)}, u32[]{:S(2)}) collective-permute-start(bf16[128,768]{0,1:T(8,128)(2,1)} %bitcast.230), channel_id=1, source_target_pairs={{0,8},{2,10},{4,12},{6,14},{8,16},{10,18},{12,20},{14,22},{16,24},... | collective-permute-start | bytes 589832 | tf_op jit(solution)/shard_map/ppermute | solution.py:116
  726.0 33.2 %copy-start.62 = (f32[512]{0:T(512)S(1)}, f32[512]{0:T(512)}, u32[]{:S(2)}) copy-start(f32[512]{0:T(512)} %copy-done.61) | copy-start | bytes 6148
  726.0 33.2 %copy-start.48 = (f32[2048,1]{0,1:T(1,128)S(1)}, f32[2048,1]{0,1:T(1,128)}, u32[]{:S(2)}) copy-start(f32[2048,1]{0,1:T(1,128)} %get-tuple-element.117) | copy-start | bytes 24580
  726.0 33.2 %copy-start.56 = (f32[512]{0:T(512)S(1)}, f32[512]{0:T(512)}, u32[]{:S(2)}) copy-start(f32[512]{0:T(512)} %copy-done.55) | copy-start | bytes 6148
  726.0 33.3 %copy-start.58 = (f32[512]{0:T(512)S(1)}, f32[512]{0:T(512)}, u32[]{:S(2)}) copy-start(f32[512]{0:T(512)} %copy-done.57) | copy-start | bytes 6148
  770.7 5.0 collective-permute-start.23
  (62 other events, 268.8 us)
Sparse Core Ops, SparseCore 0:
  17.2 109.5 all-gather.2
  129.0 116.3 all-gather.4
  555.3 115.6 reduce-scatter.6
  674.9 140.0 reduce-scatter.8

commit v4 on v2

--- a/solution.py
+++ b/solution.py
@@ -23,9 +23,17 @@
 EXP2_SCALE = SCORE_SCALE * math.log2(math.e)
 TILE = 256
 SUM_ROWS = 16
+LINK_SHARE = 0.5
 
 bf16 = jnp.bfloat16
 f32 = jnp.float32
+ANYWHERE = pl.BlockSpec(memory_space=pl.ANY)
+
+
+def cost(microseconds):
+    return pl.CostEstimate(
+        flops=int(microseconds * LINK_SHARE * 1.15e9), bytes_accessed=0, transcendentals=0
+    )
 
 
 def angles_of(positions):
@@ -63,43 +71,51 @@
 class Ring:
     def __init__(self):
         self.count = lax.axis_size("dp")
-        self.outer = self.count // 4
-        index = lax.axis_index("dp")
-        self.index = index
-        self.core = index % 2
-        self.mid = (index // 2) % 2
-        self.place = index // 4
-        self.core_pairs = [(i, i ^ 1) for i in range(self.count)]
-        self.mid_pairs = [(i, i ^ 2) for i in range(self.count)]
-
-    def pick(self, array, bit, axis):
-        return lax.dynamic_index_in_dim(array, bit, axis, keepdims=False)
-
-    def rows(self, array):
-        width, count = array.shape
-        blocks = array.reshape(self.outer, 2, 2, width // self.count, count)
-        halves = []
-        for bit in (1 - self.core, self.core):
-            half = self.pick(blocks, bit, 2)
-            both = [self.pick(half, self.mid, 1), self.pick(half, 1 - self.mid, 1)]
-            halves.append(jnp.concatenate([part.reshape(width // 4, count) for part in both]))
-        return halves
-
-    def chain(self, blocks):
-        total = self.pick(blocks, self.place, 0).astype(f32)
-        for shift in range(1, self.outer):
-            pairs = [(i, (i + 4 * shift) % self.count) for i in range(self.count)]
-            sent = self.pick(blocks, (self.place + shift) % self.outer, 0)
-            total = total + lax.ppermute(sent, "dp", pairs).astype(f32)
-        return total
-
-    def scatter(self, make):
-        got = lax.ppermute(make(0).astype(bf16), "dp", self.core_pairs)
-        both = make(1) + got.astype(f32)
-        half = both.shape[0] // 2
-        got_mid = lax.ppermute(both[half:].astype(bf16), "dp", self.mid_pairs)
-        kept = (both[:half] + got_mid.astype(f32)).astype(bf16)
-        return self.chain(kept.reshape((self.outer, -1) + kept.shape[1:]))
+        self.index = lax.axis_index("dp")
+        self.bits = [1 << at for at in range(self.count.bit_length() - 1)]
+
+    def order(self, bits):
+        order = []
+        for at in range(self.count - 1, -1, -1):
+            flips = sum(bit for place, bit in enumerate(reversed(bits)) if at >> place & 1)
+            order.append(self.index ^ flips)
+        return jnp.stack(order).astype(jnp.int32)
+
+    def chosen(self, array, bits):
+        depth = array.shape[1] // self.count
+        if depth % LANES:
+            blocks = array.T.reshape(self.count, depth, array.shape[0])
+            return jnp.take(blocks, self.order(bits), axis=0).reshape(array.shape[1], array.shape[0])
+        return transposed_blocks(self.order(bits), array, depth)
+
+
+class Scatter:
+    def __init__(self, ring, left, right, bits, tail=None):
+        self.ring, self.left, self.right, self.bits, self.tail = ring, left, right, bits, tail
+        self.got = []
+
+    def rows(self):
+        step = len(self.got)
+        last = step == len(self.bits)
+        size = self.left.shape[0] >> (step if last else step + 1)
+        start = self.left.shape[0] - (self.left.shape[0] >> step)
+        starts = [self.left.shape[0] - (self.left.shape[0] >> at + 1) for at in range(step)]
+        return size, start // size, [(start - first) // size for first in starts]
+
+    def send(self, *after):
+        size, block, blocks = self.rows()
+        sent = product(
+            self.left, self.right, size, block, list(zip(self.got, blocks)), after, self.tail
+        )
+        bit = self.bits[len(self.got)]
+        pairs = [(i, i ^ bit) for i in range(self.ring.count)]
+        self.got.append(lax.ppermute(sent, "dp", pairs))
+        return sent
+
+    def total(self, *after, transposed=False):
+        size, block, blocks = self.rows()
+        got = list(zip(self.got, blocks))
+        return product(self.left, self.right, size, block, got, after, self.tail, f32, transposed)
 
 
 def other_tensor(array):
@@ -107,9 +123,12 @@
     return lax.ppermute(array, "tensor", [(i, (i + 1) % count) for i in range(count)])
 
 
-def tensor_sum(partial):
+def tensor_sum(partial, *before):
     low = partial.astype(bf16)
-    return low.astype(f32) + other_tensor(low).astype(f32)
+    other = other_tensor(low)
+    if before:
+        other = tie(other, *before)
+    return low.astype(f32) + other.astype(f32)
 
 
 def from_behind(shard, by):
@@ -128,6 +147,377 @@
 
 def nn_dot(left, right):
     return jnp.dot(left, right, preferred_element_type=f32)
+
+
+def tie(array, *others):
+    def kernel(*refs):
+        del refs
+
+    return pl.pallas_call(
+        kernel,
+        in_specs=[pl.BlockSpec(memory_space=pl.ANY)] * (1 + len(others)),
+        out_specs=pl.BlockSpec(memory_space=pl.ANY),
+        out_shape=jax.ShapeDtypeStruct(array.shape, array.dtype),
+        input_output_aliases={0: 0},
+        cost_estimate=cost(0),
+    )(array, *others)
+
+
+def corner(array):
+    return array[: 2 * 8, :LANES]
+
+
+def transposed_blocks(order, array, depth):
+    tokens, width = array.shape
+    step = math.gcd(tokens, LANES)
+
+    def kernel(order_ref, in_ref, out_ref):
+        for at in range(width // depth):
+            column = pl.multiple_of(order_ref[at] * depth, depth)
+            out_ref[at * depth : (at + 1) * depth, :] = in_ref[:, pl.ds(column, depth)].T
+
+    return pl.pallas_call(
+        kernel,
+        grid_spec=pltpu.PrefetchScalarGridSpec(
+            num_scalar_prefetch=1,
+            grid=(tokens // step,),
+            in_specs=[pl.BlockSpec((step, width), lambda i, order: (i, 0))],
+            out_specs=pl.BlockSpec((width, step), lambda i, order: (0, i)),
+        ),
+        out_shape=jax.ShapeDtypeStruct((width, tokens), array.dtype),
+        cost_estimate=cost(4.8),
+    )(order, array)
+
+
+def product(left, right, size, block, adds, after=(), tail=None, out_type=bf16, transposed=False):
+    depth, columns = right.shape
+    most = max(LANES, min(columns, 512 * 1024 // size))
+    tile = max(t for t in range(LANES, most + 1, LANES) if columns % t == 0)
+    if tail is not None:
+        tile = LANES
+    steps = columns // tile
+
+    def kernel(left_ref, right_ref, *refs):
+        def put(total):
+            for ref in refs[: len(adds)]:
+                total = total + ref[...].astype(f32)
+            refs[-1][...] = (total.T if transposed else total).astype(out_type)
+
+        if tail is None:
+            put(nn_dot(left_ref[...], right_ref[...]))
+            return
+
+        @pl.when(pl.program_id(0) < steps)
+        def _():
+            put(nn_dot(left_ref[...], right_ref[...]))
+
+        @pl.when(pl.program_id(0) == steps)
+        def _():
+            put(refs[len(adds)][...].astype(f32))
+
+    all_columns = columns
+    in_specs = [
+        pl.BlockSpec((size, depth), lambda i: (block, 0)),
+        pl.BlockSpec((depth, tile), lambda i: (0, jnp.minimum(i, steps - 1))),
+    ] + [
+        pl.BlockSpec((size, tile), functools.partial(lambda i, row: (row, i), row=row))
+        for _, row in adds
+    ]
+    operands = [left, right, *[array for array, _ in adds]]
+    if tail is not None:
+        all_columns += LANES
+        in_specs.append(pl.BlockSpec((size, LANES), lambda i: (block, 0)))
+        operands.append(tail)
+    out_shape, out_block, out_map = (size, all_columns), (size, tile), lambda i: (0, i)
+    if transposed:
+        out_shape, out_block, out_map = (all_columns, size), (tile, size), lambda i: (i, 0)
+    return pl.pallas_call(
+        kernel,
+        grid=(all_columns // tile,),
+        in_specs=in_specs + [ANYWHERE] * len(after),
+        out_specs=pl.BlockSpec(out_block, out_map),
+        out_shape=jax.ShapeDtypeStruct(out_shape, out_type),
+        compiler_params=pltpu.CompilerParams(vmem_limit_bytes=40 * 2**20),
+        cost_estimate=cost(2 + 2 * size * depth * columns / 0.9e9),
+    )(*operands, *after)
+
+
+def product_tt(left, first, columns, right):
+    depth = left.shape[0]
+    rows = right.shape[0]
+    tile = max(t for t in range(LANES, 384 + 1, LANES) if columns % t == 0 and first % t == 0)
+
+    def kernel(left_ref, right_ref, out_ref):
+        out_ref[...] = nt_dot(left_ref[...].T, right_ref[...]).astype(bf16)
+
+    return pl.pallas_call(
+        kernel,
+        grid=(columns // tile,),
+        in_specs=[
+            pl.BlockSpec((depth, tile), lambda i: (0, i + first // tile)),
+            pl.BlockSpec((rows, depth), lambda i: (0, 0)),
+        ],
+        out_specs=pl.BlockSpec((tile, rows), lambda i: (i, 0)),
+        out_shape=jax.ShapeDtypeStruct((columns, rows), bf16),
+        compiler_params=pltpu.CompilerParams(vmem_limit_bytes=40 * 2**20),
+        cost_estimate=cost(4.3),
+    )(left, right)
+
+
+def norm_back(values, direct, part, other, gain, *after):
+    rows, width = values.shape
+    step = math.gcd(rows, 128)
+
+    def kernel(values_ref, direct_ref, part_ref, other_ref, gain_ref, *refs):
+        out_ref, low_ref, gain_out_ref = refs[len(after) :]
+        value = values_ref[...].astype(f32)
+        scale = inverse_rms(value, 1)
+        d_out = part_ref[...].astype(f32) + other_ref[...].astype(f32)
+        result = direct_ref[...].astype(f32) + rms_back(value, scale, gain_ref[...], d_out, 1)
+        out_ref[...] = result
+        low_ref[...] = result.astype(bf16)
+
+        @pl.when(pl.program_id(0) == 0)
+        def _():
+            gain_out_ref[...] = jnp.zeros_like(gain_out_ref)
+
+        gain_out_ref[...] += jnp.sum(d_out * value * scale, axis=0, keepdims=True)
+
+    block = pl.BlockSpec((step, width), lambda i: (i, 0))
+    row = pl.BlockSpec((1, width), lambda i: (0, 0))
+    return pl.pallas_call(
+        kernel,
+        grid=(rows // step,),
+        in_specs=[block] * 4 + [row] + [ANYWHERE] * len(after),
+        out_specs=[block, block, row],
+        out_shape=[
+            jax.ShapeDtypeStruct((rows, width), f32),
+            jax.ShapeDtypeStruct((rows, width), bf16),
+            jax.ShapeDtypeStruct((1, width), f32),
+        ],
+        compiler_params=pltpu.CompilerParams(vmem_limit_bytes=40 * 2**20),
+        cost_estimate=cost(7),
+    )(values, direct, part, other, gain[None, :], *after)
+
+
+def add_up(values, part, other, *after):
+    rows, width = values.shape
+    step = math.gcd(rows, 128)
+
+    def kernel(values_ref, part_ref, other_ref, *refs):
+        added = part_ref[...].astype(f32) + other_ref[...].astype(f32)
+        refs[-1][...] = (values_ref[...] + added).astype(bf16)
+
+    block = pl.BlockSpec((step, width), lambda i: (i, 0))
+    return pl.pallas_call(
+        kernel,
+        grid=(rows // step,),
+        in_specs=[block] * 3 + [ANYWHERE] * len(after),
+        out_specs=block,
+        out_shape=jax.ShapeDtypeStruct((rows, width), bf16),
+        cost_estimate=cost(3),
+    )(values, part, other, *after)
+
+
+def turn_back(d_rotated, raw, cos_table, sin_table, gain):
+    half_width = HD // 2
+    first, second = d_rotated[:half_width], d_rotated[half_width:]
+    d_normed = jnp.concatenate(
+        [first * cos_table + second * sin_table, second * cos_table - first * sin_table], axis=0
+    )
+    scale = inverse_rms(raw, 0)
+    return rms_back(raw, scale, gain, d_normed, 0), d_normed * raw * scale
+
+
+def query_back(d_query, raw, cos_table, sin_table, gain, *after):
+    width, rows = d_query.shape
+    step = GROUP * HD
+
+    def kernel(d_ref, raw_ref, cos_ref, sin_ref, gain_ref, *refs):
+        out_ref, gain_out_ref = refs[len(after) :]
+        results = []
+        d_gain = jnp.zeros((HD, rows), f32)
+        for head in range(GROUP):
+            of = slice(head * HD, (head + 1) * HD)
+            result, by_token = turn_back(
+                d_ref[of, :] * SCORE_SCALE, raw_ref[of, :], cos_ref[...], sin_ref[...], gain_ref[...]
+            )
+            results.append(result)
+            d_gain = d_gain + by_token
+        out_ref[...] = jnp.concatenate(results, axis=0).astype(bf16).T
+
+        @pl.when(pl.program_id(0) == 0)
+        def _():
+            gain_out_ref[...] = jnp.zeros_like(gain_out_ref)
+
+        gain_out_ref[...] += jnp.sum(d_gain, axis=1, keepdims=True)
+
+    block = pl.BlockSpec((step, rows), lambda i: (i, 0))
+    table = pl.BlockSpec((HD // 2, rows), lambda i: (0, 0))
+    column = pl.BlockSpec((HD, 1), lambda i: (0, 0))
+    return pl.pallas_call(
+        kernel,
+        grid=(width // step,),
+        in_specs=[block, block, table, table, column] + [ANYWHERE] * len(after),
+        out_specs=[pl.BlockSpec((rows, step), lambda i: (0, i)), column],
+        out_shape=[
+            jax.ShapeDtypeStruct((rows, width), bf16),
+            jax.ShapeDtypeStruct((HD, 1), f32),
+        ],
+        compiler_params=pltpu.CompilerParams(vmem_limit_bytes=40 * 2**20),
+        cost_estimate=cost(1.6),
+    )(d_query, raw, cos_table, sin_table, gain, *after)
+
+
+def halo_parts(d_keys, d_values, rows, *after):
+    width, count = d_keys.shape
+    parts = count // rows - 1
+
+    def kernel(d_keys_ref, d_values_ref, *refs):
+        for at, ref in enumerate(refs[len(after) :]):
+            of = slice(at * rows, (at + 1) * rows)
+            ref[:width, :] = d_keys_ref[:, of].astype(bf16)
+            ref[width:, :] = d_values_ref[:, of].astype(bf16)
+
+    whole = pl.BlockSpec((width, count), lambda i: (0, 0))
+    return pl.pallas_call(
+        kernel,
+        grid=(1,),
+        in_specs=[whole, whole] + [ANYWHERE] * len(after),
+        out_specs=[pl.BlockSpec((2 * width, rows), lambda i: (0, 0))] * parts,
+        out_shape=[jax.ShapeDtypeStruct((2 * width, rows), bf16)] * parts,
+        compiler_params=pltpu.CompilerParams(vmem_limit_bytes=40 * 2**20),
+        cost_estimate=cost(1),
+    )(d_keys, d_values, *after)
+
+
+def key_back(d_keys, d_values, got, raw, first, cos_table, sin_table, gain, *after):
+    width, count = d_keys.shape
+    rows = got[0].shape[1]
+    own = pl.BlockSpec((width, rows), lambda i: (0, count // rows - 1))
+    heads = width // HD
+
+    def kernel(d_keys_ref, d_values_ref, raw_ref, cos_ref, sin_ref, gain_ref, *refs):
+        out_ref, gain_out_ref = refs[len(got) + len(after) :]
+        d_key = d_keys_ref[...]
+        d_value = d_values_ref[...]
+        for ref in refs[: len(got)]:
+            d_key = d_key + ref[:width, :].astype(f32)
+            d_value = d_value + ref[width:, :].astype(f32)
+        results = []
+        d_gain = jnp.zeros((HD, rows), f32)
+        for head in range(heads):
+            of = slice(head * HD, (head + 1) * HD)
+            result, by_token = turn_back(
+                d_key[of] * SCORE_SCALE, raw_ref[of, :], cos_ref[...], sin_ref[...], gain_ref[...]
+            )
+            results.append(result)
+            d_gain = d_gain + by_token
+        out_ref[...] = jnp.concatenate(results + [d_value], axis=0).astype(bf16).T
+        gain_out_ref[...] = jnp.sum(d_gain, axis=1, keepdims=True)
+
+    table = pl.BlockSpec((HD // 2, rows), lambda i: (0, 0))
+    column = pl.BlockSpec((HD, 1), lambda i: (0, 0))
+    return pl.pallas_call(
+        kernel,
+        grid=(1,),
+        in_specs=[
+            own,
+            own,
+            pl.BlockSpec((width, rows), lambda i: (first // width, 0)),
+            table,
+            table,
+            column,
+        ]
+        + [pl.BlockSpec((2 * width, rows), lambda i: (0, 0))] * len(got)
+        + [ANYWHERE] * len(after),
+        out_specs=[pl.BlockSpec((rows, 2 * width), lambda i: (0, 0)), column],
+        out_shape=[
+            jax.ShapeDtypeStruct((rows, 2 * width), bf16),
+            jax.ShapeDtypeStruct((HD, 1), f32),
+        ],
+        compiler_params=pltpu.CompilerParams(vmem_limit_bytes=40 * 2**20),
+        cost_estimate=cost(1.6),
+    )(d_keys, d_values, raw, cos_table, sin_table, gain, *got, *after)
+
+
+def input_back(d_query, d_keyval, weights, values, scale, *after):
+    rows, query_width = d_query.shape
+    qkv_width = query_width + d_keyval.shape[1]
+    width = weights.shape[0]
+    tile = math.gcd(width, 256)
+
+    def kernel(d_query_ref, d_keyval_ref, weights_ref, values_ref, scale_ref, *refs):
+        out_ref, gain_out_ref = refs[len(after) :]
+        part = nt_dot(d_query_ref[...], weights_ref[:, :query_width]) + nt_dot(
+            d_keyval_ref[...], weights_ref[:, query_width:]
+        )
+        out_ref[...] = part.astype(bf16)
+        product_sum = part * values_ref[...].astype(f32) * scale_ref[...]
+        gain_out_ref[...] = jnp.sum(product_sum, axis=0, keepdims=True)
+
+    out = pl.BlockSpec((rows, tile), lambda i: (0, i))
+    return pl.pallas_call(
+        kernel,
+        grid=(width // tile,),
+        in_specs=[
+            pl.BlockSpec((rows, query_width), lambda i: (0, 0)),
+            pl.BlockSpec((rows, qkv_width - query_width), lambda i: (0, 0)),
+            pl.BlockSpec((tile, qkv_width), lambda i: (i, 0)),
+            out,
+            pl.BlockSpec((rows, 1), lambda i: (0, 0)),
+        ]
+        + [ANYWHERE] * len(after),
+        out_specs=[out, pl.BlockSpec((1, tile), lambda i: (0, i))],
+        out_shape=[
+            jax.ShapeDtypeStruct((rows, width), bf16),
+            jax.ShapeDtypeStruct((1, width), f32),
+        ],
+        compiler_params=pltpu.CompilerParams(vmem_limit_bytes=40 * 2**20),
+        cost_estimate=cost(8),
+    )(d_query, d_keyval, weights, values, scale, *after)
+
+
+def gain_block(d_attn, d_ffn, d_query, d_key, places, *after):
+    width = d_attn.shape[1]
+
+    def kernel(d_attn_ref, d_ffn_ref, d_query_ref, d_key_ref, places_ref, *refs):
+        out_ref = refs[-1]
+        out_ref[...] = jnp.zeros_like(out_ref)
+        heads = jnp.sum(
+            d_query_ref[...] * places_ref[:HD, :].astype(f32)
+            + d_key_ref[...] * places_ref[HD:, :].astype(f32),
+            axis=0,
+            keepdims=True,
+        )
+        out_ref[0:1, :] = d_attn_ref[...].astype(bf16)
+        out_ref[1:2, :] = d_ffn_ref[...].astype(bf16)
+        out_ref[2:3, :] = heads.astype(bf16)
+
+    return pl.pallas_call(
+        kernel,
+        in_specs=[pl.BlockSpec(memory_space=pltpu.VMEM)] * 5 + [ANYWHERE] * len(after),
+        out_shape=jax.ShapeDtypeStruct((LANES, width), bf16),
+        cost_estimate=cost(1),
+    )(d_attn, d_ffn, d_query, d_key, places, *after)
+
+
+def side_by_side(first, second):
+    rows, columns = first.shape
+    step = math.gcd(rows, 32)
+
+    def kernel(first_ref, second_ref, out_ref):
+        out_ref[:, 0, :] = first_ref[...]
+        out_ref[:, 1, :] = second_ref[...]
+
+    return pl.pallas_call(
+        kernel,
+        grid=(rows // step,),
+        in_specs=[pl.BlockSpec((step, columns), lambda i: (i, 0))] * 2,
+        out_specs=pl.BlockSpec((step, 2, columns), lambda i: (i, 0, 0)),
+        out_shape=jax.ShapeDtypeStruct((rows, 2, columns), first.dtype),
+        cost_estimate=cost(4),
+    )(first, second)
 
 
 def attend_kernel(shift, q_ref, k_ref, v_ref, bias_ref, out_ref, inverse_ref):
@@ -148,7 +538,9 @@
             inverse_ref[0, head : head + 1, at] = inverse
 
 
-def attend_back_kernel(shift, q_ref, k_ref, kt_ref, v_ref, d_ref, o_ref, inverse_ref, bias_ref, dq_ref, dk_ref, dv_ref):
+def attend_back_kernel(shift, operands, *refs):
+    q_ref, k_ref, kt_ref, v_ref, d_ref, o_ref, inverse_ref, bias_ref = refs[:8]
+    dq_ref, dk_ref, dv_ref = refs[operands:]
     rows = q_ref.shape[1]
     dk_ref[...] = jnp.zeros_like(dk_ref)
     dv_ref[...] = jnp.zeros_like(dv_ref)
@@ -157,7 +549,8 @@
         deltas = []
         for head in range(GROUP):
             of = slice(head * HD, (head + 1) * HD)
-            deltas.append(jnp.sum(d_ref[of, at].astype(f32) * o_ref[of, at].astype(f32), axis=0, keepdims=True))
+            product = d_ref[of, at].astype(f32) * o_ref[of, at].astype(f32)
+            deltas.append(jnp.sum(product, axis=0, keepdims=True))
         d_query = [jnp.zeros((HD, TILE), f32) for _ in range(GROUP)]
         for start in range(first + shift, first + shift + WINDOW + TILE, TILE):
             near = slice(start, start + TILE)
@@ -168,7 +561,8 @@
                 query = q_ref[of, at]
                 d_out = d_ref[of, at]
                 scores = nn_dot(k_ref[0, near, :], query)
-                prob = jnp.exp2(scores * EXP2_SCALE + bias_ref[near, at]) * inverse_ref[0, head : head + 1, at]
+                weight = jnp.exp2(scores * EXP2_SCALE + bias_ref[near, at])
+                prob = weight * inverse_ref[0, head : head + 1, at]
                 d_prob = nn_dot(v_ref[0, near, :], d_out)
                 d_scores = (prob * (d_prob - deltas[head])).astype(bf16)
                 d_query[head] = d_query[head] + nn_dot(kt_ref[:, near], d_scores)
@@ -200,28 +594,128 @@
         ],
         out_shape=[jax.ShapeDtypeStruct((kv * GROUP * HD, rows), bf16), jax.ShapeDtypeStruct((kv, 8, rows), f32)],
         compiler_params=pltpu.CompilerParams(vmem_limit_bytes=40 * 2**20),
-        cost_estimate=pl.CostEstimate(flops=4 * kv * GROUP * HD * rows * (WINDOW + TILE), bytes_accessed=8 * 2**20, transcendentals=kv * GROUP * rows * (WINDOW + TILE)),
+        cost_estimate=cost(13),
     )(q_t, k, v_ones, bias)
 
 
-def attend_back(q_t, k, k_t, v, d_t, o_t, inverse, bias):
+def attend_back(at, so_far, after, q_t, k, k_t, v, d_t, o_t, inverse, bias):
     kv, keys, _ = k.shape
     rows = q_t.shape[1]
-    head_block = pl.BlockSpec((GROUP * HD, rows), lambda h: (h, 0))
-    key_block = pl.BlockSpec((1, keys, HD), lambda h: (h, 0, 0))
-    key_t_block = pl.BlockSpec((HD, keys), lambda h: (h, 0))
-    return pl.pallas_call(
-        functools.partial(attend_back_kernel, keys - rows - WINDOW),
-        grid=(kv,),
-        in_specs=[head_block, key_block, key_t_block, key_block, head_block, head_block,
-            pl.BlockSpec((1, 8, rows), lambda h: (h, 0, 0)),
-            pl.BlockSpec((keys, rows), lambda h: (0, 0)),
+    head_block = pl.BlockSpec((GROUP * HD, rows), lambda i: (at, 0))
+    key_block = pl.BlockSpec((1, keys, HD), lambda i: (at, 0, 0))
+    key_t_block = pl.BlockSpec((HD, keys), lambda i: (at, 0))
+    waits = [*so_far, *after]
+    operands = 8 + len(waits)
+    return pl.pallas_call(
+        functools.partial(attend_back_kernel, keys - rows - WINDOW, operands),
+        grid=(1,),
+        in_specs=[
+            head_block,
+            key_block,
+            key_t_block,
+            key_block,
+            head_block,
+            head_block,
+            pl.BlockSpec((1, 8, rows), lambda i: (at, 0, 0)),
+            pl.BlockSpec((keys, rows), lambda i: (0, 0)),
+        ]
+        + [pl.BlockSpec(memory_space=pl.ANY)] * len(waits),
+        out_specs=[head_block, key_t_block, key_t_block],
+        out_shape=[
+            jax.ShapeDtypeStruct((kv * GROUP * HD, rows), f32),
+            jax.ShapeDtypeStruct((kv * HD, keys), f32),
+            jax.ShapeDtypeStruct((kv * HD, keys), f32),
         ],
-        out_specs=[head_block, key_t_block, key_t_block],
-        out_shape=[jax.ShapeDtypeStruct((kv * GROUP * HD, rows), f32), jax.ShapeDtypeStruct((kv * HD, keys), f32), jax.ShapeDtypeStruct((kv * HD, keys), f32)],
+        input_output_aliases={8 + i: i for i in range(len(so_far))},
         compiler_params=pltpu.CompilerParams(vmem_limit_bytes=40 * 2**20),
-        cost_estimate=pl.CostEstimate(flops=10 * kv * GROUP * HD * rows * (WINDOW + TILE), bytes_accessed=12 * 2**20, transcendentals=kv * GROUP * rows * (WINDOW + TILE)),
-    )(q_t, k, k_t, v, d_t, o_t, inverse, bias)
+        cost_estimate=cost(11),
+    )(q_t, k, k_t, v, d_t, o_t, inverse, bias, *waits)
+
+
+def feed_kernel(n_ref, d_act_ref, gate_ref, up_ref, *refs):
+    act_ref, d_gate_ref, d_up_ref = refs[-3:]
+    normed = n_ref[...]
+    gate = nn_dot(normed, gate_ref[...])
+    up = nn_dot(normed, up_ref[...])
+    sigmoid = 1.0 / (1.0 + jnp.exp(-gate))
+    silu = gate * sigmoid
+    act_ref[...] = (silu * up).astype(bf16)
+    d_act = d_act_ref[...]
+    d_gate_ref[...] = (d_act * up * sigmoid * (1.0 + gate * (1.0 - sigmoid))).astype(bf16)
+    d_up_ref[...] = (d_act * silu).astype(bf16)
+
+
+def feed(normed, d_act, gateup, *after):
+    rows, width = normed.shape
+    hidden = d_act.shape[1]
+    tile = math.gcd(hidden, 512)
+    steps = hidden // tile
+    hidden_block = pl.BlockSpec((rows, tile), lambda i: (0, i))
+    return pl.pallas_call(
+        feed_kernel,
+        grid=(steps,),
+        in_specs=[
+            pl.BlockSpec((rows, width), lambda i: (0, 0)),
+            hidden_block,
+            pl.BlockSpec((width, tile), lambda i: (0, i)),
+            pl.BlockSpec((width, tile), lambda i: (0, i + steps)),
+        ]
+        + [ANYWHERE] * len(after),
+        out_specs=[hidden_block] * 3,
+        out_shape=[jax.ShapeDtypeStruct((rows, hidden), bf16)] * 3,
+        compiler_params=pltpu.CompilerParams(vmem_limit_bytes=56 * 2**20),
+        cost_estimate=cost(19.5),
+    )(normed, d_act, gateup, gateup, *after)
+
+
+def feed_back(d_gate, d_up, gateup, *after):
+    rows, hidden = d_gate.shape
+    width = gateup.shape[0]
+    tile = math.gcd(width, 256)
+
+    def kernel(d_gate_ref, d_up_ref, gate_ref, up_ref, *refs):
+        total = nt_dot(d_gate_ref[...], gate_ref[...]) + nt_dot(d_up_ref[...], up_ref[...])
+        refs[-1][...] = total.astype(bf16)
+
+    whole = pl.BlockSpec((rows, hidden), lambda i: (0, 0))
+    return pl.pallas_call(
+        kernel,
+        grid=(width // tile,),
+        in_specs=[
+            whole,
+            whole,
+            pl.BlockSpec((tile, hidden), lambda i: (i, 0)),
+            pl.BlockSpec((tile, hidden), lambda i: (i, 1)),
+        ]
+        + [ANYWHERE] * len(after),
+        out_specs=pl.BlockSpec((rows, tile), lambda i: (0, i)),
+        out_shape=jax.ShapeDtypeStruct((rows, width), bf16),
+        compiler_params=pltpu.CompilerParams(vmem_limit_bytes=56 * 2**20),
+        cost_estimate=cost(17),
+    )(d_gate, d_up, gateup, gateup, *after)
+
+
+def feed_out(act, downs, down_start, *after):
+    rows, hidden = act.shape
+    width, columns = downs.shape
+    tile = math.gcd(width, 256)
+
+    def kernel(act_ref, down_ref, *refs):
+        refs[-1][...] = nt_dot(act_ref[...], down_ref[:, down_start:]).astype(bf16)
+
+    return pl.pallas_call(
+        kernel,
+        grid=(width // tile,),
+        in_specs=[
+            pl.BlockSpec((rows, hidden), lambda i: (0, 0)),
+            pl.BlockSpec((tile, columns), lambda i: (i, 0)),
+        ]
+        + [ANYWHERE] * len(after),
+        out_specs=pl.BlockSpec((rows, tile), lambda i: (0, i)),
+        out_shape=jax.ShapeDtypeStruct((rows, width), bf16),
+        compiler_params=pltpu.CompilerParams(vmem_limit_bytes=56 * 2**20),
+        cost_estimate=cost(9),
+    )(act, downs, *after)
 
 
 def shards(
@@ -319,98 +813,98 @@
     mid_part = lax.dot_general(
         attended, out_full, (((0,), (1,)), ((), ())), preferred_element_type=f32
     )
-    mid = residual + tensor_sum(mid_part)
+    near_first = ring.bits
+    far_first = [1, 4, 2] + ring.bits[3:]
+    normed_rows = ring.chosen(normed_low, near_first)
+    cotangent_rows = ring.chosen(cotangent, far_first)
+    attended_back = attended.T
+    mid = residual + tensor_sum(
+        mid_part, corner(normed_rows), corner(cotangent_rows), corner(attended_back)
+    )
 
     d_act = nn_dot(cotangent, down_full)
     ffn_scale = inverse_rms(mid, 1)
     normed2_low = (mid * ffn_scale * ffn_weight).astype(bf16)
-    gate = nn_dot(normed2_low, gateup_full[:, :hidden])
-    up = nn_dot(normed2_low, gateup_full[:, hidden:])
-    gate_sigmoid = jax.nn.sigmoid(gate)
-    gate_silu = gate * gate_sigmoid
-    act_low = (gate_silu * up).astype(bf16)
-    d_gate = (d_act * up * gate_sigmoid * (1.0 + gate * (1.0 - gate_sigmoid))).astype(bf16)
-    d_up = (d_act * gate_silu).astype(bf16)
-    d_normed2 = tensor_sum(
-        nt_dot(d_gate, gateup_full[:, :hidden]) + nt_dot(d_up, gateup_full[:, hidden:])
-    )
-    grad_down = lax.psum_scatter(
-        tn_dot(cotangent, act_low).astype(bf16), "dp", scatter_dimension=0, tiled=True
-    )
-    grad_down = grad_down.astype(f32).T
-    normed2_rows = ring.rows(normed2_low.T)
-    pieces = []
-    piece_width = hidden // 2
-    for source in (d_gate, d_up):
-        for start in range(0, hidden, piece_width):
-            piece = source[:, start : start + piece_width]
-            pieces.append(ring.scatter(lambda part, piece=piece: nn_dot(normed2_rows[part], piece)))
-    grad_gateup = jnp.concatenate(pieces, axis=1).reshape(depth, 2, hidden)
-    result = mid + tensor_sum(nt_dot(act_low, down_full))
-    output = result.astype(bf16)
-    d_ffn_weight = jnp.sum(d_normed2 * mid * ffn_scale, axis=0)
-    d_mid = cotangent.astype(f32) + rms_back(mid, ffn_scale, ffn_weight, d_normed2, 1)
-
-    d_mid_low = d_mid.astype(bf16)
-    d_mid_rows = ring.rows(d_mid_low.T)
-    grad_out = ring.scatter(lambda part: nt_dot(d_mid_rows[part], attended)).T
-    d_attended = lax.dot_general(
-        out_full, d_mid_low, (((0,), (1,)), ((), ())), preferred_element_type=f32
-    ).astype(bf16)
-    d_query, d_keys, d_values = attend_back(
-        query_low, keys, keys_t, values, d_attended, attended, inverse_total, bias
-    )
-    d_keyval_all = jnp.concatenate([d_keys * SCORE_SCALE, d_values], axis=0)
-    own_grad = d_keyval_all[:, reach_count * row_count :]
-    for step_back in range(1, reach_count + 1):
-        piece_start = (reach_count - step_back) * row_count
-        piece = d_keyval_all[:, piece_start : piece_start + row_count].astype(bf16)
-        own_grad = own_grad + from_behind(piece, -step_back).astype(f32)
-
-    def head_back(raw, scale, gain, d_rotated):
-        d_normed_head = rotate(d_rotated, cos_table, -sin_table)
-        d_gain = jnp.sum(d_normed_head * raw * scale, axis=(0, 2))
-        return rms_back(raw, scale, gain, d_normed_head, 1), d_gain
-
-    d_query_raw, d_gain_query = head_back(
-        query_raw,
-        query_scale,
-        gain_query,
-        d_query.reshape(local_heads, HD, row_count) * SCORE_SCALE,
-    )
-    d_key_raw, d_gain_key = head_back(
-        key_raw, key_scale, gain_key, own_grad[:kv_width].reshape(local_kv, HD, row_count)
-    )
-    d_qkv_low = jnp.concatenate(
-        [
-            d_query_raw.reshape(query_width, row_count),
-            d_key_raw.reshape(kv_width, row_count),
-            own_grad[kv_width:],
-        ],
-        axis=0,
-    ).astype(bf16)
-    d_normed_part = lax.dot_general(
-        d_qkv_low, qkv_full, (((0,), (1,)), ((), ())), preferred_element_type=f32
-    )
-    d_normed = tensor_sum(d_normed_part)
-    d_attn_part = jnp.sum(d_normed_part * residual * attn_scale, axis=0)
-
-    head_rows = jnp.stack([d_gain_query, d_gain_key], axis=0).reshape(2, ring.count, gain_count // 2)
-    head_rows = head_rows.transpose(1, 0, 2).reshape(ring.count, gain_count)
-    head_column = jnp.pad(head_rows, ((0, 0), (0, depth - gain_count))).reshape(model)
-    gain_grads = jnp.stack([d_attn_part, d_ffn_weight, head_column], axis=1)
-    gain_grads = jnp.pad(gain_grads, ((0, 0), (0, LANES - gain_grads.shape[1])))
-    grad_qkv = lax.dot_general(
-        normed_low, d_qkv_low, (((0,), (1,)), ((), ())), preferred_element_type=f32
-    )
-    grad_qkv = lax.psum_scatter(
-        jnp.concatenate([grad_qkv, gain_grads], axis=1).astype(bf16),
-        "dp",
-        scatter_dimension=0,
-        tiled=True,
-    )
-    grad_query = grad_qkv[:, :query_width].astype(f32)
-    shared = grad_qkv[:, query_width:]
+    normed2_rows = ring.chosen(normed2_low, near_first)
+    act_low, d_gate, d_up = feed(normed2_low, d_act, gateup_full, normed2_rows)
+    gate_sum = Scatter(ring, normed2_rows, d_gate, near_first)
+    up_sum = Scatter(ring, normed2_rows, d_up, near_first)
+    down_sum = Scatter(ring, cotangent_rows, act_low, far_first)
+    before = gate_sum.send()
+    d_normed2_low = feed_back(d_gate, d_up, gateup_full, before)
+    d_normed2_other = other_tensor(d_normed2_low)
+    before = gate_sum.send(d_normed2_low)
+    before = up_sum.send(before)
+    before = down_sum.send(before)
+    result_low = feed_out(act_low, first_full, gain_start + LANES, before)
+    before = up_sum.send(result_low)
+    before = down_sum.send(before)
+    d_mid, d_mid_low, d_ffn_weight = norm_back(
+        mid, cotangent, d_normed2_low, d_normed2_other, ffn_weight, before
+    )
+    result_low = tie(result_low, d_normed2_other)
+    result_other = other_tensor(result_low)
+
+    d_attended = product_tt(first_full, qkv_width, query_width, d_mid_low)
+    grads = ()
+    for at in range(local_kv):
+        grads = attend_back(
+            at, grads, (), query_low, keys, keys_t, values, d_attended, attended, inverse_total, bias
+        )
+    d_query, d_keys, d_values = grads
+    parts = halo_parts(d_keys, d_values, row_count)
+    got = [from_behind(part, at - reach_count) for at, part in enumerate(parts)]
+    before = gate_sum.send(parts[0])
+    d_query_low, d_gain_query = query_back(
+        d_query, qkv_raw, cos_table[0], sin_table[0], gain_query, before
+    )
+    query_sum = Scatter(ring, normed_rows, d_query_low, near_first)
+    before = query_sum.send()
+    before = down_sum.send(before)
+    d_mid_rows = ring.chosen(tie(d_mid_low, before), near_first)
+    out_sum = Scatter(ring, d_mid_rows, attended_back, near_first)
+    before = out_sum.send()
+    d_keyval_low, d_gain_key = key_back(
+        d_keys, d_values, got, qkv_raw, query_width, cos_table[0], sin_table[0], gain_key, before
+    )
+    d_normed_low, d_attn_part = input_back(
+        d_query_low, d_keyval_low, first_full, tokens, attn_scale
+    )
+    d_normed_other = other_tensor(d_normed_low)
+    places = jnp.arange(2 * HD, dtype=jnp.int32)
+    per_device = gain_count // 2
+    places = places % HD // per_device * depth + places // HD * per_device + places % per_device
+    places = (places[:, None] == jnp.arange(model, dtype=jnp.int32)[None, :]).astype(bf16)
+    gain_grads = gain_block(d_attn_part, d_ffn_weight, d_gain_query, d_gain_key, places)
+    gain_rows = ring.chosen(gain_grads, near_first)
+    shared_sum = Scatter(ring, normed_rows, d_keyval_low, near_first, gain_rows)
+    before = shared_sum.send()
+    before = up_sum.send(before)
+    before = query_sum.send(before)
+    before = out_sum.send(before)
+    before = shared_sum.send(before)
+    before = gate_sum.send(before)
+    output = add_up(mid, result_low, result_other, before)
+    before = down_sum.send(output)
+    before = query_sum.send(before)
+    before = out_sum.send(before)
+    before = shared_sum.send(before)
+    before = up_sum.send(before)
+    before = query_sum.send(before)
+    before = out_sum.send(before)
+    before = shared_sum.send(before)
+    for rest in (down_sum, gate_sum, up_sum, query_sum, out_sum, shared_sum):
+        while len(rest.got) < len(rest.bits):
+            before = rest.send(before)
+    grad_down = down_sum.total(before, transposed=True)
+    gate_total = gate_sum.total(grad_down)
+    grad_query = query_sum.total(gate_total)
+    grad_out = out_sum.total(grad_query, transposed=True)
+    shared = shared_sum.total(grad_out).astype(bf16)
+    _, input_grad, _ = norm_back(
+        tokens, d_mid, d_normed_low, d_normed_other, attn_weight, shared
+    )
+    grad_gateup = side_by_side(gate_total, up_sum.total(input_grad))
     shared_other = other_tensor(shared).astype(f32)
     shared = shared.astype(f32)
     first = tensor == 0
@@ -428,7 +922,6 @@
     grad_attn_gain = gains_sum[:, 0]
     grad_ffn_gain = gains_mine[:, 1]
     grad_heads = gains_sum[:gain_count, 2].reshape(2, gain_count // 2)
-    input_grad = (d_mid + rms_back(residual, attn_scale, attn_weight, d_normed, 1)).astype(bf16)
     return (
         output,
         input_grad,

time: 910 us -> 685 us (0.75)
  Pallas kernels: 45.3 us -> 252 us
  waiting for transfers between devices: 430 us -> 231 us
  matrix products: 138 us -> 21.8 us
  local copies, waits for them, and re-layouts: 112 us -> 65.6 us
  other arithmetic: 60.5 us -> 18.2 us
  starting transfers between devices: 100 us -> 70 us
    pallas_call x0 -> x51, Pallas kernels: none -> 207 us  [the longest x30 91.1 us: product(): pl.pallas_call(kernel, grid=(all_columns // tile,), in_specs=in_specs + [...]
    ppermute x5, waiting for transfers between devices: 141 us -> 21.2 us  [other_tensor(): lax.ppermute(array, 'tensor', [(i, (i + 1) % count) for i in range(count)])]
    dot_general x9 -> x0, matrix products: 63.7 us -> none  [the longest x5 36.2 us: nt_dot(): lax.dot_general(left, right, (((1,), (1,)), ((), ())), preferred_element_...]
    ppermute x25 -> x24, waiting for transfers between devices: 153 us -> 93.5 us  [send(): self.got.append(lax.ppermute(sent, 'dp', pairs))]
    dot_general x11 -> x1, matrix products: 64.9 us -> 10.6 us  [nn_dot(): return jnp.dot(left, right, preferred_element_type=f32)]
    ppermute x25 -> x24, starting transfers between devices: 76.8 us -> 48.8 us  [send(): self.got.append(lax.ppermute(sent, 'dp', pairs))]
    unnamed x142 -> x208, local copies, waits for them, and re-layouts: 65.3 us -> 43.1 us
    dynamic_slice x6 -> x0, local copies, waits for them, and re-layouts: 15.1 us -> none  [pick(): return lax.dynamic_index_in_dim(array, bit, axis, keepdims=False)]
  transfers between devices with their start and end apart: 40 -> 37, of which waited for: 19 -> 15; matrix products, arithmetic and copies ran while one was open for 23% -> 9% of each run, Pallas kernels for 1% -> 32%
where the time goes in v4:
time: 685 us; the launch traced here: 675 us
  Pallas kernels  252 us (37%)
  waiting for transfers between devices  231 us (34%)
  starting transfers between devices  70 us (10%)
  local copies, waits for them, and re-layouts  65.6 us (10%)
  matrix products  21.8 us (3%)
  other arithmetic  18.2 us (3%)
  between operations  15.6 us (2%)
    ppermute x24, waiting for transfers between devices, send(): self.got.append(lax.ppermute(sent, 'dp', pairs))  93.5 us
    pallas_call x30, Pallas kernels, product(): pl.pallas_call(kernel, grid=(all_columns // tile,), in_specs=in_specs + [...  91.1 us
    all_gather x1, waiting for transfers between devices, shards(): lax.all_gather(first_pack.astype(bf16), 'dp', axis=0, tiled=True)  88 us
    ppermute x24, starting transfers between devices, send(): self.got.append(lax.ppermute(sent, 'dp', pairs))  48.8 us
    unnamed x208, local copies, waits for them, and re-layouts  43.1 us
    pallas_call x3, Pallas kernels, attend_back(): pl.pallas_call(functools.partial(attend_back_kernel, keys - rows - WINDOW...  32.2 us
    pallas_call x5, Pallas kernels, transposed_blocks(): pl.pallas_call(kernel, grid_spec=pltpu.PrefetchScalarGridSpec(num_scalar_...  22.1 us
    ppermute x5, waiting for transfers between devices, other_tensor(): lax.ppermute(array, 'tensor', [(i, (i + 1) % count) for i in range(count)])  21.2 us
  transfers between devices with their start and end apart: 37, of which 15 were waited for; matrix products, arithmetic and copies ran while one was open for 9% of the time, Pallas kernels for 32%

profile of v4, /device:TPU:0, one launch (start us, length us, event | category | flops | bytes accessed | tf_op | source)
XLA Modules:
  0.0 674.9 jit_solution(11736239934173734282)
XLA Ops:
  22.4 4.4 collective-permute-start.2
  29.2 2.4 fusion.16.bias_ref.refs_7_
  31.6 88.0 %all-gather.3.cloned.1.call-done.down_ref.left_ref.weights_ref = bf16[2048,4608]{1,0:T(8,128)(2,1)} async-done(((bf16[128,4608]{1,0:T(8,128)(2,1)}), bf16[2048,4608]{1,0:T(8,128)(2,1)}) %all-gather.3.cloned.1.call-update) | async-done | bytes 18874384 | tf_op jit(solution)/shard_map/all_gather | solution.py:756
  122.8 5.8 fusion.5.raw_ref
  131.3 3.9 collective-permute-start
  135.2 2.9 collective-permute-start.1
  142.5 10.1 %collective-permute-done = bf16[384,512]{1,0:T(8,128)(2,1)} collective-permute-done((bf16[384,512]{1,0:T(8,128)(2,1)}, bf16[384,512]{1,0:T(8,128)(2,1)}, u32[]{:S(2)}, u32[]{:S(2)}) %collective-permute-start) | collective-permute-done | bytes 393248 | tf_op jit(solution)/shard_map/ppermute | solution.py:137
  160.6 13.2 %shard_map.195 = (bf16[768,512]{1,0:T(8,128)(2,1)S(1)}, f32[3,8,512]{2,1,0:T(8,128)S(1)}) custom-call(bf16[768,512]{1,0:T(8,128)(2,1)S(1)} %bitcast.69, bf16[3,1536,64]{2,1,0:T(8,128)(2,1)S(1)} %bitcast.62, bf16[3,80,1536]{2,1,0:T(8,128)(2,1)S(1)} %concatenate.32.v_ref, f32[1536,512]{1,0:T(8,128)S(1)} %copy-done.58), custom_call_target="tpu_custom_call" | custom-call | flops 7474999808 | tf_op jit(solution)/shard_map/pallas_call | solution.py:582
  173.9 5.4 fusion.17
  180.7 4.9 shard_map.197.left_ref
  186.9 4.9 shard_map.196.left_ref
  193.1 10.6 %fusion.2.d_act_ref = f32[512,2560]{1,0:T(8,128)} fusion(bf16[512,2048]{1,0:T(8,128)(2,1)} %direct_ref.1, bf16[2048,4608]{1,0:T(8,128)(2,1)} %all-gather.3.cloned.1.call-done.down_ref.left_ref.weights_ref), kind=kOutput, calls=%fused_computation.5 | convolution fusion | flops 5368709120 | bytes 17825792 | tf_op jit(solution)/shard_map/dot_general | solution.py:149
  205.8 11.2 %collective-permute-done.4.refs_0_ = bf16[512,2048]{1,0:T(8,128)(2,1)} collective-permute-done((bf16[512,2048]{1,0:T(8,128)(2,1)}, bf16[512,2048]{1,0:T(8,128)(2,1)}, u32[]{:S(2)}, u32[]{:S(2)}) %collective-permute-start.4) | collective-permute-done | bytes 2097184 | tf_op jit(solution)/shard_map/ppermute | solution.py:123
  216.9 3.3 multiply_reduce_fusion
  223.8 4.8 shard_map.199.refs_0_.left_ref
  228.6 10.7 %all-gather.5.cloned.1.call-done.gate_ref.up_ref = bf16[2048,5120]{1,0:T(8,128)(2,1)} async-done(((bf16[128,5120]{1,0:T(8,128)(2,1)}), bf16[2048,5120]{1,0:T(8,128)(2,1)}) %all-gather.5.cloned.1.call-update) | async-done | bytes 20971536 | tf_op jit(solution)/shard_map/all_gather | solution.py:757
  239.3 19.7 %shard_map.200 = (bf16[512,2560]{1,0:T(8,128)(2,1)}, bf16[512,2560]{1,0:T(8,128)(2,1)}, bf16[512,2560]{1,0:T(8,128)(2,1)}) custom-call(bf16[512,2048]{1,0:T(8,128)(2,1)} %multiply_convert_fusion.in_ref.n_ref, f32[512,2560]{1,0:T(8,128)} %fusion.2.d_act_ref, bf16[2048,5120]{1,0:T(8,128)(2,1)} %all-gather.5.cloned.1.call-done.gate_ref.up_ref, ...), custom_call_target="tpu_custom_call" | custom-call | flops 11212499968 | tf_op jit(solution)/shard_map/pallas_call | solution.py:654
  260.7 5.3 shard_map.201.refs_0_
  266.8 17.9 %shard_map.202.refs_1_.part_ref = bf16[512,2048]{1,0:T(8,128)(2,1)} custom-call(bf16[512,2560]{1,0:T(8,128)(2,1)} %get-tuple-element.39.right_ref.d_gate_ref, bf16[512,2560]{1,0:T(8,128)(2,1)} %get-tuple-element.38.d_up_ref.right_ref, bf16[2048,5120]{1,0:T(8,128)(2,1)} %all-gather.5.cloned.1.call-done.gate_ref.up_ref, ...), custom_call_target="tpu_custom_call" | custom-call | flops 9774999552 | tf_op jit(solution)/shard_map/pallas_call | solution.py:681
  284.8 4.5 shard_map.203.refs_0_
  289.3 5.4 shard_map.204.refs_0_
  294.7 5.3 shard_map.205.refs_0_
  308.9 12.5 %collective-permute-start.8 = (bf16[512,2560]{1,0:T(8,128)(2,1)}, bf16[512,2560]{1,0:T(8,128)(2,1)}, u32[]{:S(2)}, u32[]{:S(2)}) collective-permute-start(bf16[512,2560]{1,0:T(8,128)(2,1)} %copy-done.45), channel_id=1, source_target_pairs={{0,4},{2,6},{4,0},{6,2},{8,12},{10,14},{12,8},{14,10},{16,20},{18,... | collective-permute-start | bytes 7864328 | tf_op jit(solution)/shard_map/ppermute | solution.py:112
  321.4 13.4 %shard_map.206.refs_0_.refs_1_ = bf16[512,2048]{1,0:T(8,128)(2,1)} custom-call(bf16[512,2560]{1,0:T(8,128)(2,1)} %get-tuple-element.37.right_ref.act_ref, bf16[2048,4608]{1,0:T(8,128)(2,1)} %all-gather.3.cloned.1.call-done.down_ref.left_ref.weights_ref, bf16[1024,2560]{1,0:T(8,128)(2,1)} %shard_map.205.refs_0_), custom_call_target="tpu_custom_call" | custom-call | flops 5175000064 | tf_op jit(solution)/shard_map/pallas_call | solution.py:706
  334.8 5.4 shard_map.208.refs_1_
  340.4 5.4 shard_map.209.refs_0_
  345.8 2.6 collective-permute-done.6.refs_1_.other_ref
  348.4 6.9 %shard_map.210 = (f32[512,2048]{1,0:T(8,128)}, bf16[512,2048]{1,0:T(8,128)(2,1)S(1)}, f32[1,2048]{1,0:T(1,128)S(1)}) custom-call(f32[512,2048]{1,0:T(8,128)} %copy-done.89, bf16[512,2048]{1,0:T(8,128)(2,1)S(1)} %copy-done.82, bf16[512,2048]{1,0:T(8,128)(2,1)} %shard_map.202.refs_1_.part_ref, bf16[512,2048]{1,0:T(8,128)(2,1)} %collective-permute-done.6.refs_1_.other_ref, ...), custom_call_target="tpu_custom_call" | custom-call | flops 4024999936 | tf_op jit(solution)/shard_map/pallas_call | solution.py:288
  355.4 4.4 shard_map.211.refs_4_
  360.1 10.7 %shard_map.212 = (f32[768,512]{1,0:T(8,128)S(1)}, f32[192,1536]{1,0:T(8,128)S(1)}, f32[192,1536]{1,0:T(8,128)S(1)}) custom-call(bf16[768,512]{1,0:T(8,128)(2,1)S(1)} %bitcast.70, bf16[3,1536,64]{2,1,0:T(8,128)(2,1)S(1)} %bitcast.63, bf16[192,1536]{1,0:T(8,128)(2,1)S(1)} %get-tuple-element.92.refs_2_, bf16[3,1536,64]{2,1,0:T(8,128)(2,1)S(1)} %bitcast.66, ...), custom_call_target="tpu_custom_call" | custom-call | flops 6325000192 | tf_op jit(solution)/shard_map/pallas_call | solution.py:609
  370.8 10.9 %shard_map.213 = (f32[768,512]{1,0:T(8,128)S(1)}, f32[192,1536]{1,0:T(8,128)S(1)}, f32[192,1536]{1,0:T(8,128)S(1)}) custom-call(bf16[768,512]{1,0:T(8,128)(2,1)S(1)} %bitcast.71, bf16[3,1536,64]{2,1,0:T(8,128)(2,1)S(1)} %bitcast.64, bf16[192,1536]{1,0:T(8,128)(2,1)S(1)} %get-tuple-element.92.refs_2_, ...), custom_call_target="tpu_custom_call", output_to_operand_aliasing={{0}: (8, {}), {1}: (9, {}), {2}: (10, {})} | custom-call | flops 6325000192 | tf_op jit(solution)/shard_map/pallas_call | solution.py:609
  381.7 10.7 %shard_map.214 = (f32[768,512]{1,0:T(8,128)S(1)}, f32[192,1536]{1,0:T(8,128)S(1)}, f32[192,1536]{1,0:T(8,128)S(1)}) custom-call(bf16[768,512]{1,0:T(8,128)(2,1)S(1)} %bitcast.72, bf16[3,1536,64]{2,1,0:T(8,128)(2,1)S(1)} %bitcast.65, bf16[192,1536]{1,0:T(8,128)(2,1)S(1)} %get-tuple-element.92.refs_2_, ...), custom_call_target="tpu_custom_call", output_to_operand_aliasing={{0}: (8, {}), {1}: (9, {}), {2}: (10, {})} | custom-call | flops 6325000192 | tf_op jit(solution)/shard_map/pallas_call | solution.py:609
  396.0 3.7 shard_map.216.refs_0_
  399.8 15.9 %collective-permute-start.11 = (bf16[256,2560]{1,0:T(8,128)(2,1)}, bf16[256,2560]{1,0:T(8,128)(2,1)}, u32[]{:S(2)}, u32[]{:S(2)}) collective-permute-start(bf16[256,2560]{1,0:T(8,128)(2,1)} %shard_map.216.refs_0_), channel_id=1, source_target_pairs={{0,8},{2,10},{4,12},{6,14},{8,0},{10,2},{12,4},{14,6},{16,24},{18,... | collective-permute-start | bytes 3932168 | tf_op jit(solution)/shard_map/ppermute | solution.py:112
  420.3 2.4 shard_map.218.refs_2_
  423.5 3.3 shard_map.219.refs_1_
  426.8 4.8 shard_map.221.left_ref
  433.2 2.4 shard_map.222.refs_2_
  435.6 7.9 %collective-permute-done.12.refs_0_ = bf16[384,512]{1,0:T(8,128)(2,1)} collective-permute-done((bf16[384,512]{1,0:T(8,128)(2,1)S(1)}, bf16[384,512]{1,0:T(8,128)(2,1)}, u32[]{:S(2)}, u32[]{:S(2)}) %collective-permute-start.12) | collective-permute-done | bytes 393248 | tf_op jit(solution)/shard_map/ppermute | solution.py:137
  444.2 3.7 collective-permute-start.16
  449.5 8.1 %shard_map.224 = (bf16[512,2048]{1,0:T(8,128)(2,1)}, f32[1,2048]{1,0:T(1,128)S(1)}) custom-call(bf16[512,768]{1,0:T(8,128)(2,1)S(1)} %copy-done.38, bf16[512,384]{1,0:T(8,128)(2,1)S(1)} %get-tuple-element.54.d_keyval_ref.right_ref, bf16[2048,4608]{1,0:T(8,128)(2,1)} %all-gather.3.cloned.1.call-done.down_ref.left_ref.weights_ref, ...), custom_call_target="tpu_custom_call" | custom-call | flops 4600000000 | tf_op jit(solution)/shard_map/pallas_call | solution.py:460
  460.4 2.7 shard_map.226.refs_0_.refs_1_.refs_2_.refs_3_.refs_4_
  467.6 3.5 shard_map.228.refs_1_
  471.2 2.7 shard_map.229.refs_1_
  475.7 2.6 shard_map.230.refs_2_
  483.6 7.4 %collective-permute-done.7.other_ref = bf16[512,2048]{1,0:T(8,128)(2,1)} collective-permute-done((bf16[512,2048]{1,0:T(8,128)(2,1)}, bf16[512,2048]{1,0:T(8,128)(2,1)}, u32[]{:S(2)}, u32[]{:S(2)}) %collective-permute-start.7) | collective-permute-done | bytes 2097184 | tf_op jit(solution)/shard_map/ppermute | solution.py:123
  491.7 5.3 shard_map.233.refs_3_
  497.0 2.5 collective-permute-done.23.refs_2_
  504.5 3.0 shard_map.234.refs_2_
  507.5 8.8 %collective-permute-done.22.refs_1_ = bf16[512,768]{1,0:T(8,128)(2,1)} collective-permute-done((bf16[512,768]{1,0:T(8,128)(2,1)}, bf16[512,768]{1,0:T(8,128)(2,1)}, u32[]{:S(2)}, u32[]{:S(2)}) %collective-permute-start.22) | collective-permute-done | bytes 786464 | tf_op jit(solution)/shard_map/ppermute | solution.py:112
  518.6 14.6 %collective-permute-done.21.refs_1_ = bf16[512,768]{1,0:T(8,128)(2,1)} collective-permute-done((bf16[512,768]{1,0:T(8,128)(2,1)}, bf16[512,768]{1,0:T(8,128)(2,1)}, u32[]{:S(2)}, u32[]{:S(2)}) %collective-permute-start.21) | collective-permute-done | bytes 786464 | tf_op jit(solution)/shard_map/ppermute | solution.py:112
  535.5 3.4 collective-permute-start.25
  538.8 5.2 collective-permute-done.20.refs_1_
  547.8 2.5 shard_map.237.refs_3_
  550.4 3.4 collective-permute-start.24
  553.8 3.0 shard_map.238.refs_3_
  562.4 14.4 %collective-permute-done.24.refs_2_ = bf16[256,512]{1,0:T(8,128)(2,1)S(1)} collective-permute-done((bf16[256,512]{1,0:T(8,128)(2,1)S(1)}, bf16[256,512]{1,0:T(8,128)(2,1)S(1)}, u32[]{:S(2)}, u32[]{:S(2)}) %collective-permute-start.24) | collective-permute-done | bytes 262176 | tf_op jit(solution)/shard_map/ppermute | solution.py:112
  576.8 3.8 collective-permute-start.34
  582.9 3.5 shard_map.242.refs_4_
  586.5 28.7 %collective-permute-done.31.refs_3_ = bf16[128,2560]{1,0:T(8,128)(2,1)} collective-permute-done((bf16[128,2560]{1,0:T(8,128)(2,1)}, bf16[128,2560]{1,0:T(8,128)(2,1)}, u32[]{:S(2)}, u32[]{:S(2)}) %collective-permute-start.31) | collective-permute-done | bytes 655392 | tf_op jit(solution)/shard_map/ppermute | solution.py:112
  618.8 3.3 collective-permute-done.30.refs_3_
  624.5 16.0 %collective-permute-done.29.refs_3_ = bf16[128,768]{1,0:T(8,128)(2,1)} collective-permute-done((bf16[128,768]{1,0:T(8,128)(2,1)S(1)}, bf16[128,768]{1,0:T(8,128)(2,1)}, u32[]{:S(2)}, u32[]{:S(2)}) %collective-permute-start.29) | collective-permute-done | bytes 196640 | tf_op jit(solution)/shard_map/ppermute | solution.py:112
  648.4 7.6 %shard_map.247 = (f32[512,2048]{1,0:T(8,128)}, bf16[512,2048]{1,0:T(8,128)(2,1)}, f32[1,2048]{1,0:T(1,128)}) custom-call(bf16[512,2048]{1,0:T(8,128)(2,1)S(1)} %copy-done.32, f32[512,2048]{1,0:T(8,128)} %get-tuple-element.59.direct_ref, bf16[512,2048]{1,0:T(8,128)(2,1)} %get-tuple-element.60.part_ref, bf16[512,2048]{1,0:T(8,128)(2,1)} %collective-permute-done.19.other_ref, ...), custom_call_target="tpu_custom_call" | custom-call | flops 4024999936 | tf_op jit(solution)/shard_map/pallas_call | solution.py:288
  661.0 4.1 shard_map.249
  (354 shorter events, 127.5 us)
Async XLA Ops:
  7.2 112.4 %all-gather.3.cloned.1.call-start = ((), (), s32[]{:S(2)}) async-start(), calls=%async_computation | async-start | bytes 20054016 | tf_op jit(solution)/shard_map/all_gather | solution.py:756
  17.8 221.5 %all-gather.5.cloned.1.call-start = ((), (), s32[]{:S(2)}) async-start(), calls=%async_computation.1 | async-start | bytes 22282240 | tf_op jit(solution)/shard_map/all_gather | solution.py:757
  18.8 9.4 %copy-start.96 = (s32[512]{0:T(512)S(1)}, s32[512]{0:T(512)}, u32[]{:S(2)}) copy-start(s32[512]{0:T(512)} %param.22) | copy-start | bytes 6148
  18.8 9.4 %copy-start.30 = (bf16[512,2048]{1,0:T(8,128)(2,1)S(1)}, bf16[512,2048]{1,0:T(8,128)(2,1)}, u32[]{:S(2)}) copy-start(bf16[512,2048]{1,0:T(8,128)(2,1)} %values_ref.3) | copy-start | bytes 6291460
  20.1 9.0 %collective-permute-start.3 = (bf16[512]{0:T(512)(128)(2,1)S(1)}, bf16[512]{0:T(512)(128)(2,1)S(1)}, u32[]{:S(2)}, u32[]{:S(2)}) collective-permute-start(bf16[512]{0:T(512)(128)(2,1)S(1)} %add_convert_fusion.2), channel_id=1, source_target_pairs={{0,2},{2,4},{4,6},{6,8},{8,10},{10,12},{12,14},{14,16},{16,18},{18... | collective-permute-start | bytes 3080 | tf_op jit(solution)/shard_map/ppermute | solution.py:137
  22.4 6.7 collective-permute-start.2
  28.7 93.5 %copy-start.94 = (f32[512]{0:T(512)}, f32[512]{0:T(512)S(1)}, u32[]{:S(2)}) copy-start(f32[512]{0:T(512)S(1)} %add_rsqrt_fusion.3) | copy-start | bytes 6148
  29.0 113.2 %copy-start.63 = (f32[32,512]{1,0:T(8,128)}, f32[32,512]{1,0:T(8,128)S(1)}, u32[]{:S(2)}) copy-start(f32[32,512]{1,0:T(8,128)S(1)} %get-tuple-element.100.sin_ref) | copy-start | bytes 196612
  131.3 21.4 %collective-permute-start = (bf16[384,512]{1,0:T(8,128)(2,1)}, bf16[384,512]{1,0:T(8,128)(2,1)}, u32[]{:S(2)}, u32[]{:S(2)}) collective-permute-start(bf16[384,512]{1,0:T(8,128)(2,1)} %pad_maximum_fusion.1), channel_id=1, source_target_pairs={{0,4},{2,6},{4,8},{6,10},{8,12},{10,14},{12,16},{14,18},{16,20},{1... | collective-permute-start | bytes 1179656 | tf_op jit(solution)/shard_map/ppermute | solution.py:137
  135.2 17.4 %collective-permute-start.1 = (bf16[384,512]{1,0:T(8,128)(2,1)}, bf16[384,512]{1,0:T(8,128)(2,1)}, u32[]{:S(2)}, u32[]{:S(2)}) collective-permute-start(bf16[384,512]{1,0:T(8,128)(2,1)} %pad_maximum_fusion.1), channel_id=1, source_target_pairs={{0,2},{2,4},{4,6},{6,8},{8,10},{10,12},{12,14},{14,16},{16,18},{18... | collective-permute-start | bytes 1179656 | tf_op jit(solution)/shard_map/ppermute | solution.py:137
  142.5 14.8 %copy-start.74 = (bf16[12,64,512]{2,1,0:T(8,128)(2,1)}, bf16[12,64,512]{2,1,0:T(8,128)(2,1)S(1)}, u32[]{:S(2)}) copy-start(bf16[12,64,512]{2,1,0:T(8,128)(2,1)S(1)} %pad_maximum_fusion) | copy-start | bytes 2359300
  179.3 37.6 %collective-permute-start.4 = (bf16[512,2048]{1,0:T(8,128)(2,1)}, bf16[512,2048]{1,0:T(8,128)(2,1)}, u32[]{:S(2)}, u32[]{:S(2)}) collective-permute-start(bf16[512,2048]{1,0:T(8,128)(2,1)} %fusion.17), channel_id=1, source_target_pairs={{0,1},{1,0},{2,3},{3,2},{4,5},{5,4},{6,7},{7,6},{8,9},{9,8},{10,11... | collective-permute-start | bytes 6291464 | tf_op jit(solution)/shard_map/ppermute | solution.py:123
  228.6 30.3 %copy-start = (bf16[2048,512]{1,0:T(8,128)(2,1)S(1)}, bf16[2048,512]{1,0:T(8,128)(2,1)}, u32[]{:S(2)}) copy-start(bf16[2048,512]{1,0:T(8,128)(2,1)} %shard_map.199.refs_0_.left_ref) | copy-start | bytes 6291460
  266.0 18.7 %collective-permute-start.5 = (bf16[1024,2560]{1,0:T(8,128)(2,1)}, bf16[1024,2560]{1,0:T(8,128)(2,1)}, u32[]{:S(2)}, u32[]{:S(2)}) collective-permute-start(bf16[1024,2560]{1,0:T(8,128)(2,1)} %shard_map.201.refs_0_), channel_id=1, source_target_pairs={{0,2},{2,0},{4,6},{6,4},{8,10},{10,8},{12,14},{14,12},{16,18},{18,... | collective-permute-start | bytes 15728648 | tf_op jit(solution)/shard_map/ppermute | solution.py:112
  266.8 17.9 %copy-start.17 = (bf16[512,2560]{1,0:T(8,128)(2,1)S(1)}, bf16[512,2560]{1,0:T(8,128)(2,1)}, u32[]{:S(2)}) copy-start(bf16[512,2560]{1,0:T(8,128)(2,1)} %get-tuple-element.39.right_ref.d_gate_ref) | copy-start | bytes 7864324
  294.7 40.1 %collective-permute-start.10 = (bf16[1024,2560]{1,0:T(8,128)(2,1)}, bf16[1024,2560]{1,0:T(8,128)(2,1)}, u32[]{:S(2)}, u32[]{:S(2)}) collective-permute-start(bf16[1024,2560]{1,0:T(8,128)(2,1)} %shard_map.204.refs_0_), channel_id=1, source_target_pairs={{0,2},{2,0},{4,6},{6,4},{8,10},{10,8},{12,14},{14,12},{16,18},{18,... | collective-permute-start | bytes 15728648 | tf_op jit(solution)/shard_map/ppermute | solution.py:112
  300.1 40.3 %collective-permute-start.9 = (bf16[1024,2560]{1,0:T(8,128)(2,1)}, bf16[1024,2560]{1,0:T(8,128)(2,1)}, u32[]{:S(2)}, u32[]{:S(2)}) collective-permute-start(bf16[1024,2560]{1,0:T(8,128)(2,1)} %shard_map.205.refs_0_), channel_id=1, source_target_pairs={{0,2},{2,0},{4,6},{6,4},{8,10},{10,8},{12,14},{14,12},{16,18},{18,... | collective-permute-start | bytes 15728648 | tf_op jit(solution)/shard_map/ppermute | solution.py:112
  300.6 47.9 %collective-permute-start.6 = (bf16[512,2048]{1,0:T(8,128)(2,1)}, bf16[512,2048]{1,0:T(8,128)(2,1)}, u32[]{:S(2)}, u32[]{:S(2)}) collective-permute-start(bf16[512,2048]{1,0:T(8,128)(2,1)} %shard_map.202.refs_1_.part_ref), channel_id=1, source_target_pairs={{0,1},{1,0},{2,3},{3,2},{4,5},{5,4},{6,7},{7,6},{8,9},{9,8},{10,11... | collective-permute-start | bytes 6291464 | tf_op jit(solution)/shard_map/ppermute | solution.py:123
  308.9 25.9 %copy-start.8 = (bf16[512,2560]{1,0:T(8,128)(2,1)S(1)}, bf16[512,2560]{1,0:T(8,128)(2,1)}, u32[]{:S(2)}) copy-start(bf16[512,2560]{1,0:T(8,128)(2,1)} %get-tuple-element.38.d_up_ref.right_ref) | copy-start | bytes 7864324
  308.9 87.1 %collective-permute-start.8 = (bf16[512,2560]{1,0:T(8,128)(2,1)}, bf16[512,2560]{1,0:T(8,128)(2,1)}, u32[]{:S(2)}, u32[]{:S(2)}) collective-permute-start(bf16[512,2560]{1,0:T(8,128)(2,1)} %copy-done.45), channel_id=1, source_target_pairs={{0,4},{2,6},{4,0},{6,2},{8,12},{10,14},{12,8},{14,10},{16,20},{18,... | collective-permute-start | bytes 7864328 | tf_op jit(solution)/shard_map/ppermute | solution.py:112
  340.2 8.2 %copy-start.82 = (bf16[512,2048]{1,0:T(8,128)(2,1)S(1)}, bf16[512,2048]{1,0:T(8,128)(2,1)}, u32[]{:S(2)}) copy-start(bf16[512,2048]{1,0:T(8,128)(2,1)} %direct_ref.1) | copy-start | bytes 6291460
  340.2 127.3 %collective-permute-start.18 = (bf16[512,2560]{1,0:T(8,128)(2,1)}, bf16[512,2560]{1,0:T(8,128)(2,1)}, u32[]{:S(2)}, u32[]{:S(2)}) collective-permute-start(bf16[512,2560]{1,0:T(8,128)(2,1)} %shard_map.208.refs_1_), channel_id=1, source_target_pairs={{0,4},{2,6},{4,0},{6,2},{8,12},{10,14},{12,8},{14,10},{16,20},{18,... | collective-permute-start | bytes 7864328 | tf_op jit(solution)/shard_map/ppermute | solution.py:112
  345.8 76.9 %collective-permute-start.14 = (bf16[512,2560]{1,0:T(8,128)(2,1)}, bf16[512,2560]{1,0:T(8,128)(2,1)}, u32[]{:S(2)}, u32[]{:S(2)}) collective-permute-start(bf16[512,2560]{1,0:T(8,128)(2,1)} %shard_map.209.refs_0_), channel_id=1, source_target_pairs={{0,8},{2,10},{4,12},{6,14},{8,0},{10,2},{12,4},{14,6},{16,24},{18,... | collective-permute-start | bytes 7864328 | tf_op jit(solution)/shard_map/ppermute | solution.py:112
  381.7 14.3 %copy-start.18 = (bf16[512,2560]{1,0:T(8,128)(2,1)S(1)}, bf16[512,2560]{1,0:T(8,128)(2,1)}, u32[]{:S(2)}) copy-start(bf16[512,2560]{1,0:T(8,128)(2,1)} %get-tuple-element.39.right_ref.d_gate_ref) | copy-start | bytes 7864324
  393.4 50.1 %collective-permute-start.12 = (bf16[384,512]{1,0:T(8,128)(2,1)S(1)}, bf16[384,512]{1,0:T(8,128)(2,1)}, u32[]{:S(2)}, u32[]{:S(2)}) collective-permute-start(bf16[384,512]{1,0:T(8,128)(2,1)S(1)} %get-tuple-element.50.refs_2_), channel_id=1, source_target_pairs={{4,0},{6,2},{8,4},{10,6},{12,8},{14,10},{16,12},{18,14},{20,16},{2... | collective-permute-start | bytes 1179656 | tf_op jit(solution)/shard_map/ppermute | solution.py:137
  394.7 49.5 %collective-permute-start.13 = (bf16[384,512]{1,0:T(8,128)(2,1)}, bf16[384,512]{1,0:T(8,128)(2,1)}, u32[]{:S(2)}, u32[]{:S(2)}) collective-permute-start(bf16[384,512]{1,0:T(8,128)(2,1)} %get-tuple-element.51), channel_id=1, source_target_pairs={{2,0},{4,2},{6,4},{8,6},{10,8},{12,10},{14,12},{16,14},{18,16},{20... | collective-permute-start | bytes 1179656 | tf_op jit(solution)/shard_map/ppermute | solution.py:137
  399.7 15.9 %copy-start.64 = (f32[32,512]{1,0:T(8,128)S(1)}, f32[32,512]{1,0:T(8,128)}, u32[]{:S(2)}) copy-start(f32[32,512]{1,0:T(8,128)} %copy-done.63) | copy-start | bytes 196612
  399.8 15.9 %copy-start.79 = (f32[64,1]{1,0:T(8,128)S(1)}, f32[64,1]{1,0:T(8,128)}, u32[]{:S(2)}) copy-start(f32[64,1]{1,0:T(8,128)} %broadcast_in_dim_squeeze.19.gain_ref) | copy-start | bytes 772
  399.8 67.7 %collective-permute-start.11 = (bf16[256,2560]{1,0:T(8,128)(2,1)}, bf16[256,2560]{1,0:T(8,128)(2,1)}, u32[]{:S(2)}, u32[]{:S(2)}) collective-permute-start(bf16[256,2560]{1,0:T(8,128)(2,1)} %shard_map.216.refs_0_), channel_id=1, source_target_pairs={{0,8},{2,10},{4,12},{6,14},{8,0},{10,2},{12,4},{14,6},{16,24},{18,... | collective-permute-start | bytes 3932168 | tf_op jit(solution)/shard_map/ppermute | solution.py:112
  422.7 48.4 %collective-permute-start.17 = (bf16[1024,768]{1,0:T(8,128)(2,1)}, bf16[1024,768]{1,0:T(8,128)(2,1)}, u32[]{:S(2)}, u32[]{:S(2)}) collective-permute-start(bf16[1024,768]{1,0:T(8,128)(2,1)} %shard_map.218.refs_2_), channel_id=1, source_target_pairs={{0,2},{2,0},{4,6},{6,4},{8,10},{10,8},{12,14},{14,12},{16,18},{18,... | collective-permute-start | bytes 4718600 | tf_op jit(solution)/shard_map/ppermute | solution.py:112
  433.2 14.7 %copy-start.36 = (f32[1152,512]{1,0:T(8,128)S(1)}, f32[1152,512]{1,0:T(8,128)}, u32[]{:S(2)}) copy-start(f32[1152,512]{1,0:T(8,128)} %copy-done.33) | copy-start | bytes 7077892
  433.2 14.7 %copy-start.55 = (f32[192,1536]{1,0:T(8,128)S(1)}, f32[192,1536]{1,0:T(8,128)}, u32[]{:S(2)}) copy-start(f32[192,1536]{1,0:T(8,128)} %copy-done.54) | copy-start | bytes 3538948
  433.2 14.7 %copy-start.57 = (f32[192,1536]{1,0:T(8,128)S(1)}, f32[192,1536]{1,0:T(8,128)}, u32[]{:S(2)}) copy-start(f32[192,1536]{1,0:T(8,128)} %copy-done.56) | copy-start | bytes 3538948
  433.2 14.7 %copy-start.78 = (f32[64,1]{1,0:T(8,128)S(1)}, f32[64,1]{1,0:T(8,128)}, u32[]{:S(2)}) copy-start(f32[64,1]{1,0:T(8,128)} %broadcast_in_dim_squeeze.18.gain_ref) | copy-start | bytes 772
  435.6 13.9 %copy-start.31 = (bf16[512,2048]{1,0:T(8,128)(2,1)S(1)}, bf16[512,2048]{1,0:T(8,128)(2,1)}, u32[]{:S(2)}) copy-start(bf16[512,2048]{1,0:T(8,128)(2,1)} %values_ref.3) | copy-start | bytes 6291460
  435.6 13.9 %copy-start.38 = (bf16[512,768]{1,0:T(8,128)(2,1)S(1)}, bf16[512,768]{1,0:T(8,128)(2,1)}, u32[]{:S(2)}) copy-start(bf16[512,768]{1,0:T(8,128)(2,1)} %copy-done.37) | copy-start | bytes 2359300
  435.6 13.9 %copy-start.73 = (f32[512,1]{1,0:T(8,128)S(1)}, f32[512,1]{1,0:T(8,128)}, u32[]{:S(2)}) copy-start(f32[512,1]{1,0:T(8,128)} %copy.88.scale_ref) | copy-start | bytes 6148
  443.5 47.5 %collective-permute-start.7 = (bf16[512,2048]{1,0:T(8,128)(2,1)}, bf16[512,2048]{1,0:T(8,128)(2,1)}, u32[]{:S(2)}, u32[]{:S(2)}) collective-permute-start(bf16[512,2048]{1,0:T(8,128)(2,1)} %shard_map.207.part_ref), channel_id=1, source_target_pairs={{0,1},{1,0},{2,3},{3,2},{4,5},{5,4},{6,7},{7,6},{8,9},{9,8},{10,11... | collective-permute-start | bytes 6291464 | tf_op jit(solution)/shard_map/ppermute | solution.py:123
  444.2 29.7 %collective-permute-start.16 = (bf16[1024,768]{1,0:T(8,128)(2,1)}, bf16[1024,768]{1,0:T(8,128)(2,1)}, u32[]{:S(2)}, u32[]{:S(2)}) collective-permute-start(bf16[1024,768]{1,0:T(8,128)(2,1)} %shard_map.222.refs_2_), channel_id=1, source_target_pairs={{0,2},{2,0},{4,6},{6,4},{8,10},{10,8},{12,14},{14,12},{16,18},{18,... | collective-permute-start | bytes 4718600 | tf_op jit(solution)/shard_map/ppermute | solution.py:112
  467.4 10.9 %collective-permute-start.15 = (bf16[1024,512]{1,0:T(8,128)(2,1)S(1)}, bf16[1024,512]{1,0:T(8,128)(2,1)S(1)}, u32[]{:S(2)}, u32[]{:S(2)}) collective-permute-start(bf16[1024,512]{1,0:T(8,128)(2,1)S(1)} %shard_map.227.refs_2_), channel_id=1, source_target_pairs={{0,2},{2,0},{4,6},{6,4},{8,10},{10,8},{12,14},{14,12},{16,18},{18,... | collective-permute-start | bytes 3145736 | tf_op jit(solution)/shard_map/ppermute | solution.py:112
  467.5 32.0 %collective-permute-start.23 = (bf16[256,2560]{1,0:T(8,128)(2,1)}, bf16[256,2560]{1,0:T(8,128)(2,1)}, u32[]{:S(2)}, u32[]{:S(2)}) collective-permute-start(bf16[256,2560]{1,0:T(8,128)(2,1)} %shard_map.219.refs_1_), channel_id=1, source_target_pairs={{0,4},{2,6},{4,0},{6,2},{8,12},{10,14},{12,8},{14,10},{16,20},{18,... | collective-permute-start | bytes 3932168 | tf_op jit(solution)/shard_map/ppermute | solution.py:112
  471.1 64.4 %collective-permute-start.27 = (bf16[256,2560]{1,0:T(8,128)(2,1)}, bf16[256,2560]{1,0:T(8,128)(2,1)}, u32[]{:S(2)}, u32[]{:S(2)}) collective-permute-start(bf16[256,2560]{1,0:T(8,128)(2,1)} %shard_map.228.refs_1_), channel_id=1, source_target_pairs={{0,8},{2,10},{4,12},{6,14},{8,0},{10,2},{12,4},{14,6},{16,24},{18,... | collective-permute-start | bytes 3932168 | tf_op jit(solution)/shard_map/ppermute | solution.py:112
  473.9 42.4 %collective-permute-start.22 = (bf16[512,768]{1,0:T(8,128)(2,1)}, bf16[512,768]{1,0:T(8,128)(2,1)}, u32[]{:S(2)}, u32[]{:S(2)}) collective-permute-start(bf16[512,768]{1,0:T(8,128)(2,1)} %shard_map.229.refs_1_), channel_id=1, source_target_pairs={{0,4},{2,6},{4,0},{6,2},{8,12},{10,14},{12,8},{14,10},{16,20},{18,... | collective-permute-start | bytes 2359304 | tf_op jit(solution)/shard_map/ppermute | solution.py:112
  478.3 54.9 %collective-permute-start.21 = (bf16[512,768]{1,0:T(8,128)(2,1)}, bf16[512,768]{1,0:T(8,128)(2,1)}, u32[]{:S(2)}, u32[]{:S(2)}) collective-permute-start(bf16[512,768]{1,0:T(8,128)(2,1)} %shard_map.230.refs_2_), channel_id=1, source_target_pairs={{0,4},{2,6},{4,0},{6,2},{8,12},{10,14},{12,8},{14,10},{16,20},{18,... | collective-permute-start | bytes 2359304 | tf_op jit(solution)/shard_map/ppermute | solution.py:112
  491.1 157.3 %collective-permute-start.19 = (bf16[512,2048]{1,0:T(8,128)(2,1)}, bf16[512,2048]{1,0:T(8,128)(2,1)}, u32[]{:S(2)}, u32[]{:S(2)}) collective-permute-start(bf16[512,2048]{1,0:T(8,128)(2,1)} %get-tuple-element.60.part_ref), channel_id=1, source_target_pairs={{0,1},{1,0},{2,3},{3,2},{4,5},{5,4},{6,7},{7,6},{8,9},{9,8},{10,11... | collective-permute-start | bytes 6291464 | tf_op jit(solution)/shard_map/ppermute | solution.py:123
  497.0 19.3 %copy-start.4 = (bf16[2048,512]{1,0:T(8,128)(2,1)S(1)}, bf16[2048,512]{1,0:T(8,128)(2,1)}, u32[]{:S(2)}) copy-start(bf16[2048,512]{1,0:T(8,128)(2,1)} %shard_map.196.left_ref) | copy-start | bytes 6291460
  499.5 44.5 %collective-permute-start.20 = (bf16[512,512]{1,0:T(8,128)(2,1)}, bf16[512,512]{1,0:T(8,128)(2,1)}, u32[]{:S(2)}, u32[]{:S(2)}) collective-permute-start(bf16[512,512]{1,0:T(8,128)(2,1)} %copy-done.62), channel_id=1, source_target_pairs={{0,4},{2,6},{4,0},{6,2},{8,12},{10,14},{12,8},{14,10},{16,20},{18,... | collective-permute-start | bytes 1572872 | tf_op jit(solution)/shard_map/ppermute | solution.py:112
  504.5 11.9 %copy-start.40 = (bf16[512,768]{1,0:T(8,128)(2,1)S(1)}, bf16[512,768]{1,0:T(8,128)(2,1)}, u32[]{:S(2)}) copy-start(bf16[512,768]{1,0:T(8,128)(2,1)} %copy-done.37) | copy-start | bytes 2359300
  507.5 25.7 %copy-start.28 = (bf16[2048,512]{1,0:T(8,128)(2,1)S(1)}, bf16[2048,512]{1,0:T(8,128)(2,1)}, u32[]{:S(2)}) copy-start(bf16[2048,512]{1,0:T(8,128)(2,1)} %shard_map.221.left_ref) | copy-start | bytes 6291460
  518.6 31.8 %collective-permute-start.26 = (bf16[256,768]{1,0:T(8,128)(2,1)}, bf16[256,768]{1,0:T(8,128)(2,1)}, u32[]{:S(2)}, u32[]{:S(2)}) collective-permute-start(bf16[256,768]{1,0:T(8,128)(2,1)} %shard_map.235.refs_2_), channel_id=1, source_target_pairs={{0,8},{2,10},{4,12},{6,14},{8,0},{10,2},{12,4},{14,6},{16,24},{18,... | collective-permute-start | bytes 1179656 | tf_op jit(solution)/shard_map/ppermute | solution.py:112
  533.2 49.6 %collective-permute-start.32 = (bf16[128,2560]{1,0:T(8,128)(2,1)}, bf16[128,2560]{1,0:T(8,128)(2,1)}, u32[]{:S(2)}, u32[]{:S(2)}) collective-permute-start(bf16[128,2560]{1,0:T(8,128)(2,1)} %shard_map.234.refs_2_), channel_id=1, source_target_pairs={{0,16},{2,18},{4,20},{6,22},{8,24},{10,26},{12,28},{14,30},{16,0},... | collective-permute-start | bytes 1966088 | tf_op jit(solution)/shard_map/ppermute | solution.py:112
  535.5 23.6 %collective-permute-start.25 = (bf16[256,768]{1,0:T(8,128)(2,1)}, bf16[256,768]{1,0:T(8,128)(2,1)}, u32[]{:S(2)}, u32[]{:S(2)}) collective-permute-start(bf16[256,768]{1,0:T(8,128)(2,1)} %shard_map.236.refs_3_), channel_id=1, source_target_pairs={{0,8},{2,10},{4,12},{6,14},{8,0},{10,2},{12,4},{14,6},{16,24},{18,... | collective-permute-start | bytes 1179656 | tf_op jit(solution)/shard_map/ppermute | solution.py:112
  544.0 71.2 %collective-permute-start.31 = (bf16[128,2560]{1,0:T(8,128)(2,1)}, bf16[128,2560]{1,0:T(8,128)(2,1)}, u32[]{:S(2)}, u32[]{:S(2)}) collective-permute-start(bf16[128,2560]{1,0:T(8,128)(2,1)} %copy-done.60), channel_id=1, source_target_pairs={{0,16},{2,18},{4,20},{6,22},{8,24},{10,26},{12,28},{14,30},{16,0},... | collective-permute-start | bytes 1966088 | tf_op jit(solution)/shard_map/ppermute | solution.py:112
  550.4 26.4 %collective-permute-start.24 = (bf16[256,512]{1,0:T(8,128)(2,1)S(1)}, bf16[256,512]{1,0:T(8,128)(2,1)S(1)}, u32[]{:S(2)}, u32[]{:S(2)}) collective-permute-start(bf16[256,512]{1,0:T(8,128)(2,1)S(1)} %shard_map.237.refs_3_), channel_id=1, source_target_pairs={{0,8},{2,10},{4,12},{6,14},{8,0},{10,2},{12,4},{14,6},{16,24},{18,... | collective-permute-start | bytes 786440 | tf_op jit(solution)/shard_map/ppermute | solution.py:112
  559.0 21.5 %copy-start.44 = (bf16[1024,512]{1,0:T(8,128)(2,1)S(1)}, bf16[1024,512]{1,0:T(8,128)(2,1)}, u32[]{:S(2)}) copy-start(bf16[1024,512]{1,0:T(8,128)(2,1)} %copy-done.42) | copy-start | bytes 3145732
  559.0 21.5 %copy-start.49 = (bf16[2048,128]{1,0:T(8,128)(2,1)S(1)}, bf16[2048,128]{1,0:T(8,128)(2,1)}, u32[]{:S(2)}) copy-start(bf16[2048,128]{1,0:T(8,128)(2,1)} %shard_map.226.refs_0_.refs_1_.refs_2_.refs_3_.refs_4_) | copy-start | bytes 1572868
  559.0 63.1 %collective-permute-start.30 = (bf16[128,768]{1,0:T(8,128)(2,1)}, bf16[128,768]{1,0:T(8,128)(2,1)}, u32[]{:S(2)}, u32[]{:S(2)}) collective-permute-start(bf16[128,768]{1,0:T(8,128)(2,1)} %shard_map.239.refs_3_), channel_id=1, source_target_pairs={{0,16},{2,18},{4,20},{6,22},{8,24},{10,26},{12,28},{14,30},{16,0},... | collective-permute-start | bytes 589832 | tf_op jit(solution)/shard_map/ppermute | solution.py:112
  562.4 20.6 %copy-start.15 = (bf16[512,2560]{1,0:T(8,128)(2,1)S(1)}, bf16[512,2560]{1,0:T(8,128)(2,1)}, u32[]{:S(2)}) copy-start(bf16[512,2560]{1,0:T(8,128)(2,1)} %get-tuple-element.37.right_ref.act_ref) | copy-start | bytes 7864324
  562.4 20.5 %copy-start.25 = (bf16[2048,512]{1,0:T(8,128)(2,1)S(1)}, bf16[2048,512]{1,0:T(8,128)(2,1)}, u32[]{:S(2)}) copy-start(bf16[2048,512]{1,0:T(8,128)(2,1)} %shard_map.197.left_ref) | copy-start | bytes 6291460
  576.8 79.2 %collective-permute-start.34 = (bf16[128,2560]{1,0:T(8,128)(2,1)}, bf16[128,2560]{1,0:T(8,128)(2,1)}, u32[]{:S(2)}, u32[]{:S(2)}) collective-permute-start(bf16[128,2560]{1,0:T(8,128)(2,1)} %shard_map.238.refs_3_), channel_id=1, source_target_pairs={{0,16},{2,18},{4,20},{6,22},{8,24},{10,26},{12,28},{14,30},{16,0},... | collective-permute-start | bytes 1966088 | tf_op jit(solution)/shard_map/ppermute | solution.py:112
  582.8 32.3 %copy-start.20 = (bf16[512,2560]{1,0:T(8,128)(2,1)S(1)}, bf16[512,2560]{1,0:T(8,128)(2,1)}, u32[]{:S(2)}) copy-start(bf16[512,2560]{1,0:T(8,128)(2,1)} %get-tuple-element.39.right_ref.d_gate_ref) | copy-start | bytes 7864324
  582.8 57.6 %collective-permute-start.29 = (bf16[128,768]{1,0:T(8,128)(2,1)S(1)}, bf16[128,768]{1,0:T(8,128)(2,1)}, u32[]{:S(2)}, u32[]{:S(2)}) collective-permute-start(bf16[128,768]{1,0:T(8,128)(2,1)S(1)} %shard_map.240.refs_4_), channel_id=1, source_target_pairs={{0,16},{2,18},{4,20},{6,22},{8,24},{10,26},{12,28},{14,30},{16,0},... | collective-permute-start | bytes 589832 | tf_op jit(solution)/shard_map/ppermute | solution.py:112
  615.2 28.6 %collective-permute-start.28 = (bf16[128,512]{1,0:T(8,128)(2,1)S(1)}, bf16[128,512]{1,0:T(8,128)(2,1)S(1)}, u32[]{:S(2)}, u32[]{:S(2)}) collective-permute-start(bf16[128,512]{1,0:T(8,128)(2,1)S(1)} %shard_map.241.refs_4_), channel_id=1, source_target_pairs={{0,16},{2,18},{4,20},{6,22},{8,24},{10,26},{12,28},{14,30},{16,0},... | collective-permute-start | bytes 393224 | tf_op jit(solution)/shard_map/ppermute | solution.py:112
  647.1 18.0 %collective-permute-start.33 = (bf16[128,512]{1,0:T(8,128)(2,1)S(1)}, bf16[128,512]{1,0:T(8,128)(2,1)S(1)}, u32[]{:S(2)}, u32[]{:S(2)}) collective-permute-start(bf16[128,512]{1,0:T(8,128)(2,1)S(1)} %get-tuple-element.86.refs_0_), channel_id=1, source_target_pairs={{0,1},{1,0},{2,3},{3,2},{4,5},{5,4},{6,7},{7,6},{8,9},{9,8},{10,11... | collective-permute-start | bytes 393224 | tf_op jit(solution)/shard_map/ppermute | solution.py:123
  (73 other events, 254.4 us)
Sparse Core Ops, SparseCore 0:
  17.9 101.6 all-gather.2
  121.8 117.4 all-gather.4

commit v5 on v4

--- a/solution.py
+++ b/solution.py
@@ -23,7 +23,14 @@
 EXP2_SCALE = SCORE_SCALE * math.log2(math.e)
 TILE = 256
 SUM_ROWS = 16
-LINK_SHARE = 0.5
+PARTS = 4
+ORDER = (
+    "D", "G", "FB", "U", "G", "FO", "U", "NB", "DA", "H", "H", "G",
+    "H", "HP", "QB", "Q", "OP", "O", "G", "Q", "O", "KB", "U", "IB",
+    "G", "Q", "O", "GB", "K", "K", "U", "Q", "O", "K", "IG", "K",
+    "AD", "D", "U", "Q", "O", "K",
+)
+LINK_SHARE = 0.35
 
 bf16 = jnp.bfloat16
 f32 = jnp.float32
@@ -99,23 +106,31 @@
         last = step == len(self.bits)
         size = self.left.shape[0] >> (step if last else step + 1)
         start = self.left.shape[0] - (self.left.shape[0] >> step)
-        starts = [self.left.shape[0] - (self.left.shape[0] >> at + 1) for at in range(step)]
-        return size, start // size, [(start - first) // size for first in starts]
-
-    def send(self, *after):
-        size, block, blocks = self.rows()
+        adds = []
+        for at, parts in enumerate(self.got):
+            first = start - self.left.shape[0] + (self.left.shape[0] >> at + 1)
+            height = parts[0].shape[0]
+            if height >= size:
+                adds.append([(parts[first // height], first % height // size)])
+            else:
+                adds.append([(part, 0) for part in parts[first // height : (first + size) // height]])
+        return size, start // size, adds
+
+    def send(self, *after, parts=1):
+        size, block, adds = self.rows()
         sent = product(
-            self.left, self.right, size, block, list(zip(self.got, blocks)), after, self.tail
+            self.left, self.right, size, block, adds, after, self.tail, parts=parts
         )
         bit = self.bits[len(self.got)]
         pairs = [(i, i ^ bit) for i in range(self.ring.count)]
-        self.got.append(lax.ppermute(sent, "dp", pairs))
-        return sent
+        self.got.append([lax.ppermute(part, "dp", pairs) for part in sent])
+        return sent[0]
 
     def total(self, *after, transposed=False):
-        size, block, blocks = self.rows()
-        got = list(zip(self.got, blocks))
-        return product(self.left, self.right, size, block, got, after, self.tail, f32, transposed)
+        while len(self.got) < len(self.bits):
+            after = (self.send(*after),)
+        size, block, adds = self.rows()
+        return product(self.left, self.right, size, block, adds, after, self.tail, f32, transposed)[0]
 
 
 def other_tensor(array):
@@ -165,6 +180,23 @@
 
 def corner(array):
     return array[: 2 * 8, :LANES]
+
+
+def transposed(array, *after):
+    tokens, width = array.shape
+    step = math.gcd(tokens, LANES)
+
+    def kernel(in_ref, *refs):
+        refs[-1][...] = in_ref[...].T
+
+    return pl.pallas_call(
+        kernel,
+        grid=(tokens // step,),
+        in_specs=[pl.BlockSpec((step, width), lambda i: (i, 0))] + [ANYWHERE] * len(after),
+        out_specs=pl.BlockSpec((width, step), lambda i: (0, i)),
+        out_shape=jax.ShapeDtypeStruct((width, tokens), array.dtype),
+        cost_estimate=cost(4.8),
+    )(array, *after)
 
 
 def transposed_blocks(order, array, depth):
@@ -189,19 +221,28 @@
     )(order, array)
 
 
-def product(left, right, size, block, adds, after=(), tail=None, out_type=bf16, transposed=False):
+def product(
+    left, right, size, block, adds, after=(), tail=None, out_type=bf16, transposed=False, parts=1
+):
     depth, columns = right.shape
     most = max(LANES, min(columns, 512 * 1024 // size))
     tile = max(t for t in range(LANES, most + 1, LANES) if columns % t == 0)
     if tail is not None:
         tile = LANES
     steps = columns // tile
+    flat = [(array, row, size // len(add)) for add in adds for array, row in add]
 
     def kernel(left_ref, right_ref, *refs):
         def put(total):
-            for ref in refs[: len(adds)]:
-                total = total + ref[...].astype(f32)
-            refs[-1][...] = (total.T if transposed else total).astype(out_type)
+            at = 0
+            for add in adds:
+                pieces = [ref[...].astype(f32) for ref in refs[at : at + len(add)]]
+                total = total + (pieces[0] if len(add) == 1 else jnp.concatenate(pieces, axis=0))
+                at += len(add)
+            total = (total.T if transposed else total).astype(out_type)
+            height = total.shape[0] // parts
+            for at, ref in enumerate(refs[len(refs) - parts :]):
+                ref[...] = total[at * height : (at + 1) * height]
 
         if tail is None:
             put(nn_dot(left_ref[...], right_ref[...]))
@@ -213,30 +254,31 @@
 
         @pl.when(pl.program_id(0) == steps)
         def _():
-            put(refs[len(adds)][...].astype(f32))
+            put(refs[len(flat)][...].astype(f32))
 
     all_columns = columns
     in_specs = [
         pl.BlockSpec((size, depth), lambda i: (block, 0)),
         pl.BlockSpec((depth, tile), lambda i: (0, jnp.minimum(i, steps - 1))),
     ] + [
-        pl.BlockSpec((size, tile), functools.partial(lambda i, row: (row, i), row=row))
-        for _, row in adds
+        pl.BlockSpec((height, tile), functools.partial(lambda i, row: (row, i), row=row))
+        for _, row, height in flat
     ]
-    operands = [left, right, *[array for array, _ in adds]]
+    operands = [left, right, *[array for array, _, _ in flat]]
     if tail is not None:
         all_columns += LANES
         in_specs.append(pl.BlockSpec((size, LANES), lambda i: (block, 0)))
         operands.append(tail)
-    out_shape, out_block, out_map = (size, all_columns), (size, tile), lambda i: (0, i)
+    height = size // parts
+    out_shape, out_block, out_map = (height, all_columns), (height, tile), lambda i: (0, i)
     if transposed:
-        out_shape, out_block, out_map = (all_columns, size), (tile, size), lambda i: (i, 0)
+        out_shape, out_block, out_map = (all_columns, height), (tile, height), lambda i: (i, 0)
     return pl.pallas_call(
         kernel,
         grid=(all_columns // tile,),
         in_specs=in_specs + [ANYWHERE] * len(after),
-        out_specs=pl.BlockSpec(out_block, out_map),
-        out_shape=jax.ShapeDtypeStruct(out_shape, out_type),
+        out_specs=[pl.BlockSpec(out_block, out_map)] * parts,
+        out_shape=[jax.ShapeDtypeStruct(out_shape, out_type)] * parts,
         compiler_params=pltpu.CompilerParams(vmem_limit_bytes=40 * 2**20),
         cost_estimate=cost(2 + 2 * size * depth * columns / 0.9e9),
     )(*operands, *after)
@@ -500,6 +542,53 @@
         out_shape=jax.ShapeDtypeStruct((LANES, width), bf16),
         cost_estimate=cost(1),
     )(d_attn, d_ffn, d_query, d_key, places, *after)
+
+
+def turned(array, *after):
+    rows, columns = array.shape
+    tile = math.gcd(columns, 512)
+
+    def kernel(in_ref, *refs):
+        refs[-1][...] = in_ref[...].astype(f32).T
+
+    return pl.pallas_call(
+        kernel,
+        grid=(columns // tile,),
+        in_specs=[pl.BlockSpec((rows, tile), lambda i: (0, i))] + [ANYWHERE] * len(after),
+        out_specs=pl.BlockSpec((tile, rows), lambda i: (i, 0)),
+        out_shape=jax.ShapeDtypeStruct((columns, rows), f32),
+        cost_estimate=cost(2),
+    )(array, *after)
+
+
+def both_tensors(mine, theirs, tensor, width):
+    rows = mine.shape[0]
+
+    def kernel(tensor_ref, mine_ref, theirs_ref, out_ref, gains_ref):
+        own = mine_ref[...].astype(f32)
+        other = theirs_ref[...].astype(f32)
+        first = tensor_ref[0] == 0
+        low = jnp.where(first, own, other)
+        high = jnp.where(first, other, own)
+        out_ref[...] = jnp.concatenate(
+            [low[:, :width], high[:, :width], low[:, width : 2 * width], high[:, width : 2 * width]],
+            axis=1,
+        )
+        column = lax.broadcasted_iota(jnp.int32, (rows, LANES), 1)
+        own_gains = own[:, 2 * width :]
+        gains = own_gains + jnp.where(column == 1, 0.0, other[:, 2 * width :])
+        gains_ref[...] = gains.T[:8, :]
+
+    return pl.pallas_call(
+        kernel,
+        in_specs=[pl.BlockSpec(memory_space=pltpu.SMEM)]
+        + [pl.BlockSpec(memory_space=pltpu.VMEM)] * 2,
+        out_shape=[
+            jax.ShapeDtypeStruct((rows, 4 * width), f32),
+            jax.ShapeDtypeStruct((8, rows), f32),
+        ],
+        cost_estimate=cost(2),
+    )(tensor.reshape(1).astype(jnp.int32), mine, theirs)
 
 
 def side_by_side(first, second):
@@ -697,25 +786,31 @@
 
 def feed_out(act, downs, down_start, *after):
     rows, hidden = act.shape
-    width, columns = downs.shape
+    width = downs.shape[0]
     tile = math.gcd(width, 256)
-
-    def kernel(act_ref, down_ref, *refs):
-        refs[-1][...] = nt_dot(act_ref[...], down_ref[:, down_start:]).astype(bf16)
+    step = math.gcd(math.gcd(hidden, down_start), 512)
+    count = hidden // step
+
+    def kernel(act_ref, *refs):
+        total = jnp.zeros((rows, tile), f32)
+        for at, ref in enumerate(refs[:count]):
+            total = total + nt_dot(act_ref[:, at * step : (at + 1) * step], ref[...])
+        refs[-1][...] = total.astype(bf16)
 
     return pl.pallas_call(
         kernel,
         grid=(width // tile,),
-        in_specs=[
-            pl.BlockSpec((rows, hidden), lambda i: (0, 0)),
-            pl.BlockSpec((tile, columns), lambda i: (i, 0)),
+        in_specs=[pl.BlockSpec((rows, hidden), lambda i: (0, 0))]
+        + [
+            pl.BlockSpec((tile, step), functools.partial(lambda i, at: (i, at), at=at))
+            for at in range(down_start // step, down_start // step + count)
         ]
         + [ANYWHERE] * len(after),
         out_specs=pl.BlockSpec((rows, tile), lambda i: (0, i)),
         out_shape=jax.ShapeDtypeStruct((rows, width), bf16),
         compiler_params=pltpu.CompilerParams(vmem_limit_bytes=56 * 2**20),
         cost_estimate=cost(9),
-    )(act, downs, *after)
+    )(act, *[downs] * count, *after)
 
 
 def shards(
@@ -814,9 +909,8 @@
         attended, out_full, (((0,), (1,)), ((), ())), preferred_element_type=f32
     )
     near_first = ring.bits
-    far_first = [1, 4, 2] + ring.bits[3:]
     normed_rows = ring.chosen(normed_low, near_first)
-    cotangent_rows = ring.chosen(cotangent, far_first)
+    cotangent_rows = transposed(cotangent)
     attended_back = attended.T
     mid = residual + tensor_sum(
         mid_part, corner(normed_rows), corner(cotangent_rows), corner(attended_back)
@@ -829,99 +923,119 @@
     act_low, d_gate, d_up = feed(normed2_low, d_act, gateup_full, normed2_rows)
     gate_sum = Scatter(ring, normed2_rows, d_gate, near_first)
     up_sum = Scatter(ring, normed2_rows, d_up, near_first)
-    down_sum = Scatter(ring, cotangent_rows, act_low, far_first)
-    before = gate_sum.send()
-    d_normed2_low = feed_back(d_gate, d_up, gateup_full, before)
-    d_normed2_other = other_tensor(d_normed2_low)
-    before = gate_sum.send(d_normed2_low)
-    before = up_sum.send(before)
-    before = down_sum.send(before)
-    result_low = feed_out(act_low, first_full, gain_start + LANES, before)
-    before = up_sum.send(result_low)
-    before = down_sum.send(before)
-    d_mid, d_mid_low, d_ffn_weight = norm_back(
-        mid, cotangent, d_normed2_low, d_normed2_other, ffn_weight, before
-    )
-    result_low = tie(result_low, d_normed2_other)
-    result_other = other_tensor(result_low)
-
-    d_attended = product_tt(first_full, qkv_width, query_width, d_mid_low)
+    sums = {"G": gate_sum, "U": up_sum}
+    totals = {}
+    heads = 0
     grads = ()
-    for at in range(local_kv):
-        grads = attend_back(
-            at, grads, (), query_low, keys, keys_t, values, d_attended, attended, inverse_total, bias
-        )
-    d_query, d_keys, d_values = grads
-    parts = halo_parts(d_keys, d_values, row_count)
-    got = [from_behind(part, at - reach_count) for at, part in enumerate(parts)]
-    before = gate_sum.send(parts[0])
-    d_query_low, d_gain_query = query_back(
-        d_query, qkv_raw, cos_table[0], sin_table[0], gain_query, before
-    )
-    query_sum = Scatter(ring, normed_rows, d_query_low, near_first)
-    before = query_sum.send()
-    before = down_sum.send(before)
-    d_mid_rows = ring.chosen(tie(d_mid_low, before), near_first)
-    out_sum = Scatter(ring, d_mid_rows, attended_back, near_first)
-    before = out_sum.send()
-    d_keyval_low, d_gain_key = key_back(
-        d_keys, d_values, got, qkv_raw, query_width, cos_table[0], sin_table[0], gain_key, before
-    )
-    d_normed_low, d_attn_part = input_back(
-        d_query_low, d_keyval_low, first_full, tokens, attn_scale
-    )
-    d_normed_other = other_tensor(d_normed_low)
-    places = jnp.arange(2 * HD, dtype=jnp.int32)
-    per_device = gain_count // 2
-    places = places % HD // per_device * depth + places // HD * per_device + places % per_device
-    places = (places[:, None] == jnp.arange(model, dtype=jnp.int32)[None, :]).astype(bf16)
-    gain_grads = gain_block(d_attn_part, d_ffn_weight, d_gain_query, d_gain_key, places)
-    gain_rows = ring.chosen(gain_grads, near_first)
-    shared_sum = Scatter(ring, normed_rows, d_keyval_low, near_first, gain_rows)
-    before = shared_sum.send()
-    before = up_sum.send(before)
-    before = query_sum.send(before)
-    before = out_sum.send(before)
-    before = shared_sum.send(before)
-    before = gate_sum.send(before)
-    output = add_up(mid, result_low, result_other, before)
-    before = down_sum.send(output)
-    before = query_sum.send(before)
-    before = out_sum.send(before)
-    before = shared_sum.send(before)
-    before = up_sum.send(before)
-    before = query_sum.send(before)
-    before = out_sum.send(before)
-    before = shared_sum.send(before)
-    for rest in (down_sum, gate_sum, up_sum, query_sum, out_sum, shared_sum):
-        while len(rest.got) < len(rest.bits):
-            before = rest.send(before)
-    grad_down = down_sum.total(before, transposed=True)
-    gate_total = gate_sum.total(grad_down)
-    grad_query = query_sum.total(gate_total)
-    grad_out = out_sum.total(grad_query, transposed=True)
-    shared = shared_sum.total(grad_out).astype(bf16)
-    _, input_grad, _ = norm_back(
-        tokens, d_mid, d_normed_low, d_normed_other, attn_weight, shared
-    )
-    grad_gateup = side_by_side(gate_total, up_sum.total(input_grad))
-    shared_other = other_tensor(shared).astype(f32)
-    shared = shared.astype(f32)
-    first = tensor == 0
-    keyval_mine = shared[:, : 2 * kv_width].reshape(depth, 2, 1, kv_width)
-    keyval_theirs = shared_other[:, : 2 * kv_width].reshape(depth, 2, 1, kv_width)
-    grad_keyval = jnp.concatenate(
-        [
-            jnp.where(first, keyval_mine, keyval_theirs),
-            jnp.where(first, keyval_theirs, keyval_mine),
-        ],
-        axis=2,
-    ).reshape(depth, 2 * all_kv)
-    gains_mine = shared[:, 2 * kv_width :]
-    gains_sum = gains_mine + shared_other[:, 2 * kv_width :]
-    grad_attn_gain = gains_sum[:, 0]
-    grad_ffn_gain = gains_mine[:, 1]
-    grad_heads = gains_sum[:gain_count, 2].reshape(2, gain_count // 2)
+    down_low = None
+    before = None
+    for step in ORDER:
+        after = () if before is None else (before,)
+        if step in sums:
+            one = sums[step]
+            if len(one.got) < len(one.bits) and step not in totals:
+                before = one.send(*after, parts=PARTS if step in "OQK" and not one.got else 1)
+                if len(one.got) == 4:
+                    while len(one.got) < len(one.bits):
+                        before = one.send(before)
+            else:
+                before = totals[step] = one.total(*after, transposed=step == "O")
+        elif step == "D":
+            if down_low is None:
+                before = product(cotangent_rows, act_low, model, 0, [], after)[0]
+                down_low = lax.psum_scatter(before, "dp", scatter_dimension=0, tiled=True)
+            else:
+                before = totals["D"] = turned(down_low, *after)
+        elif step == "FB":
+            before = d_normed2_low = feed_back(d_gate, d_up, gateup_full, *after)
+            d_normed2_other = other_tensor(d_normed2_low)
+        elif step == "FO":
+            before = result_low = feed_out(act_low, first_full, gain_start + LANES, *after)
+        elif step == "NB":
+            d_mid, d_mid_low, d_ffn_weight = norm_back(
+                mid, cotangent, d_normed2_low, d_normed2_other, ffn_weight, *after
+            )
+            before = d_mid_low
+            result_other = other_tensor(tie(result_low, d_normed2_other))
+        elif step == "DA":
+            before = d_attended = product_tt(first_full, qkv_width, query_width, d_mid_low)
+        elif step == "H":
+            grads = attend_back(
+                heads,
+                grads,
+                after,
+                query_low,
+                keys,
+                keys_t,
+                values,
+                d_attended,
+                attended,
+                inverse_total,
+                bias,
+            )
+            heads += 1
+            d_query, d_keys, d_values = grads
+            before = d_keys
+        elif step == "HP":
+            halo_grads = halo_parts(d_keys, d_values, row_count, *after)
+            got = [from_behind(part, at - reach_count) for at, part in enumerate(halo_grads)]
+            before = halo_grads[0]
+        elif step == "QB":
+            d_query_low, d_gain_query = query_back(
+                d_query, qkv_raw, cos_table[0], sin_table[0], gain_query, *after
+            )
+            before = d_query_low
+            sums["Q"] = Scatter(ring, normed_rows, d_query_low, near_first)
+        elif step == "OP":
+            before = d_mid_rows = ring.chosen(tie(d_mid_low, *after), near_first)
+            sums["O"] = Scatter(ring, d_mid_rows, attended_back, near_first)
+        elif step == "KB":
+            d_keyval_low, d_gain_key = key_back(
+                d_keys,
+                d_values,
+                got,
+                qkv_raw,
+                query_width,
+                cos_table[0],
+                sin_table[0],
+                gain_key,
+                *after,
+            )
+            before = d_keyval_low
+        elif step == "IB":
+            d_normed_low, d_attn_part = input_back(
+                d_query_low, d_keyval_low, first_full, tokens, attn_scale, *after
+            )
+            d_normed_other = other_tensor(d_normed_low)
+            before = d_normed_low
+        elif step == "GB":
+            places = jnp.arange(2 * HD, dtype=jnp.int32)
+            per_device = gain_count // 2
+            places = (
+                places % HD // per_device * depth
+                + places // HD * per_device
+                + places % per_device
+            )
+            places = (places[:, None] == jnp.arange(model, dtype=jnp.int32)[None, :]).astype(bf16)
+            gain_grads = gain_block(
+                d_attn_part, d_ffn_weight, d_gain_query, d_gain_key, places, *after
+            )
+            before = gain_rows = ring.chosen(gain_grads, near_first)
+            sums["K"] = Scatter(ring, normed_rows, d_keyval_low, near_first, gain_rows)
+        elif step == "AD":
+            before = output = add_up(mid, result_low, result_other, *after)
+        elif step == "IG":
+            _, input_grad, _ = norm_back(
+                tokens, d_mid, d_normed_low, d_normed_other, attn_weight, *after
+            )
+            before = input_grad
+    grad_down, grad_out, grad_query = totals["D"], totals["O"], totals["Q"]
+    grad_gateup = side_by_side(totals["G"], totals["U"])
+    shared = totals["K"].astype(bf16)
+    grad_keyval, gains_t = both_tensors(shared, other_tensor(shared), tensor, kv_width)
+    grad_attn_gain = gains_t[0]
+    grad_ffn_gain = gains_t[1]
+    grad_heads = gains_t[2, :gain_count].reshape(2, gain_count // 2)
     return (
         output,
         input_grad,

time: 685 us -> 653 us (0.953)
  waiting for transfers between devices: 231 us -> 207 us
  starting transfers between devices: 70 us -> 52.7 us
  local copies, waits for them, and re-layouts: 65.6 us -> 82.6 us
  Pallas kernels: 252 us -> 244 us
    ppermute x24 -> x29, waiting for transfers between devices: 93.5 us -> 63.7 us  [send(): self.got.append([lax.ppermute(part, 'dp', pairs) for part in sent])]
    unnamed x208 -> x277, local copies, waits for them, and re-layouts: 43.1 us -> 64 us
    ppermute x24 -> x29, starting transfers between devices: 48.8 us -> 30.3 us  [send(): self.got.append([lax.ppermute(part, 'dp', pairs) for part in sent])]
    pallas_call x30 -> x26, Pallas kernels: 91.1 us -> 77.2 us  [product(): pl.pallas_call(kernel, grid=(all_columns // tile,), in_specs=in_specs + [...]
    ppermute x5, waiting for transfers between devices: 21.2 us -> 31.8 us  [other_tensor(): lax.ppermute(array, 'tensor', [(i, (i + 1) % count) for i in range(count)])]
    pallas_call x0 -> x3, Pallas kernels: none -> 10.1 us  [the longest x1 4.27 us: transposed(): pl.pallas_call(kernel, grid=(tokens // step,), in_specs=[pl.BlockSpec((st...]
    pallas_call x5 -> x4, Pallas kernels: 22.1 us -> 17.4 us  [transposed_blocks(): pl.pallas_call(kernel, grid_spec=pltpu.PrefetchScalarGridSpec(num_scalar_...]
  transfers between devices with their start and end apart: 37 -> 43, of which waited for: 15 -> 17; matrix products, arithmetic and copies ran while one was open for 9% -> 9% of each run, Pallas kernels for 32% -> 33%
where the time goes in v5:
time: 653 us; the launch traced here: 643 us
  Pallas kernels  244 us (37%)
  waiting for transfers between devices  207 us (32%)
  local copies, waits for them, and re-layouts  82.6 us (13%)
  starting transfers between devices  52.7 us (8%)
  matrix products  21.5 us (3%)
  other arithmetic  19.9 us (3%)
  between operations  15.4 us (2%)
    all_gather x1, waiting for transfers between devices, shards(): lax.all_gather(first_pack.astype(bf16), 'dp', axis=0, tiled=True)  89 us
    pallas_call x26, Pallas kernels, product(): pl.pallas_call(kernel, grid=(all_columns // tile,), in_specs=in_specs + [...  77.2 us
    unnamed x277, local copies, waits for them, and re-layouts  64 us
    ppermute x29, waiting for transfers between devices, send(): self.got.append([lax.ppermute(part, 'dp', pairs) for part in sent])  63.7 us
    pallas_call x3, Pallas kernels, attend_back(): pl.pallas_call(functools.partial(attend_back_kernel, keys - rows - WINDOW...  32.5 us
    ppermute x5, waiting for transfers between devices, other_tensor(): lax.ppermute(array, 'tensor', [(i, (i + 1) % count) for i in range(count)])  31.8 us
    ppermute x29, starting transfers between devices, send(): self.got.append([lax.ppermute(part, 'dp', pairs) for part in sent])  30.3 us
    pallas_call x1, Pallas kernels, feed(): pl.pallas_call(feed_kernel, grid=(steps,), in_specs=[pl.BlockSpec((rows,...  19.3 us
  transfers between devices with their start and end apart: 43, of which 17 were waited for; matrix products, arithmetic and copies ran while one was open for 9% of the time, Pallas kernels for 33%

profile of v5, /device:TPU:0, one launch (start us, length us, event | category | flops | bytes accessed | tf_op | source)
XLA Modules:
  0.0 642.7 jit_solution(6849459109158552950)
XLA Ops:
  20.2 2.4 collective-permute-start.3
  22.6 4.4 collective-permute-start.2
  28.3 2.4 fusion.16.bias_ref.refs_7_
  30.7 89.0 %all-gather.3.cloned.1.call-done.refs_0_.refs_1_.refs_2_.refs_3_.refs_4_.left_ref.weights_ref = bf16[2048,4608]{1,0:T(8,128)(2,1)} async-done(((bf16[128,4608]{1,0:T(8,128)(2,1)}), bf16[2048,4608]{1,0:T(8,128)(2,1)}) %all-gather.3.cloned.1.call-update) | async-done | bytes 18874384 | tf_op jit(solution)/shard_map/all_gather | solution.py:851
  122.8 5.8 fusion.5.raw_ref
  131.8 2.9 collective-permute-start.1
  134.7 3.6 collective-permute-start
  142.4 12.9 %collective-permute-done = bf16[384,512]{1,0:T(8,128)(2,1)} collective-permute-done((bf16[384,512]{1,0:T(8,128)(2,1)}, bf16[384,512]{1,0:T(8,128)(2,1)}, u32[]{:S(2)}, u32[]{:S(2)}) %collective-permute-start) | collective-permute-done | bytes 393248 | tf_op jit(solution)/shard_map/ppermute | solution.py:152
  163.2 13.2 %shard_map.195 = (bf16[768,512]{1,0:T(8,128)(2,1)S(1)}, f32[3,8,512]{2,1,0:T(8,128)S(1)}) custom-call(bf16[768,512]{1,0:T(8,128)(2,1)S(1)} %bitcast.71, bf16[3,1536,64]{2,1,0:T(8,128)(2,1)S(1)} %bitcast.64, bf16[3,80,1536]{2,1,0:T(8,128)(2,1)S(1)} %concatenate.29.v_ref, f32[1536,512]{1,0:T(8,128)S(1)} %copy-done.61), custom_call_target="tpu_custom_call" | custom-call | flops 5232500224 | tf_op jit(solution)/shard_map/pallas_call | solution.py:671
  177.3 5.1 fusion.17
  183.9 4.3 shard_map.197.left_ref
  190.1 5.0 shard_map.196.left_ref
  196.3 10.6 %fusion.2.d_act_ref = f32[512,2560]{1,0:T(8,128)} fusion(bf16[512,2048]{1,0:T(8,128)(2,1)} %direct_ref.1, bf16[2048,4608]{1,0:T(8,128)(2,1)} %all-gather.3.cloned.1.call-done.refs_0_.refs_1_.refs_2_.refs_3_.refs_4_.left_ref.weights_ref), kind=kOutput, calls=%fused_computation.5 | convolution fusion | flops 5368709120 | bytes 17825792 | tf_op jit(solution)/shard_map/dot_general | solution.py:164
  209.0 13.1 %collective-permute-done.4.refs_0_ = bf16[512,2048]{1,0:T(8,128)(2,1)} collective-permute-done((bf16[512,2048]{1,0:T(8,128)(2,1)}, bf16[512,2048]{1,0:T(8,128)(2,1)}, u32[]{:S(2)}, u32[]{:S(2)}) %collective-permute-start.4) | collective-permute-done | bytes 2097184 | tf_op jit(solution)/shard_map/ppermute | solution.py:138
  222.1 3.4 multiply_reduce_fusion
  229.2 4.8 shard_map.199.refs_0_.left_ref
  233.9 5.4 all-gather.5.cloned.1.call-done.gate_ref.up_ref
  239.4 19.3 %shard_map.200 = (bf16[512,2560]{1,0:T(8,128)(2,1)}, bf16[512,2560]{1,0:T(8,128)(2,1)}, bf16[512,2560]{1,0:T(8,128)(2,1)}) custom-call(bf16[512,2048]{1,0:T(8,128)(2,1)} %multiply_convert_fusion.in_ref.n_ref, f32[512,2560]{1,0:T(8,128)} %fusion.2.d_act_ref, bf16[2048,5120]{1,0:T(8,128)(2,1)} %all-gather.5.cloned.1.call-done.gate_ref.up_ref, ...), custom_call_target="tpu_custom_call" | custom-call | flops 7848750080 | tf_op jit(solution)/shard_map/pallas_call | solution.py:743
  260.4 9.7 %shard_map.201.refs_0_ = bf16[2048,2560]{1,0:T(8,128)(2,1)} custom-call(bf16[2048,512]{1,0:T(8,128)(2,1)S(1)} %copy-done.67, bf16[512,2560]{1,0:T(8,128)(2,1)S(1)} %copy-done.42), custom_call_target="tpu_custom_call" | custom-call | flops 3206006016 | tf_op jit(solution)/shard_map/pallas_call | solution.py:276
  273.4 5.4 shard_map.202.refs_0_
  278.8 3.9 collective-permute-start.5
  282.7 19.0 %shard_map.203.refs_0_.part_ref = bf16[512,2048]{1,0:T(8,128)(2,1)} custom-call(bf16[512,2560]{1,0:T(8,128)(2,1)} %get-tuple-element.52.right_ref.d_gate_ref, bf16[512,2560]{1,0:T(8,128)(2,1)} %get-tuple-element.53.d_up_ref.right_ref, bf16[2048,5120]{1,0:T(8,128)(2,1)} %all-gather.5.cloned.1.call-done.gate_ref.up_ref, ...), custom_call_target="tpu_custom_call" | custom-call | flops 6842500096 | tf_op jit(solution)/shard_map/pallas_call | solution.py:770
  301.7 5.4 shard_map.204.refs_1_
  308.6 5.3 shard_map.205.refs_5_
  313.9 2.5 collective-permute-start.9
  317.8 12.1 %shard_map.206.refs_1_.part_ref = bf16[512,2048]{1,0:T(8,128)(2,1)} custom-call(bf16[512,2560]{1,0:T(8,128)(2,1)} %get-tuple-element.51.right_ref.act_ref, bf16[2048,4608]{1,0:T(8,128)(2,1)} %all-gather.3.cloned.1.call-done.refs_0_.refs_1_.refs_2_.refs_3_.refs_4_.left_ref.weights_ref, ...), custom_call_target="tpu_custom_call" | custom-call | flops 3622500096 | tf_op jit(solution)/shard_map/pallas_call | solution.py:800
  331.4 5.3 shard_map.208.refs_0_
  336.8 18.7 %collective-permute-done.6.refs_1_.other_ref = bf16[512,2048]{1,0:T(8,128)(2,1)} collective-permute-done((bf16[512,2048]{1,0:T(8,128)(2,1)}, bf16[512,2048]{1,0:T(8,128)(2,1)}, u32[]{:S(2)}, u32[]{:S(2)}) %collective-permute-start.6) | collective-permute-done | bytes 2097184 | tf_op jit(solution)/shard_map/ppermute | solution.py:138
  355.5 7.2 %shard_map.209 = (f32[512,2048]{1,0:T(8,128)}, bf16[512,2048]{1,0:T(8,128)(2,1)S(1)}, f32[1,2048]{1,0:T(1,128)S(1)}) custom-call(f32[512,2048]{1,0:T(8,128)} %copy-done.118, bf16[512,2048]{1,0:T(8,128)(2,1)S(1)} %copy-done.69, bf16[512,2048]{1,0:T(8,128)(2,1)} %shard_map.203.refs_0_.part_ref, bf16[512,2048]{1,0:T(8,128)(2,1)} %collective-permute-done.6.refs_1_.other_ref, ...), custom_call_target="tpu_custom_call" | custom-call | flops 2817499904 | tf_op jit(solution)/shard_map/pallas_call | solution.py:330
  362.7 4.6 shard_map.210.refs_4_.refs_8_
  367.6 10.7 %shard_map.211 = (f32[768,512]{1,0:T(8,128)S(1)}, f32[192,1536]{1,0:T(8,128)S(1)}, f32[192,1536]{1,0:T(8,128)S(1)}) custom-call(bf16[768,512]{1,0:T(8,128)(2,1)S(1)} %bitcast.72, bf16[3,1536,64]{2,1,0:T(8,128)(2,1)S(1)} %bitcast.65, bf16[192,1536]{1,0:T(8,128)(2,1)S(1)} %get-tuple-element.98.refs_2_, bf16[3,1536,64]{2,1,0:T(8,128)(2,1)S(1)} %bitcast.68, ...), custom_call_target="tpu_custom_call" | custom-call | flops 4427500032 | tf_op jit(solution)/shard_map/pallas_call | solution.py:698
  379.4 11.1 %shard_map.212 = (f32[768,512]{1,0:T(8,128)S(1)}, f32[192,1536]{1,0:T(8,128)S(1)}, f32[192,1536]{1,0:T(8,128)S(1)}) custom-call(bf16[768,512]{1,0:T(8,128)(2,1)S(1)} %bitcast.73, bf16[3,1536,64]{2,1,0:T(8,128)(2,1)S(1)} %bitcast.66, bf16[192,1536]{1,0:T(8,128)(2,1)S(1)} %copy-done.65, ...), custom_call_target="tpu_custom_call", output_to_operand_aliasing={{0}: (8, {}), {1}: (9, {}), {2}: (10, {})} | custom-call | flops 4427500032 | tf_op jit(solution)/shard_map/pallas_call | solution.py:698
  390.5 14.3 %collective-permute-done.9.refs_1_ = bf16[512,2560]{1,0:T(8,128)(2,1)} collective-permute-done((bf16[512,2560]{1,0:T(8,128)(2,1)}, bf16[512,2560]{1,0:T(8,128)(2,1)}, u32[]{:S(2)}, u32[]{:S(2)}) %collective-permute-start.9) | collective-permute-done | bytes 2621472 | tf_op jit(solution)/shard_map/ppermute | solution.py:126
  404.8 3.3 shard_map.213.refs_11_
  421.3 10.7 %shard_map.214 = (f32[768,512]{1,0:T(8,128)S(1)}, f32[192,1536]{1,0:T(8,128)S(1)}, f32[192,1536]{1,0:T(8,128)S(1)}) custom-call(bf16[768,512]{1,0:T(8,128)(2,1)S(1)} %bitcast.74, bf16[3,1536,64]{2,1,0:T(8,128)(2,1)S(1)} %bitcast.67, bf16[192,1536]{1,0:T(8,128)(2,1)S(1)} %copy-done.66, ...), custom_call_target="tpu_custom_call", output_to_operand_aliasing={{0}: (8, {}), {1}: (9, {}), {2}: (10, {})} | custom-call | flops 4427500032 | tf_op jit(solution)/shard_map/pallas_call | solution.py:698
  439.6 2.4 shard_map.217
  443.3 4.9 shard_map.219.left_ref.refs_0_
  450.9 2.2 shard_map.220
  459.7 3.1 shard_map.221.refs_2_
  462.8 2.7 shard_map.222.refs_2_
  466.8 2.7 shard_map.223.refs_2_
  469.5 3.8 collective-permute-start.22
  473.3 3.7 collective-permute-done.10.refs_0_
  478.6 2.1 collective-permute-start.21
  480.6 3.4 shard_map.225.refs_0_
  484.1 8.2 %shard_map.226 = (bf16[512,2048]{1,0:T(8,128)(2,1)}, f32[1,2048]{1,0:T(1,128)S(1)}) custom-call(bf16[512,768]{1,0:T(8,128)(2,1)S(1)} %copy-done.36, bf16[512,384]{1,0:T(8,128)(2,1)S(1)} %get-tuple-element.72.refs_2_.d_keyval_ref.right_ref, bf16[2048,4608]{1,0:T(8,128)(2,1)} %all-gather.3.cloned.1.call-done.refs_0_.refs_1_.refs_2_.refs_3_.refs_4_.left_ref.weights_ref, ...), custom_call_target="tpu_custom_call" | custom-call | flops 3220000000 | tf_op jit(solution)/shard_map/pallas_call | solution.py:502
  497.1 4.8 collective-permute-done.22.refs_3_
  504.6 2.4 shard_map.227.refs_2_.first_ref
  507.0 4.1 collective-permute-done.21.refs_1_
  518.6 2.1 shard_map.230.in_ref
  520.7 2.8 shard_map.231.refs_0_.refs_1_.refs_2_.refs_3_.refs_4_
  532.1 22.4 %collective-permute-done.31.refs_2_ = bf16[256,768]{1,0:T(8,128)(2,1)S(1)} collective-permute-done((bf16[256,768]{1,0:T(8,128)(2,1)S(1)}, bf16[256,768]{1,0:T(8,128)(2,1)S(1)}, u32[]{:S(2)}, u32[]{:S(2)}) %collective-permute-start.31) | collective-permute-done | bytes 393248 | tf_op jit(solution)/shard_map/ppermute | solution.py:126
  556.1 3.1 shard_map.234.refs_3_
  561.3 3.9 collective-permute-done.29.refs_2_
  572.8 7.6 %shard_map.238 = (f32[512,2048]{1,0:T(8,128)}, bf16[512,2048]{1,0:T(8,128)(2,1)}, f32[1,2048]{1,0:T(1,128)}) custom-call(bf16[512,2048]{1,0:T(8,128)(2,1)S(1)} %copy-done.24, f32[512,2048]{1,0:T(8,128)} %get-tuple-element.86.direct_ref, bf16[512,2048]{1,0:T(8,128)(2,1)} %get-tuple-element.79.refs_4_.part_ref, ...), custom_call_target="tpu_custom_call" | custom-call | flops 2817499904 | tf_op jit(solution)/shard_map/pallas_call | solution.py:330
  582.2 9.9 %collective-permute-done.33.refs_2_ = bf16[256,512]{1,0:T(8,128)(2,1)S(1)} collective-permute-done((bf16[256,512]{1,0:T(8,128)(2,1)S(1)}, bf16[256,512]{1,0:T(8,128)(2,1)S(1)}, u32[]{:S(2)}, u32[]{:S(2)}) %collective-permute-start.33) | collective-permute-done | bytes 262176 | tf_op jit(solution)/shard_map/ppermute | solution.py:126
  595.7 3.1 collective-permute-start.37
  598.7 5.3 shard_map.240.refs_0_
  604.0 4.0 shard_map.241.refs_4_
  611.4 2.5 shard_map.242.refs_4_.second_ref
  614.0 2.7 collective-permute-done.35.refs_3_
  619.9 2.2 shard_map.244.refs_5_
  623.1 2.1 shard_map.245
  626.8 4.1 shard_map.247
  (425 shorter events, 142.3 us)
Async XLA Ops:
  7.2 112.5 %all-gather.3.cloned.1.call-start = ((), (), s32[]{:S(2)}) async-start(), calls=%async_computation.1 | async-start | bytes 20054016 | tf_op jit(solution)/shard_map/all_gather | solution.py:851
  17.9 221.5 %all-gather.5.cloned.1.call-start = ((), (), s32[]{:S(2)}) async-start(), calls=%async_computation.2 | async-start | bytes 22282240 | tf_op jit(solution)/shard_map/all_gather | solution.py:852
  20.1 583.9 %reduce-scatter.2.cloned.1.call-start = ((), (), s32[]{:S(2)}) async-start(), calls=%async_computation.3 | async-start | bytes 11141120 | tf_op jit(solution)/shard_map/reduce_scatter | solution.py:946
  20.2 7.8 %collective-permute-start.3 = (bf16[512]{0:T(512)(128)(2,1)S(1)}, bf16[512]{0:T(512)(128)(2,1)S(1)}, u32[]{:S(2)}, u32[]{:S(2)}) collective-permute-start(bf16[512]{0:T(512)(128)(2,1)S(1)} %add_convert_fusion.2), channel_id=1, source_target_pairs={{0,2},{2,4},{4,6},{6,8},{8,10},{10,12},{12,14},{14,16},{16,18},{18... | collective-permute-start | bytes 3080 | tf_op jit(solution)/shard_map/ppermute | solution.py:152
  22.6 5.7 collective-permute-start.2
  27.6 94.6 %copy-start.129 = (f32[512]{0:T(512)}, f32[512]{0:T(512)S(1)}, u32[]{:S(2)}) copy-start(f32[512]{0:T(512)S(1)} %add_rsqrt_fusion.3) | copy-start | bytes 6148
  27.9 114.1 %copy-start.70 = (f32[32,512]{1,0:T(8,128)}, f32[32,512]{1,0:T(8,128)S(1)}, u32[]{:S(2)}) copy-start(f32[32,512]{1,0:T(8,128)S(1)} %get-tuple-element.106.sin_ref) | copy-start | bytes 196612
  131.8 10.7 %collective-permute-start.1 = (bf16[384,512]{1,0:T(8,128)(2,1)}, bf16[384,512]{1,0:T(8,128)(2,1)}, u32[]{:S(2)}, u32[]{:S(2)}) collective-permute-start(bf16[384,512]{1,0:T(8,128)(2,1)} %pad_maximum_fusion.1), channel_id=1, source_target_pairs={{0,2},{2,4},{4,6},{6,8},{8,10},{10,12},{12,14},{14,16},{16,18},{18... | collective-permute-start | bytes 1179656 | tf_op jit(solution)/shard_map/ppermute | solution.py:152
  134.7 20.6 %collective-permute-start = (bf16[384,512]{1,0:T(8,128)(2,1)}, bf16[384,512]{1,0:T(8,128)(2,1)}, u32[]{:S(2)}, u32[]{:S(2)}) collective-permute-start(bf16[384,512]{1,0:T(8,128)(2,1)} %pad_maximum_fusion.1), channel_id=1, source_target_pairs={{0,4},{2,6},{4,8},{6,10},{8,12},{10,14},{12,16},{14,18},{16,20},{1... | collective-permute-start | bytes 1179656 | tf_op jit(solution)/shard_map/ppermute | solution.py:152
  142.1 13.2 %copy-start.124 = (bf16[192,512]{1,0:T(8,128)(2,1)S(1)}, bf16[192,512]{1,0:T(8,128)(2,1)}, u32[]{:S(2)}) copy-start(bf16[192,512]{1,0:T(8,128)(2,1)} %copy-done.123) | copy-start | bytes 589828
  142.4 17.5 %copy-start.96 = (bf16[12,64,512]{2,1,0:T(8,128)(2,1)}, bf16[12,64,512]{2,1,0:T(8,128)(2,1)S(1)}, u32[]{:S(2)}) copy-start(bf16[12,64,512]{2,1,0:T(8,128)(2,1)S(1)} %pad_maximum_fusion) | copy-start | bytes 2359300
  157.4 210.0 %copy-start.64 = (bf16[192,1536]{1,0:T(8,128)(2,1)}, bf16[192,1536]{1,0:T(8,128)(2,1)S(1)}, u32[]{:S(2)}) copy-start(bf16[192,1536]{1,0:T(8,128)(2,1)S(1)} %get-tuple-element.98.refs_2_) | copy-start | bytes 1769476
  182.4 39.7 %collective-permute-start.4 = (bf16[512,2048]{1,0:T(8,128)(2,1)}, bf16[512,2048]{1,0:T(8,128)(2,1)}, u32[]{:S(2)}, u32[]{:S(2)}) collective-permute-start(bf16[512,2048]{1,0:T(8,128)(2,1)} %fusion.17), channel_id=1, source_target_pairs={{0,1},{1,0},{2,3},{3,2},{4,5},{5,4},{6,7},{7,6},{8,9},{9,8},{10,11... | collective-permute-start | bytes 6291464 | tf_op jit(solution)/shard_map/ppermute | solution.py:138
  208.3 13.8 %copy-start.27 = (bf16[768,512]{0,1:T(8,128)(2,1)}, bf16[768,512]{0,1:T(8,128)(2,1)S(1)}, u32[]{:S(2)}) copy-start(bf16[768,512]{0,1:T(8,128)(2,1)S(1)} %copy.76) | copy-start | bytes 2359300
  233.9 24.7 %copy-start.67 = (bf16[2048,512]{1,0:T(8,128)(2,1)S(1)}, bf16[2048,512]{1,0:T(8,128)(2,1)}, u32[]{:S(2)}) copy-start(bf16[2048,512]{1,0:T(8,128)(2,1)} %shard_map.197.left_ref) | copy-start | bytes 6291460
  278.8 29.8 %collective-permute-start.5 = (bf16[1024,2560]{1,0:T(8,128)(2,1)}, bf16[1024,2560]{1,0:T(8,128)(2,1)}, u32[]{:S(2)}, u32[]{:S(2)}) collective-permute-start(bf16[1024,2560]{1,0:T(8,128)(2,1)} %shard_map.202.refs_0_), channel_id=1, source_target_pairs={{0,2},{2,0},{4,6},{6,4},{8,10},{10,8},{12,14},{14,12},{16,18},{18,... | collective-permute-start | bytes 15728648 | tf_op jit(solution)/shard_map/ppermute | solution.py:126
  282.7 19.0 %copy-start.12 = (bf16[512,2560]{1,0:T(8,128)(2,1)S(1)}, bf16[512,2560]{1,0:T(8,128)(2,1)}, u32[]{:S(2)}) copy-start(bf16[512,2560]{1,0:T(8,128)(2,1)} %get-tuple-element.53.d_up_ref.right_ref) | copy-start | bytes 7864324
  307.1 22.7 %collective-permute-start.8 = (bf16[1024,2560]{1,0:T(8,128)(2,1)}, bf16[1024,2560]{1,0:T(8,128)(2,1)}, u32[]{:S(2)}, u32[]{:S(2)}) collective-permute-start(bf16[1024,2560]{1,0:T(8,128)(2,1)} %shard_map.204.refs_1_), channel_id=1, source_target_pairs={{0,2},{2,0},{4,6},{6,4},{8,10},{10,8},{12,14},{14,12},{16,18},{18,... | collective-permute-start | bytes 15728648 | tf_op jit(solution)/shard_map/ppermute | solution.py:126
  307.2 48.2 %collective-permute-start.6 = (bf16[512,2048]{1,0:T(8,128)(2,1)}, bf16[512,2048]{1,0:T(8,128)(2,1)}, u32[]{:S(2)}, u32[]{:S(2)}) collective-permute-start(bf16[512,2048]{1,0:T(8,128)(2,1)} %shard_map.203.refs_0_.part_ref), channel_id=1, source_target_pairs={{0,1},{1,0},{2,3},{3,2},{4,5},{5,4},{6,7},{7,6},{8,9},{9,8},{10,11... | collective-permute-start | bytes 6291464 | tf_op jit(solution)/shard_map/ppermute | solution.py:138
  313.9 90.9 %collective-permute-start.9 = (bf16[512,2560]{1,0:T(8,128)(2,1)}, bf16[512,2560]{1,0:T(8,128)(2,1)}, u32[]{:S(2)}, u32[]{:S(2)}) collective-permute-start(bf16[512,2560]{1,0:T(8,128)(2,1)} %shard_map.205.refs_5_), channel_id=1, source_target_pairs={{0,4},{2,6},{4,0},{6,2},{8,12},{10,14},{12,8},{14,10},{16,20},{18,... | collective-permute-start | bytes 7864328 | tf_op jit(solution)/shard_map/ppermute | solution.py:126
  317.8 12.1 %copy-start.13 = (bf16[512,2560]{1,0:T(8,128)(2,1)S(1)}, bf16[512,2560]{1,0:T(8,128)(2,1)}, u32[]{:S(2)}) copy-start(bf16[512,2560]{1,0:T(8,128)(2,1)} %get-tuple-element.53.d_up_ref.right_ref) | copy-start | bytes 7864324
  331.4 24.0 %copy-start.69 = (bf16[512,2048]{1,0:T(8,128)(2,1)S(1)}, bf16[512,2048]{1,0:T(8,128)(2,1)}, u32[]{:S(2)}) copy-start(bf16[512,2048]{1,0:T(8,128)(2,1)} %direct_ref.1) | copy-start | bytes 6291460
  336.8 141.8 %collective-permute-start.17 = (bf16[512,2560]{1,0:T(8,128)(2,1)}, bf16[512,2560]{1,0:T(8,128)(2,1)}, u32[]{:S(2)}, u32[]{:S(2)}) collective-permute-start(bf16[512,2560]{1,0:T(8,128)(2,1)} %shard_map.208.refs_0_), channel_id=1, source_target_pairs={{0,4},{2,6},{4,0},{6,2},{8,12},{10,14},{12,8},{14,10},{16,20},{18,... | collective-permute-start | bytes 7864328 | tf_op jit(solution)/shard_map/ppermute | solution.py:126
  379.4 25.4 %copy-start.9 = (bf16[512,2560]{1,0:T(8,128)(2,1)S(1)}, bf16[512,2560]{1,0:T(8,128)(2,1)}, u32[]{:S(2)}) copy-start(bf16[512,2560]{1,0:T(8,128)(2,1)} %get-tuple-element.52.right_ref.d_gate_ref) | copy-start | bytes 7864324
  390.5 17.6 %copy-start.54 = (f32[192,1536]{1,0:T(8,128)}, f32[192,1536]{1,0:T(8,128)S(1)}, u32[]{:S(2)}) copy-start(f32[192,1536]{1,0:T(8,128)S(1)} %get-tuple-element.61.refs_10_) | copy-start | bytes 3538948
  390.5 17.6 %copy-start.74 = (f32[768,512]{1,0:T(8,128)}, f32[768,512]{1,0:T(8,128)S(1)}, u32[]{:S(2)}) copy-start(f32[768,512]{1,0:T(8,128)S(1)} %get-tuple-element.59.refs_8_) | copy-start | bytes 4718596
  408.1 47.6 %collective-permute-start.16 = (bf16[256,2560]{1,0:T(8,128)(2,1)}, bf16[256,2560]{1,0:T(8,128)(2,1)}, u32[]{:S(2)}, u32[]{:S(2)}) collective-permute-start(bf16[256,2560]{1,0:T(8,128)(2,1)} %shard_map.213.refs_11_), channel_id=1, source_target_pairs={{0,8},{2,10},{4,12},{6,14},{8,0},{10,2},{12,4},{14,6},{16,24},{18,... | collective-permute-start | bytes 3932168 | tf_op jit(solution)/shard_map/ppermute | solution.py:126
  421.3 15.2 %copy-start.71 = (f32[32,512]{1,0:T(8,128)S(1)}, f32[32,512]{1,0:T(8,128)}, u32[]{:S(2)}) copy-start(f32[32,512]{1,0:T(8,128)} %copy-done.70) | copy-start | bytes 196612
  442.8 11.1 %collective-permute-start.15 = (bf16[256,768]{1,0:T(8,128)(2,1)}, bf16[256,768]{1,0:T(8,128)(2,1)}, u32[]{:S(2)}, u32[]{:S(2)}) collective-permute-start(bf16[256,768]{1,0:T(8,128)(2,1)} %get-tuple-element.71), channel_id=1, source_target_pairs={{0,2},{2,0},{4,6},{6,4},{8,10},{10,8},{12,14},{14,12},{16,18},{18,... | collective-permute-start | bytes 1179656 | tf_op jit(solution)/shard_map/ppermute | solution.py:126
  442.8 11.6 %collective-permute-start.14 = (bf16[256,768]{1,0:T(8,128)(2,1)}, bf16[256,768]{1,0:T(8,128)(2,1)}, u32[]{:S(2)}, u32[]{:S(2)}) collective-permute-start(bf16[256,768]{1,0:T(8,128)(2,1)} %get-tuple-element.68.refs_1_), channel_id=1, source_target_pairs={{0,2},{2,0},{4,6},{6,4},{8,10},{10,8},{12,14},{14,12},{16,18},{18,... | collective-permute-start | bytes 1179656 | tf_op jit(solution)/shard_map/ppermute | solution.py:126
  453.9 11.7 %collective-permute-start.13 = (bf16[256,768]{1,0:T(8,128)(2,1)}, bf16[256,768]{1,0:T(8,128)(2,1)}, u32[]{:S(2)}, u32[]{:S(2)}) collective-permute-start(bf16[256,768]{1,0:T(8,128)(2,1)} %get-tuple-element.70), channel_id=1, source_target_pairs={{0,2},{2,0},{4,6},{6,4},{8,10},{10,8},{12,14},{14,12},{16,18},{18,... | collective-permute-start | bytes 1179656 | tf_op jit(solution)/shard_map/ppermute | solution.py:126
  453.9 12.8 %collective-permute-start.12 = (bf16[256,768]{1,0:T(8,128)(2,1)}, bf16[256,768]{1,0:T(8,128)(2,1)}, u32[]{:S(2)}, u32[]{:S(2)}) collective-permute-start(bf16[256,768]{1,0:T(8,128)(2,1)} %get-tuple-element.69.refs_3_), channel_id=1, source_target_pairs={{0,2},{2,0},{4,6},{6,4},{8,10},{10,8},{12,14},{14,12},{16,18},{18,... | collective-permute-start | bytes 1179656 | tf_op jit(solution)/shard_map/ppermute | solution.py:126
  454.4 15.1 %collective-permute-start.11 = (bf16[384,512]{1,0:T(8,128)(2,1)}, bf16[384,512]{1,0:T(8,128)(2,1)}, u32[]{:S(2)}, u32[]{:S(2)}) collective-permute-start(bf16[384,512]{1,0:T(8,128)(2,1)} %get-tuple-element.65), channel_id=1, source_target_pairs={{2,0},{4,2},{6,4},{8,6},{10,8},{12,10},{14,12},{16,14},{18,16},{20... | collective-permute-start | bytes 1179656 | tf_op jit(solution)/shard_map/ppermute | solution.py:152
  455.7 21.2 %collective-permute-start.10 = (bf16[384,512]{1,0:T(8,128)(2,1)}, bf16[384,512]{1,0:T(8,128)(2,1)}, u32[]{:S(2)}, u32[]{:S(2)}) collective-permute-start(bf16[384,512]{1,0:T(8,128)(2,1)} %get-tuple-element.64.refs_0_), channel_id=1, source_target_pairs={{4,0},{6,2},{8,4},{10,6},{12,8},{14,10},{16,12},{18,14},{20,16},{2... | collective-permute-start | bytes 1179656 | tf_op jit(solution)/shard_map/ppermute | solution.py:152
  465.5 27.4 %collective-permute-start.20 = (bf16[256,768]{1,0:T(8,128)(2,1)S(1)}, bf16[256,768]{1,0:T(8,128)(2,1)S(1)}, u32[]{:S(2)}, u32[]{:S(2)}) collective-permute-start(bf16[256,768]{1,0:T(8,128)(2,1)S(1)} %copy-done.115), channel_id=1, source_target_pairs={{0,2},{2,0},{4,6},{6,4},{8,10},{10,8},{12,14},{14,12},{16,18},{18,... | collective-permute-start | bytes 1179656 | tf_op jit(solution)/shard_map/ppermute | solution.py:126
  466.7 48.2 %collective-permute-start.18 = (bf16[256,768]{1,0:T(8,128)(2,1)}, bf16[256,768]{1,0:T(8,128)(2,1)}, u32[]{:S(2)}, u32[]{:S(2)}) collective-permute-start(bf16[256,768]{1,0:T(8,128)(2,1)} %get-tuple-element.77), channel_id=1, source_target_pairs={{0,2},{2,0},{4,6},{6,4},{8,10},{10,8},{12,14},{14,12},{16,18},{18,... | collective-permute-start | bytes 1179656 | tf_op jit(solution)/shard_map/ppermute | solution.py:126
  469.5 32.5 %collective-permute-start.22 = (bf16[128,2560]{1,0:T(8,128)(2,1)}, bf16[128,2560]{1,0:T(8,128)(2,1)}, u32[]{:S(2)}, u32[]{:S(2)}) collective-permute-start(bf16[128,2560]{1,0:T(8,128)(2,1)} %shard_map.221.refs_2_), channel_id=1, source_target_pairs={{0,16},{2,18},{4,20},{6,22},{8,24},{10,26},{12,28},{14,30},{16,0},... | collective-permute-start | bytes 1966088 | tf_op jit(solution)/shard_map/ppermute | solution.py:126
  476.9 39.4 %collective-permute-start.19 = (bf16[512,768]{1,0:T(8,128)(2,1)}, bf16[512,768]{1,0:T(8,128)(2,1)}, u32[]{:S(2)}, u32[]{:S(2)}) collective-permute-start(bf16[512,768]{1,0:T(8,128)(2,1)} %shard_map.223.refs_2_), channel_id=1, source_target_pairs={{0,4},{2,6},{4,0},{6,2},{8,12},{10,14},{12,8},{14,10},{16,20},{18,... | collective-permute-start | bytes 2359304 | tf_op jit(solution)/shard_map/ppermute | solution.py:126
  478.6 32.6 %collective-permute-start.21 = (bf16[512,768]{1,0:T(8,128)(2,1)}, bf16[512,768]{1,0:T(8,128)(2,1)S(1)}, u32[]{:S(2)}, u32[]{:S(2)}) collective-permute-start(bf16[512,768]{1,0:T(8,128)(2,1)} %shard_map.222.refs_2_), channel_id=1, source_target_pairs={{0,4},{2,6},{4,0},{6,2},{8,12},{10,14},{12,8},{14,10},{16,20},{18,... | collective-permute-start | bytes 2359304 | tf_op jit(solution)/shard_map/ppermute | solution.py:126
  493.7 77.5 %collective-permute-start.34 = (bf16[512,2048]{1,0:T(8,128)(2,1)}, bf16[512,2048]{1,0:T(8,128)(2,1)}, u32[]{:S(2)}, u32[]{:S(2)}) collective-permute-start(bf16[512,2048]{1,0:T(8,128)(2,1)} %get-tuple-element.79.refs_4_.part_ref), channel_id=1, source_target_pairs={{0,1},{1,0},{2,3},{3,2},{4,5},{5,4},{6,7},{7,6},{8,9},{9,8},{10,11... | collective-permute-start | bytes 6291464 | tf_op jit(solution)/shard_map/ppermute | solution.py:138
  497.1 14.9 %copy-start.105 = (bf16[256,768]{1,0:T(8,128)(2,1)S(1)}, bf16[256,768]{1,0:T(8,128)(2,1)}, u32[]{:S(2)}) copy-start(bf16[256,768]{1,0:T(8,128)(2,1)} %copy-done.104) | copy-start | bytes 1179652
  497.1 14.9 %copy-start.3 = (bf16[2048,512]{1,0:T(8,128)(2,1)S(1)}, bf16[2048,512]{1,0:T(8,128)(2,1)}, u32[]{:S(2)}) copy-start(bf16[2048,512]{1,0:T(8,128)(2,1)} %shard_map.196.left_ref) | copy-start | bytes 6291460
  502.0 96.8 %collective-permute-start.7 = (bf16[512,2048]{1,0:T(8,128)(2,1)}, bf16[512,2048]{1,0:T(8,128)(2,1)}, u32[]{:S(2)}, u32[]{:S(2)}) collective-permute-start(bf16[512,2048]{1,0:T(8,128)(2,1)} %shard_map.207), channel_id=1, source_target_pairs={{0,1},{1,0},{2,3},{3,2},{4,5},{5,4},{6,7},{7,6},{8,9},{9,8},{10,11... | collective-permute-start | bytes 6291464 | tf_op jit(solution)/shard_map/ppermute | solution.py:138
  512.1 16.0 %collective-permute-start.30 = (bf16[256,768]{1,0:T(8,128)(2,1)}, bf16[256,768]{1,0:T(8,128)(2,1)}, u32[]{:S(2)}, u32[]{:S(2)}) collective-permute-start(bf16[256,768]{1,0:T(8,128)(2,1)} %get-tuple-element.85), channel_id=1, source_target_pairs={{0,2},{2,0},{4,6},{6,4},{8,10},{10,8},{12,14},{14,12},{16,18},{18,... | collective-permute-start | bytes 1179656 | tf_op jit(solution)/shard_map/ppermute | solution.py:126
  514.8 41.2 %collective-permute-start.32 = (bf16[256,2560]{1,0:T(8,128)(2,1)}, bf16[256,2560]{1,0:T(8,128)(2,1)}, u32[]{:S(2)}, u32[]{:S(2)}) collective-permute-start(bf16[256,2560]{1,0:T(8,128)(2,1)} %shard_map.225.refs_0_), channel_id=1, source_target_pairs={{0,8},{2,10},{4,12},{6,14},{8,0},{10,2},{12,4},{14,6},{16,24},{18,... | collective-permute-start | bytes 3932168 | tf_op jit(solution)/shard_map/ppermute | solution.py:126
  527.9 1.6 collective-permute-start.25
  528.0 1.8 collective-permute-start.24
  529.5 25.0 %copy-start.79 = (bf16[256,768]{1,0:T(8,128)(2,1)S(1)}, bf16[256,768]{1,0:T(8,128)(2,1)}, u32[]{:S(2)}) copy-start(bf16[256,768]{1,0:T(8,128)(2,1)} %copy-done.78) | copy-start | bytes 1179652
  529.5 26.6 %copy-start.15 = (bf16[512,2560]{1,0:T(8,128)(2,1)S(1)}, bf16[512,2560]{1,0:T(8,128)(2,1)}, u32[]{:S(2)}) copy-start(bf16[512,2560]{1,0:T(8,128)(2,1)} %get-tuple-element.53.d_up_ref.right_ref) | copy-start | bytes 7864324
  529.5 2.2 collective-permute-start.28
  529.9 24.6 %collective-permute-start.31 = (bf16[256,768]{1,0:T(8,128)(2,1)S(1)}, bf16[256,768]{1,0:T(8,128)(2,1)S(1)}, u32[]{:S(2)}, u32[]{:S(2)}) collective-permute-start(bf16[256,768]{1,0:T(8,128)(2,1)S(1)} %copy-done.73), channel_id=1, source_target_pairs={{0,8},{2,10},{4,12},{6,14},{8,0},{10,2},{12,4},{14,6},{16,24},{18,... | collective-permute-start | bytes 1179656 | tf_op jit(solution)/shard_map/ppermute | solution.py:126
  531.7 35.2 %copy-start.80 = (bf16[256,768]{1,0:T(8,128)(2,1)}, bf16[256,768]{1,0:T(8,128)(2,1)S(1)}, u32[]{:S(2)}) copy-start(bf16[256,768]{1,0:T(8,128)(2,1)S(1)} %collective-permute-done.28.refs_0_) | copy-start | bytes 1179652
  531.7 37.2 %collective-permute-start.26 = (bf16[512,512]{1,0:T(8,128)(2,1)S(1)}, bf16[512,512]{1,0:T(8,128)(2,1)S(1)}, u32[]{:S(2)}, u32[]{:S(2)}) collective-permute-start(bf16[512,512]{1,0:T(8,128)(2,1)S(1)} %shard_map.233.refs_3_), channel_id=1, source_target_pairs={{0,4},{2,6},{4,0},{6,2},{8,12},{10,14},{12,8},{14,10},{16,20},{18,... | collective-permute-start | bytes 1572872 | tf_op jit(solution)/shard_map/ppermute | solution.py:126
  554.5 10.7 %collective-permute-start.29 = (bf16[256,768]{1,0:T(8,128)(2,1)S(1)}, bf16[256,768]{1,0:T(8,128)(2,1)S(1)}, u32[]{:S(2)}, u32[]{:S(2)}) collective-permute-start(bf16[256,768]{1,0:T(8,128)(2,1)S(1)} %copy-done.79), channel_id=1, source_target_pairs={{0,8},{2,10},{4,12},{6,14},{8,0},{10,2},{12,4},{14,6},{16,24},{18,... | collective-permute-start | bytes 1179656 | tf_op jit(solution)/shard_map/ppermute | solution.py:126
  556.0 12.8 %collective-permute-start.27 = (bf16[256,512]{1,0:T(8,128)(2,1)S(1)}, bf16[256,512]{1,0:T(8,128)(2,1)S(1)}, u32[]{:S(2)}, u32[]{:S(2)}) collective-permute-start(bf16[256,512]{1,0:T(8,128)(2,1)S(1)} %get-tuple-element.83), channel_id=1, source_target_pairs={{0,2},{2,0},{4,6},{6,4},{8,10},{10,8},{12,14},{14,12},{16,18},{18,... | collective-permute-start | bytes 786440 | tf_op jit(solution)/shard_map/ppermute | solution.py:126
  565.2 43.1 %collective-permute-start.36 = (bf16[128,2560]{1,0:T(8,128)(2,1)}, bf16[128,2560]{1,0:T(8,128)(2,1)}, u32[]{:S(2)}, u32[]{:S(2)}) collective-permute-start(bf16[128,2560]{1,0:T(8,128)(2,1)} %shard_map.234.refs_3_), channel_id=1, source_target_pairs={{0,16},{2,18},{4,20},{6,22},{8,24},{10,26},{12,28},{14,30},{16,0},... | collective-permute-start | bytes 1966088 | tf_op jit(solution)/shard_map/ppermute | solution.py:126
  568.9 11.6 %collective-permute-start.23 = (bf16[256,512]{1,0:T(8,128)(2,1)S(1)}, bf16[256,512]{1,0:T(8,128)(2,1)S(1)}, u32[]{:S(2)}, u32[]{:S(2)}) collective-permute-start(bf16[256,512]{1,0:T(8,128)(2,1)S(1)} %get-tuple-element.80), channel_id=1, source_target_pairs={{0,2},{2,0},{4,6},{6,4},{8,10},{10,8},{12,14},{14,12},{16,18},{18,... | collective-permute-start | bytes 786440 | tf_op jit(solution)/shard_map/ppermute | solution.py:126
  568.9 23.2 %copy-start.59 = (bf16[512,512]{1,0:T(8,128)(2,1)}, bf16[512,512]{1,0:T(8,128)(2,1)S(1)}, u32[]{:S(2)}) copy-start(bf16[512,512]{1,0:T(8,128)(2,1)S(1)} %collective-permute-done.26.refs_1_) | copy-start | bytes 1572868
  569.0 49.8 %collective-permute-start.38 = (bf16[128,768]{1,0:T(8,128)(2,1)}, bf16[128,768]{1,0:T(8,128)(2,1)}, u32[]{:S(2)}, u32[]{:S(2)}) collective-permute-start(bf16[128,768]{1,0:T(8,128)(2,1)} %shard_map.236.refs_3_), channel_id=1, source_target_pairs={{0,16},{2,18},{4,20},{6,22},{8,24},{10,26},{12,28},{14,30},{16,0},... | collective-permute-start | bytes 589832 | tf_op jit(solution)/shard_map/ppermute | solution.py:126
  571.2 20.9 %collective-permute-start.33 = (bf16[256,512]{1,0:T(8,128)(2,1)S(1)}, bf16[256,512]{1,0:T(8,128)(2,1)S(1)}, u32[]{:S(2)}, u32[]{:S(2)}) collective-permute-start(bf16[256,512]{1,0:T(8,128)(2,1)S(1)} %shard_map.237.refs_0_), channel_id=1, source_target_pairs={{0,8},{2,10},{4,12},{6,14},{8,0},{10,2},{12,4},{14,6},{16,24},{18,... | collective-permute-start | bytes 786440 | tf_op jit(solution)/shard_map/ppermute | solution.py:126
  572.8 19.4 %copy-start.44 = (bf16[2048,128]{1,0:T(8,128)(2,1)S(1)}, bf16[2048,128]{1,0:T(8,128)(2,1)}, u32[]{:S(2)}) copy-start(bf16[2048,128]{1,0:T(8,128)(2,1)} %shard_map.231.refs_0_.refs_1_.refs_2_.refs_3_.refs_4_) | copy-start | bytes 1572868
  580.4 36.2 %collective-permute-start.35 = (bf16[128,768]{1,0:T(8,128)(2,1)}, bf16[128,768]{1,0:T(8,128)(2,1)}, u32[]{:S(2)}, u32[]{:S(2)}) collective-permute-start(bf16[128,768]{1,0:T(8,128)(2,1)} %shard_map.235.refs_3_), channel_id=1, source_target_pairs={{0,16},{2,18},{4,20},{6,22},{8,24},{10,26},{12,28},{14,30},{16,0},... | collective-permute-start | bytes 589832 | tf_op jit(solution)/shard_map/ppermute | solution.py:126
  595.7 26.4 %collective-permute-start.37 = (bf16[128,512]{1,0:T(8,128)(2,1)}, bf16[128,512]{1,0:T(8,128)(2,1)}, u32[]{:S(2)}, u32[]{:S(2)}) collective-permute-start(bf16[128,512]{1,0:T(8,128)(2,1)} %shard_map.239.refs_0_), channel_id=1, source_target_pairs={{0,16},{2,18},{4,20},{6,22},{8,24},{10,26},{12,28},{14,30},{16,0},... | collective-permute-start | bytes 393224 | tf_op jit(solution)/shard_map/ppermute | solution.py:126
  625.3 5.6 collective-permute-start.39
  (113 other events, 405.8 us)
Sparse Core Ops, SparseCore 0:
  18.0 101.6 all-gather.2
  121.8 117.4 all-gather.4
  270.2 161.6 reduce-scatter.1

commit v6 on v5

--- a/solution.py
+++ b/solution.py
@@ -25,7 +25,7 @@
 SUM_ROWS = 16
 PARTS = 4
 ORDER = (
-    "D", "G", "FB", "U", "G", "FO", "U", "NB", "DA", "H", "H", "G",
+    "G", "D", "FB", "U", "G", "FO", "U", "NB", "DA", "H", "H", "G",
     "H", "HP", "QB", "Q", "OP", "O", "G", "Q", "O", "KB", "U", "IB",
     "G", "Q", "O", "GB", "K", "K", "U", "Q", "O", "K", "IG", "K",
     "AD", "D", "U", "Q", "O", "K",

time: 653 us -> 652 us (level)
    ppermute x29, waiting for transfers between devices: 63.7 us -> 78.1 us  [send(): self.got.append([lax.ppermute(part, 'dp', pairs) for part in sent])]
    ppermute x5, waiting for transfers between devices: 31.8 us -> 18.1 us  [other_tensor(): lax.ppermute(array, 'tensor', [(i, (i + 1) % count) for i in range(count)])]
    unnamed x277 -> x273, local copies, waits for them, and re-layouts: 64 us -> 58.9 us
  transfers between devices with their start and end apart: 43 -> 43, of which waited for: 17 -> 16; matrix products, arithmetic and copies ran while one was open for 9% -> 9% of each run, Pallas kernels for 33% -> 32%
where the time goes in v6:
time: 652 us; the launch traced here: 641 us
  Pallas kernels  243 us (37%)
  waiting for transfers between devices  209 us (32%)
  local copies, waits for them, and re-layouts  77.5 us (12%)
  starting transfers between devices  56.8 us (9%)
  matrix products  21.8 us (3%)
  other arithmetic  18.2 us (3%)
  between operations  15.5 us (2%)
    all_gather x1, waiting for transfers between devices, shards(): lax.all_gather(first_pack.astype(bf16), 'dp', axis=0, tiled=True)  89 us
    ppermute x29, waiting for transfers between devices, send(): self.got.append([lax.ppermute(part, 'dp', pairs) for part in sent])  78.1 us
    pallas_call x26, Pallas kernels, product(): pl.pallas_call(kernel, grid=(all_columns // tile,), in_specs=in_specs + [...  78.1 us
    unnamed x273, local copies, waits for them, and re-layouts  58.9 us
    ppermute x29, starting transfers between devices, send(): self.got.append([lax.ppermute(part, 'dp', pairs) for part in sent])  34.4 us
    pallas_call x3, Pallas kernels, attend_back(): pl.pallas_call(functools.partial(attend_back_kernel, keys - rows - WINDOW...  32.5 us
    pallas_call x1, Pallas kernels, feed(): pl.pallas_call(feed_kernel, grid=(steps,), in_specs=[pl.BlockSpec((rows,...  19.3 us
    ppermute x5, waiting for transfers between devices, other_tensor(): lax.ppermute(array, 'tensor', [(i, (i + 1) % count) for i in range(count)])  18.1 us
  transfers between devices with their start and end apart: 43, of which 16 were waited for; matrix products, arithmetic and copies ran while one was open for 9% of the time, Pallas kernels for 32%

profile of v6, /device:TPU:0, one launch (start us, length us, event | category | flops | bytes accessed | tf_op | source)
XLA Modules:
  0.0 641.5 jit_solution(11502627556062685168)
XLA Ops:
  20.1 2.4 collective-permute-start.3
  22.5 4.4 collective-permute-start.2
  28.2 2.4 fusion.16.bias_ref.refs_7_
  30.6 89.0 %all-gather.3.cloned.1.call-done.refs_0_.refs_1_.refs_2_.refs_3_.refs_4_.left_ref.weights_ref = bf16[2048,4608]{1,0:T(8,128)(2,1)} async-done(((bf16[128,4608]{1,0:T(8,128)(2,1)}), bf16[2048,4608]{1,0:T(8,128)(2,1)}) %all-gather.3.cloned.1.call-update) | async-done | bytes 18874384 | tf_op jit(solution)/shard_map/all_gather | solution.py:851
  122.7 5.8 fusion.5.raw_ref
  131.7 3.9 collective-permute-start
  135.6 3.1 collective-permute-start.1
  142.8 10.2 %collective-permute-done = bf16[384,512]{1,0:T(8,128)(2,1)} collective-permute-done((bf16[384,512]{1,0:T(8,128)(2,1)}, bf16[384,512]{1,0:T(8,128)(2,1)}, u32[]{:S(2)}, u32[]{:S(2)}) %collective-permute-start) | collective-permute-done | bytes 393248 | tf_op jit(solution)/shard_map/ppermute | solution.py:152
  160.9 13.2 %shard_map.195 = (bf16[768,512]{1,0:T(8,128)(2,1)S(1)}, f32[3,8,512]{2,1,0:T(8,128)S(1)}) custom-call(bf16[768,512]{1,0:T(8,128)(2,1)S(1)} %bitcast.71, bf16[3,1536,64]{2,1,0:T(8,128)(2,1)S(1)} %bitcast.64, bf16[3,80,1536]{2,1,0:T(8,128)(2,1)S(1)} %concatenate.29.v_ref, f32[1536,512]{1,0:T(8,128)S(1)} %copy-done.57), custom_call_target="tpu_custom_call" | custom-call | flops 5232500224 | tf_op jit(solution)/shard_map/pallas_call | solution.py:671
  174.2 5.4 fusion.17
  181.1 4.2 shard_map.197.left_ref
  187.1 4.9 shard_map.196.left_ref
  193.3 10.6 %fusion.2.d_act_ref = f32[512,2560]{1,0:T(8,128)} fusion(bf16[512,2048]{1,0:T(8,128)(2,1)} %direct_ref.1, bf16[2048,4608]{1,0:T(8,128)(2,1)} %all-gather.3.cloned.1.call-done.refs_0_.refs_1_.refs_2_.refs_3_.refs_4_.left_ref.weights_ref), kind=kOutput, calls=%fused_computation.5 | convolution fusion | flops 5368709120 | bytes 17825792 | tf_op jit(solution)/shard_map/dot_general | solution.py:164
  206.0 11.1 %collective-permute-done.4.refs_0_ = bf16[512,2048]{1,0:T(8,128)(2,1)} collective-permute-done((bf16[512,2048]{1,0:T(8,128)(2,1)}, bf16[512,2048]{1,0:T(8,128)(2,1)}, u32[]{:S(2)}, u32[]{:S(2)}) %collective-permute-start.4) | collective-permute-done | bytes 2097184 | tf_op jit(solution)/shard_map/ppermute | solution.py:138
  217.1 3.2 multiply_reduce_fusion
  224.1 4.8 shard_map.199.refs_0_.left_ref
  228.8 10.4 %all-gather.5.cloned.1.call-done.gate_ref.up_ref = bf16[2048,5120]{1,0:T(8,128)(2,1)} async-done(((bf16[128,5120]{1,0:T(8,128)(2,1)}), bf16[2048,5120]{1,0:T(8,128)(2,1)}) %all-gather.5.cloned.1.call-update) | async-done | bytes 20971536 | tf_op jit(solution)/shard_map/all_gather | solution.py:852
  239.3 19.3 %shard_map.200 = (bf16[512,2560]{1,0:T(8,128)(2,1)}, bf16[512,2560]{1,0:T(8,128)(2,1)}, bf16[512,2560]{1,0:T(8,128)(2,1)}) custom-call(bf16[512,2048]{1,0:T(8,128)(2,1)} %multiply_convert_fusion.in_ref.n_ref, f32[512,2560]{1,0:T(8,128)} %fusion.2.d_act_ref, bf16[2048,5120]{1,0:T(8,128)(2,1)} %all-gather.5.cloned.1.call-done.gate_ref.up_ref, ...), custom_call_target="tpu_custom_call" | custom-call | flops 7848750080 | tf_op jit(solution)/shard_map/pallas_call | solution.py:743
  260.4 4.1 shard_map.201.refs_0_
  264.4 9.7 %shard_map.202.refs_0_ = bf16[2048,2560]{1,0:T(8,128)(2,1)} custom-call(bf16[2048,512]{1,0:T(8,128)(2,1)S(1)} %copy-done.63, bf16[512,2560]{1,0:T(8,128)(2,1)S(1)} %copy-done.43, bf16[1024,2560]{1,0:T(8,128)(2,1)S(1)} %shard_map.201.refs_0_), custom_call_target="tpu_custom_call" | custom-call | flops 3206006016 | tf_op jit(solution)/shard_map/pallas_call | solution.py:276
  274.1 2.3 copy-done.31
  277.7 17.6 %shard_map.203.refs_0_.part_ref = bf16[512,2048]{1,0:T(8,128)(2,1)} custom-call(bf16[512,2560]{1,0:T(8,128)(2,1)} %get-tuple-element.52.right_ref.d_gate_ref, bf16[512,2560]{1,0:T(8,128)(2,1)} %get-tuple-element.53.d_up_ref.right_ref, bf16[2048,5120]{1,0:T(8,128)(2,1)} %all-gather.5.cloned.1.call-done.gate_ref.up_ref, ...), custom_call_target="tpu_custom_call" | custom-call | flops 6842500096 | tf_op jit(solution)/shard_map/pallas_call | solution.py:770
  295.3 5.4 shard_map.204.refs_1_
  302.2 5.5 shard_map.205.refs_5_
  307.7 13.7 %collective-permute-start.9 = (bf16[512,2560]{1,0:T(8,128)(2,1)}, bf16[512,2560]{1,0:T(8,128)(2,1)}, u32[]{:S(2)}, u32[]{:S(2)}) collective-permute-start(bf16[512,2560]{1,0:T(8,128)(2,1)} %shard_map.205.refs_5_), channel_id=1, source_target_pairs={{0,4},{2,6},{4,0},{6,2},{8,12},{10,14},{12,8},{14,10},{16,20},{18,... | collective-permute-start | bytes 7864328 | tf_op jit(solution)/shard_map/ppermute | solution.py:126
  322.8 12.3 %shard_map.206.refs_1_.part_ref = bf16[512,2048]{1,0:T(8,128)(2,1)} custom-call(bf16[512,2560]{1,0:T(8,128)(2,1)} %get-tuple-element.51.right_ref.act_ref, bf16[2048,4608]{1,0:T(8,128)(2,1)} %all-gather.3.cloned.1.call-done.refs_0_.refs_1_.refs_2_.refs_3_.refs_4_.left_ref.weights_ref, ...), custom_call_target="tpu_custom_call" | custom-call | flops 3622500096 | tf_op jit(solution)/shard_map/pallas_call | solution.py:800
  336.7 5.3 shard_map.208.refs_0_
  342.1 7.0 %collective-permute-done.6.refs_1_.other_ref = bf16[512,2048]{1,0:T(8,128)(2,1)} collective-permute-done((bf16[512,2048]{1,0:T(8,128)(2,1)}, bf16[512,2048]{1,0:T(8,128)(2,1)}, u32[]{:S(2)}, u32[]{:S(2)}) %collective-permute-start.6) | collective-permute-done | bytes 2097184 | tf_op jit(solution)/shard_map/ppermute | solution.py:138
  349.1 7.0 %shard_map.209 = (f32[512,2048]{1,0:T(8,128)}, bf16[512,2048]{1,0:T(8,128)(2,1)S(1)}, f32[1,2048]{1,0:T(1,128)S(1)}) custom-call(f32[512,2048]{1,0:T(8,128)} %copy-done.114, bf16[512,2048]{1,0:T(8,128)(2,1)S(1)} %copy-done.65, bf16[512,2048]{1,0:T(8,128)(2,1)} %shard_map.203.refs_0_.part_ref, bf16[512,2048]{1,0:T(8,128)(2,1)} %collective-permute-done.6.refs_1_.other_ref, ...), custom_call_target="tpu_custom_call" | custom-call | flops 2817499904 | tf_op jit(solution)/shard_map/pallas_call | solution.py:330
  356.1 4.5 shard_map.210.refs_4_.refs_8_
  360.9 10.7 %shard_map.211 = (f32[768,512]{1,0:T(8,128)S(1)}, f32[192,1536]{1,0:T(8,128)S(1)}, f32[192,1536]{1,0:T(8,128)S(1)}) custom-call(bf16[768,512]{1,0:T(8,128)(2,1)S(1)} %bitcast.72, bf16[3,1536,64]{2,1,0:T(8,128)(2,1)S(1)} %bitcast.65, bf16[192,1536]{1,0:T(8,128)(2,1)S(1)} %get-tuple-element.98.refs_2_, bf16[3,1536,64]{2,1,0:T(8,128)(2,1)S(1)} %bitcast.68, ...), custom_call_target="tpu_custom_call" | custom-call | flops 4427500032 | tf_op jit(solution)/shard_map/pallas_call | solution.py:698
  372.6 11.1 %shard_map.212 = (f32[768,512]{1,0:T(8,128)S(1)}, f32[192,1536]{1,0:T(8,128)S(1)}, f32[192,1536]{1,0:T(8,128)S(1)}) custom-call(bf16[768,512]{1,0:T(8,128)(2,1)S(1)} %bitcast.73, bf16[3,1536,64]{2,1,0:T(8,128)(2,1)S(1)} %bitcast.66, bf16[192,1536]{1,0:T(8,128)(2,1)S(1)} %copy-done.61, ...), custom_call_target="tpu_custom_call", output_to_operand_aliasing={{0}: (8, {}), {1}: (9, {}), {2}: (10, {})} | custom-call | flops 4427500032 | tf_op jit(solution)/shard_map/pallas_call | solution.py:698
  383.8 23.7 %collective-permute-done.9.refs_1_ = bf16[512,2560]{1,0:T(8,128)(2,1)} collective-permute-done((bf16[512,2560]{1,0:T(8,128)(2,1)}, bf16[512,2560]{1,0:T(8,128)(2,1)}, u32[]{:S(2)}, u32[]{:S(2)}) %collective-permute-start.9) | collective-permute-done | bytes 2621472 | tf_op jit(solution)/shard_map/ppermute | solution.py:126
  407.5 3.3 shard_map.213.refs_11_
  422.6 10.7 %shard_map.214 = (f32[768,512]{1,0:T(8,128)S(1)}, f32[192,1536]{1,0:T(8,128)S(1)}, f32[192,1536]{1,0:T(8,128)S(1)}) custom-call(bf16[768,512]{1,0:T(8,128)(2,1)S(1)} %bitcast.74, bf16[3,1536,64]{2,1,0:T(8,128)(2,1)S(1)} %bitcast.67, bf16[192,1536]{1,0:T(8,128)(2,1)S(1)} %copy-done.62, ...), custom_call_target="tpu_custom_call", output_to_operand_aliasing={{0}: (8, {}), {1}: (9, {}), {2}: (10, {})} | custom-call | flops 4427500032 | tf_op jit(solution)/shard_map/pallas_call | solution.py:698
  439.3 2.4 shard_map.217
  443.0 4.9 shard_map.219.left_ref.refs_0_
  450.6 2.2 shard_map.220
  455.4 6.7 %collective-permute-done.16.refs_2_ = bf16[256,2560]{1,0:T(8,128)(2,1)} collective-permute-done((bf16[256,2560]{1,0:T(8,128)(2,1)}, bf16[256,2560]{1,0:T(8,128)(2,1)}, u32[]{:S(2)}, u32[]{:S(2)}) %collective-permute-start.16) | collective-permute-done | bytes 1310752 | tf_op jit(solution)/shard_map/ppermute | solution.py:126
  466.1 3.1 shard_map.221.refs_2_
  469.2 2.7 shard_map.222.refs_2_
  473.2 2.7 shard_map.223.refs_2_
  475.9 2.4 collective-permute-done.10.refs_0_
  478.3 3.8 collective-permute-start.21
  484.3 3.4 shard_map.225.refs_0_
  487.7 8.2 %shard_map.226 = (bf16[512,2048]{1,0:T(8,128)(2,1)}, f32[1,2048]{1,0:T(1,128)S(1)}) custom-call(bf16[512,768]{1,0:T(8,128)(2,1)S(1)} %copy-done.37, bf16[512,384]{1,0:T(8,128)(2,1)S(1)} %get-tuple-element.72.refs_2_.d_keyval_ref.right_ref, bf16[2048,4608]{1,0:T(8,128)(2,1)} %all-gather.3.cloned.1.call-done.refs_0_.refs_1_.refs_2_.refs_3_.refs_4_.left_ref.weights_ref, ...), custom_call_target="tpu_custom_call" | custom-call | flops 3220000000 | tf_op jit(solution)/shard_map/pallas_call | solution.py:502
  500.1 9.3 %collective-permute-done.22.refs_3_ = bf16[128,2560]{1,0:T(8,128)(2,1)} collective-permute-done((bf16[128,2560]{1,0:T(8,128)(2,1)}, bf16[128,2560]{1,0:T(8,128)(2,1)}, u32[]{:S(2)}, u32[]{:S(2)}) %collective-permute-start.22) | collective-permute-done | bytes 655392 | tf_op jit(solution)/shard_map/ppermute | solution.py:126
  511.6 2.4 shard_map.227.refs_2_.first_ref
  519.0 2.1 shard_map.230.in_ref
  521.1 2.8 shard_map.231.refs_0_.refs_1_.refs_2_.refs_3_.refs_4_
  534.2 21.5 %collective-permute-done.31.refs_2_ = bf16[256,768]{1,0:T(8,128)(2,1)S(1)} collective-permute-done((bf16[256,768]{1,0:T(8,128)(2,1)S(1)}, bf16[256,768]{1,0:T(8,128)(2,1)S(1)}, u32[]{:S(2)}, u32[]{:S(2)}) %collective-permute-start.31) | collective-permute-done | bytes 393248 | tf_op jit(solution)/shard_map/ppermute | solution.py:126
  556.0 3.1 shard_map.234.refs_3_
  559.1 2.1 shard_map.235.refs_3_
  561.3 4.9 collective-permute-done.29.refs_2_
  572.9 7.6 %shard_map.238 = (f32[512,2048]{1,0:T(8,128)}, bf16[512,2048]{1,0:T(8,128)(2,1)}, f32[1,2048]{1,0:T(1,128)}) custom-call(bf16[512,2048]{1,0:T(8,128)(2,1)S(1)} %copy-done.24, f32[512,2048]{1,0:T(8,128)} %get-tuple-element.86.direct_ref, bf16[512,2048]{1,0:T(8,128)(2,1)} %get-tuple-element.79.refs_4_.part_ref, ...), custom_call_target="tpu_custom_call" | custom-call | flops 2817499904 | tf_op jit(solution)/shard_map/pallas_call | solution.py:330
  582.5 9.9 %collective-permute-done.33.refs_2_ = bf16[256,512]{1,0:T(8,128)(2,1)S(1)} collective-permute-done((bf16[256,512]{1,0:T(8,128)(2,1)S(1)}, bf16[256,512]{1,0:T(8,128)(2,1)S(1)}, u32[]{:S(2)}, u32[]{:S(2)}) %collective-permute-start.33) | collective-permute-done | bytes 262176 | tf_op jit(solution)/shard_map/ppermute | solution.py:126
  595.9 3.1 collective-permute-start.37
  598.9 5.3 shard_map.240.refs_0_
  604.2 4.0 shard_map.241.refs_4_
  611.8 2.4 shard_map.242.refs_4_.second_ref
  614.4 2.7 shard_map.243.refs_4_
  618.2 2.2 shard_map.244.refs_5_
  621.4 2.1 shard_map.245
  625.5 4.1 shard_map.247
  (421 shorter events, 129.5 us)
Async XLA Ops:
  7.2 112.4 %all-gather.3.cloned.1.call-start = ((), (), s32[]{:S(2)}) async-start(), calls=%async_computation.1 | async-start | bytes 20054016 | tf_op jit(solution)/shard_map/all_gather | solution.py:851
  17.8 221.5 %all-gather.5.cloned.1.call-start = ((), (), s32[]{:S(2)}) async-start(), calls=%async_computation.2 | async-start | bytes 22282240 | tf_op jit(solution)/shard_map/all_gather | solution.py:852
  20.0 584.1 %reduce-scatter.2.cloned.1.call-start = ((), (), s32[]{:S(2)}) async-start(), calls=%async_computation.3 | async-start | bytes 11141120 | tf_op jit(solution)/shard_map/reduce_scatter | solution.py:946
  20.1 7.8 %collective-permute-start.3 = (bf16[512]{0:T(512)(128)(2,1)S(1)}, bf16[512]{0:T(512)(128)(2,1)S(1)}, u32[]{:S(2)}, u32[]{:S(2)}) collective-permute-start(bf16[512]{0:T(512)(128)(2,1)S(1)} %add_convert_fusion.2), channel_id=1, source_target_pairs={{0,2},{2,4},{4,6},{6,8},{8,10},{10,12},{12,14},{14,16},{16,18},{18... | collective-permute-start | bytes 3080 | tf_op jit(solution)/shard_map/ppermute | solution.py:152
  22.5 5.7 collective-permute-start.2
  27.5 94.6 %copy-start.124 = (f32[512]{0:T(512)}, f32[512]{0:T(512)S(1)}, u32[]{:S(2)}) copy-start(f32[512]{0:T(512)S(1)} %add_rsqrt_fusion.3) | copy-start | bytes 6148
  27.9 114.6 %copy-start.66 = (f32[32,512]{1,0:T(8,128)}, f32[32,512]{1,0:T(8,128)S(1)}, u32[]{:S(2)}) copy-start(f32[32,512]{1,0:T(8,128)S(1)} %get-tuple-element.106.sin_ref) | copy-start | bytes 196612
  131.7 21.4 %collective-permute-start = (bf16[384,512]{1,0:T(8,128)(2,1)}, bf16[384,512]{1,0:T(8,128)(2,1)}, u32[]{:S(2)}, u32[]{:S(2)}) collective-permute-start(bf16[384,512]{1,0:T(8,128)(2,1)} %pad_maximum_fusion.1), channel_id=1, source_target_pairs={{0,4},{2,6},{4,8},{6,10},{8,12},{10,14},{12,16},{14,18},{16,20},{1... | collective-permute-start | bytes 1179656 | tf_op jit(solution)/shard_map/ppermute | solution.py:152
  135.6 17.4 %collective-permute-start.1 = (bf16[384,512]{1,0:T(8,128)(2,1)}, bf16[384,512]{1,0:T(8,128)(2,1)}, u32[]{:S(2)}, u32[]{:S(2)}) collective-permute-start(bf16[384,512]{1,0:T(8,128)(2,1)} %pad_maximum_fusion.1), channel_id=1, source_target_pairs={{0,2},{2,4},{4,6},{6,8},{8,10},{10,12},{12,14},{14,16},{16,18},{18... | collective-permute-start | bytes 1179656 | tf_op jit(solution)/shard_map/ppermute | solution.py:152
  142.8 14.9 %copy-start.92 = (bf16[12,64,512]{2,1,0:T(8,128)(2,1)}, bf16[12,64,512]{2,1,0:T(8,128)(2,1)S(1)}, u32[]{:S(2)}) copy-start(bf16[12,64,512]{2,1,0:T(8,128)(2,1)S(1)} %pad_maximum_fusion) | copy-start | bytes 2359300
  155.2 205.5 %copy-start.60 = (bf16[192,1536]{1,0:T(8,128)(2,1)}, bf16[192,1536]{1,0:T(8,128)(2,1)S(1)}, u32[]{:S(2)}) copy-start(bf16[192,1536]{1,0:T(8,128)(2,1)S(1)} %get-tuple-element.98.refs_2_) | copy-start | bytes 1769476
  179.6 37.6 %collective-permute-start.4 = (bf16[512,2048]{1,0:T(8,128)(2,1)}, bf16[512,2048]{1,0:T(8,128)(2,1)}, u32[]{:S(2)}, u32[]{:S(2)}) collective-permute-start(bf16[512,2048]{1,0:T(8,128)(2,1)} %fusion.17), channel_id=1, source_target_pairs={{0,1},{1,0},{2,3},{3,2},{4,5},{5,4},{6,7},{7,6},{8,9},{9,8},{10,11... | collective-permute-start | bytes 6291464 | tf_op jit(solution)/shard_map/ppermute | solution.py:138
  205.4 11.8 %copy-start.27 = (bf16[768,512]{0,1:T(8,128)(2,1)}, bf16[768,512]{0,1:T(8,128)(2,1)S(1)}, u32[]{:S(2)}) copy-start(bf16[768,512]{0,1:T(8,128)(2,1)S(1)} %copy.76) | copy-start | bytes 2359300
  228.8 29.8 %copy-start = (bf16[2048,512]{1,0:T(8,128)(2,1)S(1)}, bf16[2048,512]{1,0:T(8,128)(2,1)}, u32[]{:S(2)}) copy-start(bf16[2048,512]{1,0:T(8,128)(2,1)} %shard_map.199.refs_0_.left_ref) | copy-start | bytes 6291460
  276.5 25.7 %collective-permute-start.5 = (bf16[1024,2560]{1,0:T(8,128)(2,1)}, bf16[1024,2560]{1,0:T(8,128)(2,1)}, u32[]{:S(2)}, u32[]{:S(2)}) collective-permute-start(bf16[1024,2560]{1,0:T(8,128)(2,1)} %copy-done.31), channel_id=1, source_target_pairs={{0,2},{2,0},{4,6},{6,4},{8,10},{10,8},{12,14},{14,12},{16,18},{18,... | collective-permute-start | bytes 15728648 | tf_op jit(solution)/shard_map/ppermute | solution.py:126
  277.7 17.6 %copy-start.12 = (bf16[512,2560]{1,0:T(8,128)(2,1)S(1)}, bf16[512,2560]{1,0:T(8,128)(2,1)}, u32[]{:S(2)}) copy-start(bf16[512,2560]{1,0:T(8,128)(2,1)} %get-tuple-element.53.d_up_ref.right_ref) | copy-start | bytes 7864324
  300.7 20.7 %copy-start.116 = (bf16[192,1536]{1,0:T(8,128)(2,1)S(1)}, bf16[192,1536]{1,0:T(8,128)(2,1)}, u32[]{:S(2)}) copy-start(bf16[192,1536]{1,0:T(8,128)(2,1)} %get-tuple-element.97) | copy-start | bytes 1769476
  300.7 34.4 %collective-permute-start.8 = (bf16[1024,2560]{1,0:T(8,128)(2,1)}, bf16[1024,2560]{1,0:T(8,128)(2,1)}, u32[]{:S(2)}, u32[]{:S(2)}) collective-permute-start(bf16[1024,2560]{1,0:T(8,128)(2,1)} %shard_map.204.refs_1_), channel_id=1, source_target_pairs={{0,2},{2,0},{4,6},{6,4},{8,10},{10,8},{12,14},{14,12},{16,18},{18,... | collective-permute-start | bytes 15728648 | tf_op jit(solution)/shard_map/ppermute | solution.py:126
  300.7 48.4 %collective-permute-start.6 = (bf16[512,2048]{1,0:T(8,128)(2,1)}, bf16[512,2048]{1,0:T(8,128)(2,1)}, u32[]{:S(2)}, u32[]{:S(2)}) collective-permute-start(bf16[512,2048]{1,0:T(8,128)(2,1)} %shard_map.203.refs_0_.part_ref), channel_id=1, source_target_pairs={{0,1},{1,0},{2,3},{3,2},{4,5},{5,4},{6,7},{7,6},{8,9},{9,8},{10,11... | collective-permute-start | bytes 6291464 | tf_op jit(solution)/shard_map/ppermute | solution.py:138
  307.7 99.8 %collective-permute-start.9 = (bf16[512,2560]{1,0:T(8,128)(2,1)}, bf16[512,2560]{1,0:T(8,128)(2,1)}, u32[]{:S(2)}, u32[]{:S(2)}) collective-permute-start(bf16[512,2560]{1,0:T(8,128)(2,1)} %shard_map.205.refs_5_), channel_id=1, source_target_pairs={{0,4},{2,6},{4,0},{6,2},{8,12},{10,14},{12,8},{14,10},{16,20},{18,... | collective-permute-start | bytes 7864328 | tf_op jit(solution)/shard_map/ppermute | solution.py:126
  322.8 12.3 %copy-start.13 = (bf16[512,2560]{1,0:T(8,128)(2,1)S(1)}, bf16[512,2560]{1,0:T(8,128)(2,1)}, u32[]{:S(2)}) copy-start(bf16[512,2560]{1,0:T(8,128)(2,1)} %get-tuple-element.53.d_up_ref.right_ref) | copy-start | bytes 7864324
  336.7 12.4 %copy-start.65 = (bf16[512,2048]{1,0:T(8,128)(2,1)S(1)}, bf16[512,2048]{1,0:T(8,128)(2,1)}, u32[]{:S(2)}) copy-start(bf16[512,2048]{1,0:T(8,128)(2,1)} %direct_ref.1) | copy-start | bytes 6291460
  342.0 141.7 %collective-permute-start.17 = (bf16[512,2560]{1,0:T(8,128)(2,1)}, bf16[512,2560]{1,0:T(8,128)(2,1)}, u32[]{:S(2)}, u32[]{:S(2)}) collective-permute-start(bf16[512,2560]{1,0:T(8,128)(2,1)} %shard_map.208.refs_0_), channel_id=1, source_target_pairs={{0,4},{2,6},{4,0},{6,2},{8,12},{10,14},{12,8},{14,10},{16,20},{18,... | collective-permute-start | bytes 7864328 | tf_op jit(solution)/shard_map/ppermute | solution.py:126
  372.6 34.9 %copy-start.9 = (bf16[512,2560]{1,0:T(8,128)(2,1)S(1)}, bf16[512,2560]{1,0:T(8,128)(2,1)}, u32[]{:S(2)}) copy-start(bf16[512,2560]{1,0:T(8,128)(2,1)} %get-tuple-element.52.right_ref.d_gate_ref) | copy-start | bytes 7864324
  383.8 27.0 %copy-start.51 = (f32[192,1536]{1,0:T(8,128)}, f32[192,1536]{1,0:T(8,128)S(1)}, u32[]{:S(2)}) copy-start(f32[192,1536]{1,0:T(8,128)S(1)} %get-tuple-element.61.refs_10_) | copy-start | bytes 3538948
  383.8 27.0 %copy-start.70 = (f32[768,512]{1,0:T(8,128)}, f32[768,512]{1,0:T(8,128)S(1)}, u32[]{:S(2)}) copy-start(f32[768,512]{1,0:T(8,128)S(1)} %get-tuple-element.59.refs_8_) | copy-start | bytes 4718596
  410.8 51.2 %collective-permute-start.16 = (bf16[256,2560]{1,0:T(8,128)(2,1)}, bf16[256,2560]{1,0:T(8,128)(2,1)}, u32[]{:S(2)}, u32[]{:S(2)}) collective-permute-start(bf16[256,2560]{1,0:T(8,128)(2,1)} %shard_map.213.refs_11_), channel_id=1, source_target_pairs={{0,8},{2,10},{4,12},{6,14},{8,0},{10,2},{12,4},{14,6},{16,24},{18,... | collective-permute-start | bytes 3932168 | tf_op jit(solution)/shard_map/ppermute | solution.py:126
  442.5 11.1 %collective-permute-start.14 = (bf16[256,768]{1,0:T(8,128)(2,1)}, bf16[256,768]{1,0:T(8,128)(2,1)}, u32[]{:S(2)}, u32[]{:S(2)}) collective-permute-start(bf16[256,768]{1,0:T(8,128)(2,1)} %get-tuple-element.68.refs_1_), channel_id=1, source_target_pairs={{0,2},{2,0},{4,6},{6,4},{8,10},{10,8},{12,14},{14,12},{16,18},{18,... | collective-permute-start | bytes 1179656 | tf_op jit(solution)/shard_map/ppermute | solution.py:126
  442.5 11.6 %collective-permute-start.15 = (bf16[256,768]{1,0:T(8,128)(2,1)}, bf16[256,768]{1,0:T(8,128)(2,1)}, u32[]{:S(2)}, u32[]{:S(2)}) collective-permute-start(bf16[256,768]{1,0:T(8,128)(2,1)} %get-tuple-element.71), channel_id=1, source_target_pairs={{0,2},{2,0},{4,6},{6,4},{8,10},{10,8},{12,14},{14,12},{16,18},{18,... | collective-permute-start | bytes 1179656 | tf_op jit(solution)/shard_map/ppermute | solution.py:126
  450.6 12.8 %copy-start.125 = (f32[512]{0:T(512)S(1)}, f32[512]{0:T(512)}, u32[]{:S(2)}) copy-start(f32[512]{0:T(512)} %copy-done.124) | copy-start | bytes 6148
  450.6 13.7 %copy-start.123 = (f32[1,16,4]{2,1,0:T(8,128)S(1)}, f32[1,16,4]{2,1,0:T(8,128)}, u32[]{:S(2)}) copy-start(f32[1,16,4]{2,1,0:T(8,128)} %copy-done.122) | copy-start | bytes 772
  453.6 18.3 %collective-permute-start.12 = (bf16[256,768]{1,0:T(8,128)(2,1)}, bf16[256,768]{1,0:T(8,128)(2,1)}, u32[]{:S(2)}, u32[]{:S(2)}) collective-permute-start(bf16[256,768]{1,0:T(8,128)(2,1)} %get-tuple-element.69.refs_3_), channel_id=1, source_target_pairs={{0,2},{2,0},{4,6},{6,4},{8,10},{10,8},{12,14},{14,12},{16,18},{18,... | collective-permute-start | bytes 1179656 | tf_op jit(solution)/shard_map/ppermute | solution.py:126
  453.6 19.5 %collective-permute-start.13 = (bf16[256,768]{1,0:T(8,128)(2,1)}, bf16[256,768]{1,0:T(8,128)(2,1)}, u32[]{:S(2)}, u32[]{:S(2)}) collective-permute-start(bf16[256,768]{1,0:T(8,128)(2,1)} %get-tuple-element.70), channel_id=1, source_target_pairs={{0,2},{2,0},{4,6},{6,4},{8,10},{10,8},{12,14},{14,12},{16,18},{18,... | collective-permute-start | bytes 1179656 | tf_op jit(solution)/shard_map/ppermute | solution.py:126
  454.1 24.2 %collective-permute-start.10 = (bf16[384,512]{1,0:T(8,128)(2,1)}, bf16[384,512]{1,0:T(8,128)(2,1)}, u32[]{:S(2)}, u32[]{:S(2)}) collective-permute-start(bf16[384,512]{1,0:T(8,128)(2,1)} %get-tuple-element.64.refs_0_), channel_id=1, source_target_pairs={{4,0},{6,2},{8,4},{10,6},{12,8},{14,10},{16,12},{18,14},{20,16},{2... | collective-permute-start | bytes 1179656 | tf_op jit(solution)/shard_map/ppermute | solution.py:152
  462.1 16.2 %collective-permute-start.11 = (bf16[384,512]{1,0:T(8,128)(2,1)}, bf16[384,512]{1,0:T(8,128)(2,1)}, u32[]{:S(2)}, u32[]{:S(2)}) collective-permute-start(bf16[384,512]{1,0:T(8,128)(2,1)} %get-tuple-element.65), channel_id=1, source_target_pairs={{2,0},{4,2},{6,4},{8,6},{10,8},{12,10},{14,12},{16,14},{18,16},{20... | collective-permute-start | bytes 1179656 | tf_op jit(solution)/shard_map/ppermute | solution.py:152
  471.9 24.6 %collective-permute-start.20 = (bf16[256,768]{1,0:T(8,128)(2,1)S(1)}, bf16[256,768]{1,0:T(8,128)(2,1)S(1)}, u32[]{:S(2)}, u32[]{:S(2)}) collective-permute-start(bf16[256,768]{1,0:T(8,128)(2,1)S(1)} %copy-done.111), channel_id=1, source_target_pairs={{0,2},{2,0},{4,6},{6,4},{8,10},{10,8},{12,14},{14,12},{16,18},{18,... | collective-permute-start | bytes 1179656 | tf_op jit(solution)/shard_map/ppermute | solution.py:126
  473.1 43.1 %collective-permute-start.18 = (bf16[256,768]{1,0:T(8,128)(2,1)}, bf16[256,768]{1,0:T(8,128)(2,1)}, u32[]{:S(2)}, u32[]{:S(2)}) collective-permute-start(bf16[256,768]{1,0:T(8,128)(2,1)} %get-tuple-element.77), channel_id=1, source_target_pairs={{0,2},{2,0},{4,6},{6,4},{8,10},{10,8},{12,14},{14,12},{16,18},{18,... | collective-permute-start | bytes 1179656 | tf_op jit(solution)/shard_map/ppermute | solution.py:126
  478.3 31.1 %collective-permute-start.22 = (bf16[128,2560]{1,0:T(8,128)(2,1)}, bf16[128,2560]{1,0:T(8,128)(2,1)}, u32[]{:S(2)}, u32[]{:S(2)}) collective-permute-start(bf16[128,2560]{1,0:T(8,128)(2,1)} %shard_map.221.refs_2_), channel_id=1, source_target_pairs={{0,16},{2,18},{4,20},{6,22},{8,24},{10,26},{12,28},{14,30},{16,0},... | collective-permute-start | bytes 1966088 | tf_op jit(solution)/shard_map/ppermute | solution.py:126
  478.3 35.7 %collective-permute-start.21 = (bf16[512,768]{1,0:T(8,128)(2,1)}, bf16[512,768]{1,0:T(8,128)(2,1)}, u32[]{:S(2)}, u32[]{:S(2)}) collective-permute-start(bf16[512,768]{1,0:T(8,128)(2,1)} %shard_map.222.refs_2_), channel_id=1, source_target_pairs={{0,4},{2,6},{4,0},{6,2},{8,12},{10,14},{12,8},{14,10},{16,20},{18,... | collective-permute-start | bytes 2359304 | tf_op jit(solution)/shard_map/ppermute | solution.py:126
  483.7 33.1 %collective-permute-start.19 = (bf16[512,768]{1,0:T(8,128)(2,1)}, bf16[512,768]{1,0:T(8,128)(2,1)}, u32[]{:S(2)}, u32[]{:S(2)}) collective-permute-start(bf16[512,768]{1,0:T(8,128)(2,1)} %shard_map.223.refs_2_), channel_id=1, source_target_pairs={{0,4},{2,6},{4,0},{6,2},{8,12},{10,14},{12,8},{14,10},{16,20},{18,... | collective-permute-start | bytes 2359304 | tf_op jit(solution)/shard_map/ppermute | solution.py:126
  497.3 75.0 %collective-permute-start.34 = (bf16[512,2048]{1,0:T(8,128)(2,1)}, bf16[512,2048]{1,0:T(8,128)(2,1)}, u32[]{:S(2)}, u32[]{:S(2)}) collective-permute-start(bf16[512,2048]{1,0:T(8,128)(2,1)} %get-tuple-element.79.refs_4_.part_ref), channel_id=1, source_target_pairs={{0,1},{1,0},{2,3},{3,2},{4,5},{5,4},{6,7},{7,6},{8,9},{9,8},{10,11... | collective-permute-start | bytes 6291464 | tf_op jit(solution)/shard_map/ppermute | solution.py:138
  500.1 14.0 %copy-start.101 = (bf16[256,768]{1,0:T(8,128)(2,1)S(1)}, bf16[256,768]{1,0:T(8,128)(2,1)}, u32[]{:S(2)}) copy-start(bf16[256,768]{1,0:T(8,128)(2,1)} %copy-done.100) | copy-start | bytes 1179652
  500.1 14.0 %copy-start.3 = (bf16[2048,512]{1,0:T(8,128)(2,1)S(1)}, bf16[2048,512]{1,0:T(8,128)(2,1)}, u32[]{:S(2)}) copy-start(bf16[2048,512]{1,0:T(8,128)(2,1)} %shard_map.196.left_ref) | copy-start | bytes 6291460
  509.4 89.5 %collective-permute-start.7 = (bf16[512,2048]{1,0:T(8,128)(2,1)}, bf16[512,2048]{1,0:T(8,128)(2,1)}, u32[]{:S(2)}, u32[]{:S(2)}) collective-permute-start(bf16[512,2048]{1,0:T(8,128)(2,1)} %shard_map.207), channel_id=1, source_target_pairs={{0,1},{1,0},{2,3},{3,2},{4,5},{5,4},{6,7},{7,6},{8,9},{9,8},{10,11... | collective-permute-start | bytes 6291464 | tf_op jit(solution)/shard_map/ppermute | solution.py:138
  514.1 15.3 %collective-permute-start.30 = (bf16[256,768]{1,0:T(8,128)(2,1)}, bf16[256,768]{1,0:T(8,128)(2,1)}, u32[]{:S(2)}, u32[]{:S(2)}) collective-permute-start(bf16[256,768]{1,0:T(8,128)(2,1)} %get-tuple-element.85), channel_id=1, source_target_pairs={{0,2},{2,0},{4,6},{6,4},{8,10},{10,8},{12,14},{14,12},{16,18},{18,... | collective-permute-start | bytes 1179656 | tf_op jit(solution)/shard_map/ppermute | solution.py:126
  516.1 39.9 %collective-permute-start.32 = (bf16[256,2560]{1,0:T(8,128)(2,1)}, bf16[256,2560]{1,0:T(8,128)(2,1)}, u32[]{:S(2)}, u32[]{:S(2)}) collective-permute-start(bf16[256,2560]{1,0:T(8,128)(2,1)} %shard_map.225.refs_0_), channel_id=1, source_target_pairs={{0,8},{2,10},{4,12},{6,14},{8,0},{10,2},{12,4},{14,6},{16,24},{18,... | collective-permute-start | bytes 3932168 | tf_op jit(solution)/shard_map/ppermute | solution.py:126
  528.3 2.2 collective-permute-start.24
  529.4 1.5 collective-permute-start.25
  530.5 25.2 %copy-start.75 = (bf16[256,768]{1,0:T(8,128)(2,1)S(1)}, bf16[256,768]{1,0:T(8,128)(2,1)}, u32[]{:S(2)}) copy-start(bf16[256,768]{1,0:T(8,128)(2,1)} %copy-done.74) | copy-start | bytes 1179652
  530.5 25.5 %copy-start.15 = (bf16[512,2560]{1,0:T(8,128)(2,1)S(1)}, bf16[512,2560]{1,0:T(8,128)(2,1)}, u32[]{:S(2)}) copy-start(bf16[512,2560]{1,0:T(8,128)(2,1)} %get-tuple-element.53.d_up_ref.right_ref) | copy-start | bytes 7864324
  530.5 2.6 collective-permute-start.28
  530.9 24.8 %collective-permute-start.31 = (bf16[256,768]{1,0:T(8,128)(2,1)S(1)}, bf16[256,768]{1,0:T(8,128)(2,1)S(1)}, u32[]{:S(2)}, u32[]{:S(2)}) collective-permute-start(bf16[256,768]{1,0:T(8,128)(2,1)S(1)} %copy-done.69), channel_id=1, source_target_pairs={{0,8},{2,10},{4,12},{6,14},{8,0},{10,2},{12,4},{14,6},{16,24},{18,... | collective-permute-start | bytes 1179656 | tf_op jit(solution)/shard_map/ppermute | solution.py:126
  533.1 34.1 %copy-start.76 = (bf16[256,768]{1,0:T(8,128)(2,1)}, bf16[256,768]{1,0:T(8,128)(2,1)S(1)}, u32[]{:S(2)}) copy-start(bf16[256,768]{1,0:T(8,128)(2,1)S(1)} %collective-permute-done.28.refs_0_) | copy-start | bytes 1179652
  533.1 36.0 %collective-permute-start.26 = (bf16[512,512]{1,0:T(8,128)(2,1)S(1)}, bf16[512,512]{1,0:T(8,128)(2,1)S(1)}, u32[]{:S(2)}, u32[]{:S(2)}) collective-permute-start(bf16[512,512]{1,0:T(8,128)(2,1)S(1)} %shard_map.233.refs_3_), channel_id=1, source_target_pairs={{0,4},{2,6},{4,0},{6,2},{8,12},{10,14},{12,8},{14,10},{16,20},{18,... | collective-permute-start | bytes 1572872 | tf_op jit(solution)/shard_map/ppermute | solution.py:126
  555.7 10.5 %collective-permute-start.29 = (bf16[256,768]{1,0:T(8,128)(2,1)S(1)}, bf16[256,768]{1,0:T(8,128)(2,1)S(1)}, u32[]{:S(2)}, u32[]{:S(2)}) collective-permute-start(bf16[256,768]{1,0:T(8,128)(2,1)S(1)} %copy-done.75), channel_id=1, source_target_pairs={{0,8},{2,10},{4,12},{6,14},{8,0},{10,2},{12,4},{14,6},{16,24},{18,... | collective-permute-start | bytes 1179656 | tf_op jit(solution)/shard_map/ppermute | solution.py:126
  556.0 13.0 %collective-permute-start.27 = (bf16[256,512]{1,0:T(8,128)(2,1)S(1)}, bf16[256,512]{1,0:T(8,128)(2,1)S(1)}, u32[]{:S(2)}, u32[]{:S(2)}) collective-permute-start(bf16[256,512]{1,0:T(8,128)(2,1)S(1)} %get-tuple-element.83), channel_id=1, source_target_pairs={{0,2},{2,0},{4,6},{6,4},{8,10},{10,8},{12,14},{14,12},{16,18},{18,... | collective-permute-start | bytes 786440 | tf_op jit(solution)/shard_map/ppermute | solution.py:126
  566.2 42.4 %collective-permute-start.36 = (bf16[128,2560]{1,0:T(8,128)(2,1)}, bf16[128,2560]{1,0:T(8,128)(2,1)}, u32[]{:S(2)}, u32[]{:S(2)}) collective-permute-start(bf16[128,2560]{1,0:T(8,128)(2,1)} %shard_map.234.refs_3_), channel_id=1, source_target_pairs={{0,16},{2,18},{4,20},{6,22},{8,24},{10,26},{12,28},{14,30},{16,0},... | collective-permute-start | bytes 1966088 | tf_op jit(solution)/shard_map/ppermute | solution.py:126
  569.1 11.5 %collective-permute-start.23 = (bf16[256,512]{1,0:T(8,128)(2,1)S(1)}, bf16[256,512]{1,0:T(8,128)(2,1)S(1)}, u32[]{:S(2)}, u32[]{:S(2)}) collective-permute-start(bf16[256,512]{1,0:T(8,128)(2,1)S(1)} %get-tuple-element.80), channel_id=1, source_target_pairs={{0,2},{2,0},{4,6},{6,4},{8,10},{10,8},{12,14},{14,12},{16,18},{18,... | collective-permute-start | bytes 786440 | tf_op jit(solution)/shard_map/ppermute | solution.py:126
  569.2 23.2 %copy-start.55 = (bf16[512,512]{1,0:T(8,128)(2,1)}, bf16[512,512]{1,0:T(8,128)(2,1)S(1)}, u32[]{:S(2)}) copy-start(bf16[512,512]{1,0:T(8,128)(2,1)S(1)} %collective-permute-done.26.refs_1_) | copy-start | bytes 1572868
  569.2 45.1 %collective-permute-start.35 = (bf16[128,768]{1,0:T(8,128)(2,1)}, bf16[128,768]{1,0:T(8,128)(2,1)}, u32[]{:S(2)}, u32[]{:S(2)}) collective-permute-start(bf16[128,768]{1,0:T(8,128)(2,1)} %shard_map.235.refs_3_), channel_id=1, source_target_pairs={{0,16},{2,18},{4,20},{6,22},{8,24},{10,26},{12,28},{14,30},{16,0},... | collective-permute-start | bytes 589832 | tf_op jit(solution)/shard_map/ppermute | solution.py:126
  572.3 20.1 %collective-permute-start.33 = (bf16[256,512]{1,0:T(8,128)(2,1)S(1)}, bf16[256,512]{1,0:T(8,128)(2,1)S(1)}, u32[]{:S(2)}, u32[]{:S(2)}) collective-permute-start(bf16[256,512]{1,0:T(8,128)(2,1)S(1)} %shard_map.237.refs_0_), channel_id=1, source_target_pairs={{0,8},{2,10},{4,12},{6,14},{8,0},{10,2},{12,4},{14,6},{16,24},{18,... | collective-permute-start | bytes 786440 | tf_op jit(solution)/shard_map/ppermute | solution.py:126
  580.5 36.5 %collective-permute-start.38 = (bf16[128,768]{1,0:T(8,128)(2,1)}, bf16[128,768]{1,0:T(8,128)(2,1)}, u32[]{:S(2)}, u32[]{:S(2)}) collective-permute-start(bf16[128,768]{1,0:T(8,128)(2,1)} %shard_map.236.refs_3_), channel_id=1, source_target_pairs={{0,16},{2,18},{4,20},{6,22},{8,24},{10,26},{12,28},{14,30},{16,0},... | collective-permute-start | bytes 589832 | tf_op jit(solution)/shard_map/ppermute | solution.py:126
  595.9 24.5 %collective-permute-start.37 = (bf16[128,512]{1,0:T(8,128)(2,1)}, bf16[128,512]{1,0:T(8,128)(2,1)}, u32[]{:S(2)}, u32[]{:S(2)}) collective-permute-start(bf16[128,512]{1,0:T(8,128)(2,1)} %shard_map.239.refs_0_), channel_id=1, source_target_pairs={{0,16},{2,18},{4,20},{6,22},{8,24},{10,26},{12,28},{14,30},{16,0},... | collective-permute-start | bytes 393224 | tf_op jit(solution)/shard_map/ppermute | solution.py:126
  623.5 6.1 collective-permute-start.39
  (111 other events, 383.2 us)
Sparse Core Ops, SparseCore 0:
  17.9 101.6 all-gather.2
  121.8 117.4 all-gather.4
  276.6 176.3 reduce-scatter.1

commit v7 on v6

--- a/solution.py
+++ b/solution.py
@@ -25,7 +25,7 @@
 SUM_ROWS = 16
 PARTS = 4
 ORDER = (
-    "G", "D", "FB", "U", "G", "FO", "U", "NB", "DA", "H", "H", "G",
+    "G", "D", "FB", "G", "U", "FO", "U", "NB", "DA", "H", "H", "G",
     "H", "HP", "QB", "Q", "OP", "O", "G", "Q", "O", "KB", "U", "IB",
     "G", "Q", "O", "GB", "K", "K", "U", "Q", "O", "K", "IG", "K",
     "AD", "D", "U", "Q", "O", "K",

time: 652 us -> 651 us (level)
    ppermute x29, waiting for transfers between devices: 78.1 us -> 68.5 us  [send(): self.got.append([lax.ppermute(part, 'dp', pairs) for part in sent])]
  transfers between devices with their start and end apart: 43 -> 43, of which waited for: 16 -> 16; matrix products, arithmetic and copies ran while one was open for 9% -> 9% of each run, Pallas kernels for 32% -> 34%
where the time goes in v7:
time: 651 us; the launch traced here: 641 us
  Pallas kernels  245 us (38%)
  waiting for transfers between devices  206 us (32%)
  local copies, waits for them, and re-layouts  77.6 us (12%)
  starting transfers between devices  57.6 us (9%)
  matrix products  21.5 us (3%)
  other arithmetic  18.3 us (3%)
  between operations  15.5 us (2%)
    all_gather x1, waiting for transfers between devices, shards(): lax.all_gather(first_pack.astype(bf16), 'dp', axis=0, tiled=True)  89 us
    pallas_call x26, Pallas kernels, product(): pl.pallas_call(kernel, grid=(all_columns // tile,), in_specs=in_specs + [...  79.7 us
    ppermute x29, waiting for transfers between devices, send(): self.got.append([lax.ppermute(part, 'dp', pairs) for part in sent])  68.5 us
    unnamed x273, local copies, waits for them, and re-layouts  58.9 us
    ppermute x29, starting transfers between devices, send(): self.got.append([lax.ppermute(part, 'dp', pairs) for part in sent])  35.5 us
    pallas_call x3, Pallas kernels, attend_back(): pl.pallas_call(functools.partial(attend_back_kernel, keys - rows - WINDOW...  32.5 us
    ppermute x5, waiting for transfers between devices, other_tensor(): lax.ppermute(array, 'tensor', [(i, (i + 1) % count) for i in range(count)])  22.8 us
    pallas_call x1, Pallas kernels, feed(): pl.pallas_call(feed_kernel, grid=(steps,), in_specs=[pl.BlockSpec((rows,...  19.3 us
  transfers between devices with their start and end apart: 43, of which 16 were waited for; matrix products, arithmetic and copies ran while one was open for 9% of the time, Pallas kernels for 34%

profile of v7, /device:TPU:0, one launch (start us, length us, event | category | flops | bytes accessed | tf_op | source)
XLA Modules:
  0.0 641.4 jit_solution(4227361648436478949)
XLA Ops:
  20.1 2.4 collective-permute-start.3
  22.5 4.4 collective-permute-start.2
  28.2 2.4 fusion.16.bias_ref.refs_7_
  30.6 89.0 %all-gather.3.cloned.1.call-done.refs_0_.refs_1_.refs_2_.refs_3_.refs_4_.left_ref.weights_ref = bf16[2048,4608]{1,0:T(8,128)(2,1)} async-done(((bf16[128,4608]{1,0:T(8,128)(2,1)}), bf16[2048,4608]{1,0:T(8,128)(2,1)}) %all-gather.3.cloned.1.call-update) | async-done | bytes 18874384 | tf_op jit(solution)/shard_map/all_gather | solution.py:851
  122.7 5.8 fusion.5.raw_ref
  131.7 3.9 collective-permute-start
  135.6 3.1 collective-permute-start.1
  142.8 10.2 %collective-permute-done = bf16[384,512]{1,0:T(8,128)(2,1)} collective-permute-done((bf16[384,512]{1,0:T(8,128)(2,1)}, bf16[384,512]{1,0:T(8,128)(2,1)}, u32[]{:S(2)}, u32[]{:S(2)}) %collective-permute-start) | collective-permute-done | bytes 393248 | tf_op jit(solution)/shard_map/ppermute | solution.py:152
  160.9 13.2 %shard_map.195 = (bf16[768,512]{1,0:T(8,128)(2,1)S(1)}, f32[3,8,512]{2,1,0:T(8,128)S(1)}) custom-call(bf16[768,512]{1,0:T(8,128)(2,1)S(1)} %bitcast.71, bf16[3,1536,64]{2,1,0:T(8,128)(2,1)S(1)} %bitcast.64, bf16[3,80,1536]{2,1,0:T(8,128)(2,1)S(1)} %concatenate.29.v_ref, f32[1536,512]{1,0:T(8,128)S(1)} %copy-done.57), custom_call_target="tpu_custom_call" | custom-call | flops 5232500224 | tf_op jit(solution)/shard_map/pallas_call | solution.py:671
  175.0 5.1 fusion.17
  181.6 4.3 shard_map.197.left_ref
  187.7 4.9 shard_map.196.left_ref
  193.9 10.7 %fusion.2.d_act_ref = f32[512,2560]{1,0:T(8,128)} fusion(bf16[512,2048]{1,0:T(8,128)(2,1)} %direct_ref.1, bf16[2048,4608]{1,0:T(8,128)(2,1)} %all-gather.3.cloned.1.call-done.refs_0_.refs_1_.refs_2_.refs_3_.refs_4_.left_ref.weights_ref), kind=kOutput, calls=%fused_computation.5 | convolution fusion | flops 5368709120 | bytes 17825792 | tf_op jit(solution)/shard_map/dot_general | solution.py:164
  206.7 11.1 %collective-permute-done.4.refs_0_ = bf16[512,2048]{1,0:T(8,128)(2,1)} collective-permute-done((bf16[512,2048]{1,0:T(8,128)(2,1)}, bf16[512,2048]{1,0:T(8,128)(2,1)}, u32[]{:S(2)}, u32[]{:S(2)}) %collective-permute-start.4) | collective-permute-done | bytes 2097184 | tf_op jit(solution)/shard_map/ppermute | solution.py:138
  217.7 3.4 multiply_reduce_fusion
  221.1 2.0 copy-done.114
  224.8 4.8 shard_map.199.refs_0_.left_ref
  229.6 9.7 %all-gather.5.cloned.1.call-done.gate_ref.up_ref = bf16[2048,5120]{1,0:T(8,128)(2,1)} async-done(((bf16[128,5120]{1,0:T(8,128)(2,1)}), bf16[2048,5120]{1,0:T(8,128)(2,1)}) %all-gather.5.cloned.1.call-update) | async-done | bytes 20971536 | tf_op jit(solution)/shard_map/all_gather | solution.py:852
  239.3 19.3 %shard_map.200 = (bf16[512,2560]{1,0:T(8,128)(2,1)}, bf16[512,2560]{1,0:T(8,128)(2,1)}, bf16[512,2560]{1,0:T(8,128)(2,1)}) custom-call(bf16[512,2048]{1,0:T(8,128)(2,1)} %multiply_convert_fusion.in_ref.n_ref, f32[512,2560]{1,0:T(8,128)} %fusion.2.d_act_ref, bf16[2048,5120]{1,0:T(8,128)(2,1)} %all-gather.5.cloned.1.call-done.gate_ref.up_ref, ...), custom_call_target="tpu_custom_call" | custom-call | flops 7848750080 | tf_op jit(solution)/shard_map/pallas_call | solution.py:743
  260.4 5.5 shard_map.201.refs_0_
  267.4 9.7 %shard_map.202.refs_0_ = bf16[2048,2560]{1,0:T(8,128)(2,1)} custom-call(bf16[2048,512]{1,0:T(8,128)(2,1)S(1)} %copy-done.63, bf16[512,2560]{1,0:T(8,128)(2,1)S(1)} %copy-done.42, bf16[1024,2560]{1,0:T(8,128)(2,1)} %shard_map.201.refs_0_), custom_call_target="tpu_custom_call" | custom-call | flops 3206006016 | tf_op jit(solution)/shard_map/pallas_call | solution.py:276
  277.1 17.6 %shard_map.203.refs_1_.part_ref = bf16[512,2048]{1,0:T(8,128)(2,1)} custom-call(bf16[512,2560]{1,0:T(8,128)(2,1)} %get-tuple-element.53.right_ref.d_gate_ref, bf16[512,2560]{1,0:T(8,128)(2,1)} %get-tuple-element.52.d_up_ref.right_ref, bf16[2048,5120]{1,0:T(8,128)(2,1)} %all-gather.5.cloned.1.call-done.gate_ref.up_ref, ...), custom_call_target="tpu_custom_call" | custom-call | flops 6842500096 | tf_op jit(solution)/shard_map/pallas_call | solution.py:770
  294.7 5.7 shard_map.204.refs_0_
  300.4 5.4 shard_map.205.refs_5_
  307.3 14.5 %collective-permute-start.9 = (bf16[512,2560]{1,0:T(8,128)(2,1)}, bf16[512,2560]{1,0:T(8,128)(2,1)}, u32[]{:S(2)}, u32[]{:S(2)}) collective-permute-start(bf16[512,2560]{1,0:T(8,128)(2,1)} %shard_map.204.refs_0_), channel_id=1, source_target_pairs={{0,4},{2,6},{4,0},{6,2},{8,12},{10,14},{12,8},{14,10},{16,20},{18,... | collective-permute-start | bytes 7864328 | tf_op jit(solution)/shard_map/ppermute | solution.py:126
  323.1 12.1 %shard_map.206.refs_1_.part_ref = bf16[512,2048]{1,0:T(8,128)(2,1)} custom-call(bf16[512,2560]{1,0:T(8,128)(2,1)} %get-tuple-element.51.right_ref.act_ref, bf16[2048,4608]{1,0:T(8,128)(2,1)} %all-gather.3.cloned.1.call-done.refs_0_.refs_1_.refs_2_.refs_3_.refs_4_.left_ref.weights_ref, ...), custom_call_target="tpu_custom_call" | custom-call | flops 3622500096 | tf_op jit(solution)/shard_map/pallas_call | solution.py:800
  336.8 5.3 shard_map.208.refs_0_
  342.4 11.7 %collective-permute-done.6.refs_1_.other_ref = bf16[512,2048]{1,0:T(8,128)(2,1)} collective-permute-done((bf16[512,2048]{1,0:T(8,128)(2,1)}, bf16[512,2048]{1,0:T(8,128)(2,1)}, u32[]{:S(2)}, u32[]{:S(2)}) %collective-permute-start.6) | collective-permute-done | bytes 2097184 | tf_op jit(solution)/shard_map/ppermute | solution.py:138
  354.2 7.1 %shard_map.209 = (f32[512,2048]{1,0:T(8,128)}, bf16[512,2048]{1,0:T(8,128)(2,1)S(1)}, f32[1,2048]{1,0:T(1,128)S(1)}) custom-call(f32[512,2048]{1,0:T(8,128)} %copy-done.114, bf16[512,2048]{1,0:T(8,128)(2,1)S(1)} %copy-done.65, bf16[512,2048]{1,0:T(8,128)(2,1)} %shard_map.203.refs_1_.part_ref, bf16[512,2048]{1,0:T(8,128)(2,1)} %collective-permute-done.6.refs_1_.other_ref, ...), custom_call_target="tpu_custom_call" | custom-call | flops 2817499904 | tf_op jit(solution)/shard_map/pallas_call | solution.py:330
  361.4 4.5 shard_map.210.refs_4_.refs_8_
  366.1 10.7 %shard_map.211 = (f32[768,512]{1,0:T(8,128)S(1)}, f32[192,1536]{1,0:T(8,128)S(1)}, f32[192,1536]{1,0:T(8,128)S(1)}) custom-call(bf16[768,512]{1,0:T(8,128)(2,1)S(1)} %bitcast.72, bf16[3,1536,64]{2,1,0:T(8,128)(2,1)S(1)} %bitcast.65, bf16[192,1536]{1,0:T(8,128)(2,1)S(1)} %get-tuple-element.98.refs_2_, bf16[3,1536,64]{2,1,0:T(8,128)(2,1)S(1)} %bitcast.68, ...), custom_call_target="tpu_custom_call" | custom-call | flops 4427500032 | tf_op jit(solution)/shard_map/pallas_call | solution.py:698
  377.9 11.1 %shard_map.212 = (f32[768,512]{1,0:T(8,128)S(1)}, f32[192,1536]{1,0:T(8,128)S(1)}, f32[192,1536]{1,0:T(8,128)S(1)}) custom-call(bf16[768,512]{1,0:T(8,128)(2,1)S(1)} %bitcast.73, bf16[3,1536,64]{2,1,0:T(8,128)(2,1)S(1)} %bitcast.66, bf16[192,1536]{1,0:T(8,128)(2,1)S(1)} %copy-done.61, ...), custom_call_target="tpu_custom_call", output_to_operand_aliasing={{0}: (8, {}), {1}: (9, {}), {2}: (10, {})} | custom-call | flops 4427500032 | tf_op jit(solution)/shard_map/pallas_call | solution.py:698
  389.0 18.8 %collective-permute-done.9.refs_1_ = bf16[512,2560]{1,0:T(8,128)(2,1)} collective-permute-done((bf16[512,2560]{1,0:T(8,128)(2,1)}, bf16[512,2560]{1,0:T(8,128)(2,1)}, u32[]{:S(2)}, u32[]{:S(2)}) %collective-permute-start.9) | collective-permute-done | bytes 2621472 | tf_op jit(solution)/shard_map/ppermute | solution.py:126
  407.8 3.3 shard_map.213.refs_11_
  422.9 10.7 %shard_map.214 = (f32[768,512]{1,0:T(8,128)S(1)}, f32[192,1536]{1,0:T(8,128)S(1)}, f32[192,1536]{1,0:T(8,128)S(1)}) custom-call(bf16[768,512]{1,0:T(8,128)(2,1)S(1)} %bitcast.74, bf16[3,1536,64]{2,1,0:T(8,128)(2,1)S(1)} %bitcast.67, bf16[192,1536]{1,0:T(8,128)(2,1)S(1)} %copy-done.62, ...), custom_call_target="tpu_custom_call", output_to_operand_aliasing={{0}: (8, {}), {1}: (9, {}), {2}: (10, {})} | custom-call | flops 4427500032 | tf_op jit(solution)/shard_map/pallas_call | solution.py:698
  441.1 2.4 shard_map.217
  444.8 4.9 shard_map.219.left_ref.refs_0_
  452.4 2.2 shard_map.220
  463.2 3.1 shard_map.221.refs_2_
  466.3 2.7 shard_map.222.refs_2_
  470.3 2.7 shard_map.223.refs_2_
  473.0 5.6 collective-permute-done.10.refs_0_
  478.6 3.8 collective-permute-start.21
  484.6 3.4 shard_map.225.refs_0_
  488.1 8.2 %shard_map.226 = (bf16[512,2048]{1,0:T(8,128)(2,1)}, f32[1,2048]{1,0:T(1,128)S(1)}) custom-call(bf16[512,768]{1,0:T(8,128)(2,1)S(1)} %copy-done.36, bf16[512,384]{1,0:T(8,128)(2,1)S(1)} %get-tuple-element.72.refs_2_.d_keyval_ref.right_ref, bf16[2048,4608]{1,0:T(8,128)(2,1)} %all-gather.3.cloned.1.call-done.refs_0_.refs_1_.refs_2_.refs_3_.refs_4_.left_ref.weights_ref, ...), custom_call_target="tpu_custom_call" | custom-call | flops 3220000000 | tf_op jit(solution)/shard_map/pallas_call | solution.py:502
  500.5 8.8 %collective-permute-done.22.refs_3_ = bf16[128,2560]{1,0:T(8,128)(2,1)} collective-permute-done((bf16[128,2560]{1,0:T(8,128)(2,1)}, bf16[128,2560]{1,0:T(8,128)(2,1)}, u32[]{:S(2)}, u32[]{:S(2)}) %collective-permute-start.22) | collective-permute-done | bytes 655392 | tf_op jit(solution)/shard_map/ppermute | solution.py:126
  511.5 2.4 shard_map.227.refs_2_.first_ref
  519.3 2.1 shard_map.230.in_ref
  521.4 2.8 shard_map.231.refs_0_.refs_1_.refs_2_.refs_3_.refs_4_
  534.5 21.4 %collective-permute-done.31.refs_2_ = bf16[256,768]{1,0:T(8,128)(2,1)S(1)} collective-permute-done((bf16[256,768]{1,0:T(8,128)(2,1)S(1)}, bf16[256,768]{1,0:T(8,128)(2,1)S(1)}, u32[]{:S(2)}, u32[]{:S(2)}) %collective-permute-start.31) | collective-permute-done | bytes 393248 | tf_op jit(solution)/shard_map/ppermute | solution.py:126
  556.2 3.1 shard_map.234.refs_3_
  559.3 2.1 shard_map.235.refs_3_
  561.4 5.2 collective-permute-done.29.refs_2_
  569.4 2.3 collective-permute-start.35
  573.2 7.6 %shard_map.238 = (f32[512,2048]{1,0:T(8,128)}, bf16[512,2048]{1,0:T(8,128)(2,1)}, f32[1,2048]{1,0:T(1,128)}) custom-call(bf16[512,2048]{1,0:T(8,128)(2,1)S(1)} %copy-done.24, f32[512,2048]{1,0:T(8,128)} %get-tuple-element.86.direct_ref, bf16[512,2048]{1,0:T(8,128)(2,1)} %get-tuple-element.79.refs_4_.part_ref, ...), custom_call_target="tpu_custom_call" | custom-call | flops 2817499904 | tf_op jit(solution)/shard_map/pallas_call | solution.py:330
  582.8 9.8 %collective-permute-done.33.refs_2_ = bf16[256,512]{1,0:T(8,128)(2,1)S(1)} collective-permute-done((bf16[256,512]{1,0:T(8,128)(2,1)S(1)}, bf16[256,512]{1,0:T(8,128)(2,1)S(1)}, u32[]{:S(2)}, u32[]{:S(2)}) %collective-permute-start.33) | collective-permute-done | bytes 262176 | tf_op jit(solution)/shard_map/ppermute | solution.py:126
  596.1 3.1 collective-permute-start.37
  599.2 5.3 shard_map.240.refs_0_
  604.5 4.0 shard_map.241.refs_4_
  612.2 2.4 shard_map.242.refs_4_.second_ref
  614.7 2.7 shard_map.243.refs_4_
  618.5 2.2 shard_map.244.refs_5_
  621.7 2.1 shard_map.245
  625.5 4.1 shard_map.247
  (421 shorter events, 130.1 us)
Async XLA Ops:
  7.2 112.4 %all-gather.3.cloned.1.call-start = ((), (), s32[]{:S(2)}) async-start(), calls=%async_computation.1 | async-start | bytes 20054016 | tf_op jit(solution)/shard_map/all_gather | solution.py:851
  17.8 221.5 %all-gather.5.cloned.1.call-start = ((), (), s32[]{:S(2)}) async-start(), calls=%async_computation.2 | async-start | bytes 22282240 | tf_op jit(solution)/shard_map/all_gather | solution.py:852
  20.0 584.4 %reduce-scatter.2.cloned.1.call-start = ((), (), s32[]{:S(2)}) async-start(), calls=%async_computation.3 | async-start | bytes 11141120 | tf_op jit(solution)/shard_map/reduce_scatter | solution.py:946
  20.1 7.8 %collective-permute-start.3 = (bf16[512]{0:T(512)(128)(2,1)S(1)}, bf16[512]{0:T(512)(128)(2,1)S(1)}, u32[]{:S(2)}, u32[]{:S(2)}) collective-permute-start(bf16[512]{0:T(512)(128)(2,1)S(1)} %add_convert_fusion.2), channel_id=1, source_target_pairs={{0,2},{2,4},{4,6},{6,8},{8,10},{10,12},{12,14},{14,16},{16,18},{18... | collective-permute-start | bytes 3080 | tf_op jit(solution)/shard_map/ppermute | solution.py:152
  22.5 5.7 collective-permute-start.2
  27.5 94.6 %copy-start.124 = (f32[512]{0:T(512)}, f32[512]{0:T(512)S(1)}, u32[]{:S(2)}) copy-start(f32[512]{0:T(512)S(1)} %add_rsqrt_fusion.3) | copy-start | bytes 6148
  27.9 114.6 %copy-start.66 = (f32[32,512]{1,0:T(8,128)}, f32[32,512]{1,0:T(8,128)S(1)}, u32[]{:S(2)}) copy-start(f32[32,512]{1,0:T(8,128)S(1)} %get-tuple-element.106.sin_ref) | copy-start | bytes 196612
  131.7 21.4 %collective-permute-start = (bf16[384,512]{1,0:T(8,128)(2,1)}, bf16[384,512]{1,0:T(8,128)(2,1)}, u32[]{:S(2)}, u32[]{:S(2)}) collective-permute-start(bf16[384,512]{1,0:T(8,128)(2,1)} %pad_maximum_fusion.1), channel_id=1, source_target_pairs={{0,4},{2,6},{4,8},{6,10},{8,12},{10,14},{12,16},{14,18},{16,20},{1... | collective-permute-start | bytes 1179656 | tf_op jit(solution)/shard_map/ppermute | solution.py:152
  135.6 17.4 %collective-permute-start.1 = (bf16[384,512]{1,0:T(8,128)(2,1)}, bf16[384,512]{1,0:T(8,128)(2,1)}, u32[]{:S(2)}, u32[]{:S(2)}) collective-permute-start(bf16[384,512]{1,0:T(8,128)(2,1)} %pad_maximum_fusion.1), channel_id=1, source_target_pairs={{0,2},{2,4},{4,6},{6,8},{8,10},{10,12},{12,14},{14,16},{16,18},{18... | collective-permute-start | bytes 1179656 | tf_op jit(solution)/shard_map/ppermute | solution.py:152
  142.8 14.9 %copy-start.92 = (bf16[12,64,512]{2,1,0:T(8,128)(2,1)}, bf16[12,64,512]{2,1,0:T(8,128)(2,1)S(1)}, u32[]{:S(2)}) copy-start(bf16[12,64,512]{2,1,0:T(8,128)(2,1)S(1)} %pad_maximum_fusion) | copy-start | bytes 2359300
  155.2 210.7 %copy-start.60 = (bf16[192,1536]{1,0:T(8,128)(2,1)}, bf16[192,1536]{1,0:T(8,128)(2,1)S(1)}, u32[]{:S(2)}) copy-start(bf16[192,1536]{1,0:T(8,128)(2,1)S(1)} %get-tuple-element.98.refs_2_) | copy-start | bytes 1769476
  180.1 37.6 %collective-permute-start.4 = (bf16[512,2048]{1,0:T(8,128)(2,1)}, bf16[512,2048]{1,0:T(8,128)(2,1)}, u32[]{:S(2)}, u32[]{:S(2)}) collective-permute-start(bf16[512,2048]{1,0:T(8,128)(2,1)} %fusion.17), channel_id=1, source_target_pairs={{0,1},{1,0},{2,3},{3,2},{4,5},{5,4},{6,7},{7,6},{8,9},{9,8},{10,11... | collective-permute-start | bytes 6291464 | tf_op jit(solution)/shard_map/ppermute | solution.py:138
  229.6 29.0 %copy-start = (bf16[2048,512]{1,0:T(8,128)(2,1)S(1)}, bf16[2048,512]{1,0:T(8,128)(2,1)}, u32[]{:S(2)}) copy-start(bf16[2048,512]{1,0:T(8,128)(2,1)} %shard_map.199.refs_0_.left_ref) | copy-start | bytes 6291460
  265.8 28.9 %collective-permute-start.5 = (bf16[1024,2560]{1,0:T(8,128)(2,1)}, bf16[1024,2560]{1,0:T(8,128)(2,1)}, u32[]{:S(2)}, u32[]{:S(2)}) collective-permute-start(bf16[1024,2560]{1,0:T(8,128)(2,1)} %shard_map.201.refs_0_), channel_id=1, source_target_pairs={{0,2},{2,0},{4,6},{6,4},{8,10},{10,8},{12,14},{14,12},{16,18},{18,... | collective-permute-start | bytes 15728648 | tf_op jit(solution)/shard_map/ppermute | solution.py:126
  277.1 17.6 %copy-start.8 = (bf16[512,2560]{1,0:T(8,128)(2,1)S(1)}, bf16[512,2560]{1,0:T(8,128)(2,1)}, u32[]{:S(2)}) copy-start(bf16[512,2560]{1,0:T(8,128)(2,1)} %get-tuple-element.53.right_ref.d_gate_ref) | copy-start | bytes 7864324
  300.4 21.3 %copy-start.116 = (bf16[192,1536]{1,0:T(8,128)(2,1)S(1)}, bf16[192,1536]{1,0:T(8,128)(2,1)}, u32[]{:S(2)}) copy-start(bf16[192,1536]{1,0:T(8,128)(2,1)} %get-tuple-element.97) | copy-start | bytes 1769476
  305.8 29.4 %collective-permute-start.8 = (bf16[1024,2560]{1,0:T(8,128)(2,1)}, bf16[1024,2560]{1,0:T(8,128)(2,1)}, u32[]{:S(2)}, u32[]{:S(2)}) collective-permute-start(bf16[1024,2560]{1,0:T(8,128)(2,1)} %shard_map.205.refs_5_), channel_id=1, source_target_pairs={{0,2},{2,0},{4,6},{6,4},{8,10},{10,8},{12,14},{14,12},{16,18},{18,... | collective-permute-start | bytes 15728648 | tf_op jit(solution)/shard_map/ppermute | solution.py:126
  305.8 48.4 %collective-permute-start.6 = (bf16[512,2048]{1,0:T(8,128)(2,1)}, bf16[512,2048]{1,0:T(8,128)(2,1)}, u32[]{:S(2)}, u32[]{:S(2)}) collective-permute-start(bf16[512,2048]{1,0:T(8,128)(2,1)} %shard_map.203.refs_1_.part_ref), channel_id=1, source_target_pairs={{0,1},{1,0},{2,3},{3,2},{4,5},{5,4},{6,7},{7,6},{8,9},{9,8},{10,11... | collective-permute-start | bytes 6291464 | tf_op jit(solution)/shard_map/ppermute | solution.py:138
  307.3 100.6 %collective-permute-start.9 = (bf16[512,2560]{1,0:T(8,128)(2,1)}, bf16[512,2560]{1,0:T(8,128)(2,1)}, u32[]{:S(2)}, u32[]{:S(2)}) collective-permute-start(bf16[512,2560]{1,0:T(8,128)(2,1)} %shard_map.204.refs_0_), channel_id=1, source_target_pairs={{0,4},{2,6},{4,0},{6,2},{8,12},{10,14},{12,8},{14,10},{16,20},{18,... | collective-permute-start | bytes 7864328 | tf_op jit(solution)/shard_map/ppermute | solution.py:126
  336.8 17.4 %copy-start.65 = (bf16[512,2048]{1,0:T(8,128)(2,1)S(1)}, bf16[512,2048]{1,0:T(8,128)(2,1)}, u32[]{:S(2)}) copy-start(bf16[512,2048]{1,0:T(8,128)(2,1)} %direct_ref.1) | copy-start | bytes 6291460
  342.1 141.9 %collective-permute-start.17 = (bf16[512,2560]{1,0:T(8,128)(2,1)}, bf16[512,2560]{1,0:T(8,128)(2,1)}, u32[]{:S(2)}, u32[]{:S(2)}) collective-permute-start(bf16[512,2560]{1,0:T(8,128)(2,1)} %shard_map.208.refs_0_), channel_id=1, source_target_pairs={{0,4},{2,6},{4,0},{6,2},{8,12},{10,14},{12,8},{14,10},{16,20},{18,... | collective-permute-start | bytes 7864328 | tf_op jit(solution)/shard_map/ppermute | solution.py:126
  377.9 30.0 %copy-start.9 = (bf16[512,2560]{1,0:T(8,128)(2,1)S(1)}, bf16[512,2560]{1,0:T(8,128)(2,1)}, u32[]{:S(2)}) copy-start(bf16[512,2560]{1,0:T(8,128)(2,1)} %get-tuple-element.53.right_ref.d_gate_ref) | copy-start | bytes 7864324
  389.0 22.2 %copy-start.50 = (f32[192,1536]{1,0:T(8,128)}, f32[192,1536]{1,0:T(8,128)S(1)}, u32[]{:S(2)}) copy-start(f32[192,1536]{1,0:T(8,128)S(1)} %get-tuple-element.61.refs_10_) | copy-start | bytes 3538948
  389.0 22.1 %copy-start.70 = (f32[768,512]{1,0:T(8,128)}, f32[768,512]{1,0:T(8,128)S(1)}, u32[]{:S(2)}) copy-start(f32[768,512]{1,0:T(8,128)S(1)} %get-tuple-element.59.refs_8_) | copy-start | bytes 4718596
  411.2 48.0 %collective-permute-start.16 = (bf16[256,2560]{1,0:T(8,128)(2,1)}, bf16[256,2560]{1,0:T(8,128)(2,1)}, u32[]{:S(2)}, u32[]{:S(2)}) collective-permute-start(bf16[256,2560]{1,0:T(8,128)(2,1)} %shard_map.213.refs_11_), channel_id=1, source_target_pairs={{0,8},{2,10},{4,12},{6,14},{8,0},{10,2},{12,4},{14,6},{16,24},{18,... | collective-permute-start | bytes 3932168 | tf_op jit(solution)/shard_map/ppermute | solution.py:126
  422.9 15.2 %copy-start.67 = (f32[32,512]{1,0:T(8,128)S(1)}, f32[32,512]{1,0:T(8,128)}, u32[]{:S(2)}) copy-start(f32[32,512]{1,0:T(8,128)} %copy-done.66) | copy-start | bytes 196612
  444.3 11.1 %collective-permute-start.14 = (bf16[256,768]{1,0:T(8,128)(2,1)}, bf16[256,768]{1,0:T(8,128)(2,1)}, u32[]{:S(2)}, u32[]{:S(2)}) collective-permute-start(bf16[256,768]{1,0:T(8,128)(2,1)} %get-tuple-element.68.refs_1_), channel_id=1, source_target_pairs={{0,2},{2,0},{4,6},{6,4},{8,10},{10,8},{12,14},{14,12},{16,18},{18,... | collective-permute-start | bytes 1179656 | tf_op jit(solution)/shard_map/ppermute | solution.py:126
  444.3 11.6 %collective-permute-start.15 = (bf16[256,768]{1,0:T(8,128)(2,1)}, bf16[256,768]{1,0:T(8,128)(2,1)}, u32[]{:S(2)}, u32[]{:S(2)}) collective-permute-start(bf16[256,768]{1,0:T(8,128)(2,1)} %get-tuple-element.71), channel_id=1, source_target_pairs={{0,2},{2,0},{4,6},{6,4},{8,10},{10,8},{12,14},{14,12},{16,18},{18,... | collective-permute-start | bytes 1179656 | tf_op jit(solution)/shard_map/ppermute | solution.py:126
  455.4 13.6 %collective-permute-start.12 = (bf16[256,768]{1,0:T(8,128)(2,1)}, bf16[256,768]{1,0:T(8,128)(2,1)}, u32[]{:S(2)}, u32[]{:S(2)}) collective-permute-start(bf16[256,768]{1,0:T(8,128)(2,1)} %get-tuple-element.69.refs_3_), channel_id=1, source_target_pairs={{0,2},{2,0},{4,6},{6,4},{8,10},{10,8},{12,14},{14,12},{16,18},{18,... | collective-permute-start | bytes 1179656 | tf_op jit(solution)/shard_map/ppermute | solution.py:126
  455.4 14.7 %collective-permute-start.13 = (bf16[256,768]{1,0:T(8,128)(2,1)}, bf16[256,768]{1,0:T(8,128)(2,1)}, u32[]{:S(2)}, u32[]{:S(2)}) collective-permute-start(bf16[256,768]{1,0:T(8,128)(2,1)} %get-tuple-element.70), channel_id=1, source_target_pairs={{0,2},{2,0},{4,6},{6,4},{8,10},{10,8},{12,14},{14,12},{16,18},{18,... | collective-permute-start | bytes 1179656 | tf_op jit(solution)/shard_map/ppermute | solution.py:126
  455.9 22.7 %collective-permute-start.10 = (bf16[384,512]{1,0:T(8,128)(2,1)}, bf16[384,512]{1,0:T(8,128)(2,1)}, u32[]{:S(2)}, u32[]{:S(2)}) collective-permute-start(bf16[384,512]{1,0:T(8,128)(2,1)} %get-tuple-element.64.refs_0_), channel_id=1, source_target_pairs={{4,0},{6,2},{8,4},{10,6},{12,8},{14,10},{16,12},{18,14},{20,16},{2... | collective-permute-start | bytes 1179656 | tf_op jit(solution)/shard_map/ppermute | solution.py:152
  459.2 19.4 %collective-permute-start.11 = (bf16[384,512]{1,0:T(8,128)(2,1)}, bf16[384,512]{1,0:T(8,128)(2,1)}, u32[]{:S(2)}, u32[]{:S(2)}) collective-permute-start(bf16[384,512]{1,0:T(8,128)(2,1)} %get-tuple-element.65), channel_id=1, source_target_pairs={{2,0},{4,2},{6,4},{8,6},{10,8},{12,10},{14,12},{16,14},{18,16},{20... | collective-permute-start | bytes 1179656 | tf_op jit(solution)/shard_map/ppermute | solution.py:152
  469.0 27.8 %collective-permute-start.20 = (bf16[256,768]{1,0:T(8,128)(2,1)S(1)}, bf16[256,768]{1,0:T(8,128)(2,1)S(1)}, u32[]{:S(2)}, u32[]{:S(2)}) collective-permute-start(bf16[256,768]{1,0:T(8,128)(2,1)S(1)} %copy-done.111), channel_id=1, source_target_pairs={{0,2},{2,0},{4,6},{6,4},{8,10},{10,8},{12,14},{14,12},{16,18},{18,... | collective-permute-start | bytes 1179656 | tf_op jit(solution)/shard_map/ppermute | solution.py:126
  470.2 12.2 %copy-start.34 = (f32[1152,512]{1,0:T(8,128)S(1)}, f32[1152,512]{1,0:T(8,128)}, u32[]{:S(2)}) copy-start(f32[1152,512]{1,0:T(8,128)} %copy-done.31) | copy-start | bytes 7077892
  470.2 12.2 %copy-start.54 = (f32[192,1536]{1,0:T(8,128)S(1)}, f32[192,1536]{1,0:T(8,128)}, u32[]{:S(2)}) copy-start(f32[192,1536]{1,0:T(8,128)} %copy-done.52) | copy-start | bytes 3538948
  470.2 45.9 %collective-permute-start.18 = (bf16[256,768]{1,0:T(8,128)(2,1)}, bf16[256,768]{1,0:T(8,128)(2,1)}, u32[]{:S(2)}, u32[]{:S(2)}) collective-permute-start(bf16[256,768]{1,0:T(8,128)(2,1)} %get-tuple-element.77), channel_id=1, source_target_pairs={{0,2},{2,0},{4,6},{6,4},{8,10},{10,8},{12,14},{14,12},{16,18},{18,... | collective-permute-start | bytes 1179656 | tf_op jit(solution)/shard_map/ppermute | solution.py:126
  478.6 30.7 %collective-permute-start.22 = (bf16[128,2560]{1,0:T(8,128)(2,1)}, bf16[128,2560]{1,0:T(8,128)(2,1)}, u32[]{:S(2)}, u32[]{:S(2)}) collective-permute-start(bf16[128,2560]{1,0:T(8,128)(2,1)} %shard_map.221.refs_2_), channel_id=1, source_target_pairs={{0,16},{2,18},{4,20},{6,22},{8,24},{10,26},{12,28},{14,30},{16,0},... | collective-permute-start | bytes 1966088 | tf_op jit(solution)/shard_map/ppermute | solution.py:126
  478.6 35.4 %collective-permute-start.21 = (bf16[512,768]{1,0:T(8,128)(2,1)}, bf16[512,768]{1,0:T(8,128)(2,1)}, u32[]{:S(2)}, u32[]{:S(2)}) collective-permute-start(bf16[512,768]{1,0:T(8,128)(2,1)} %shard_map.222.refs_2_), channel_id=1, source_target_pairs={{0,4},{2,6},{4,0},{6,2},{8,12},{10,14},{12,8},{14,10},{16,20},{18,... | collective-permute-start | bytes 2359304 | tf_op jit(solution)/shard_map/ppermute | solution.py:126
  484.0 33.1 %collective-permute-start.19 = (bf16[512,768]{1,0:T(8,128)(2,1)}, bf16[512,768]{1,0:T(8,128)(2,1)}, u32[]{:S(2)}, u32[]{:S(2)}) collective-permute-start(bf16[512,768]{1,0:T(8,128)(2,1)} %shard_map.223.refs_2_), channel_id=1, source_target_pairs={{0,4},{2,6},{4,0},{6,2},{8,12},{10,14},{12,8},{14,10},{16,20},{18,... | collective-permute-start | bytes 2359304 | tf_op jit(solution)/shard_map/ppermute | solution.py:126
  497.6 75.1 %collective-permute-start.34 = (bf16[512,2048]{1,0:T(8,128)(2,1)}, bf16[512,2048]{1,0:T(8,128)(2,1)}, u32[]{:S(2)}, u32[]{:S(2)}) collective-permute-start(bf16[512,2048]{1,0:T(8,128)(2,1)} %get-tuple-element.79.refs_4_.part_ref), channel_id=1, source_target_pairs={{0,1},{1,0},{2,3},{3,2},{4,5},{5,4},{6,7},{7,6},{8,9},{9,8},{10,11... | collective-permute-start | bytes 6291464 | tf_op jit(solution)/shard_map/ppermute | solution.py:138
  500.5 13.6 %copy-start.101 = (bf16[256,768]{1,0:T(8,128)(2,1)S(1)}, bf16[256,768]{1,0:T(8,128)(2,1)}, u32[]{:S(2)}) copy-start(bf16[256,768]{1,0:T(8,128)(2,1)} %copy-done.100) | copy-start | bytes 1179652
  500.5 13.6 %copy-start.3 = (bf16[2048,512]{1,0:T(8,128)(2,1)S(1)}, bf16[2048,512]{1,0:T(8,128)(2,1)}, u32[]{:S(2)}) copy-start(bf16[2048,512]{1,0:T(8,128)(2,1)} %shard_map.196.left_ref) | copy-start | bytes 6291460
  509.3 90.0 %collective-permute-start.7 = (bf16[512,2048]{1,0:T(8,128)(2,1)}, bf16[512,2048]{1,0:T(8,128)(2,1)}, u32[]{:S(2)}, u32[]{:S(2)}) collective-permute-start(bf16[512,2048]{1,0:T(8,128)(2,1)} %shard_map.207), channel_id=1, source_target_pairs={{0,1},{1,0},{2,3},{3,2},{4,5},{5,4},{6,7},{7,6},{8,9},{9,8},{10,11... | collective-permute-start | bytes 6291464 | tf_op jit(solution)/shard_map/ppermute | solution.py:138
  514.0 15.7 %collective-permute-start.30 = (bf16[256,768]{1,0:T(8,128)(2,1)}, bf16[256,768]{1,0:T(8,128)(2,1)}, u32[]{:S(2)}, u32[]{:S(2)}) collective-permute-start(bf16[256,768]{1,0:T(8,128)(2,1)} %get-tuple-element.85), channel_id=1, source_target_pairs={{0,2},{2,0},{4,6},{6,4},{8,10},{10,8},{12,14},{14,12},{16,18},{18,... | collective-permute-start | bytes 1179656 | tf_op jit(solution)/shard_map/ppermute | solution.py:126
  516.1 40.1 %collective-permute-start.32 = (bf16[256,2560]{1,0:T(8,128)(2,1)}, bf16[256,2560]{1,0:T(8,128)(2,1)}, u32[]{:S(2)}, u32[]{:S(2)}) collective-permute-start(bf16[256,2560]{1,0:T(8,128)(2,1)} %shard_map.225.refs_0_), channel_id=1, source_target_pairs={{0,8},{2,10},{4,12},{6,14},{8,0},{10,2},{12,4},{14,6},{16,24},{18,... | collective-permute-start | bytes 3932168 | tf_op jit(solution)/shard_map/ppermute | solution.py:126
  528.6 2.2 collective-permute-start.24
  529.7 1.5 collective-permute-start.25
  530.8 25.1 %copy-start.75 = (bf16[256,768]{1,0:T(8,128)(2,1)S(1)}, bf16[256,768]{1,0:T(8,128)(2,1)}, u32[]{:S(2)}) copy-start(bf16[256,768]{1,0:T(8,128)(2,1)} %copy-done.74) | copy-start | bytes 1179652
  530.8 25.3 %copy-start.15 = (bf16[512,2560]{1,0:T(8,128)(2,1)S(1)}, bf16[512,2560]{1,0:T(8,128)(2,1)}, u32[]{:S(2)}) copy-start(bf16[512,2560]{1,0:T(8,128)(2,1)} %get-tuple-element.52.d_up_ref.right_ref) | copy-start | bytes 7864324
  530.9 2.2 collective-permute-start.28
  531.2 24.7 %collective-permute-start.31 = (bf16[256,768]{1,0:T(8,128)(2,1)S(1)}, bf16[256,768]{1,0:T(8,128)(2,1)S(1)}, u32[]{:S(2)}, u32[]{:S(2)}) collective-permute-start(bf16[256,768]{1,0:T(8,128)(2,1)S(1)} %copy-done.69), channel_id=1, source_target_pairs={{0,8},{2,10},{4,12},{6,14},{8,0},{10,2},{12,4},{14,6},{16,24},{18,... | collective-permute-start | bytes 1179656 | tf_op jit(solution)/shard_map/ppermute | solution.py:126
  533.1 34.3 %copy-start.76 = (bf16[256,768]{1,0:T(8,128)(2,1)}, bf16[256,768]{1,0:T(8,128)(2,1)S(1)}, u32[]{:S(2)}) copy-start(bf16[256,768]{1,0:T(8,128)(2,1)S(1)} %collective-permute-done.28.refs_0_) | copy-start | bytes 1179652
  533.1 36.3 %collective-permute-start.26 = (bf16[512,512]{1,0:T(8,128)(2,1)S(1)}, bf16[512,512]{1,0:T(8,128)(2,1)S(1)}, u32[]{:S(2)}, u32[]{:S(2)}) collective-permute-start(bf16[512,512]{1,0:T(8,128)(2,1)S(1)} %shard_map.233.refs_3_), channel_id=1, source_target_pairs={{0,4},{2,6},{4,0},{6,2},{8,12},{10,14},{12,8},{14,10},{16,20},{18,... | collective-permute-start | bytes 1572872 | tf_op jit(solution)/shard_map/ppermute | solution.py:126
  555.9 10.8 %collective-permute-start.29 = (bf16[256,768]{1,0:T(8,128)(2,1)S(1)}, bf16[256,768]{1,0:T(8,128)(2,1)S(1)}, u32[]{:S(2)}, u32[]{:S(2)}) collective-permute-start(bf16[256,768]{1,0:T(8,128)(2,1)S(1)} %copy-done.75), channel_id=1, source_target_pairs={{0,8},{2,10},{4,12},{6,14},{8,0},{10,2},{12,4},{14,6},{16,24},{18,... | collective-permute-start | bytes 1179656 | tf_op jit(solution)/shard_map/ppermute | solution.py:126
  556.2 13.1 %collective-permute-start.27 = (bf16[256,512]{1,0:T(8,128)(2,1)S(1)}, bf16[256,512]{1,0:T(8,128)(2,1)S(1)}, u32[]{:S(2)}, u32[]{:S(2)}) collective-permute-start(bf16[256,512]{1,0:T(8,128)(2,1)S(1)} %get-tuple-element.83), channel_id=1, source_target_pairs={{0,2},{2,0},{4,6},{6,4},{8,10},{10,8},{12,14},{14,12},{16,18},{18,... | collective-permute-start | bytes 786440 | tf_op jit(solution)/shard_map/ppermute | solution.py:126
  566.7 42.3 %collective-permute-start.36 = (bf16[128,2560]{1,0:T(8,128)(2,1)}, bf16[128,2560]{1,0:T(8,128)(2,1)}, u32[]{:S(2)}, u32[]{:S(2)}) collective-permute-start(bf16[128,2560]{1,0:T(8,128)(2,1)} %shard_map.234.refs_3_), channel_id=1, source_target_pairs={{0,16},{2,18},{4,20},{6,22},{8,24},{10,26},{12,28},{14,30},{16,0},... | collective-permute-start | bytes 1966088 | tf_op jit(solution)/shard_map/ppermute | solution.py:126
  569.3 11.6 %collective-permute-start.23 = (bf16[256,512]{1,0:T(8,128)(2,1)S(1)}, bf16[256,512]{1,0:T(8,128)(2,1)S(1)}, u32[]{:S(2)}, u32[]{:S(2)}) collective-permute-start(bf16[256,512]{1,0:T(8,128)(2,1)S(1)} %get-tuple-element.80), channel_id=1, source_target_pairs={{0,2},{2,0},{4,6},{6,4},{8,10},{10,8},{12,14},{14,12},{16,18},{18,... | collective-permute-start | bytes 786440 | tf_op jit(solution)/shard_map/ppermute | solution.py:126
  569.4 23.2 %copy-start.55 = (bf16[512,512]{1,0:T(8,128)(2,1)}, bf16[512,512]{1,0:T(8,128)(2,1)S(1)}, u32[]{:S(2)}) copy-start(bf16[512,512]{1,0:T(8,128)(2,1)S(1)} %collective-permute-done.26.refs_1_) | copy-start | bytes 1572868
  569.4 45.3 %collective-permute-start.35 = (bf16[128,768]{1,0:T(8,128)(2,1)}, bf16[128,768]{1,0:T(8,128)(2,1)}, u32[]{:S(2)}, u32[]{:S(2)}) collective-permute-start(bf16[128,768]{1,0:T(8,128)(2,1)} %shard_map.235.refs_3_), channel_id=1, source_target_pairs={{0,16},{2,18},{4,20},{6,22},{8,24},{10,26},{12,28},{14,30},{16,0},... | collective-permute-start | bytes 589832 | tf_op jit(solution)/shard_map/ppermute | solution.py:126
  572.7 19.9 %collective-permute-start.33 = (bf16[256,512]{1,0:T(8,128)(2,1)S(1)}, bf16[256,512]{1,0:T(8,128)(2,1)S(1)}, u32[]{:S(2)}, u32[]{:S(2)}) collective-permute-start(bf16[256,512]{1,0:T(8,128)(2,1)S(1)} %shard_map.237.refs_0_), channel_id=1, source_target_pairs={{0,8},{2,10},{4,12},{6,14},{8,0},{10,2},{12,4},{14,6},{16,24},{18,... | collective-permute-start | bytes 786440 | tf_op jit(solution)/shard_map/ppermute | solution.py:126
  573.2 19.4 %copy-start.44 = (bf16[2048,128]{1,0:T(8,128)(2,1)S(1)}, bf16[2048,128]{1,0:T(8,128)(2,1)}, u32[]{:S(2)}) copy-start(bf16[2048,128]{1,0:T(8,128)(2,1)} %shard_map.231.refs_0_.refs_1_.refs_2_.refs_3_.refs_4_) | copy-start | bytes 1572868
  580.9 36.5 %collective-permute-start.38 = (bf16[128,768]{1,0:T(8,128)(2,1)}, bf16[128,768]{1,0:T(8,128)(2,1)}, u32[]{:S(2)}, u32[]{:S(2)}) collective-permute-start(bf16[128,768]{1,0:T(8,128)(2,1)} %shard_map.236.refs_3_), channel_id=1, source_target_pairs={{0,16},{2,18},{4,20},{6,22},{8,24},{10,26},{12,28},{14,30},{16,0},... | collective-permute-start | bytes 589832 | tf_op jit(solution)/shard_map/ppermute | solution.py:126
  596.1 24.6 %collective-permute-start.37 = (bf16[128,512]{1,0:T(8,128)(2,1)}, bf16[128,512]{1,0:T(8,128)(2,1)}, u32[]{:S(2)}, u32[]{:S(2)}) collective-permute-start(bf16[128,512]{1,0:T(8,128)(2,1)} %shard_map.239.refs_0_), channel_id=1, source_target_pairs={{0,16},{2,18},{4,20},{6,22},{8,24},{10,26},{12,28},{14,30},{16,0},... | collective-permute-start | bytes 393224 | tf_op jit(solution)/shard_map/ppermute | solution.py:126
  623.9 5.7 collective-permute-start.39
  (111 other events, 395.9 us)
Sparse Core Ops, SparseCore 0:
  17.9 101.6 all-gather.2
  121.8 117.4 all-gather.4
  277.3 170.7 reduce-scatter.1
